TPU v7x, 32 devices: a whole 2x2x4 slice. The times are simulated.
32 devices in a mesh: ctx: 16 (over z, y, core), fsdp: 2 (over x).
Axes of the slice: x: 2, y: 2, z: 4, core: 2. Of those that a mesh axis runs over, the one named last changes fastest.
Arguments:
- tokens: bfloat16 [2, 4096, 1024], P('fsdp', 'ctx'), may hold values from -6 to 6
- qkv_weight: bfloat16 [1024, 2048], P('fsdp'), may hold values from -0.1875 to 0.1875
- out_weight: bfloat16 [1024, 1024], P('fsdp'), may hold values from -1.5 to 1.5
- gate_up_weight: bfloat16 [1024, 2, 4608], P('fsdp'), may hold values from -0.1875 to 0.1875
- down_weight: bfloat16 [4608, 1024], P('fsdp'), may hold values from -0.1875 to 0.1875
- attn_gain: bfloat16 [1024], P('fsdp'), may hold values from 0.25 to 1.75
- ffn_gain: bfloat16 [1024], P('fsdp'), may hold values from 0.25 to 1.75
- query_gain: bfloat16 [64], P('fsdp'), may hold values from 0.796875 to 2
- key_gain: bfloat16 [64], P('fsdp'), may hold values from 0.796875 to 2
- seq_lengths: int32 [2, 3], P('fsdp'), may hold values from 1024 to 2048, as said below
- block_order: int32 [2, 32], P('fsdp'), may hold values from 0 to 31, as said below
- cotangent: bfloat16 [2, 4096, 1024], P('fsdp', 'ctx'), may hold values from -6 to 6
Outputs:
- output: bfloat16 [2, 4096, 1024], P('fsdp', 'ctx')
- input_grad: float32 [2, 4096, 1024], P('fsdp', 'ctx')
- grad_qkv: float32 [1024, 2048], P('fsdp')
- grad_out: float32 [1024, 1024], P('fsdp')
- grad_gate_up: float32 [1024, 2, 4608], P('fsdp')
- grad_down: float32 [4608, 1024], P('fsdp')
- grad_attn_gain: float32 [1024], P('fsdp')
- grad_ffn_gain: float32 [1024], P('fsdp')
- grad_query_gain: float32 [64], P('fsdp')
- grad_key_gain: float32 [64], P('fsdp')
Inputs may be any that keep to these rules, and one draw needn't show every extreme that they name: `seq_lengths`: the 3 lengths of a group add up to 4096; one of them is exactly 2048 and one is exactly 1024. `block_order`: each row is a permutation of the numbers 0 to 31.
All inputs are finite; a program needn't handle non-finite values.
Results may differ from a plain program's by a relative error of at most 0.03.
Values may be sent and summed in bfloat16 or wider, within the bound.
No kernel may reach another device: no remote copies, remote signals or barrier semaphores. Data moves between devices by JAX's collectives and lax.ppermute only.
A program may use at most 256 MiB of HBM per device.

v0:
```python
import jax
import jax.numpy as jnp
from jax import lax
from jax.sharding import PartitionSpec as P

HEADS = 16
KV_HEADS = 8
HD = 64
BLK = 128


EPSILON = 1e-05
ROPE_BASE = 1000000.0
NEGATIVE = -1e30


def shifted(block, axis, distance):
    devices = range(lax.axis_size(axis))
    route = [((i - distance) % len(devices), i) for i in devices]
    return lax.ppermute(block, axis, route)


def rms_scale(values):
    return lax.rsqrt(jnp.mean(values * values, axis=-1, keepdims=True) + EPSILON)


def rotate_half(values):
    half = values.shape[-1] // 2
    return jnp.concatenate([-values[..., half:], values[..., :half]], axis=-1)


def rotate_back(values):
    half = values.shape[-1] // 2
    return jnp.concatenate([values[..., half:], -values[..., :half]], axis=-1)


def norm_back(grad_normed, inputs, scale, gain):
    scaled = grad_normed * gain
    grad_in = scale * scaled - inputs * scale * scale * scale * jnp.mean(
        scaled * inputs, axis=-1, keepdims=True
    )
    return (grad_in, grad_normed * inputs * scale)


def slot_info(order_row, lengths_row, first, rows_here):
    slots = first + jnp.arange(rows_here, dtype=jnp.int32)
    table = (slots // BLK)[:, None] == jnp.arange(order_row.shape[0], dtype=jnp.int32)[None, :]
    packed = jnp.sum(jnp.where(table, order_row[None, :], 0), axis=1) * BLK + slots % BLK
    ends = jnp.cumsum(lengths_row)
    past = packed[:, None] >= ends[None, :]
    segment = jnp.sum(past.astype(jnp.int32), axis=1)
    local = packed - jnp.sum(jnp.where(past, lengths_row[None, :], 0), axis=1)
    return (packed, segment, local)


def on_device(
    tokens,
    qkv_weight,
    out_weight,
    gate_up_weight,
    down_weight,
    attn_gain,
    ffn_gain,
    query_gain,
    key_gain,
    seq_lengths,
    block_order,
    cotangent,
):
    inputs = tokens[0].astype(jnp.float32)
    rows_here = inputs.shape[0]
    ctx_size = lax.axis_size("ctx")
    ctx_index = lax.axis_index("ctx")
    per_group = HEADS // KV_HEADS
    q_width = HEADS * HD
    kv_width = KV_HEADS * HD
    order_row = block_order[0]
    lengths_row = seq_lengths[0]
    q_packed, q_segment, q_local = slot_info(
        order_row, lengths_row, ctx_index * rows_here, rows_here
    )
    frequency = ROPE_BASE ** (-2.0 * jnp.arange(HD // 2, dtype=jnp.float32) / HD)
    angle = q_local.astype(jnp.float32)[:, None] * frequency[None, :]
    cosine = jnp.concatenate([jnp.cos(angle), jnp.cos(angle)], axis=-1)[:, None, :]
    sine_table = jnp.concatenate([jnp.sin(angle), jnp.sin(angle)], axis=-1)[:, None, :]

    def fetch_attention():
        return (
            lax.all_gather(qkv_weight, "fsdp", axis=0, tiled=True),
            lax.all_gather(out_weight, "fsdp", axis=0, tiled=True),
            lax.all_gather(attn_gain, "fsdp", axis=0, tiled=True),
            lax.all_gather(ffn_gain, "fsdp", axis=0, tiled=True),
            lax.all_gather(query_gain, "fsdp", axis=0, tiled=True),
            lax.all_gather(key_gain, "fsdp", axis=0, tiled=True),
        )

    w_qkv, w_out, gain_attn, gain_ffn, gain_query, gain_key = fetch_attention()
    gain_attn = gain_attn.astype(jnp.float32)
    gain_ffn = gain_ffn.astype(jnp.float32)
    gain_query = gain_query.astype(jnp.float32)
    gain_key = gain_key.astype(jnp.float32)
    scale_one = rms_scale(inputs)
    normed = (inputs * scale_one * gain_attn).astype(jnp.bfloat16)
    projected = jnp.dot(normed, w_qkv, preferred_element_type=jnp.float32)
    q_raw = projected[:, :q_width].reshape(rows_here, HEADS, HD)
    k_raw = projected[:, q_width : q_width + kv_width].reshape(rows_here, KV_HEADS, HD)
    values_here = (
        projected[:, q_width + kv_width :].reshape(rows_here, KV_HEADS, HD).astype(jnp.bfloat16)
    )
    q_scale = rms_scale(q_raw)
    k_scale = rms_scale(k_raw)
    q_normed = q_raw * q_scale * gain_query
    k_normed = k_raw * k_scale * gain_key
    queries = (q_normed * cosine + rotate_half(q_normed) * sine_table).astype(jnp.bfloat16)
    keys_here = (k_normed * cosine + rotate_half(k_normed) * sine_table).astype(jnp.bfloat16)
    q_heads = jnp.transpose(queries.reshape(rows_here, KV_HEADS, per_group, HD), (1, 2, 0, 3))

    def scores_for(key_block, source):
        k_packed, k_segment, _ = slot_info(order_row, lengths_row, source * rows_here, rows_here)
        allowed = (q_segment[:, None] == k_segment[None, :]) & (
            k_packed[None, :] <= q_packed[:, None]
        )
        raw_scores = jnp.einsum(
            "hgqd,khd->hgqk", q_heads, key_block, preferred_element_type=jnp.float32
        ) * HD ** (-0.5)
        return (jnp.where(allowed[None, None], raw_scores, NEGATIVE), allowed)

    def absorb(state, key_block, value_block, source):
        top_old, total_old, summed_old = state
        masked, allowed = scores_for(key_block, source)
        top_new = jnp.maximum(top_old, jnp.max(masked, axis=-1))
        lifted = jnp.where(allowed[None, None], jnp.exp(masked - top_new[..., None]), 0.0)
        fade = jnp.exp(top_old - top_new)
        total_new = total_old * fade + jnp.sum(lifted, axis=-1)
        summed_new = summed_old * fade[..., None] + jnp.einsum(
            "hgqk,khd->hgqd",
            lifted.astype(jnp.bfloat16),
            value_block,
            preferred_element_type=jnp.float32,
        )
        return (top_new, total_new, summed_new)

    start_state = (
        jnp.full((KV_HEADS, per_group, rows_here), NEGATIVE, jnp.float32),
        jnp.zeros((KV_HEADS, per_group, rows_here), jnp.float32),
        jnp.zeros((KV_HEADS, per_group, rows_here, HD), jnp.float32),
    )
    state = absorb(start_state, keys_here, values_here, ctx_index)
    kept_depth = 1
    kept_keys = jnp.zeros((kept_depth,) + keys_here.shape, jnp.bfloat16).at[0].set(keys_here)
    kept_values = jnp.zeros((kept_depth,) + values_here.shape, jnp.bfloat16).at[0].set(values_here)

    def forward_step(step, carry):
        state, key_block, value_block, stored_keys, stored_values = carry
        key_block, value_block = shifted((key_block, value_block), "ctx", 1)
        source = (ctx_index - step + ctx_size) % ctx_size
        state = absorb(state, key_block, value_block, source)
        return (state, key_block, value_block, stored_keys, stored_values)

    state, _, _, kept_keys, kept_values = lax.fori_loop(
        1, ctx_size, forward_step, (state, keys_here, values_here, kept_keys, kept_values)
    )
    top, total, summed = state
    log_total = top + jnp.log(total)
    attn_heads = summed / total[..., None]
    attn_in = (
        jnp.transpose(attn_heads, (2, 0, 1, 3)).reshape(rows_here, q_width).astype(jnp.bfloat16)
    )
    h_one = inputs + jnp.dot(attn_in, w_out, preferred_element_type=jnp.float32)
    scale_two = rms_scale(h_one)
    normed_two = (h_one * scale_two * gain_ffn).astype(jnp.bfloat16)
    columns = normed_two
    gate_up = jnp.einsum(
        "tr,rgf->tgf",
        columns,
        lax.all_gather(gate_up_weight, "fsdp", axis=0, tiled=True),
        preferred_element_type=jnp.float32,
    )
    gate = gate_up[:, 0]
    upper = gate_up[:, 1]
    sigma = jax.nn.sigmoid(gate)
    hidden = (gate * sigma * upper).astype(jnp.bfloat16)
    columns = hidden
    ffn_out = jnp.dot(
        columns,
        lax.all_gather(down_weight, "fsdp", axis=0, tiled=True),
        preferred_element_type=jnp.float32,
    )
    output = (h_one + ffn_out).astype(jnp.bfloat16)
    d_out = cotangent[0].astype(jnp.float32)
    d_ffn = d_out.astype(jnp.bfloat16)
    d_hidden = lax.dot_general(
        d_ffn,
        lax.all_gather(down_weight, "fsdp", axis=0, tiled=True),
        (((1,), (1,)), ((), ())),
        preferred_element_type=jnp.float32,
    )
    d_gate = d_hidden * upper * sigma * (1.0 + gate * (1.0 - sigma))
    d_upper = d_hidden * gate * sigma
    d_gate_up = jnp.stack([d_gate, d_upper], axis=1).astype(jnp.bfloat16)
    d_normed_two = jnp.einsum(
        "tgf,rgf->tr",
        d_gate_up,
        lax.all_gather(gate_up_weight, "fsdp", axis=0, tiled=True),
        preferred_element_type=jnp.float32,
    )
    columns = normed_two
    grad_gate_up = lax.psum_scatter(
        jnp.einsum("tr,tgf->rgf", columns, d_gate_up, preferred_element_type=jnp.float32).astype(
            jnp.bfloat16
        ),
        "fsdp",
        scatter_dimension=0,
        tiled=True,
    )
    columns = hidden
    grad_down = lax.psum_scatter(
        lax.dot_general(
            columns, d_ffn, (((0,), (0,)), ((), ())), preferred_element_type=jnp.float32
        ).astype(jnp.bfloat16),
        "fsdp",
        scatter_dimension=0,
        tiled=True,
    )
    d_norm_two, ffn_gain_term = norm_back(d_normed_two, h_one, scale_two, gain_ffn)
    d_h_one = d_out + d_norm_two
    d_attn = d_h_one.astype(jnp.bfloat16)
    grad_out_here = lax.dot_general(
        attn_in, d_attn, (((0,), (0,)), ((), ())), preferred_element_type=jnp.float32
    )
    w_qkv, w_out, _, _, _, _ = fetch_attention()
    d_attn_in = lax.dot_general(
        d_attn, w_out, (((1,), (1,)), ((), ())), preferred_element_type=jnp.float32
    ).astype(jnp.bfloat16)
    d_heads = jnp.transpose(d_attn_in.reshape(rows_here, KV_HEADS, per_group, HD), (1, 2, 0, 3))
    delta = jnp.sum(d_heads.astype(jnp.float32) * attn_heads, axis=-1)

    def block_grads(key_block, value_block, source):
        masked, allowed = scores_for(key_block, source)
        shares = jnp.where(allowed[None, None], jnp.exp(masked - log_total[..., None]), 0.0)
        d_shares = jnp.einsum(
            "hgqd,khd->hgqk", d_heads, value_block, preferred_element_type=jnp.float32
        )
        d_scores = (shares * (d_shares - delta[..., None]) * HD ** (-0.5)).astype(jnp.bfloat16)
        d_query = jnp.einsum(
            "hgqk,khd->qhgd", d_scores, key_block, preferred_element_type=jnp.float32
        )
        d_key = jnp.einsum("hgqk,hgqd->khd", d_scores, q_heads, preferred_element_type=jnp.float32)
        d_value = jnp.einsum(
            "hgqk,hgqd->khd",
            shares.astype(jnp.bfloat16),
            d_heads,
            preferred_element_type=jnp.float32,
        )
        return (d_query, d_key, d_value)

    def pass_grads(d_key, d_value):
        return (
            shifted(d_key.astype(jnp.bfloat16), "ctx", 1).astype(d_key.dtype),
            shifted(d_value.astype(jnp.bfloat16), "ctx", 1).astype(d_value.dtype),
        )

    d_query, d_key, d_value = block_grads(keys_here, values_here, ctx_index)
    d_key, d_value = pass_grads(d_key, d_value)

    def backward_step(step, carry):
        d_query, d_key, d_value, key_block, value_block = carry
        key_block, value_block = shifted((key_block, value_block), "ctx", 1)
        source = (ctx_index - step + ctx_size) % ctx_size
        more_query, more_key, more_value = block_grads(key_block, value_block, source)
        d_key, d_value = pass_grads(d_key + more_key, d_value + more_value)
        return (d_query + more_query, d_key, d_value, key_block, value_block)

    d_query, d_key, d_value, _, _ = lax.fori_loop(
        1, ctx_size, backward_step, (d_query, d_key, d_value, keys_here, values_here)
    )
    d_query = d_query.reshape(rows_here, HEADS, HD)
    dq_normed = d_query * cosine + rotate_back(d_query * sine_table)
    dk_normed = d_key * cosine + rotate_back(d_key * sine_table)
    dq_raw, query_term = norm_back(dq_normed, q_raw, q_scale, gain_query)
    dk_raw, key_term = norm_back(dk_normed, k_raw, k_scale, gain_key)
    d_projected = jnp.concatenate(
        [
            dq_raw.reshape(rows_here, q_width),
            dk_raw.reshape(rows_here, kv_width),
            d_value.reshape(rows_here, kv_width),
        ],
        axis=1,
    ).astype(jnp.bfloat16)
    grad_qkv_here = lax.dot_general(
        normed, d_projected, (((0,), (0,)), ((), ())), preferred_element_type=jnp.float32
    )
    d_normed = lax.dot_general(
        d_projected, w_qkv, (((1,), (1,)), ((), ())), preferred_element_type=jnp.float32
    )
    d_norm_one, attn_gain_term = norm_back(d_normed, inputs, scale_one, gain_attn)
    d_inputs = d_h_one + d_norm_one
    shard_qkv, shard_out, shard_attn_gain, shard_ffn_gain, shard_query_gain, shard_key_gain = (
        lax.psum_scatter(
            grad_qkv_here.astype(jnp.bfloat16), "fsdp", scatter_dimension=0, tiled=True
        ).astype(jnp.float32),
        lax.psum_scatter(
            grad_out_here.astype(jnp.bfloat16), "fsdp", scatter_dimension=0, tiled=True
        ).astype(jnp.float32),
        lax.psum_scatter(
            jnp.sum(attn_gain_term, axis=0).astype(jnp.bfloat16),
            "fsdp",
            scatter_dimension=0,
            tiled=True,
        ).astype(jnp.float32),
        lax.psum_scatter(
            jnp.sum(ffn_gain_term, axis=0).astype(jnp.bfloat16),
            "fsdp",
            scatter_dimension=0,
            tiled=True,
        ).astype(jnp.float32),
        lax.psum_scatter(
            jnp.sum(query_term, axis=(0, 1)).astype(jnp.bfloat16),
            "fsdp",
            scatter_dimension=0,
            tiled=True,
        ).astype(jnp.float32),
        lax.psum_scatter(
            jnp.sum(key_term, axis=(0, 1)).astype(jnp.bfloat16),
            "fsdp",
            scatter_dimension=0,
            tiled=True,
        ).astype(jnp.float32),
    )
    summed_grads = (
        lax.psum(shard_qkv.astype(jnp.bfloat16), "ctx").astype(jnp.float32),
        lax.psum(shard_out.astype(jnp.bfloat16), "ctx").astype(jnp.float32),
        lax.psum(grad_gate_up, "ctx").astype(jnp.float32),
        lax.psum(grad_down, "ctx").astype(jnp.float32),
        lax.psum(shard_attn_gain.astype(jnp.bfloat16), "ctx").astype(jnp.float32),
        lax.psum(shard_ffn_gain.astype(jnp.bfloat16), "ctx").astype(jnp.float32),
        lax.psum(shard_query_gain.astype(jnp.bfloat16), "ctx").astype(jnp.float32),
        lax.psum(shard_key_gain.astype(jnp.bfloat16), "ctx").astype(jnp.float32),
    )
    return (
        output[None],
        d_inputs[None],
        summed_grads[0],
        summed_grads[1],
        summed_grads[2],
        summed_grads[3],
        summed_grads[4],
        summed_grads[5],
        summed_grads[6],
        summed_grads[7],
    )


def solution(mesh):
    return jax.shard_map(
        on_device,
        mesh=mesh,
        in_specs=(
            P("fsdp", "ctx", None),
            P("fsdp", None),
            P("fsdp", None),
            P("fsdp", None, None),
            P("fsdp", None),
            P("fsdp"),
            P("fsdp"),
            P("fsdp"),
            P("fsdp"),
            P("fsdp", None),
            P("fsdp", None),
            P("fsdp", "ctx", None),
        ),
        out_specs=(
            P("fsdp", "ctx", None),
            P("fsdp", "ctx", None),
            P("fsdp", None),
            P("fsdp", None),
            P("fsdp", None, None),
            P("fsdp", None),
            P("fsdp"),
            P("fsdp"),
            P("fsdp"),
            P("fsdp"),
        ),
        check_vma=False,
    )
```

profile of v0, /device:TPU:0, one launch (start us, length us, event | category | flops | bytes accessed | tf_op | source)
XLA Modules:
  0.0 1707.9 jit_solution(5730193455260130014)
XLA Ops:
  8.7 8.9 copy.106
  39.8 29.4 %all-gather.7.cloned.1.call-done = bf16[1024,2048]{1,0:T(8,128)(2,1)} async-done(((bf16[512,2048]{1,0:T(8,128)(2,1)}), bf16[1024,2048]{1,0:T(8,128)(2,1)}) %all-gather.7.cloned.1.call-update) | async-done | bytes 4194320 | tf_op jit(solution)/shard_map/all_gather | solution.py:89
  91.5 200.5 %while.48 = (s32[]{:T(128)}, f32[8,2,256]{2,1,0:T(2,128)S(1)}, f32[8,2,256]{2,1,0:T(2,128)}, f32[8,2,256,64]{2,3,1,0:T(8,128)S(1)}, bf16[256,8,64]{0,2,1:T(8,128...) while((s32[]{:T(128)}, f32[8,2,256]{2,1,0:T(2,128)S(1)}, ...), condition=%wide.region_15.16_spmd, body=%wide.region_10.15_spmd.sunk | while | flops 282830080 | bytes 19541576 | solution.py:160
  296.9 34.3 %all-gather.11.cloned.1.call-done = bf16[1024,2,4608]{2,0,1:T(8,128)(2,1)} async-done(((bf16[512,2,4608]{2,0,1:T(8,128)(2,1)}), bf16[1024,2,4608]{2,0,1:T(8,128)(2,1)}) %all-gather.11.cloned.1.call-update) | async-done | bytes 18874384 | tf_op jit(solution)/shard_map/all_gather | solution.py:176
  331.1 14.2 fusion.131
  345.3 105.2 %all-gather.13.cloned.1.call-done = bf16[4608,1024]{1,0:T(8,128)(2,1)} async-done(((bf16[2304,1024]{1,0:T(8,128)(2,1)}), bf16[4608,1024]{1,0:T(8,128)(2,1)}) %all-gather.13.cloned.1.call-update) | async-done | bytes 9437200 | tf_op jit(solution)/shard_map/all_gather | solution.py:186
  450.6 9.7 fusion.60
  460.3 23.2 %multiply_reduce_fusion.1 = (bf16[1024]{0:T(1024)(128)(2,1)}, f32[256]{0:T(256)S(1)}, f32[256,1024]{1,0:T(8,128)}) fusion(f32[256,1024]{1,0:T(8,128)S(1)} %get-tuple-element.927, f32[256]{0:T(256)S(1)} %add_rsqrt_fusion.2, f32[1024]{0:T(1024)S(1)} %bitcast.339, bf16[1024,2,4608]{2,0,1:T(8,128)(2,1)} %all-gather.11.cloned.1.call-done, ...), kind=kOutput, calls=%fused_computation.147 | convolution fusion | flops 4835769344 | bytes 25698304 | tf_op jit(solution)/shard_map/tgf,rgf->tr/dot_general | solution.py:201
  514.1 415.4 %while.49 = (s32[]{:T(128)}, f32[256,8,2,64]{0,3,2,1:T(8,128)S(1)}, f32[256,8,64]{0,2,1:T(8,128)S(1)}, f32[256,8,64]{0,2,1:T(8,128)}, bf16[256,8,64]{0,2,1:T(8,1...) while((s32[]{:T(128)}, f32[256,8,2,64]{0,3,2,1:T(8,128)S(1)}, ...), condition=%wide.region_22.23_spmd, body=%wide.region_19.22_spmd.sunk | while | flops 685999360 | bytes 36827404 | solution.py:274
  543.7 6.9 collective-permute-done.2
  571.4 6.9 collective-permute-done.2
  599.0 6.9 collective-permute-done.2
  626.7 6.9 collective-permute-done.2
  654.4 6.9 collective-permute-done.2
  682.1 6.9 collective-permute-done.2
  947.3 11.0 convolution_convert_fusion.1
  959.6 12.2 convolution_convert_fusion
  971.9 25.9 %reduce-scatter.5.cloned.1.call-done = bf16[512,2048]{1,0:T(8,128)(2,1)} async-done(((bf16[1024,2048]{1,0:T(8,128)(2,1)}), bf16[512,2048]{1,0:T(8,128)(2,1)}) %reduce-scatter.5.cloned.1.call-update) | async-done | bytes 2097168 | tf_op jit(solution)/shard_map/reduce_scatter | solution.py:299
  997.8 112.9 %reduce-scatter.11.cloned.1.call-done = bf16[2304,1024]{1,0:T(8,128)(2,1)} async-done(((bf16[4608,1024]{1,0:T(8,128)(2,1)}), bf16[2304,1024]{1,0:T(8,128)(2,1)}) %reduce-scatter.11.cloned.1.call-update) | async-done | bytes 4718608 | tf_op jit(solution)/shard_map/reduce_scatter | solution.py:217
  1110.7 214.6 %reduce-scatter.9.cloned.1.call-done = bf16[512,2,4608]{2,0,1:T(8,128)(2,1)} async-done(((bf16[1024,2,4608]{2,0,1:T(8,128)(2,1)}), bf16[512,2,4608]{2,0,1:T(8,128)(2,1)}) %reduce-scatter.9.cloned.1.call-update) | async-done | bytes 9437200 | tf_op jit(solution)/shard_map/reduce_scatter | solution.py:208
  1326.4 10.0 fusion.83
  1345.7 34.6 %all-reduce.6 = (bf16[512]{0:T(512)(128)(2,1)S(1)}, bf16[512]{0:T(512)(128)(2,1)S(1)}, bf16[32]{0:T(256)(128)(2,1)S(1)}, bf16[32]{0:T(256)(128)(2,1)S(1)}) all-reduce(bf16[512]{0:T(512)(128)(2,1)S(1)} %dynamic-slice.3, bf16[512]{0:T(512)(128)(2,1)S(1)} %dynamic-slice.5, ...), channel_id=1, replica_groups=mesh['ctx'=16,'fsdp'=2] {'ctx'}, use_global_device_ids=true, to_apply=%region_36.37 | all-reduce | flops 1088 | bytes 4352 | tf_op jit(solution)/shard_map/psum | solution.py:335
  1383.9 253.4 %all-reduce.12.cloned.1.call-done = (bf16[512,2,4608]{2,0,1:T(8,128)(2,1)}, bf16[512,2048]{1,0:T(8,128)(2,1)}, bf16[512,1024]{1,0:T(8,128)(2,1)}, bf16[2304,1024]{1,0:T(8,128)(2,1)}) async-done(((bf16[512,2,4608]{2,0,1:T(8,128)(2,1)}, bf16[512,2048]{1,0:T(8,128)(2,1)}, bf16[512,1024]{1,0:T(8,128)(2,1)}, bf16[2304,1024]{1,0:T(8,128)(2,1)}), (bf16[512,2,4608]{2,0,1:T(8,128)(2,1)}, ...) | async-done | bytes 17301520 | tf_op jit(solution)/shard_map/psum | solution.py:333
  1644.9 51.1 %copy.124 = f32[512,2,4608]{2,1,0:T(2,128)} copy(bf16[512,2,4608]{2,0,1:T(8,128)(2,1)S(1)} %copy-done.8) | data formatting | bytes 28311552
  (1051 shorter events, 694.4 us)
Async XLA Ops:
  7.2 62.0 %all-gather.7.cloned.1.call-start = ((), (), s32[]{:S(2)}) async-start(), calls=%async_computation.4 | async-start | bytes 6291456 | tf_op jit(solution)/shard_map/all_gather | solution.py:89
  7.9 286.4 %all-gather.9.cloned.1.call-start = ((), (), s32[]{:S(2)}) async-start(), calls=%async_computation.5 | async-start | bytes 3145728 | tf_op jit(solution)/shard_map/all_gather | solution.py:90
  8.7 322.5 %all-gather.11.cloned.1.call-start = ((), (), s32[]{:S(2)}) async-start(), calls=%async_computation.6 | async-start | bytes 28311552 | tf_op jit(solution)/shard_map/all_gather | solution.py:176
  17.7 432.9 %all-gather.13.cloned.1.call-start = ((), (), s32[]{:S(2)}) async-start(), calls=%async_computation.7 | async-start | bytes 14155776 | tf_op jit(solution)/shard_map/all_gather | solution.py:186
  18.3 953.6 %reduce-scatter.7.cloned.1.call-start = ((), (), s32[]{:S(2)}) async-start(), calls=%async_computation.9 | async-start | bytes 3145728 | tf_op jit(solution)/shard_map/reduce_scatter | solution.py:302
  503.6 494.2 %reduce-scatter.5.cloned.1.call-start = ((), (), s32[]{:S(2)}) async-start(), calls=%async_computation.8 | async-start | bytes 6291456 | tf_op jit(solution)/shard_map/reduce_scatter | solution.py:299
  514.2 11.6 collective-permute-start.3
  541.9 11.6 collective-permute-start.3
  569.6 11.6 collective-permute-start.3
  597.3 11.6 collective-permute-start.3
  624.9 11.6 collective-permute-start.3
  652.6 11.6 collective-permute-start.3
  680.3 11.6 collective-permute-start.3
  708.0 11.6 collective-permute-start.3
  735.7 11.6 collective-permute-start.3
  763.4 11.6 collective-permute-start.3
  791.1 11.6 collective-permute-start.3
  818.8 11.6 collective-permute-start.3
  846.4 11.6 collective-permute-start.3
  874.1 11.6 collective-permute-start.3
  901.8 11.6 collective-permute-start.3
  947.3 163.4 %reduce-scatter.11.cloned.1.call-start = ((), (), s32[]{:S(2)}) async-start(), calls=%async_computation.11 | async-start | bytes 14155776 | tf_op jit(solution)/shard_map/reduce_scatter | solution.py:217
  958.4 366.9 %reduce-scatter.9.cloned.1.call-start = ((), (), s32[]{:S(2)}) async-start(), calls=%async_computation.10 | async-start | bytes 28311552 | tf_op jit(solution)/shard_map/reduce_scatter | solution.py:208
  971.8 665.5 %all-reduce.12.cloned.1.call-start = ((), (), s32[]{:S(2)}) async-start(), calls=%async_computation.12 | async-start | bytes 34603008 | tf_op jit(solution)/shard_map/psum | solution.py:333
  (247 other events, 3253.0 us)
Sparse Core Ops, SparseCore 0:
  9.6 59.6 all-gather.6
  70.7 33.1 all-gather.8
  106.0 225.0 all-gather.10
  332.5 117.9 all-gather.12
  503.7 30.9 reduce-scatter.6
  947.4 50.3 reduce-scatter.4
  1000.1 110.5 reduce-scatter.10
  1113.5 211.6 reduce-scatter.8
  1329.7 307.5 all-reduce.11
where the time goes:
time: 1720 us; the launch traced here: 1710 us
  waiting for transfers between devices  1120 us (65%)
  matrix products  244 us (14%)
  local copies, waits for them, and re-layouts  132 us (8%)
  other arithmetic  127 us (7%)
  blocking collectives  54.2 us (3%)
    ppermute x92, waiting for transfers between devices, shifted(): return lax.ppermute(block, axis, route)  345 us
    psum x1, waiting for transfers between devices, on_device(): lax.psum(grad_gate_up, 'ctx').astype(jnp.float32)  253 us
    reduce_scatter x1, waiting for transfers between devices, on_device(): lax.psum_scatter(jnp.einsum('tr,tgf->rgf', columns, d_gate_up, preferred_...  215 us
    reduce_scatter x1, waiting for transfers between devices, on_device(): lax.psum_scatter(lax.dot_general(columns, d_ffn, (((0,), (0,)), ((), ()))...  113 us
    all_gather x1, waiting for transfers between devices, on_device(): lax.all_gather(down_weight, 'fsdp', axis=0, tiled=True)  105 us
    unnamed x142, local copies, waits for them, and re-layouts  71 us
    dot_general x16, matrix products, block_grads(): jnp.einsum('hgqd,khd->hgqk', d_heads, value_block, preferred_element_type...  52.8 us
    while x285, local copies, waits for them, and re-layouts  47.2 us
  transfers between devices with their start and end apart: 101, of which 99 were waited for; matrix products, arithmetic and copies ran while one was open for 22% of the time, Pallas kernels for 0%

commit v1 on v0

v1 whole, which is shorter than its diff:
```python
import functools

import jax
import jax.numpy as jnp
from jax import lax
from jax.experimental import pallas as pl
from jax.experimental.pallas import tpu as pltpu
from jax.sharding import PartitionSpec as P

HEADS = 16
KV_HEADS = 8
HD = 64
BLK = 128
TILE = 256


EPSILON = 1e-05
ROPE_BASE = 1000000.0
LOG2E = 1.4426950408889634
SCORE_SCALE = LOG2E * HD ** (-0.5)


def rms_scale(values, axis=-1):
    return lax.rsqrt(jnp.mean(values * values, axis=axis, keepdims=True) + EPSILON)


def norm_back(grad_normed, inputs, scale, gain, axis=-1):
    scaled = grad_normed * gain
    grad_in = scale * scaled - inputs * scale * scale * scale * jnp.mean(
        scaled * inputs, axis=axis, keepdims=True
    )
    return (grad_in, grad_normed * inputs * scale)


def rope(values, cosine, sine):
    half = HD // 2
    first, second = values[:, :half], values[:, half:]
    return jnp.concatenate([first * cosine - second * sine, second * cosine + first * sine], axis=1)


def rope_back(values, cosine, sine):
    half = HD // 2
    first, second = values[:, :half], values[:, half:]
    return jnp.concatenate([first * cosine + second * sine, second * cosine - first * sine], axis=1)


def starts_of(packed, lengths_row):
    ends = jnp.cumsum(lengths_row)
    past = packed[:, None] >= ends[None, :]
    return jnp.sum(jnp.where(past, lengths_row[None, :], 0), axis=1)


def block_tables(order, lengths_row):
    count = order.shape[0]
    rank = jnp.sum((order[None, :] < order[:, None]).astype(jnp.int32), axis=1)
    hit = rank[None, :] == jnp.arange(count, dtype=jnp.int32)[:, None]
    slot = jnp.sum(jnp.where(hit, jnp.arange(count, dtype=jnp.int32)[None, :], 0), axis=1)
    block = jnp.sum(jnp.where(hit, order[None, :], 0), axis=1)
    place = (block[:, None] * BLK + jnp.arange(BLK, dtype=jnp.int32)[None, :]).reshape(-1)
    return (slot, place, starts_of(place, lengths_row))


def attend_kernel(
    q_slot, kv_slot, first, last, qkv_ref, place_ref, start_ref,
    out_ref, q_ref, qt_ref, k_ref, kt_ref, v_ref, ot_ref, total_ref, vt_ref
):
    per_device = qkv_ref.shape[2] // BLK
    kv_blocks = k_ref.shape[0] // BLK
    q_blocks = q_ref.shape[0] // BLK

    def piece(slot, lower):
        return qkv_ref[
            slot // per_device,
            lower : lower + HD,
            pl.ds(pl.multiple_of((slot % per_device) * BLK, BLK), BLK),
        ]

    for i in range(kv_blocks):
        here = slice(i * BLK, (i + 1) * BLK)
        keys = piece(kv_slot[i], HD)
        kt_ref[:, here] = keys
        k_ref[here, :] = keys.T
        values = piece(kv_slot[i], 2 * HD)
        vt_ref[:, here] = values
        v_ref[here, :] = values.T
    for i in range(q_blocks):
        here = slice(i * BLK, (i + 1) * BLK)
        queries = piece(q_slot[i], 0)
        qt_ref[:, here] = queries
        q_ref[here, :] = queries.T
    if q_blocks < kv_blocks:
        out_ref[...] = jnp.zeros_like(out_ref)

    def tile(i, carry):
        rows = pl.ds(pl.multiple_of(i * TILE, TILE), TILE)
        queries = qt_ref[:, rows]
        place = place_ref[:, rows]
        start = start_ref[:, rows]

        def step(j, state):
            total, summed = state
            at = pl.multiple_of(j * TILE, TILE)
            scores = jnp.dot(
                k_ref[pl.ds(at, TILE), :], queries, preferred_element_type=jnp.float32
            )
            key_place = lax.broadcasted_iota(jnp.int32, (TILE, TILE), 0) + at
            allowed = (key_place <= place) & (key_place >= start)
            lifted = jnp.where(allowed, jnp.exp2(scores * SCORE_SCALE), 0.0)
            total = total + jnp.sum(lifted, axis=0, keepdims=True)
            summed = summed + jnp.dot(
                vt_ref[:, pl.ds(at, TILE)],
                lifted.astype(jnp.bfloat16),
                preferred_element_type=jnp.float32,
            )
            return (total, summed)

        total, summed = lax.fori_loop(
            first[i],
            last[i],
            step,
            (jnp.zeros((1, TILE), jnp.float32), jnp.zeros((HD, TILE), jnp.float32)),
        )
        attn = summed / total
        ot_ref[:, rows] = attn
        total_ref[:, rows] = jnp.log(total) * LOG2E
        rounded = attn.astype(jnp.bfloat16)
        for part in range(TILE // BLK):
            slot = q_slot[i * (TILE // BLK) + part]
            out_ref[
                slot // per_device,
                :,
                pl.ds(pl.multiple_of((slot % per_device) * BLK, BLK), BLK),
            ] = rounded[:, part * BLK : (part + 1) * BLK]
        return carry

    lax.fori_loop(0, q_blocks * BLK // TILE, tile, 0)


def attend_back_kernel(
    q_slot, kv_slot, first, last, d_ref, place_ref, start_ref,
    q_ref, qt_ref, k_ref, kt_ref, v_ref, ot_ref, total_ref,
    out_ref, dt_ref, do_ref, dk_ref, dv_ref
):
    per_device = d_ref.shape[2] // BLK
    kv_blocks = k_ref.shape[0] // BLK
    q_blocks = q_ref.shape[0] // BLK

    def lanes(slot):
        return pl.ds(pl.multiple_of((slot % per_device) * BLK, BLK), BLK)

    for i in range(q_blocks):
        here = slice(i * BLK, (i + 1) * BLK)
        slot = q_slot[i]
        grads = d_ref[slot // per_device, :, lanes(slot)]
        dt_ref[:, here] = grads
        do_ref[here, :] = grads.T
    dk_ref[...] = jnp.zeros_like(dk_ref)
    dv_ref[...] = jnp.zeros_like(dv_ref)
    if q_blocks < kv_blocks:
        out_ref[...] = jnp.zeros_like(out_ref)

    def tile(i, carry):
        rows = pl.ds(pl.multiple_of(i * TILE, TILE), TILE)
        queries = qt_ref[:, rows]
        grads = dt_ref[:, rows]
        place = place_ref[:, rows]
        start = start_ref[:, rows]
        delta = jnp.sum(grads.astype(jnp.float32) * ot_ref[:, rows], axis=0, keepdims=True)
        total = total_ref[:, rows]

        def step(j, d_query):
            at = pl.multiple_of(j * TILE, TILE)
            here = pl.ds(at, TILE)
            scores = jnp.dot(k_ref[here, :], queries, preferred_element_type=jnp.float32)
            key_place = lax.broadcasted_iota(jnp.int32, (TILE, TILE), 0) + at
            allowed = (key_place <= place) & (key_place >= start)
            shares = jnp.where(allowed, jnp.exp2(scores * SCORE_SCALE - total), 0.0)
            d_shares = jnp.dot(v_ref[here, :], grads, preferred_element_type=jnp.float32)
            d_scores = (shares * (d_shares - delta)).astype(jnp.bfloat16)
            dv_ref[here, :] += jnp.dot(
                shares.astype(jnp.bfloat16), do_ref[rows, :], preferred_element_type=jnp.float32
            )
            dk_ref[here, :] += jnp.dot(
                d_scores, q_ref[rows, :], preferred_element_type=jnp.float32
            )
            return d_query + jnp.dot(
                kt_ref[:, here], d_scores, preferred_element_type=jnp.float32
            )

        d_query = lax.fori_loop(first[i], last[i], step, jnp.zeros((HD, TILE), jnp.float32))
        rounded = (d_query * HD ** (-0.5)).astype(jnp.bfloat16)
        for part in range(TILE // BLK):
            slot = q_slot[i * (TILE // BLK) + part]
            out_ref[slot // per_device, 0:HD, lanes(slot)] = rounded[
                :, part * BLK : (part + 1) * BLK
            ]
        return carry

    lax.fori_loop(0, q_blocks * BLK // TILE, tile, 0)
    for i in range(kv_blocks):
        here = slice(i * BLK, (i + 1) * BLK)
        slot = kv_slot[i]
        out_ref[slot // per_device, HD : 2 * HD, lanes(slot)] = (
            (dk_ref[here, :] * HD ** (-0.5)).T.astype(jnp.bfloat16)
        )
        out_ref[slot // per_device, 2 * HD : 3 * HD, lanes(slot)] = (
            dv_ref[here, :].T.astype(jnp.bfloat16)
        )


def kernel_call(kernel, tables, arrays, outs, scratch):
    smem = pl.BlockSpec(memory_space=pltpu.SMEM)
    vmem = pl.BlockSpec(memory_space=pltpu.VMEM)
    return pl.pallas_call(
        kernel,
        out_shape=outs,
        in_specs=[smem] * len(tables) + [vmem] * len(arrays),
        out_specs=[vmem] * len(outs),
        scratch_shapes=scratch,
        compiler_params=pltpu.CompilerParams(vmem_limit_bytes=48 * 1024 * 1024),
    )(*tables, *arrays)


def on_device(
    tokens,
    qkv_weight,
    out_weight,
    gate_up_weight,
    down_weight,
    attn_gain,
    ffn_gain,
    query_gain,
    key_gain,
    seq_lengths,
    block_order,
    cotangent,
):
    inputs = tokens[0].astype(jnp.float32)
    rows_here = inputs.shape[0]
    ctx_size = lax.axis_size("ctx")
    ctx_index = lax.axis_index("ctx")
    per_group = HEADS // KV_HEADS
    q_width = HEADS * HD
    kv_width = KV_HEADS * HD
    order_row = block_order[0]
    lengths_row = seq_lengths[0]
    slots = jnp.arange(rows_here, dtype=jnp.int32) // BLK + ctx_index * (rows_here // BLK)
    table = slots[:, None] == jnp.arange(order_row.shape[0], dtype=jnp.int32)[None, :]
    packed = (
        jnp.sum(jnp.where(table, order_row[None, :], 0), axis=1) * BLK
        + jnp.arange(rows_here, dtype=jnp.int32) % BLK
    )
    local = packed - starts_of(packed, lengths_row)
    frequency = ROPE_BASE ** (-2.0 * jnp.arange(HD // 2, dtype=jnp.float32) / HD)
    angle = frequency[:, None] * local.astype(jnp.float32)[None, :]
    cosine = jnp.cos(angle)[None]
    sine = jnp.sin(angle)[None]
    bf16, f32 = jnp.bfloat16, jnp.float32
    parts = ctx_size // HEADS
    part = ctx_index // HEADS
    part_blocks = HEADS * rows_here // BLK
    q_order = lax.dynamic_slice_in_dim(order_row, part * part_blocks, part_blocks)
    q_slot, q_place, q_start = block_tables(q_order, lengths_row)
    q_slot = q_slot + part * part_blocks
    kv_slot, _, _ = block_tables(order_row, lengths_row)
    first = jnp.min(q_start.reshape(-1, TILE), axis=1) // TILE
    last = jnp.max(q_place.reshape(-1, TILE), axis=1) // TILE + 1
    tables = (q_slot, kv_slot, first, last)
    q_rows, kv_rows = part_blocks * BLK, order_row.shape[0] * BLK

    def fetch_attention():
        return (
            lax.all_gather(qkv_weight, "fsdp", axis=0, tiled=True),
            lax.all_gather(out_weight, "fsdp", axis=0, tiled=True),
            lax.all_gather(attn_gain, "fsdp", axis=0, tiled=True),
            lax.all_gather(ffn_gain, "fsdp", axis=0, tiled=True),
            lax.all_gather(query_gain, "fsdp", axis=0, tiled=True),
            lax.all_gather(key_gain, "fsdp", axis=0, tiled=True),
        )

    w_qkv, w_out, gain_attn, gain_ffn, gain_query, gain_key = fetch_attention()
    gain_attn = gain_attn.astype(jnp.float32)
    gain_ffn = gain_ffn.astype(jnp.float32)
    gain_query = gain_query.astype(jnp.float32)
    gain_key = gain_key.astype(jnp.float32)
    scale_one = rms_scale(inputs)
    normed = (inputs * scale_one * gain_attn).astype(jnp.bfloat16)
    projected = lax.dot_general(
        w_qkv, normed, (((0,), (1,)), ((), ())), preferred_element_type=f32
    )
    q_raw = projected[:q_width].reshape(HEADS, HD, rows_here)
    k_raw = projected[q_width : q_width + kv_width].reshape(KV_HEADS, HD, rows_here)
    values_here = projected[q_width + kv_width :].reshape(KV_HEADS, HD, rows_here).astype(bf16)
    q_scale = rms_scale(q_raw, 1)
    k_scale = rms_scale(k_raw, 1)
    column_query, column_key = gain_query[:, None], gain_key[:, None]
    queries = rope(q_raw * q_scale * column_query, cosine, sine).astype(bf16)
    keys_here = rope(k_raw * k_scale * column_key, cosine, sine).astype(bf16)
    sent = jnp.concatenate(
        [queries, jnp.repeat(keys_here, per_group, 0), jnp.repeat(values_here, per_group, 0)], axis=1
    )
    sent = jnp.concatenate([sent] * parts, axis=0)
    got = lax.all_to_all(sent, "ctx", 0, 0, tiled=True)
    q_place, q_start = q_place[None], q_start[None]
    shape = jax.ShapeDtypeStruct
    attn_sent, *held = kernel_call(
        attend_kernel,
        tables,
        (got, q_place, q_start),
        [
            shape((ctx_size, HD, rows_here), bf16),
            shape((q_rows, HD), bf16),
            shape((HD, q_rows), bf16),
            shape((kv_rows, HD), bf16),
            shape((HD, kv_rows), bf16),
            shape((kv_rows, HD), bf16),
            shape((HD, q_rows), f32),
            shape((1, q_rows), f32),
        ],
        [pltpu.VMEM((HD, kv_rows), bf16)],
    )
    attn_in = lax.dynamic_slice_in_dim(
        lax.all_to_all(attn_sent, "ctx", 0, 0, tiled=True), part * HEADS, HEADS
    ).reshape(q_width, rows_here)
    h_one = inputs + lax.dot_general(
        attn_in, w_out, (((0,), (0,)), ((), ())), preferred_element_type=f32
    )
    scale_two = rms_scale(h_one)
    normed_two = (h_one * scale_two * gain_ffn).astype(jnp.bfloat16)
    columns = normed_two
    gate_up = jnp.einsum(
        "tr,rgf->tgf",
        columns,
        lax.all_gather(gate_up_weight, "fsdp", axis=0, tiled=True),
        preferred_element_type=jnp.float32,
    )
    gate = gate_up[:, 0]
    upper = gate_up[:, 1]
    sigma = jax.nn.sigmoid(gate)
    hidden = (gate * sigma * upper).astype(jnp.bfloat16)
    columns = hidden
    ffn_out = jnp.dot(
        columns,
        lax.all_gather(down_weight, "fsdp", axis=0, tiled=True),
        preferred_element_type=jnp.float32,
    )
    output = (h_one + ffn_out).astype(jnp.bfloat16)
    d_out = cotangent[0].astype(jnp.float32)
    d_ffn = d_out.astype(jnp.bfloat16)
    d_hidden = lax.dot_general(
        d_ffn,
        lax.all_gather(down_weight, "fsdp", axis=0, tiled=True),
        (((1,), (1,)), ((), ())),
        preferred_element_type=jnp.float32,
    )
    d_gate = d_hidden * upper * sigma * (1.0 + gate * (1.0 - sigma))
    d_upper = d_hidden * gate * sigma
    d_gate_up = jnp.stack([d_gate, d_upper], axis=1).astype(jnp.bfloat16)
    d_normed_two = jnp.einsum(
        "tgf,rgf->tr",
        d_gate_up,
        lax.all_gather(gate_up_weight, "fsdp", axis=0, tiled=True),
        preferred_element_type=jnp.float32,
    )
    columns = normed_two
    grad_gate_up = lax.psum_scatter(
        jnp.einsum("tr,tgf->rgf", columns, d_gate_up, preferred_element_type=jnp.float32).astype(
            jnp.bfloat16
        ),
        "fsdp",
        scatter_dimension=0,
        tiled=True,
    )
    columns = hidden
    grad_down = lax.psum_scatter(
        lax.dot_general(
            columns, d_ffn, (((0,), (0,)), ((), ())), preferred_element_type=jnp.float32
        ).astype(jnp.bfloat16),
        "fsdp",
        scatter_dimension=0,
        tiled=True,
    )
    d_norm_two, ffn_gain_term = norm_back(d_normed_two, h_one, scale_two, gain_ffn)
    d_h_one = d_out + d_norm_two
    d_attn = d_h_one.astype(jnp.bfloat16)
    grad_out_here = jnp.dot(attn_in, d_attn, preferred_element_type=f32)
    d_heads = lax.dot_general(
        w_out, d_attn, (((1,), (1,)), ((), ())), preferred_element_type=f32
    ).astype(bf16)
    d_heads = jnp.concatenate([d_heads.reshape(HEADS, HD, rows_here)] * parts, axis=0)
    d_got = lax.all_to_all(d_heads, "ctx", 0, 0, tiled=True)
    (d_sent,) = kernel_call(
        attend_back_kernel,
        tables,
        (d_got, q_place, q_start, *held),
        [shape((ctx_size, 3 * HD, rows_here), bf16)],
        [
            pltpu.VMEM((HD, q_rows), bf16),
            pltpu.VMEM((q_rows, HD), bf16),
            pltpu.VMEM((kv_rows, HD), f32),
            pltpu.VMEM((kv_rows, HD), f32),
        ],
    )
    d_back = lax.all_to_all(d_sent, "ctx", 0, 0, tiled=True)
    d_query = lax.dynamic_slice_in_dim(d_back[:, :HD], part * HEADS, HEADS).astype(f32)
    d_key_value = jnp.sum(
        d_back[:, HD:].reshape(parts, KV_HEADS, per_group, 2 * HD, rows_here).astype(f32),
        axis=(0, 2),
    )
    dq_normed = rope_back(d_query, cosine, sine)
    dk_normed = rope_back(d_key_value[:, :HD], cosine, sine)
    dq_raw, query_term = norm_back(dq_normed, q_raw, q_scale, column_query, 1)
    dk_raw, key_term = norm_back(dk_normed, k_raw, k_scale, column_key, 1)
    d_projected = jnp.concatenate(
        [
            dq_raw.reshape(q_width, rows_here).astype(bf16),
            dk_raw.reshape(kv_width, rows_here).astype(bf16),
            d_key_value[:, HD:].reshape(kv_width, rows_here).astype(bf16),
        ],
        axis=0,
    )
    grad_qkv_here = lax.dot_general(
        normed, d_projected, (((0,), (1,)), ((), ())), preferred_element_type=f32
    )
    d_normed = lax.dot_general(
        d_projected, w_qkv, (((0,), (1,)), ((), ())), preferred_element_type=f32
    )
    d_norm_one, attn_gain_term = norm_back(d_normed, inputs, scale_one, gain_attn)
    d_inputs = d_h_one + d_norm_one
    shard_qkv, shard_out, shard_attn_gain, shard_ffn_gain, shard_query_gain, shard_key_gain = (
        lax.psum_scatter(
            grad_qkv_here.astype(jnp.bfloat16), "fsdp", scatter_dimension=0, tiled=True
        ).astype(jnp.float32),
        lax.psum_scatter(
            grad_out_here.astype(jnp.bfloat16), "fsdp", scatter_dimension=0, tiled=True
        ).astype(jnp.float32),
        lax.psum_scatter(
            jnp.sum(attn_gain_term, axis=0).astype(jnp.bfloat16),
            "fsdp",
            scatter_dimension=0,
            tiled=True,
        ).astype(jnp.float32),
        lax.psum_scatter(
            jnp.sum(ffn_gain_term, axis=0).astype(jnp.bfloat16),
            "fsdp",
            scatter_dimension=0,
            tiled=True,
        ).astype(jnp.float32),
        lax.psum_scatter(
            jnp.sum(query_term, axis=(0, 2)).astype(jnp.bfloat16),
            "fsdp",
            scatter_dimension=0,
            tiled=True,
        ).astype(jnp.float32),
        lax.psum_scatter(
            jnp.sum(key_term, axis=(0, 2)).astype(jnp.bfloat16),
            "fsdp",
            scatter_dimension=0,
            tiled=True,
        ).astype(jnp.float32),
    )
    summed_grads = (
        lax.psum(shard_qkv.astype(jnp.bfloat16), "ctx").astype(jnp.float32),
        lax.psum(shard_out.astype(jnp.bfloat16), "ctx").astype(jnp.float32),
        lax.psum(grad_gate_up, "ctx").astype(jnp.float32),
        lax.psum(grad_down, "ctx").astype(jnp.float32),
        lax.psum(shard_attn_gain.astype(jnp.bfloat16), "ctx").astype(jnp.float32),
        lax.psum(shard_ffn_gain.astype(jnp.bfloat16), "ctx").astype(jnp.float32),
        lax.psum(shard_query_gain.astype(jnp.bfloat16), "ctx").astype(jnp.float32),
        lax.psum(shard_key_gain.astype(jnp.bfloat16), "ctx").astype(jnp.float32),
    )
    return (
        output[None],
        d_inputs[None],
        summed_grads[0],
        summed_grads[1],
        summed_grads[2],
        summed_grads[3],
        summed_grads[4],
        summed_grads[5],
        summed_grads[6],
        summed_grads[7],
    )


def solution(mesh):
    return jax.shard_map(
        on_device,
        mesh=mesh,
        in_specs=(
            P("fsdp", "ctx", None),
            P("fsdp", None),
            P("fsdp", None),
            P("fsdp", None, None),
            P("fsdp", None),
            P("fsdp"),
            P("fsdp"),
            P("fsdp"),
            P("fsdp"),
            P("fsdp", None),
            P("fsdp", None),
            P("fsdp", "ctx", None),
        ),
        out_specs=(
            P("fsdp", "ctx", None),
            P("fsdp", "ctx", None),
            P("fsdp", None),
            P("fsdp", None),
            P("fsdp", None, None),
            P("fsdp", None),
            P("fsdp"),
            P("fsdp"),
            P("fsdp"),
            P("fsdp"),
        ),
        check_vma=False,
    )
```

time: 1720 us -> 1360 us (0.79)
  matrix products: 244 us -> 86.8 us
  waiting for transfers between devices: 1120 us -> 991 us
  other arithmetic: 127 us -> 28.7 us
  Pallas kernels: 0 us -> 46.5 us
  local copies, waits for them, and re-layouts: 132 us -> 90.9 us
  blocking collectives: 54.2 us -> 74.4 us
    ppermute x92 -> x0, waiting for transfers between devices: 345 us -> none  [shifted(): return lax.ppermute(block, axis, route)]
    dot_general x117 -> x6, matrix products: 164 us -> 22.1 us  [the longest x1 4.55 us: on_device(): lax.dot_general(normed, d_projected, (((0,), (1,)), ((), ())), preferred_...]
    all_gather x1, waiting for transfers between devices: 34.3 us -> 163 us  [on_device(): lax.all_gather(gate_up_weight, 'fsdp', axis=0, tiled=True)]
    all_to_all x0 -> x3, waiting for transfers between devices: none -> 66.4 us  [the longest x1 30.9 us: on_device(): got = lax.all_to_all(sent, 'ctx', 0, 0, tiled=True)]
    reduce_sum x85 -> x13, other arithmetic: 58.1 us -> 5.19 us  [the longest x2 2.5 us: on_device(): jnp.sum(query_term, axis=(0, 2)).astype(jnp.bfloat16)]
    while x285 -> x0, local copies, waits for them, and re-layouts: 47.2 us -> none
    pallas_call x0 -> x2, Pallas kernels: none -> 46.5 us  [kernel_call(): pl.pallas_call(kernel, out_shape=outs, in_specs=[smem] * len(tables) + [v...]
    and x31 -> x0, other arithmetic: 25.3 us -> none  [scores_for(): (q_segment[:, None] == k_segment[None, :]) & (k_packed[None, :] <= q_pack...]
  transfers between devices with their start and end apart: 101 -> 12, of which waited for: 99 -> 10; matrix products, arithmetic and copies ran while one was open for 22% -> 8% of each run, Pallas kernels for 0% -> 2%
where the time goes in v1:
time: 1360 us; the launch traced here: 1350 us
  waiting for transfers between devices  991 us (73%)
  local copies, waits for them, and re-layouts  90.9 us (7%)
  matrix products  86.8 us (6%)
  blocking collectives  74.4 us (5%)
  Pallas kernels  46.5 us (3%)
  other arithmetic  28.7 us (2%)
  starting transfers between devices  19.9 us (1%)
  between operations  17 us (1%)
    psum x1, waiting for transfers between devices, on_device(): lax.psum(grad_gate_up, 'ctx').astype(jnp.float32)  253 us
    reduce_scatter x1, waiting for transfers between devices, on_device(): lax.psum_scatter(jnp.einsum('tr,tgf->rgf', columns, d_gate_up, preferred_...  215 us
    all_gather x1, waiting for transfers between devices, on_device(): lax.all_gather(gate_up_weight, 'fsdp', axis=0, tiled=True)  163 us
    reduce_scatter x1, waiting for transfers between devices, on_device(): lax.psum_scatter(lax.dot_general(columns, d_ffn, (((0,), (0,)), ((), ()))...  113 us
    all_gather x1, waiting for transfers between devices, on_device(): lax.all_gather(down_weight, 'fsdp', axis=0, tiled=True)  107 us
    unnamed x89, local copies, waits for them, and re-layouts  74.8 us
    pallas_call x2, Pallas kernels, kernel_call(): pl.pallas_call(kernel, out_shape=outs, in_specs=[smem] * len(tables) + [v...  46.5 us
    all_gather x1, waiting for transfers between devices, fetch_attention(): lax.all_gather(qkv_weight, 'fsdp', axis=0, tiled=True)  37.6 us
  transfers between devices with their start and end apart: 12, of which 10 were waited for; matrix products, arithmetic and copies ran while one was open for 8% of the time, Pallas kernels for 2%

profile of v1, /device:TPU:0, one launch (start us, length us, event | category | flops | bytes accessed | tf_op | source)
XLA Modules:
  0.0 1354.8 jit_solution(14869333216840800577)
XLA Ops:
  8.7 8.9 copy.91
  31.5 37.6 %all-gather.7.cloned.1.call-done = bf16[1024,2048]{1,0:T(8,128)(2,1)} async-done(((bf16[512,2048]{1,0:T(8,128)(2,1)}), bf16[1024,2048]{1,0:T(8,128)(2,1)}) %all-gather.7.cloned.1.call-update) | async-done | bytes 4194320 | tf_op jit(solution)/shard_map/all_gather | solution.py:273
  77.0 5.6 all-to-all-start
  83.7 30.9 %all-to-all-done.qkv_ref = bf16[16,192,256]{2,1,0:T(8,128)(2,1)S(1)} async-done(((bf16[16,192,256]{2,1,0:T(8,128)(2,1)}), bf16[16,192,256]{2,1,0:T(8,128)(2,1)S(1)}, u32[]{:S(2)}, u32[]{:S(2)}) %all-to-all-start) | async-done | bytes 1572896 | tf_op jit(solution)/shard_map/all_to_all | solution.py:303
  115.8 21.5 %shard_map.195 = (bf16[16,64,256]{2,1,0:T(8,128)(2,1)S(1)}, bf16[4096,64]{1,0:T(8,128)(2,1)S(1)}, bf16[64,4096]{1,0:T(8,128)(2,1)S(1)}, bf16[4096,64]{1,0:T(8,12...) custom-call(s32[32]{0:T(128)S(1)} %broadcast_add_fusion.q_slot, ...), custom_call_target="tpu_custom_call" | custom-call | tf_op jit(solution)/shard_map/pallas_call | solution.py:214
  140.7 9.4 all-to-all-start.1
  154.6 9.9 all-to-all-done.1
  168.2 163.0 %all-gather.11.cloned.1.call-done = bf16[1024,2,4608]{2,0,1:T(8,128)(2,1)} async-done(((bf16[512,2,4608]{2,0,1:T(8,128)(2,1)}), bf16[1024,2,4608]{2,0,1:T(8,128)(2,1)}) %all-gather.11.cloned.1.call-update) | async-done | bytes 18874384 | tf_op jit(solution)/shard_map/all_gather | solution.py:334
  331.1 12.1 fusion.55
  343.3 107.3 %all-gather.13.cloned.1.call-done = bf16[4608,1024]{1,0:T(8,128)(2,1)} async-done(((bf16[2304,1024]{1,0:T(8,128)(2,1)}), bf16[4608,1024]{1,0:T(8,128)(2,1)}) %all-gather.13.cloned.1.call-update) | async-done | bytes 9437200 | tf_op jit(solution)/shard_map/all_gather | solution.py:344
  450.6 10.1 fusion.15
  460.7 10.6 multiply_reduce_fusion.1
  478.9 20.1 %all_to_all.20.d_ref = bf16[16,64,256]{2,1,0:T(8,128)(2,1)S(1)} all-to-all(bf16[16,64,256]{2,1,0:T(8,128)(2,1)} %bitcast.153), channel_id=1, replica_groups=mesh['ctx'=16,'fsdp'=2] {'ctx'}, dimensions={0} | all-to-all | bytes 1048576 | tf_op jit(solution)/shard_map/all_to_all | solution.py:391
  502.3 24.9 %shard_map.196 = bf16[16,192,256]{2,1,0:T(8,128)(2,1)} custom-call(s32[32]{0:T(128)S(1)} %broadcast_add_fusion.q_slot, s32[32]{0:T(128)S(1)} %get-tuple-element.71.kv_slot, s32[16]{0:T(128)S(1)} %get-tuple-element.114.first, s32[16]{0:T(128)S(1)} %get-tuple-element.115.last, bf16[16,64,256]{2,1,0:T(8,128)(2,1)S(1)} %all_to_all.20.d_ref, ...), custom_call_target="tpu_custom_call" | custom-call | tf_op jit(solution)/shard_map/pallas_call | solution.py:214
  537.8 25.6 %all-to-all-done.3 = bf16[16,192,256]{2,1,0:T(8,128)(2,1)S(1)} async-done(((bf16[16,192,256]{2,1,0:T(8,128)(2,1)}), bf16[16,192,256]{2,1,0:T(8,128)(2,1)S(1)}, u32[]{:S(2)}, u32[]{:S(2)}) %all-to-all-start.3) | async-done | bytes 1572896 | tf_op jit(solution)/shard_map/all_to_all | solution.py:404
  586.7 10.5 convolution_convert_fusion.1
  599.2 11.2 convolution_convert_fusion
  610.8 33.8 %reduce-scatter.5.cloned.1.call-done = bf16[512,2048]{1,0:T(8,128)(2,1)} async-done(((bf16[1024,2048]{1,0:T(8,128)(2,1)}), bf16[512,2048]{1,0:T(8,128)(2,1)}) %reduce-scatter.5.cloned.1.call-update) | async-done | bytes 2097168 | tf_op jit(solution)/shard_map/reduce_scatter | solution.py:431
  644.6 112.9 %reduce-scatter.11.cloned.1.call-done = bf16[2304,1024]{1,0:T(8,128)(2,1)} async-done(((bf16[4608,1024]{1,0:T(8,128)(2,1)}), bf16[2304,1024]{1,0:T(8,128)(2,1)}) %reduce-scatter.11.cloned.1.call-update) | async-done | bytes 4718608 | tf_op jit(solution)/shard_map/reduce_scatter | solution.py:375
  757.5 214.6 %reduce-scatter.9.cloned.1.call-done = bf16[512,2,4608]{2,0,1:T(8,128)(2,1)} async-done(((bf16[1024,2,4608]{2,0,1:T(8,128)(2,1)}), bf16[512,2,4608]{2,0,1:T(8,128)(2,1)}) %reduce-scatter.9.cloned.1.call-update) | async-done | bytes 9437200 | tf_op jit(solution)/shard_map/reduce_scatter | solution.py:366
  973.4 10.1 fusion.26
  992.9 34.5 %all-reduce.6 = (bf16[512]{0:T(512)(128)(2,1)S(1)}, bf16[512]{0:T(512)(128)(2,1)S(1)}, bf16[32]{0:T(256)(128)(2,1)S(1)}, bf16[32]{0:T(256)(128)(2,1)S(1)}) all-reduce(bf16[512]{0:T(512)(128)(2,1)S(1)} %dynamic-slice.3, bf16[512]{0:T(512)(128)(2,1)S(1)} %dynamic-slice.5, ...), channel_id=1, replica_groups=mesh['ctx'=16,'fsdp'=2] {'ctx'}, use_global_device_ids=true, to_apply=%region_28.29 | all-reduce | flops 1088 | bytes 4352 | tf_op jit(solution)/shard_map/psum | solution.py:467
  1031.0 253.1 %all-reduce.12.cloned.1.call-done = (bf16[512,2,4608]{2,0,1:T(8,128)(2,1)}, bf16[512,2048]{1,0:T(8,128)(2,1)}, bf16[512,1024]{1,0:T(8,128)(2,1)}, bf16[2304,1024]{1,0:T(8,128)(2,1)}) async-done(((bf16[512,2,4608]{2,0,1:T(8,128)(2,1)}, bf16[512,2048]{1,0:T(8,128)(2,1)}, bf16[512,1024]{1,0:T(8,128)(2,1)}, bf16[2304,1024]{1,0:T(8,128)(2,1)}), (bf16[512,2,4608]{2,0,1:T(8,128)(2,1)}, ...) | async-done | bytes 17301520 | tf_op jit(solution)/shard_map/psum | solution.py:465
  1291.7 51.1 %copy.111 = f32[512,2,4608]{2,1,0:T(2,128)} copy(bf16[512,2,4608]{2,0,1:T(8,128)(2,1)S(1)} %copy-done.13) | data formatting | bytes 28311552
  (206 shorter events, 108.4 us)
Async XLA Ops:
  7.2 62.0 %all-gather.7.cloned.1.call-start = ((), (), s32[]{:S(2)}) async-start(), calls=%async_computation.8 | async-start | bytes 6291456 | tf_op jit(solution)/shard_map/all_gather | solution.py:273
  7.9 146.7 %all-gather.9.cloned.1.call-start = ((), (), s32[]{:S(2)}) async-start(), calls=%async_computation.9 | async-start | bytes 3145728 | tf_op jit(solution)/shard_map/all_gather | solution.py:274
  8.7 322.5 %all-gather.11.cloned.1.call-start = ((), (), s32[]{:S(2)}) async-start(), calls=%async_computation.10 | async-start | bytes 28311552 | tf_op jit(solution)/shard_map/all_gather | solution.py:334
  17.6 8.2 copy-start.34
  17.7 8.4 copy-start.35
  17.7 432.9 %all-gather.13.cloned.1.call-start = ((), (), s32[]{:S(2)}) async-start(), calls=%async_computation.11 | async-start | bytes 14155776 | tf_op jit(solution)/shard_map/all_gather | solution.py:344
  75.7 74.3 %copy-start.33 = (bf16[512]{0:T(512)(128)(2,1)S(1)}, bf16[512]{0:T(512)(128)(2,1)}, u32[]{:S(2)}) copy-start(bf16[512]{0:T(512)(128)(2,1)} %param.18) | copy-start | bytes 3076
  77.0 37.6 %all-to-all-start = ((bf16[16,192,256]{2,1,0:T(8,128)(2,1)}), bf16[16,192,256]{2,1,0:T(8,128)(2,1)S(1)}, u32[]{:S(2)}, u32[]{:S(2)}) async-start(bf16[16,192,256]{2,1,0:T(8,128)(2,1)} %pad_maximum_fusion.3), calls=%async_computation | async-start | bytes 3145728 | tf_op jit(solution)/shard_map/all_to_all | solution.py:303
  140.7 23.9 %all-to-all-start.1 = ((bf16[16,64,256]{2,1,0:T(8,128)(2,1)}), bf16[16,64,256]{2,1,0:T(8,128)(2,1)}, u32[]{:S(2)}, u32[]{:S(2)}) async-start(bf16[16,64,256]{2,1,0:T(8,128)(2,1)} %copy-done.6), calls=%async_computation.1 | async-start | bytes 1048576 | tf_op jit(solution)/shard_map/all_to_all | solution.py:323
  450.6 10.2 copy-start.7
  527.3 36.1 %all-to-all-start.3 = ((bf16[16,192,256]{2,1,0:T(8,128)(2,1)}), bf16[16,192,256]{2,1,0:T(8,128)(2,1)S(1)}, u32[]{:S(2)}, u32[]{:S(2)}) async-start(bf16[16,192,256]{2,1,0:T(8,128)(2,1)} %shard_map.196), calls=%async_computation.3 | async-start | bytes 3145728 | tf_op jit(solution)/shard_map/all_to_all | solution.py:404
  531.4 79.5 %reduce-scatter.7.cloned.1.call-start = ((), (), s32[]{:S(2)}) async-start(), calls=%async_computation.13 | async-start | bytes 3145728 | tf_op jit(solution)/shard_map/reduce_scatter | solution.py:434
  534.9 31.6 %copy-start.15 = (f32[512,256]{1,0:T(8,128)S(1)}, f32[512,256]{1,0:T(8,128)}, u32[]{:S(2)}) copy-start(f32[512,256]{1,0:T(8,128)} %copy-done.14) | copy-start | bytes 1572868
  534.9 109.7 %reduce-scatter.5.cloned.1.call-start = ((), (), s32[]{:S(2)}) async-start(), calls=%async_computation.12 | async-start | bytes 6291456 | tf_op jit(solution)/shard_map/reduce_scatter | solution.py:431
  586.7 170.8 %reduce-scatter.11.cloned.1.call-start = ((), (), s32[]{:S(2)}) async-start(), calls=%async_computation.15 | async-start | bytes 14155776 | tf_op jit(solution)/shard_map/reduce_scatter | solution.py:375
  597.3 374.8 %reduce-scatter.9.cloned.1.call-start = ((), (), s32[]{:S(2)}) async-start(), calls=%async_computation.14 | async-start | bytes 28311552 | tf_op jit(solution)/shard_map/reduce_scatter | solution.py:366
  610.5 673.6 %all-reduce.12.cloned.1.call-start = ((), (), s32[]{:S(2)}) async-start(), calls=%async_computation.16 | async-start | bytes 34603008 | tf_op jit(solution)/shard_map/psum | solution.py:465
  973.4 10.3 copy-start.21
  973.4 10.3 copy-start.25
  973.4 10.3 copy-start.28
  983.7 45.9 %copy-start.12 = (f32[256,1024]{1,0:T(8,128)S(1)}, f32[256,1024]{1,0:T(8,128)}, u32[]{:S(2)}) copy-start(f32[256,1024]{1,0:T(8,128)} %copy-done.11) | copy-start | bytes 3145732
  1284.1 7.6 copy-start.13
  1288.5 54.4 %slice-start = ((s8[4718592]{0:T(1024)(128)(4,1)}), s8[4194304]{0:T(1024)(128)(4,1)S(1)}, s32[]{:S(2)}) async-start(s8[4718592]{0:T(1024)(128)(4,1)} %bitcast.147), calls=%async_computation.17 | async-start | bytes 8388608
  1291.7 51.1 %slice-start.1 = ((s8[4718592]{0:T(1024)(128)(4,1)}), s8[524288]{0:T(1024)(128)(4,1)S(1)}, s32[]{:S(2)}) async-start(s8[4718592]{0:T(1024)(128)(4,1)} %bitcast.147), calls=%async_computation.18 | async-start | bytes 1048576
  (26 other events, 66.6 us)
Sparse Core Ops, SparseCore 0:
  9.6 59.5 all-gather.6
  70.7 33.1 all-gather.8
  106.0 225.0 all-gather.10
  332.5 117.9 all-gather.12
  535.0 32.2 reduce-scatter.6
  586.8 57.7 reduce-scatter.4
  646.9 110.5 reduce-scatter.10
  760.4 211.6 reduce-scatter.8
  976.5 307.5 all-reduce.11

commit v2 on v1

--- a/solution.py
+++ b/solution.py
@@ -12,6 +12,7 @@
 HD = 64
 BLK = 128
 TILE = 256
+CHUNKS = 2
 
 
 EPSILON = 1e-05
@@ -221,6 +222,183 @@
     )(*tables, *arrays)
 
 
+class Links:
+    def __init__(self, ctx_size):
+        self.depth = ctx_size // 4
+        index = lax.axis_index("ctx")
+        self.core = index % 2
+        self.y = (index // 2) % 2
+        self.side = lax.axis_index("fsdp")
+        self.half = ((index // 4 + 1) // 2) % 2
+
+    def route(self, place):
+        pairs = []
+        for z in range(self.depth):
+            for y in range(2):
+                for core in range(2):
+                    to_z, to_y, to_core = place(z, y, core)
+                    pairs.append(((z * 2 + y) * 2 + core, (to_z * 2 + to_y) * 2 + to_core))
+        return pairs
+
+    def over_core(self, value):
+        return lax.ppermute(value, "ctx", self.route(lambda z, y, c: (z, y, 1 - c)))
+
+    def over_y(self, value):
+        return lax.ppermute(value, "ctx", self.route(lambda z, y, c: (z, 1 - y, c)))
+
+    def over_z(self, value):
+        return lax.ppermute(value, "ctx", self.route(lambda z, y, c: (z ^ 1, y, c)))
+
+    def mirror_z(self, value):
+        return lax.ppermute(value, "ctx", self.route(lambda z, y, c: (self.depth - 1 - z, y, c)))
+
+    def over_x(self, value):
+        return lax.ppermute(value, "fsdp", [(0, 1), (1, 0)])
+
+    def gather_plane(self, value):
+        pair = jnp.stack([value, self.over_y(value)])
+        other = self.over_core(pair)
+        return jnp.stack([pair[0], other[0], pair[1], other[1]])
+
+    def sum_depth(self, value):
+        halves = value.reshape(2, value.shape[0] // 2, value.shape[1])
+        mine = pick(halves, self.half, 0)
+        part = add(mine, self.over_z(pick(halves, 1 - self.half, 0)))
+        full = add(part, self.mirror_z(part))
+        return jnp.stack([full, self.over_z(full)])
+
+    def spread_plane(self, value):
+        beside = self.over_y(value)
+        return (value, beside, self.over_core(value), self.over_core(beside))
+
+
+def pick(value, index, axis):
+    return lax.dynamic_index_in_dim(value, index, axis, keepdims=False)
+
+
+def add(left, right):
+    return (left.astype(jnp.float32) + right.astype(jnp.float32)).astype(jnp.bfloat16)
+
+
+def place_gate_up_kernel(here, *refs):
+    out_ref = refs[-1]
+    half, core, y = here[0], here[1], here[2]
+    wide = refs[0].shape[2]
+    for chunk in range(len(refs) // 4):
+        mine, beside, across, diagonal = (r[0] for r in refs[4 * chunk : 4 * chunk + 4])
+        for kind in range(2):
+            for column in range(2):
+                value = jnp.where(
+                    core == kind,
+                    jnp.where(y == column, mine, beside),
+                    jnp.where(y == column, across, diagonal),
+                )
+                at = (2 * chunk + column) * wide
+                out_ref[:, kind, at : at + wide] = value.astype(jnp.float32)
+
+
+def place_gate_up(here, chunks):
+    _, rows, wide = chunks[0][0].shape
+    step = 32
+    flat = [array for chunk in chunks for array in chunk]
+
+    def piece(i, here):
+        return ((i // (rows // step)) ^ here[0], i % (rows // step), 0)
+
+    return pl.pallas_call(
+        place_gate_up_kernel,
+        grid_spec=pltpu.PrefetchScalarGridSpec(
+            num_scalar_prefetch=1,
+            grid=(2 * rows // step,),
+            in_specs=[pl.BlockSpec((1, step, wide), piece)] * len(flat),
+            out_specs=pl.BlockSpec((step, 2, 2 * wide * len(chunks)), lambda i, here: (i, 0, 0)),
+        ),
+        out_shape=jax.ShapeDtypeStruct((2 * rows, 2, 2 * wide * len(chunks)), jnp.float32),
+        compiler_params=pltpu.CompilerParams(vmem_limit_bytes=40 * 1024 * 1024),
+    )(here, *flat)
+
+
+def place_pieces(here, pieces, cuts, by_rows):
+    _, rows, _ = pieces[0].shape
+
+    def kernel(here, *refs):
+        s = pl.program_id(0)
+        for a in range(4):
+
+            @pl.when(s // 2 == a)
+            def _(a=a):
+                at = 0
+                for out_ref in refs[4:]:
+                    wide = out_ref.shape[1]
+                    out_ref[...] = refs[a][0, :, at : at + wide].astype(jnp.float32)
+                    at += wide
+
+    def source(a):
+        return lambda s, here: (jnp.clip(s - 2 * a, 0, 1), 0, 0)
+
+    def target(s, here):
+        half = (s % 2) ^ here[0]
+        core = (s // 4) ^ here[1]
+        y = ((s // 2) % 2) ^ here[2]
+        if by_rows:
+            return ((core * 2 + y) * 2 + half, 0)
+        return (half, core * 2 + y)
+
+    across, along = (1, 8) if by_rows else (4, 2)
+    return pl.pallas_call(
+        kernel,
+        grid_spec=pltpu.PrefetchScalarGridSpec(
+            num_scalar_prefetch=1,
+            grid=(8,),
+            in_specs=[pl.BlockSpec((1, rows, sum(cuts)), source(a)) for a in range(4)],
+            out_specs=[pl.BlockSpec((rows, wide), target) for wide in cuts],
+        ),
+        out_shape=[
+            jax.ShapeDtypeStruct((rows * along, wide * across), jnp.float32) for wide in cuts
+        ],
+        compiler_params=pltpu.CompilerParams(vmem_limit_bytes=40 * 1024 * 1024),
+    )(here, *pieces)
+
+
+def contract(left, right, axes):
+    return lax.dot_general(
+        left, right, ((axes[:1], axes[1:]), ((), ())), preferred_element_type=jnp.float32
+    )
+
+
+def side_sum(links, both):
+    got = links.over_x(both(1 - links.side).astype(jnp.bfloat16))
+    return (both(links.side) + got.astype(jnp.float32)).astype(jnp.bfloat16)
+
+
+def wide_grads(links, rows_plane, kinds):
+    stacked = jnp.stack(kinds)
+    tokens, columns = kinds[0].shape
+    mine = pick(stacked, links.core, 0)
+    pair = jnp.stack([mine, links.over_core(pick(stacked, 1 - links.core, 0))])
+    pair = pair.reshape(2 * tokens, 2, columns // 2)
+    kept = pick(pair, links.y, 1)
+    got = links.over_y(pick(pair, 1 - links.y, 1))
+    terms = jnp.concatenate([kept, got])
+    rows = rows_plane.shape[1] // 2
+
+    def both(side):
+        return contract(
+            lax.dynamic_slice_in_dim(rows_plane, side * rows, rows, 1), terms, (0, 0)
+        )
+
+    return links.spread_plane(links.sum_depth(side_sum(links, both)))
+
+
+def exchange_plane(links, value):
+    mine = pick(value, links.core, 0)
+    across = links.over_core(pick(value, 1 - links.core, 0))
+    pair = jnp.stack([mine, across])
+    got = links.over_y(pick(pair, 1 - links.y, 1))
+    kept = pick(pair, links.y, 1)
+    return (kept[0], kept[1], got[0], got[1])
+
+
 def on_device(
     tokens,
     qkv_weight,
@@ -239,6 +417,7 @@
     rows_here = inputs.shape[0]
     ctx_size = lax.axis_size("ctx")
     ctx_index = lax.axis_index("ctx")
+    fast = lax.axis_size("fsdp") == 2 and ctx_size == 16
     per_group = HEADS // KV_HEADS
     q_width = HEADS * HD
     kv_width = KV_HEADS * HD
@@ -363,27 +542,55 @@
         preferred_element_type=jnp.float32,
     )
     columns = normed_two
-    grad_gate_up = lax.psum_scatter(
-        jnp.einsum("tr,tgf->rgf", columns, d_gate_up, preferred_element_type=jnp.float32).astype(
-            jnp.bfloat16
-        ),
-        "fsdp",
-        scatter_dimension=0,
-        tiled=True,
-    )
-    columns = hidden
-    grad_down = lax.psum_scatter(
-        lax.dot_general(
-            columns, d_ffn, (((0,), (0,)), ((), ())), preferred_element_type=jnp.float32
-        ).astype(jnp.bfloat16),
-        "fsdp",
-        scatter_dimension=0,
-        tiled=True,
-    )
+    if fast:
+        links = Links(ctx_size)
+        here = jnp.stack([links.half, links.core, links.y])
+        normed_plane = links.gather_plane(normed).reshape(4 * rows_here, -1)
+        attn_plane = links.gather_plane(attn_in)
+        attn_plane = jnp.concatenate(list(attn_plane), axis=1)
+        two_plane = links.gather_plane(normed_two).reshape(4 * rows_here, -1)
+        ffn_plane = links.gather_plane(d_ffn).reshape(4 * rows_here, -1)
+        ff_width = hidden.shape[1]
+        chunk = ff_width // CHUNKS
+        gate_up_pieces = [
+            wide_grads(
+                links, two_plane, [d_gate_up[:, j, i * chunk : (i + 1) * chunk] for j in range(2)]
+            )
+            for i in range(CHUNKS)
+        ]
+        grad_gate_up = place_gate_up(here, gate_up_pieces)
+        hidden_t = hidden.T.reshape(2, 2, 2, ff_width // 8, rows_here)
+        hidden_t = jnp.transpose(hidden_t, (1, 2, 0, 3, 4))
+        hidden_plane = jnp.concatenate(exchange_plane(links, hidden_t), axis=-1)
+        down_pieces = links.spread_plane(
+            links.sum_depth(
+                side_sum(
+                    links, lambda side: contract(pick(hidden_plane, side, 0), ffn_plane, (1, 0))
+                )
+            )
+        )
+        (grad_down,) = place_pieces(here, down_pieces, (d_ffn.shape[1],), True)
+    else:
+        grad_gate_up = lax.psum_scatter(
+            jnp.einsum("tr,tgf->rgf", columns, d_gate_up, preferred_element_type=jnp.float32).astype(
+                jnp.bfloat16
+            ),
+            "fsdp",
+            scatter_dimension=0,
+            tiled=True,
+        )
+        columns = hidden
+        grad_down = lax.psum_scatter(
+            lax.dot_general(
+                columns, d_ffn, (((0,), (0,)), ((), ())), preferred_element_type=jnp.float32
+            ).astype(jnp.bfloat16),
+            "fsdp",
+            scatter_dimension=0,
+            tiled=True,
+        )
     d_norm_two, ffn_gain_term = norm_back(d_normed_two, h_one, scale_two, gain_ffn)
     d_h_one = d_out + d_norm_two
     d_attn = d_h_one.astype(jnp.bfloat16)
-    grad_out_here = jnp.dot(attn_in, d_attn, preferred_element_type=f32)
     d_heads = lax.dot_general(
         w_out, d_attn, (((1,), (1,)), ((), ())), preferred_element_type=f32
     ).astype(bf16)
@@ -419,67 +626,74 @@
         ],
         axis=0,
     )
-    grad_qkv_here = lax.dot_general(
-        normed, d_projected, (((0,), (1,)), ((), ())), preferred_element_type=f32
-    )
     d_normed = lax.dot_general(
         d_projected, w_qkv, (((0,), (1,)), ((), ())), preferred_element_type=f32
     )
     d_norm_one, attn_gain_term = norm_back(d_normed, inputs, scale_one, gain_attn)
     d_inputs = d_h_one + d_norm_one
-    shard_qkv, shard_out, shard_attn_gain, shard_ffn_gain, shard_query_gain, shard_key_gain = (
-        lax.psum_scatter(
-            grad_qkv_here.astype(jnp.bfloat16), "fsdp", scatter_dimension=0, tiled=True
-        ).astype(jnp.float32),
-        lax.psum_scatter(
-            grad_out_here.astype(jnp.bfloat16), "fsdp", scatter_dimension=0, tiled=True
-        ).astype(jnp.float32),
-        lax.psum_scatter(
-            jnp.sum(attn_gain_term, axis=0).astype(jnp.bfloat16),
-            "fsdp",
-            scatter_dimension=0,
-            tiled=True,
-        ).astype(jnp.float32),
-        lax.psum_scatter(
-            jnp.sum(ffn_gain_term, axis=0).astype(jnp.bfloat16),
-            "fsdp",
-            scatter_dimension=0,
-            tiled=True,
-        ).astype(jnp.float32),
-        lax.psum_scatter(
-            jnp.sum(query_term, axis=(0, 2)).astype(jnp.bfloat16),
-            "fsdp",
-            scatter_dimension=0,
-            tiled=True,
-        ).astype(jnp.float32),
-        lax.psum_scatter(
-            jnp.sum(key_term, axis=(0, 2)).astype(jnp.bfloat16),
-            "fsdp",
-            scatter_dimension=0,
-            tiled=True,
-        ).astype(jnp.float32),
-    )
-    summed_grads = (
-        lax.psum(shard_qkv.astype(jnp.bfloat16), "ctx").astype(jnp.float32),
-        lax.psum(shard_out.astype(jnp.bfloat16), "ctx").astype(jnp.float32),
-        lax.psum(grad_gate_up, "ctx").astype(jnp.float32),
-        lax.psum(grad_down, "ctx").astype(jnp.float32),
-        lax.psum(shard_attn_gain.astype(jnp.bfloat16), "ctx").astype(jnp.float32),
-        lax.psum(shard_ffn_gain.astype(jnp.bfloat16), "ctx").astype(jnp.float32),
-        lax.psum(shard_query_gain.astype(jnp.bfloat16), "ctx").astype(jnp.float32),
-        lax.psum(shard_key_gain.astype(jnp.bfloat16), "ctx").astype(jnp.float32),
-    )
+    gains = jnp.concatenate(
+        [
+            jnp.sum(attn_gain_term, axis=0),
+            jnp.sum(ffn_gain_term, axis=0),
+            jnp.sum(query_term, axis=(0, 2)),
+            jnp.sum(key_term, axis=(0, 2)),
+        ]
+    )
+    gains = lax.psum(gains, ("ctx", "fsdp"))
+    gain_grads = []
+    at = 0
+    for gain in (attn_gain, ffn_gain, query_gain, key_gain):
+        size = gain.shape[0]
+        gain_grads.append(
+            lax.dynamic_slice_in_dim(gains, at + lax.axis_index("fsdp") * size, size)
+        )
+        at += size * lax.axis_size("fsdp")
+    if fast:
+        projected_plane = jnp.concatenate(
+            exchange_plane(links, d_projected.reshape(2, 2, -1, rows_here)), axis=1
+        )
+        attn_columns = jnp.transpose(d_attn.reshape(rows_here, 2, 2, -1), (1, 2, 0, 3))
+        out_plane = jnp.concatenate(exchange_plane(links, attn_columns), axis=0)
+        rows = normed_plane.shape[1] // 2
+
+        def both(side):
+            return jnp.concatenate(
+                [
+                    contract(
+                        lax.dynamic_slice_in_dim(normed_plane, side * rows, rows, 1),
+                        projected_plane,
+                        (0, 1),
+                    ),
+                    contract(
+                        lax.dynamic_slice_in_dim(attn_plane, side * rows, rows, 0),
+                        out_plane,
+                        (1, 0),
+                    ),
+                ],
+                axis=1,
+            )
+
+        pieces = links.spread_plane(links.sum_depth(side_sum(links, both)))
+        grad_qkv, grad_out = place_pieces(
+            here, pieces, (projected_plane.shape[0], out_plane.shape[1]), False
+        )
+    else:
+        grad_qkv, grad_out = (
+            lax.psum_scatter(grad.astype(bf16), "fsdp", scatter_dimension=0, tiled=True)
+            for grad in (contract(normed, d_projected, (0, 1)), jnp.dot(attn_in, d_attn, preferred_element_type=f32))
+        )
+        grad_qkv, grad_out, grad_gate_up, grad_down = (
+            lax.psum(grad, "ctx").astype(f32)
+            for grad in (grad_qkv, grad_out, grad_gate_up, grad_down)
+        )
     return (
         output[None],
         d_inputs[None],
-        summed_grads[0],
-        summed_grads[1],
-        summed_grads[2],
-        summed_grads[3],
-        summed_grads[4],
-        summed_grads[5],
-        summed_grads[6],
-        summed_grads[7],
+        grad_qkv,
+        grad_out,
+        grad_gate_up,
+        grad_down,
+        *gain_grads,
     )
 
 

time: 1360 us -> 971 us (0.71)
  waiting for transfers between devices: 991 us -> 429 us
  starting transfers between devices: 19.9 us -> 123 us
  other arithmetic: 28.7 us -> 68.7 us
  Pallas kernels: 46.5 us -> 78.6 us
  local copies, waits for them, and re-layouts: 90.9 us -> 112 us
  blocking collectives: 74.4 us -> 55.7 us
    reduce_scatter x4 -> x0, waiting for transfers between devices: 361 us -> none  [the longest x1 215 us: on_device(): lax.psum_scatter(jnp.einsum('tr,tgf->rgf', columns, d_gate_up, preferred_...]
    psum x1 -> x0, waiting for transfers between devices: 253 us -> none  [on_device(): lax.psum(grad_gate_up, 'ctx').astype(jnp.float32)]
    ppermute x0 -> x46, waiting for transfers between devices: none -> 148 us  [the longest x13 67.6 us: over_y(): return lax.ppermute(value, 'ctx', self.route(lambda z, y, c: (z, 1 - y, c)))]
    ppermute x0 -> x46, starting transfers between devices: none -> 95.5 us  [the longest x8 65.8 us: over_z(): return lax.ppermute(value, 'ctx', self.route(lambda z, y, c: (z ^ 1, y, c)))]
    all_gather x1, waiting for transfers between devices: 163 us -> 104 us  [on_device(): lax.all_gather(gate_up_weight, 'fsdp', axis=0, tiled=True)]
    unnamed x89 -> x191, local copies, waits for them, and re-layouts: 74.8 us -> 35.2 us
    another operation x3 -> x23, other arithmetic: 0.4 us -> 39.9 us  [the longest x5 9.02 us: gather_plane(): pair = jnp.stack([value, self.over_y(value)])]
    pallas_call x0 -> x3, Pallas kernels: none -> 31.2 us  [the longest x1 16.6 us: place_gate_up(): pl.pallas_call(place_gate_up_kernel, grid_spec=pltpu.PrefetchScalarGridSp...]
  transfers between devices with their start and end apart: 12 -> 54, of which waited for: 10 -> 20; matrix products, arithmetic and copies ran while one was open for 8% -> 21% of each run, Pallas kernels for 2% -> 7%
where the time goes in v2:
time: 971 us; the launch traced here: 962 us
  waiting for transfers between devices  429 us (44%)
  starting transfers between devices  123 us (13%)
  local copies, waits for them, and re-layouts  112 us (12%)
  matrix products  78.8 us (8%)
  Pallas kernels  78.6 us (8%)
  other arithmetic  68.7 us (7%)
  blocking collectives  55.7 us (6%)
  between operations  16.3 us (2%)
    all_gather x1, waiting for transfers between devices, on_device(): lax.all_gather(down_weight, 'fsdp', axis=0, tiled=True)  108 us
    all_gather x1, waiting for transfers between devices, on_device(): lax.all_gather(gate_up_weight, 'fsdp', axis=0, tiled=True)  104 us
    ppermute x13, waiting for transfers between devices, over_y(): return lax.ppermute(value, 'ctx', self.route(lambda z, y, c: (z, 1 - y, c)))  67.6 us
    ppermute x8, starting transfers between devices, over_z(): return lax.ppermute(value, 'ctx', self.route(lambda z, y, c: (z ^ 1, y, c)))  65.8 us
    pallas_call x2, Pallas kernels, kernel_call(): pl.pallas_call(kernel, out_shape=outs, in_specs=[smem] * len(tables) + [v...  47.4 us
    ppermute x4, waiting for transfers between devices, over_x(): return lax.ppermute(value, 'fsdp', [(0, 1), (1, 0)])  41 us
    psum x1, blocking collectives, on_device(): gains = lax.psum(gains, ('ctx', 'fsdp'))  41 us
    all_gather x1, waiting for transfers between devices, fetch_attention(): lax.all_gather(qkv_weight, 'fsdp', axis=0, tiled=True)  37.3 us
  transfers between devices with their start and end apart: 54, of which 20 were waited for; matrix products, arithmetic and copies ran while one was open for 21% of the time, Pallas kernels for 7%

profile of v2, /device:TPU:0, one launch (start us, length us, event | category | flops | bytes accessed | tf_op | source)
XLA Modules:
  0.0 961.6 jit_solution(6704911956255185929)
XLA Ops:
  8.7 8.9 copy.113
  31.8 37.3 %all-gather.7.cloned.1.call-done = bf16[1024,2048]{1,0:T(8,128)(2,1)} async-done(((bf16[512,2048]{1,0:T(8,128)(2,1)}), bf16[1024,2048]{1,0:T(8,128)(2,1)}) %all-gather.7.cloned.1.call-update) | async-done | bytes 4194320 | tf_op jit(solution)/shard_map/all_gather | solution.py:452
  84.8 30.3 %all-to-all-done.qkv_ref = bf16[16,192,256]{2,1,0:T(8,128)(2,1)S(1)} async-done(((bf16[16,192,256]{2,1,0:T(8,128)(2,1)}), bf16[16,192,256]{2,1,0:T(8,128)(2,1)S(1)}, u32[]{:S(2)}, u32[]{:S(2)}) %all-to-all-start) | async-done | bytes 1572896 | tf_op jit(solution)/shard_map/all_to_all | solution.py:482
  116.3 22.5 %shard_map.195 = (bf16[16,64,256]{2,1,0:T(8,128)(2,1)}, bf16[4096,64]{1,0:T(8,128)(2,1)S(1)}, bf16[64,4096]{1,0:T(8,128)(2,1)S(1)}, bf16[4096,64]{1,0:T(8,128)(2...) custom-call(s32[32]{0:T(128)S(1)} %broadcast_add_fusion.q_slot, ...), custom_call_target="tpu_custom_call" | custom-call | tf_op jit(solution)/shard_map/pallas_call | solution.py:215
  141.6 9.2 all-to-all-start.1
  157.7 13.5 %collective-permute-done = bf16[256,1024]{1,0:T(8,128)(2,1)S(1)} collective-permute-done((bf16[256,1024]{1,0:T(8,128)(2,1)}, bf16[256,1024]{1,0:T(8,128)(2,1)S(1)}, u32[]{:S(2)}, u32[]{:S(2)}) %collective-permute-start) | collective-permute-done | bytes 524320 | tf_op jit(solution)/shard_map/ppermute | solution.py:247
  227.1 104.1 %all-gather.11.cloned.1.call-done = bf16[1024,2,4608]{2,0,1:T(8,128)(2,1)} async-done(((bf16[512,2,4608]{2,0,1:T(8,128)(2,1)}), bf16[1024,2,4608]{2,0,1:T(8,128)(2,1)}) %all-gather.11.cloned.1.call-update) | async-done | bytes 18874384 | tf_op jit(solution)/shard_map/all_gather | solution.py:513
  331.2 11.8 %fusion.69 = f32[256,2,4608]{2,0,1:T(8,128)} fusion(bf16[1024,2,4608]{2,0,1:T(8,128)(2,1)} %all-gather.11.cloned.1.call-done, bf16[256,1024]{1,0:T(8,128)(2,1)} %copy-done.37), kind=kOutput, calls=%fused_computation.174 | convolution fusion | flops 4831838208 | bytes 28835840 | tf_op jit(solution)/shard_map/tr,rgf->tgf/dot_general | solution.py:510
  343.0 107.6 %all-gather.13.cloned.1.call-done = bf16[4608,1024]{1,0:T(8,128)(2,1)} async-done(((bf16[2304,1024]{1,0:T(8,128)(2,1)}), bf16[4608,1024]{1,0:T(8,128)(2,1)}) %all-gather.13.cloned.1.call-update) | async-done | bytes 9437200 | tf_op jit(solution)/shard_map/all_gather | solution.py:523
  450.6 13.6 %fusion.7 = (bf16[256,1,4608]{2,0,1:T(8,128)(2,1)S(1)}, bf16[256,1,4608]{2,0,1:T(8,128)(2,1)S(1)}, bf16[256,4608]{1,0:T(8,128)(2,1)}) fusion(f32[256,2,4608]{2,0,1:T(8,128)} %fusion.69, bf16[4608,1024]{1,0:T(8,128)(2,1)} %all-gather.13.cloned.1.call-done, bf16[1,256,1024]{2,1,0:T(8,128)(2,1)S(1)} %copy-done.18), kind=kOutput, calls=%fused_computation.36 | convolution fusion | flops 2434793472 | bytes 26476544 | tf_op jit(solution)/shard_map/dot_general | solution.py:529
  468.4 11.9 %multiply_reduce_fusion.1 = (f32[1024]{0:T(1024)}, f32[256]{0:T(256)S(1)}, f32[256,1024]{1,0:T(8,128)}) fusion(f32[256,1024]{1,0:T(8,128)S(1)} %copy-done.9, f32[256]{0:T(256)S(1)} %add_rsqrt_fusion.2, f32[1024]{0:T(1024)S(1)} %bitcast.314, bf16[1024,2,4608]{2,0,1:T(8,128)(2,1)} %all-gather.11.cloned.1.call-done, bf16[256,1,4608]{2,0,1:T(8,128)(2,1)} %copy-done.34, ...), kind=kOutput, calls=%fused_computation.126 | convolution fusion | flops 4835769344 | bytes 25700352 | tf_op jit(solution)/shard_map/tgf,rgf->tr/dot_general | solution.py:538
  543.8 8.6 constant_dynamic-slice_fusion.1
  565.9 24.9 %shard_map.196 = bf16[16,192,256]{2,1,0:T(8,128)(2,1)} custom-call(s32[32]{0:T(128)S(1)} %broadcast_add_fusion.q_slot, s32[32]{0:T(128)S(1)} %get-tuple-element.35.kv_slot, s32[16]{0:T(128)S(1)} %get-tuple-element.113.first, s32[16]{0:T(128)S(1)} %get-tuple-element.114.last, bf16[16,64,256]{2,1,0:T(8,128)(2,1)S(1)} %all-to-all-done.2.d_ref, ...), custom_call_target="tpu_custom_call" | custom-call | tf_op jit(solution)/shard_map/pallas_call | solution.py:215
  606.7 16.1 %collective-permute-done.36 = bf16[2,2,576,256]{3,2,1,0:T(8,128)(2,1)} collective-permute-done((bf16[2,2,576,256]{3,2,1,0:T(8,128)(2,1)}, bf16[2,2,576,256]{3,2,1,0:T(8,128)(2,1)}, u32[]{:S(2)}, u32[]{:S(2)}) %collective-permute-start.36) | collective-permute-done | bytes 1179680 | tf_op jit(solution)/shard_map/ppermute | solution.py:247
  636.0 19.5 %collective-permute-done.28 = bf16[512,1152]{1,0:T(8,128)(2,1)S(1)} collective-permute-done((bf16[512,1152]{1,0:T(8,128)(2,1)S(1)}, bf16[512,1152]{1,0:T(8,128)(2,1)S(1)}, u32[]{:S(2)}, u32[]{:S(2)}) %collective-permute-start.28) | collective-permute-done | bytes 1179680 | tf_op jit(solution)/shard_map/ppermute | solution.py:256
  661.2 19.0 %collective-permute-done.39 = bf16[576,1024]{1,0:T(8,128)(2,1)S(1)} collective-permute-done((bf16[576,1024]{1,0:T(8,128)(2,1)S(1)}, bf16[576,1024]{1,0:T(8,128)(2,1)S(1)}, u32[]{:S(2)}, u32[]{:S(2)}) %collective-permute-start.39) | collective-permute-done | bytes 1179680 | tf_op jit(solution)/shard_map/ppermute | solution.py:256
  731.5 27.9 %collective-permute-start.22 = (bf16[256,1152]{1,0:T(8,128)(2,1)S(1)}, bf16[256,1152]{1,0:T(8,128)(2,1)}, u32[]{:S(2)}, u32[]{:S(2)}) collective-permute-start(bf16[256,1152]{1,0:T(8,128)(2,1)S(1)} %add_convert_fusion.3), channel_id=1, source_target_pairs={{0,8},{2,10},{4,12},{6,14},{8,0},{10,2},{12,4},{14,6},{16,24},{18,... | collective-permute-start | bytes 1769480 | tf_op jit(solution)/shard_map/ppermute | solution.py:250
  759.7 24.7 %collective-permute-start.42 = (bf16[288,1024]{1,0:T(8,128)(2,1)S(1)}, bf16[288,1024]{1,0:T(8,128)(2,1)}, u32[]{:S(2)}, u32[]{:S(2)}) collective-permute-start(bf16[288,1024]{1,0:T(8,128)(2,1)S(1)} %add_convert_fusion.1), channel_id=1, source_target_pairs={{0,8},{2,10},{4,12},{6,14},{8,0},{10,2},{12,4},{14,6},{16,24},{18,... | collective-permute-start | bytes 1769480 | tf_op jit(solution)/shard_map/ppermute | solution.py:250
  789.0 9.7 %collective-permute-done.42 = bf16[288,1024]{1,0:T(8,128)(2,1)} collective-permute-done((bf16[288,1024]{1,0:T(8,128)(2,1)S(1)}, bf16[288,1024]{1,0:T(8,128)(2,1)}, u32[]{:S(2)}, u32[]{:S(2)}) %collective-permute-start.42) | collective-permute-done | bytes 589856 | tf_op jit(solution)/shard_map/ppermute | solution.py:250
  810.9 9.3 collective-permute-done.10
  832.8 8.9 collective-permute-done.43.refs_1_
  857.3 9.8 %collective-permute-done.32.refs_5_ = bf16[2,256,1152]{2,1,0:T(8,128)(2,1)} collective-permute-done((bf16[2,256,1152]{2,1,0:T(8,128)(2,1)S(1)}, bf16[2,256,1152]{2,1,0:T(8,128)(2,1)}, u32[]{:S(2)}, u32[]{:S(2)}) %collective-permute-start.32) | collective-permute-done | bytes 1179680 | tf_op jit(solution)/shard_map/ppermute | solution.py:247
  874.6 41.0 %psum.7 = f32[2176]{0:T(1024)} all-reduce(f32[2176]{0:T(1024)} %concatenate.66), channel_id=1, replica_groups=mesh['ctx'=16,'fsdp'=2] {'ctx','fsdp'}, use_global_device_ids=true, to_apply=%region_24.25 | all-reduce | flops 2176 | bytes 17408 | tf_op jit(solution)/shard_map/psum | solution.py:642
  931.5 16.6 %shard_map.198 = f32[512,2,4608]{2,1,0:T(2,128)} custom-call(s32[3]{0:T(128)S(1)} %pad_add_fusion.here, bf16[2,256,1152]{2,1,0:T(8,128)(2,1)S(1)} %pad_maximum_fusion.14.refs_0_, bf16[2,256,1152]{2,1,0:T(8,128)(2,1)} %collective-permute-done.23.refs_1_, bf16[2,256,1152]{2,1,0:T(8,128)(2,1)} %collective-permute-done.24.refs_2_, ...), custom_call_target="tpu_custom_call" | custom-call | tf_op jit(solution)/shard_map/pallas_call | solution.py:308
  (453 shorter events, 338.5 us)
Async XLA Ops:
  7.2 61.9 %all-gather.7.cloned.1.call-start = ((), (), s32[]{:S(2)}) async-start(), calls=%async_computation.4 | async-start | bytes 6291456 | tf_op jit(solution)/shard_map/all_gather | solution.py:452
  7.9 164.5 %all-gather.9.cloned.1.call-start = ((), (), s32[]{:S(2)}) async-start(), calls=%async_computation.5 | async-start | bytes 3145728 | tf_op jit(solution)/shard_map/all_gather | solution.py:453
  8.7 322.5 %all-gather.11.cloned.1.call-start = ((), (), s32[]{:S(2)}) async-start(), calls=%async_computation.6 | async-start | bytes 28311552 | tf_op jit(solution)/shard_map/all_gather | solution.py:513
  83.2 367.4 %all-gather.13.cloned.1.call-start = ((), (), s32[]{:S(2)}) async-start(), calls=%async_computation.7 | async-start | bytes 14155776 | tf_op jit(solution)/shard_map/all_gather | solution.py:523
  490.8 71.6 %all-to-all-start.2 = ((bf16[16,64,256]{2,1,0:T(8,128)(2,1)}), bf16[16,64,256]{2,1,0:T(8,128)(2,1)S(1)}, u32[]{:S(2)}, u32[]{:S(2)}) async-start(bf16[16,64,256]{2,1,0:T(8,128)(2,1)} %bitcast.289), calls=%async_computation.2 | async-start | bytes 1048576 | tf_op jit(solution)/shard_map/all_to_all | solution.py:598
  514.6 44.3 %collective-permute-start.7 = (bf16[2,256,256]{2,1,0:T(8,128)(2,1)}, bf16[2,256,256]{2,1,0:T(8,128)(2,1)}, u32[]{:S(2)}, u32[]{:S(2)}) collective-permute-start(bf16[2,256,256]{2,1,0:T(8,128)(2,1)} %get-tuple-element.92), channel_id=1, source_target_pairs={{0,4},{2,6},{4,0},{6,2},{8,12},{10,14},{12,8},{14,10},{16,20},{18,... | collective-permute-start | bytes 786440 | tf_op jit(solution)/shard_map/ppermute | solution.py:247
  534.6 62.3 %collective-permute-start.18 = (bf16[512,1152]{1,0:T(8,128)(2,1)}, bf16[512,1152]{1,0:T(8,128)(2,1)}, u32[]{:S(2)}, u32[]{:S(2)}) collective-permute-start(bf16[512,1152]{1,0:T(8,128)(2,1)} %bitcast.262), channel_id=1, source_target_pairs={{0,4},{2,6},{4,0},{6,2},{8,12},{10,14},{12,8},{14,10},{16,20},{18,... | collective-permute-start | bytes 3538952 | tf_op jit(solution)/shard_map/ppermute | solution.py:247
  553.8 49.4 %collective-permute-start.27 = (bf16[512,1152]{1,0:T(8,128)(2,1)}, bf16[512,1152]{1,0:T(8,128)(2,1)}, u32[]{:S(2)}, u32[]{:S(2)}) collective-permute-start(bf16[512,1152]{1,0:T(8,128)(2,1)} %bitcast.260), channel_id=1, source_target_pairs={{0,4},{2,6},{4,0},{6,2},{8,12},{10,14},{12,8},{14,10},{16,20},{18,... | collective-permute-start | bytes 3538952 | tf_op jit(solution)/shard_map/ppermute | solution.py:247
  558.4 64.4 %collective-permute-start.36 = (bf16[2,2,576,256]{3,2,1,0:T(8,128)(2,1)}, bf16[2,2,576,256]{3,2,1,0:T(8,128)(2,1)}, u32[]{:S(2)}, u32[]{:S(2)}) collective-permute-start(bf16[2,2,576,256]{3,2,1,0:T(8,128)(2,1)} %get-tuple-element.46), channel_id=1, source_target_pairs={{0,4},{2,6},{4,0},{6,2},{8,12},{10,14},{12,8},{14,10},{16,20},{18,... | collective-permute-start | bytes 3538952 | tf_op jit(solution)/shard_map/ppermute | solution.py:247
  590.8 91.9 %all-to-all-start.3 = ((bf16[16,192,256]{2,1,0:T(8,128)(2,1)}), bf16[16,192,256]{2,1,0:T(8,128)(2,1)}, u32[]{:S(2)}, u32[]{:S(2)}) async-start(bf16[16,192,256]{2,1,0:T(8,128)(2,1)} %shard_map.196), calls=%async_computation.3 | async-start | bytes 3145728 | tf_op jit(solution)/shard_map/all_to_all | solution.py:611
  606.1 49.4 %collective-permute-start.28 = (bf16[512,1152]{1,0:T(8,128)(2,1)S(1)}, bf16[512,1152]{1,0:T(8,128)(2,1)S(1)}, u32[]{:S(2)}, u32[]{:S(2)}) collective-permute-start(bf16[512,1152]{1,0:T(8,128)(2,1)S(1)} %convolution_convert_fusion), channel_id=1, source_target_pairs={{0,1},{1,0},{2,3},{3,2},{4,5},{5,4},{6,7},{7,6},{8,9},{9,8},{10,11... | collective-permute-start | bytes 3538952 | tf_op jit(solution)/shard_map/ppermute | solution.py:256
  627.1 53.1 %collective-permute-start.39 = (bf16[576,1024]{1,0:T(8,128)(2,1)S(1)}, bf16[576,1024]{1,0:T(8,128)(2,1)S(1)}, u32[]{:S(2)}, u32[]{:S(2)}) collective-permute-start(bf16[576,1024]{1,0:T(8,128)(2,1)S(1)} %convolution_convert_fusion.2), channel_id=1, source_target_pairs={{0,1},{1,0},{2,3},{3,2},{4,5},{5,4},{6,7},{7,6},{8,9},{9,8},{10,11... | collective-permute-start | bytes 3538952 | tf_op jit(solution)/shard_map/ppermute | solution.py:256
  634.1 68.6 %collective-permute-start.20 = (bf16[256,1152]{1,0:T(8,128)(2,1)}, bf16[256,1152]{1,0:T(8,128)(2,1)}, u32[]{:S(2)}, u32[]{:S(2)}) collective-permute-start(bf16[256,1152]{1,0:T(8,128)(2,1)} %dynamic-slice_bitcast_fusion.4), channel_id=1, source_target_pairs={{0,8},{2,10},{4,12},{6,14},{8,0},{10,2},{12,4},{14,6},{16,24},{18,... | collective-permute-start | bytes 1769480 | tf_op jit(solution)/shard_map/ppermute | solution.py:250
  659.3 49.9 %collective-permute-start.29 = (bf16[256,1152]{1,0:T(8,128)(2,1)}, bf16[256,1152]{1,0:T(8,128)(2,1)}, u32[]{:S(2)}, u32[]{:S(2)}) collective-permute-start(bf16[256,1152]{1,0:T(8,128)(2,1)} %dynamic-slice_bitcast_fusion.3), channel_id=1, source_target_pairs={{0,8},{2,10},{4,12},{6,14},{8,0},{10,2},{12,4},{14,6},{16,24},{18,... | collective-permute-start | bytes 1769480 | tf_op jit(solution)/shard_map/ppermute | solution.py:250
  711.3 97.3 %collective-permute-start.30 = (bf16[256,1152]{1,0:T(8,128)(2,1)}, bf16[256,1152]{1,0:T(8,128)(2,1)}, u32[]{:S(2)}, u32[]{:S(2)}) collective-permute-start(bf16[256,1152]{1,0:T(8,128)(2,1)} %fusion.31), channel_id=1, source_target_pairs={{0,24},{2,26},{4,28},{6,30},{8,16},{10,18},{12,20},{14,22},{16,8},... | collective-permute-start | bytes 1769480 | tf_op jit(solution)/shard_map/ppermute | solution.py:253
  722.6 62.5 %collective-permute-start.8 = (bf16[512,768]{0,1:T(8,128)(2,1)S(1)}, bf16[512,768]{0,1:T(8,128)(2,1)S(1)}, u32[]{:S(2)}, u32[]{:S(2)}) collective-permute-start(bf16[512,768]{0,1:T(8,128)(2,1)S(1)} %pad_maximum_fusion.24), channel_id=1, source_target_pairs={{0,1},{1,0},{2,3},{3,2},{4,5},{5,4},{6,7},{7,6},{8,9},{9,8},{10,11... | collective-permute-start | bytes 2359304 | tf_op jit(solution)/shard_map/ppermute | solution.py:256
  731.5 54.8 %collective-permute-start.22 = (bf16[256,1152]{1,0:T(8,128)(2,1)S(1)}, bf16[256,1152]{1,0:T(8,128)(2,1)}, u32[]{:S(2)}, u32[]{:S(2)}) collective-permute-start(bf16[256,1152]{1,0:T(8,128)(2,1)S(1)} %add_convert_fusion.3), channel_id=1, source_target_pairs={{0,8},{2,10},{4,12},{6,14},{8,0},{10,2},{12,4},{14,6},{16,24},{18,... | collective-permute-start | bytes 1769480 | tf_op jit(solution)/shard_map/ppermute | solution.py:250
  787.5 57.9 %collective-permute-start.23 = (bf16[2,256,1152]{2,1,0:T(8,128)(2,1)S(1)}, bf16[2,256,1152]{2,1,0:T(8,128)(2,1)}, u32[]{:S(2)}, u32[]{:S(2)}) collective-permute-start(bf16[2,256,1152]{2,1,0:T(8,128)(2,1)S(1)} %pad_maximum_fusion.14.refs_0_), channel_id=1, source_target_pairs={{0,4},{2,6},{4,0},{6,2},{8,12},{10,14},{12,8},{14,10},{16,20},{18,... | collective-permute-start | bytes 3538952 | tf_op jit(solution)/shard_map/ppermute | solution.py:247
  810.9 46.5 %collective-permute-start.24 = (bf16[2,256,1152]{2,1,0:T(8,128)(2,1)S(1)}, bf16[2,256,1152]{2,1,0:T(8,128)(2,1)}, u32[]{:S(2)}, u32[]{:S(2)}) collective-permute-start(bf16[2,256,1152]{2,1,0:T(8,128)(2,1)S(1)} %pad_maximum_fusion.14.refs_0_), channel_id=1, source_target_pairs={{0,2},{2,0},{4,6},{6,4},{8,10},{10,8},{12,14},{14,12},{16,18},{18,... | collective-permute-start | bytes 3538952 | tf_op jit(solution)/shard_map/ppermute | solution.py:244
  842.8 72.8 %collective-permute-start.45 = (bf16[2,288,1024]{2,1,0:T(8,128)(2,1)}, bf16[2,288,1024]{2,1,0:T(8,128)(2,1)}, u32[]{:S(2)}, u32[]{:S(2)}) collective-permute-start(bf16[2,288,1024]{2,1,0:T(8,128)(2,1)} %copy-done), channel_id=1, source_target_pairs={{0,2},{2,0},{4,6},{6,4},{8,10},{10,8},{12,14},{14,12},{16,18},{18,... | collective-permute-start | bytes 3538952 | tf_op jit(solution)/shard_map/ppermute | solution.py:244
  845.4 70.2 %collective-permute-start.12 = (bf16[2,256,768]{2,1,0:T(8,128)(2,1)}, bf16[2,256,768]{2,1,0:T(8,128)(2,1)}, u32[]{:S(2)}, u32[]{:S(2)}) collective-permute-start(bf16[2,256,768]{2,1,0:T(8,128)(2,1)} %pad_maximum_fusion.25.refs_0_), channel_id=1, source_target_pairs={{0,4},{2,6},{4,0},{6,2},{8,12},{10,14},{12,8},{14,10},{16,20},{18,... | collective-permute-start | bytes 2359304 | tf_op jit(solution)/shard_map/ppermute | solution.py:247
  857.3 74.1 %collective-permute-start.33 = (bf16[2,256,1152]{2,1,0:T(8,128)(2,1)S(1)}, bf16[2,256,1152]{2,1,0:T(8,128)(2,1)}, u32[]{:S(2)}, u32[]{:S(2)}) collective-permute-start(bf16[2,256,1152]{2,1,0:T(8,128)(2,1)S(1)} %pad_maximum_fusion.15.refs_4_), channel_id=1, source_target_pairs={{0,2},{2,0},{4,6},{6,4},{8,10},{10,8},{12,14},{14,12},{16,18},{18,... | collective-permute-start | bytes 3538952 | tf_op jit(solution)/shard_map/ppermute | solution.py:244
  867.1 64.3 %collective-permute-start.25 = (bf16[2,256,1152]{2,1,0:T(8,128)(2,1)}, bf16[2,256,1152]{2,1,0:T(8,128)(2,1)}, u32[]{:S(2)}, u32[]{:S(2)}) collective-permute-start(bf16[2,256,1152]{2,1,0:T(8,128)(2,1)} %collective-permute-done.23.refs_1_), channel_id=1, source_target_pairs={{0,2},{2,0},{4,6},{6,4},{8,10},{10,8},{12,14},{14,12},{16,18},{18,... | collective-permute-start | bytes 3538952 | tf_op jit(solution)/shard_map/ppermute | solution.py:244
  867.1 64.3 %collective-permute-start.34 = (bf16[2,256,1152]{2,1,0:T(8,128)(2,1)}, bf16[2,256,1152]{2,1,0:T(8,128)(2,1)}, u32[]{:S(2)}, u32[]{:S(2)}) collective-permute-start(bf16[2,256,1152]{2,1,0:T(8,128)(2,1)} %collective-permute-done.32.refs_5_), channel_id=1, source_target_pairs={{0,2},{2,0},{4,6},{6,4},{8,10},{10,8},{12,14},{14,12},{16,18},{18,... | collective-permute-start | bytes 3538952 | tf_op jit(solution)/shard_map/ppermute | solution.py:244
  (118 other events, 2390.0 us)
Sparse Core Ops, SparseCore 0:
  9.6 59.5 all-gather.6
  70.7 33.1 all-gather.8
  106.0 225.1 all-gather.10
  332.6 117.9 all-gather.12

commit v3 on v1

--- a/solution.py
+++ b/solution.py
@@ -12,6 +12,7 @@
 HD = 64
 BLK = 128
 TILE = 256
+CHUNKS = 2
 
 
 EPSILON = 1e-05
@@ -219,6 +220,729 @@
         scratch_shapes=scratch,
         compiler_params=pltpu.CompilerParams(vmem_limit_bytes=48 * 1024 * 1024),
     )(*tables, *arrays)
+
+
+class Links:
+    def __init__(self, ctx_size):
+        self.depth = ctx_size // 4
+        index = lax.axis_index("ctx")
+        self.core = index % 2
+        self.y = (index // 2) % 2
+        self.side = lax.axis_index("fsdp")
+        self.half = ((index // 4 + 1) // 2) % 2
+        self.quarter = index % 2 * 2 + self.y
+        self.here = jnp.stack([self.half, self.core, self.y, self.side]).astype(jnp.int32)
+
+    def route(self, place):
+        pairs = []
+        for z in range(self.depth):
+            for y in range(2):
+                for core in range(2):
+                    to_z, to_y, to_core = place(z, y, core)
+                    pairs.append(((z * 2 + y) * 2 + core, (to_z * 2 + to_y) * 2 + to_core))
+        return pairs
+
+    def over_core(self, value):
+        return lax.ppermute(value, "ctx", self.route(lambda z, y, c: (z, y, 1 - c)))
+
+    def over_y(self, value):
+        return lax.ppermute(value, "ctx", self.route(lambda z, y, c: (z, 1 - y, c)))
+
+    def over_z(self, value):
+        return lax.ppermute(value, "ctx", self.route(lambda z, y, c: (z ^ 1, y, c)))
+
+    def mirror_z(self, value):
+        return lax.ppermute(value, "ctx", self.route(lambda z, y, c: (self.depth - 1 - z, y, c)))
+
+    def over_x(self, value):
+        return lax.ppermute(value, "fsdp", [(0, 1), (1, 0)])
+
+    def spread_plane(self, value):
+        across = self.over_core(value)
+        beside = self.over_y(value)
+        return (value, across, beside, self.over_core(beside))
+
+    def deal_plane(self, keep, keep_far, give, give_far):
+        got, got_far = self.over_core(give), self.over_core(give_far)
+        return (keep, got, self.over_y(keep_far), self.over_y(got_far))
+
+    def sum_depth(self, kept, got):
+        rows = kept.shape[0] // 2
+
+        def half(index):
+            return add(
+                lax.dynamic_slice_in_dim(kept, index * rows, rows),
+                lax.dynamic_slice_in_dim(got, index * rows, rows),
+            )
+
+        given = self.over_z(half(1 - self.half))
+        part = add(half(self.half), given)
+        full = add(part, self.mirror_z(part))
+        return (full, self.over_z(full))
+
+    def reduce(self, sent, kept):
+        return [self.spread_plane(v) for v in self.sum_depth(kept, self.over_x(sent))]
+
+    def total(self, value):
+        for swap in (self.over_core, self.over_y, self.over_x, self.over_z, self.mirror_z):
+            value = value + swap(value)
+        return value
+
+
+def pick(value, index, axis):
+    return lax.dynamic_index_in_dim(value, index, axis, keepdims=False)
+
+
+def add(left, right):
+    return (left.astype(jnp.float32) + right.astype(jnp.float32)).astype(jnp.bfloat16)
+
+
+def after(value, *others):
+    return lax.optimization_barrier((value, *others))[0]
+
+
+def contract(left, right, axes):
+    return lax.dot_general(
+        left, right, ((axes[:1], axes[1:]), ((), ())), preferred_element_type=jnp.float32
+    )
+
+
+PARAMS = pltpu.CompilerParams(vmem_limit_bytes=56 * 1024 * 1024)
+
+
+def call_with_here(kernel, here, grid, arrays, specs, outs, out_specs, scratch=(), aliases=None):
+    return pl.pallas_call(
+        kernel,
+        grid_spec=pltpu.PrefetchScalarGridSpec(
+            num_scalar_prefetch=1,
+            grid=grid,
+            in_specs=specs,
+            out_specs=out_specs,
+            scratch_shapes=list(scratch),
+        ),
+        out_shape=outs,
+        input_output_aliases=aliases or {},
+        compiler_params=PARAMS,
+    )(here, *arrays)
+
+
+def whole(array):
+    rank = len(array.shape)
+    return pl.BlockSpec(array.shape, lambda i, here: (0,) * rank)
+
+
+def place_rows(here, own, pieces):
+    rows, columns = own.shape
+    part = rows // 4
+
+    def kernel(here, own_ref, *refs):
+        out_ref = refs[-1]
+        s = pl.program_id(0)
+
+        @pl.when(s < 4)
+        def _():
+            out_ref[...] = own_ref[...]
+
+        for p in range(4):
+
+            @pl.when(s == 4 + p)
+            def _(p=p):
+                out_ref[...] = refs[p][...]
+
+    def target(s, here):
+        p = s - 4
+        other = (1 - here[3]) * 4 + ((p % 2) ^ here[1]) * 2 + ((p // 2) ^ here[2])
+        return (jnp.where(s < 4, here[3] * 4 + s, other), 0)
+
+    (out,) = call_with_here(
+        kernel,
+        here,
+        (8,),
+        [own, *pieces],
+        [pl.BlockSpec((part, columns), lambda s, here: (jnp.minimum(s, 3), 0))]
+        + [whole(p) for p in pieces],
+        [jax.ShapeDtypeStruct((2 * rows, columns), own.dtype)],
+        [pl.BlockSpec((part, columns), target)],
+    )
+    return out
+
+
+def ffn_kernel(chunk, here, *refs):
+    two_ref, d_ref, own_ref = refs[:3]
+    gate_pieces, down_ref, down_pieces = refs[3:7], refs[7], refs[8:12]
+    before_out, before_two = refs[12:14]
+    keep, give, hidden_keep, hidden_give = refs[14:16], refs[16:18], refs[18:20], refs[20:22]
+    out_ref, d_two_ref = refs[22:24]
+    weight, down, hidden_t = refs[24:27]
+    core, y, side = here[1], here[2], here[3]
+    t = pl.program_id(0)
+    f32, bf16 = jnp.float32, jnp.bfloat16
+    own_rows = own_ref.shape[1]
+    part = own_rows // 4
+
+    @pl.when(t == 0)
+    def _():
+        out_ref[...] = before_out[...]
+        d_two_ref[...] = before_two[...]
+
+    def quarter(p):
+        return ((p % 2) ^ core) * 2 + ((p // 2) ^ y)
+
+    weight[:, pl.ds(pl.multiple_of(side * own_rows, own_rows), own_rows), :] = own_ref[...]
+    for p in range(4):
+        at = pl.multiple_of((1 - side) * own_rows + quarter(p) * part, part)
+        weight[:, pl.ds(at, part), :] = gate_pieces[p][...]
+
+    @pl.when(side == chunk)
+    def _():
+        down[...] = down_ref[...]
+
+    @pl.when(side != chunk)
+    def _():
+        for p in range(4):
+            wide = down_pieces[p].shape[1]
+            at = pl.multiple_of(quarter(p) * wide, wide)
+            down[:, pl.ds(at, wide)] = down_pieces[p][...]
+
+    two = two_ref[...]
+    d_ffn = d_ref[...]
+    tile = own_ref.shape[2]
+    first = (tile // 2) // 256 * 256
+    for begin, end in ((0, first), (first, tile)):
+        at = slice(begin, end)
+        gate = jnp.dot(two, weight[0, :, at], preferred_element_type=f32)
+        upper = jnp.dot(two, weight[1, :, at], preferred_element_type=f32)
+        d_hidden = contract(d_ffn, down[at, :], (1, 1))
+        sigma = jax.nn.sigmoid(gate)
+        silu = gate * sigma
+        hidden = (silu * upper).astype(bf16)
+        d_gate = (d_hidden * upper * sigma * (1.0 + gate * (1.0 - sigma))).astype(bf16)
+        d_upper = (d_hidden * silu).astype(bf16)
+        out_ref[...] += jnp.dot(hidden, down[at, :], preferred_element_type=f32)
+        d_two_ref[...] += contract(d_gate, weight[0, :, at], (1, 1)) + contract(
+            d_upper, weight[1, :, at], (1, 1)
+        )
+        hidden_t[at, :] = hidden.T
+        mine = jnp.where(core == 0, d_gate, d_upper)
+        other = jnp.where(core == 0, d_upper, d_gate)
+        for far in range(2):
+
+            @pl.when((t == y) == (far == 0))
+            def _(far=far):
+                keep[far][:, at] = mine
+                give[far][:, at] = other
+
+    share = tile // 2
+    for far in range(2):
+        at = pl.multiple_of((y ^ far) * share, share)
+
+        @pl.when(t == core)
+        def _(far=far, at=at):
+            hidden_keep[far][...] = hidden_t[pl.ds(at, share), :]
+
+        @pl.when(t != core)
+        def _(far=far, at=at):
+            hidden_give[far][...] = hidden_t[pl.ds(at, share), :]
+
+
+def ffn(here, chunk, two, d_ffn, own, pieces, down, down_pieces, before):
+    tokens, width = two.shape
+    tile = own.shape[2] // 4
+    share = tile // 2
+    shape = jax.ShapeDtypeStruct
+    f32, bf16 = jnp.float32, jnp.bfloat16
+    outs = (
+        [shape((tokens, tile), bf16)] * 4
+        + [shape((share, tokens), bf16)] * 4
+        + [shape((tokens, width), f32)] * 2
+    )
+
+    def own_down(t, here):
+        return (jnp.where(here[3] == chunk, t, 0), 0)
+
+    def other_down(t, here):
+        return (jnp.where(here[3] == chunk, 0, t), 0)
+
+    specs = (
+        [whole(two), whole(d_ffn)]
+        + [pl.BlockSpec((2, own.shape[1], tile), lambda t, here: (0, 0, 2 * chunk + t))]
+        + [pl.BlockSpec((2, own.shape[1] // 4, tile), lambda t, here: (0, 0, t))] * 4
+        + [pl.BlockSpec((tile, width), own_down)]
+        + [pl.BlockSpec((tile, width // 4), other_down)] * 4
+        + [whole(before[0]), whole(before[1])]
+    )
+    got = call_with_here(
+        functools.partial(ffn_kernel, chunk),
+        here,
+        (2,),
+        [two, d_ffn, own, *pieces, down, *down_pieces, *before],
+        specs,
+        outs,
+        [whole(o) for o in outs],
+        [
+            pltpu.VMEM((2, width, tile), bf16),
+            pltpu.VMEM((tile, width), bf16),
+            pltpu.VMEM((tile, tokens), bf16),
+        ],
+    )
+    return got[:4], got[4:8], got[8:]
+
+
+def wide_product_kernel(here, *refs):
+    planes, terms = refs[:4], refs[4:8]
+    sent, kept, left, right = refs[8:]
+    tokens = planes[0].shape[0]
+    for i in range(4):
+        left[:, i * tokens : (i + 1) * tokens] = planes[i][...].T
+        right[i * tokens : (i + 1) * tokens, :] = terms[i][...]
+    side = here[3]
+    rows = kept.shape[0]
+    step = 256
+    for at in range(0, rows, step):
+        for owner, out_ref in ((1 - side, sent), (side, kept)):
+            place = pl.multiple_of(owner * rows + at, step)
+            out_ref[at : at + step, :] = jnp.dot(
+                left[pl.ds(place, step), :], right[...], preferred_element_type=jnp.float32
+            ).astype(out_ref.dtype)
+
+
+def wide_products(here, planes, terms):
+    tokens, rows = planes[0].shape
+    columns = terms[0].shape[1]
+    outs = [
+        jax.ShapeDtypeStruct((rows // 2, columns), jnp.bfloat16),
+        jax.ShapeDtypeStruct((rows // 2, columns), jnp.float32),
+    ]
+    arrays = [*planes, *terms]
+    return call_with_here(
+        wide_product_kernel,
+        here,
+        (1,),
+        arrays,
+        [whole(a) for a in arrays],
+        outs,
+        [whole(o) for o in outs],
+        [
+            pltpu.VMEM((rows, 4 * tokens), jnp.bfloat16),
+            pltpu.VMEM((4 * tokens, columns), jnp.bfloat16),
+        ],
+    )
+
+
+def down_product_kernel(here, *refs):
+    planes, terms = refs[:4], (refs[4:8], refs[8:12])
+    sent, kept, left, right = refs[12:]
+    tokens = planes[0].shape[0]
+    for i in range(4):
+        right[i * tokens : (i + 1) * tokens, :] = planes[i][...]
+    for chunk in range(2):
+        for i in range(4):
+            left[:, i * tokens : (i + 1) * tokens] = terms[chunk][i][...]
+        product = jnp.dot(left[...], right[...], preferred_element_type=jnp.float32)
+
+        @pl.when(here[3] == chunk)
+        def _(product=product):
+            kept[...] = product
+
+        @pl.when(here[3] != chunk)
+        def _(product=product):
+            sent[...] = product.astype(sent.dtype)
+
+
+def down_products(here, planes, first, second):
+    tokens, columns = planes[0].shape
+    rows = first[0].shape[0]
+    outs = [
+        jax.ShapeDtypeStruct((rows, columns), jnp.bfloat16),
+        jax.ShapeDtypeStruct((rows, columns), jnp.float32),
+    ]
+    arrays = [*planes, *first, *second]
+    return call_with_here(
+        down_product_kernel,
+        here,
+        (1,),
+        arrays,
+        [whole(a) for a in arrays],
+        outs,
+        [whole(o) for o in outs],
+        [
+            pltpu.VMEM((rows, 4 * tokens), jnp.bfloat16),
+            pltpu.VMEM((4 * tokens, columns), jnp.bfloat16),
+        ],
+    )
+
+
+def attention_product_kernel(here, *refs):
+    normed, projected, attn, d_attn = refs[:4], refs[4:8], refs[8:12], refs[12:16]
+    sent, kept, left, right, left_out, right_out = refs[16:]
+    tokens = normed[0].shape[0]
+    for i in range(4):
+        at = slice(i * tokens, (i + 1) * tokens)
+        left[:, at] = normed[i][...].T
+        right[at, :] = projected[i][...].T
+        left_out[:, at] = attn[i][...]
+        right_out[at, :] = d_attn[i][...]
+    rows = kept.shape[0]
+    cut = right.shape[1]
+    for owner, out_ref in ((1 - here[3], sent), (here[3], kept)):
+        at = pl.ds(pl.multiple_of(owner * rows, rows), rows)
+        out_ref[:, :cut] = jnp.dot(
+            left[at, :], right[...], preferred_element_type=jnp.float32
+        ).astype(out_ref.dtype)
+        out_ref[:, cut:] = jnp.dot(
+            left_out[at, :], right_out[...], preferred_element_type=jnp.float32
+        ).astype(out_ref.dtype)
+
+
+def attention_products(here, normed, projected, attn, d_attn):
+    tokens, rows = normed[0].shape
+    cut, rest = projected[0].shape[0], d_attn[0].shape[1]
+    outs = [
+        jax.ShapeDtypeStruct((rows // 2, cut + rest), jnp.bfloat16),
+        jax.ShapeDtypeStruct((rows // 2, cut + rest), jnp.float32),
+    ]
+    arrays = [*normed, *projected, *attn, *d_attn]
+    return call_with_here(
+        attention_product_kernel,
+        here,
+        (1,),
+        arrays,
+        [whole(a) for a in arrays],
+        outs,
+        [whole(o) for o in outs],
+        [
+            pltpu.VMEM((rows, 4 * tokens), jnp.bfloat16),
+            pltpu.VMEM((4 * tokens, cut), jnp.bfloat16),
+            pltpu.VMEM((rows, 4 * tokens), jnp.bfloat16),
+            pltpu.VMEM((4 * tokens, rest), jnp.bfloat16),
+        ],
+    )
+
+
+def place_gate_up_kernel(blocks, here, *refs):
+    out_ref = refs[-1]
+    pieces = refs[:8]
+    wide = pieces[0].shape[1]
+    far_half = (pl.program_id(0) // blocks) ^ here[0]
+    for case in range(8):
+        half, core, y = case // 4, case // 2 % 2, case % 2
+
+        @pl.when((far_half == half) & (here[1] == core) & (here[2] == y))
+        def _(half=half, core=core, y=y):
+            for kind in range(2):
+                for column in range(2):
+                    value = pieces[half * 4 + (y ^ column) * 2 + (core ^ kind)][...]
+                    out_ref[:, kind, column * wide : (column + 1) * wide] = value.astype(
+                        jnp.float32
+                    )
+
+
+def place_gate_up(here, chunk, pieces, before):
+    rows, wide = pieces[0][0].shape
+    step = 64
+    blocks = rows // step
+
+    def source(half):
+        return lambda i, here: (jnp.clip(i - blocks * (here[0] ^ half), 0, blocks - 1), 0)
+
+    arrays = [v for plane in pieces for v in plane]
+    specs = [pl.BlockSpec((step, wide), source(n // 4)) for n in range(8)]
+    aliases = {}
+    if before is not None:
+        arrays.append(before)
+        specs.append(pl.BlockSpec(memory_space=pl.ANY))
+        aliases = {9: 0}
+    (out,) = call_with_here(
+        functools.partial(place_gate_up_kernel, blocks),
+        here,
+        (2 * blocks,),
+        arrays,
+        specs,
+        [jax.ShapeDtypeStruct((2 * rows, 2, 2 * wide * CHUNKS), jnp.float32)],
+        [pl.BlockSpec((step, 2, 2 * wide), lambda i, here: (i, 0, chunk))],
+        aliases=aliases,
+    )
+    return out
+
+
+def place_pieces(here, pieces, cuts, by_rows):
+    rows = pieces[0][0].shape[0]
+    flat = [v for plane in pieces for v in plane]
+
+    def kernel(here, *refs):
+        for s in range(8):
+
+            @pl.when(pl.program_id(0) == s)
+            def _(s=s):
+                at = 0
+                for out_ref in refs[8:]:
+                    wide = out_ref.shape[1]
+                    out_ref[...] = refs[s][:, at : at + wide].astype(jnp.float32)
+                    at += wide
+
+    def target(s, here):
+        half = (s // 4) ^ here[0]
+        y = ((s // 2) % 2) ^ here[2]
+        core = (s % 2) ^ here[1]
+        if by_rows:
+            return ((core * 2 + y) * 2 + half, 0)
+        return (half, core * 2 + y)
+
+    across, along = (1, 8) if by_rows else (4, 2)
+    return call_with_here(
+        kernel,
+        here,
+        (8,),
+        flat,
+        [whole(v) for v in flat],
+        [jax.ShapeDtypeStruct((rows * along, wide * across), jnp.float32) for wide in cuts],
+        [pl.BlockSpec((rows, wide), target) for wide in cuts],
+    )
+
+
+def on_block(
+    tokens,
+    qkv_weight,
+    out_weight,
+    gate_up_weight,
+    down_weight,
+    attn_gain,
+    ffn_gain,
+    query_gain,
+    key_gain,
+    seq_lengths,
+    block_order,
+    cotangent,
+):
+    inputs = tokens[0].astype(jnp.float32)
+    rows_here = inputs.shape[0]
+    ctx_size = lax.axis_size("ctx")
+    ctx_index = lax.axis_index("ctx")
+    per_group = HEADS // KV_HEADS
+    q_width = HEADS * HD
+    kv_width = KV_HEADS * HD
+    order_row = block_order[0]
+    lengths_row = seq_lengths[0]
+    slots = jnp.arange(rows_here, dtype=jnp.int32) // BLK + ctx_index * (rows_here // BLK)
+    table = slots[:, None] == jnp.arange(order_row.shape[0], dtype=jnp.int32)[None, :]
+    packed = (
+        jnp.sum(jnp.where(table, order_row[None, :], 0), axis=1) * BLK
+        + jnp.arange(rows_here, dtype=jnp.int32) % BLK
+    )
+    local = packed - starts_of(packed, lengths_row)
+    frequency = ROPE_BASE ** (-2.0 * jnp.arange(HD // 2, dtype=jnp.float32) / HD)
+    angle = frequency[:, None] * local.astype(jnp.float32)[None, :]
+    cosine = jnp.cos(angle)[None]
+    sine = jnp.sin(angle)[None]
+    bf16, f32 = jnp.bfloat16, jnp.float32
+    parts = ctx_size // HEADS
+    part = ctx_index // HEADS
+    part_blocks = HEADS * rows_here // BLK
+    q_order = lax.dynamic_slice_in_dim(order_row, part * part_blocks, part_blocks)
+    q_slot, q_place, q_start = block_tables(q_order, lengths_row)
+    q_slot = q_slot + part * part_blocks
+    kv_slot, _, _ = block_tables(order_row, lengths_row)
+    first = jnp.min(q_start.reshape(-1, TILE), axis=1) // TILE
+    last = jnp.max(q_place.reshape(-1, TILE), axis=1) // TILE + 1
+    tables = (q_slot, kv_slot, first, last)
+    q_rows, kv_rows = part_blocks * BLK, order_row.shape[0] * BLK
+
+    links = Links(ctx_size)
+    here = links.here
+    width = inputs.shape[1]
+    rows = qkv_weight.shape[0]
+    part_rows = rows // 4
+
+    def quarter_rows(weight):
+        return lax.dynamic_slice_in_dim(weight, links.quarter * part_rows, part_rows)
+
+    gains_here = jnp.concatenate([attn_gain, ffn_gain, query_gain, key_gain])
+    gains_there = links.over_x(gains_here)
+
+    def gain_of(at, size):
+        mine, other = gains_here[at : at + size], gains_there[at : at + size]
+        return jnp.where(
+            links.side == 0, jnp.concatenate([mine, other]), jnp.concatenate([other, mine])
+        ).astype(f32)
+
+    gain_attn = gain_of(0, rows)
+    gain_ffn = gain_of(rows, rows)
+    gain_query = gain_of(2 * rows, HD // 2)
+    gain_key = gain_of(2 * rows + HD // 2, HD // 2)
+    qkv_there = links.over_x(quarter_rows(qkv_weight))
+    qkv_pieces = links.spread_plane(qkv_there)
+    gate_up = jnp.transpose(gate_up_weight, (1, 0, 2))
+    ff_chunk = gate_up.shape[2] // CHUNKS
+    out_there = links.over_x(after(quarter_rows(out_weight), qkv_there))
+
+    def gate_up_piece(chunk):
+        return lax.dynamic_slice(
+            gate_up, (0, links.quarter * part_rows, chunk * ff_chunk), (2, part_rows, ff_chunk)
+        )
+
+    first_there = links.over_x(after(gate_up_piece(0), qkv_there))
+    down_there = links.over_x(
+        after(
+            lax.dynamic_slice_in_dim(down_weight, links.quarter * (width // 4), width // 4, 1),
+            out_there,
+        )
+    )
+    second_there = links.over_x(after(gate_up_piece(1), first_there))
+    out_pieces = links.spread_plane(out_there)
+    gate_up_pieces = [links.spread_plane(first_there), links.spread_plane(second_there)]
+    down_pieces = links.spread_plane(down_there)
+    w_out = place_rows(here, out_weight, out_pieces)
+    scale_one = rms_scale(inputs)
+    normed = (inputs * scale_one * gain_attn).astype(jnp.bfloat16)
+    w_qkv = place_rows(here, qkv_weight, qkv_pieces)
+    projected = lax.dot_general(
+        w_qkv, normed, (((0,), (1,)), ((), ())), preferred_element_type=f32
+    )
+    q_raw = projected[:q_width].reshape(HEADS, HD, rows_here)
+    k_raw = projected[q_width : q_width + kv_width].reshape(KV_HEADS, HD, rows_here)
+    values_here = projected[q_width + kv_width :].reshape(KV_HEADS, HD, rows_here).astype(bf16)
+    q_scale = rms_scale(q_raw, 1)
+    k_scale = rms_scale(k_raw, 1)
+    column_query, column_key = gain_query[:, None], gain_key[:, None]
+    queries = rope(q_raw * q_scale * column_query, cosine, sine).astype(bf16)
+    keys_here = rope(k_raw * k_scale * column_key, cosine, sine).astype(bf16)
+    sent = jnp.concatenate(
+        [queries, jnp.repeat(keys_here, per_group, 0), jnp.repeat(values_here, per_group, 0)], axis=1
+    )
+    sent = jnp.concatenate([sent] * parts, axis=0)
+    got = lax.all_to_all(sent, "ctx", 0, 0, tiled=True)
+    q_place, q_start = q_place[None], q_start[None]
+    shape = jax.ShapeDtypeStruct
+    attn_sent, *held = kernel_call(
+        attend_kernel,
+        tables,
+        (got, q_place, q_start),
+        [
+            shape((ctx_size, HD, rows_here), bf16),
+            shape((q_rows, HD), bf16),
+            shape((HD, q_rows), bf16),
+            shape((kv_rows, HD), bf16),
+            shape((HD, kv_rows), bf16),
+            shape((kv_rows, HD), bf16),
+            shape((HD, q_rows), f32),
+            shape((1, q_rows), f32),
+        ],
+        [pltpu.VMEM((HD, kv_rows), bf16)],
+    )
+    attn_in = lax.dynamic_slice_in_dim(
+        lax.all_to_all(attn_sent, "ctx", 0, 0, tiled=True), part * HEADS, HEADS
+    ).reshape(q_width, rows_here)
+    normed_plane = links.spread_plane(after(normed, got))
+    d_ffn = cotangent[0]
+    ffn_plane = links.spread_plane(after(d_ffn, got))
+    attn_plane = links.spread_plane(attn_in)
+    h_one = inputs + contract(attn_in, w_out, (0, 0))
+    scale_two = rms_scale(h_one)
+    normed_two = (h_one * scale_two * gain_ffn).astype(bf16)
+    two_plane = links.spread_plane(normed_two)
+    sums = [h_one, jnp.zeros_like(h_one)]
+    products, hidden_plane = [], []
+    for chunk in range(CHUNKS):
+        d_wide, hidden, sums = ffn(
+            here, chunk, normed_two, d_ffn, gate_up, gate_up_pieces[chunk],
+            down_weight, down_pieces, sums,
+        )
+        products.append(wide_products(here, two_plane, links.deal_plane(*d_wide)))
+        hidden_plane.append(links.deal_plane(*hidden))
+    output = sums[0].astype(bf16)
+    d_norm_two, ffn_gain_term = norm_back(sums[1], h_one, scale_two, gain_ffn)
+    d_h_one = d_ffn.astype(f32) + d_norm_two
+    d_attn = d_h_one.astype(bf16)
+    d_heads = lax.dot_general(
+        w_out, d_attn, (((1,), (1,)), ((), ())), preferred_element_type=f32
+    ).astype(bf16)
+    d_heads = jnp.concatenate([d_heads.reshape(HEADS, HD, rows_here)] * parts, axis=0)
+    d_got = lax.all_to_all(d_heads, "ctx", 0, 0, tiled=True)
+    (d_sent,) = kernel_call(
+        attend_back_kernel,
+        tables,
+        (d_got, q_place, q_start, *held),
+        [shape((ctx_size, 3 * HD, rows_here), bf16)],
+        [
+            pltpu.VMEM((HD, q_rows), bf16),
+            pltpu.VMEM((q_rows, HD), bf16),
+            pltpu.VMEM((kv_rows, HD), f32),
+            pltpu.VMEM((kv_rows, HD), f32),
+        ],
+    )
+    d_back = lax.all_to_all(d_sent, "ctx", 0, 0, tiled=True)
+    d_query = lax.dynamic_slice_in_dim(d_back[:, :HD], part * HEADS, HEADS).astype(f32)
+    d_key_value = jnp.sum(
+        d_back[:, HD:].reshape(parts, KV_HEADS, per_group, 2 * HD, rows_here).astype(f32),
+        axis=(0, 2),
+    )
+    dq_normed = rope_back(d_query, cosine, sine)
+    dk_normed = rope_back(d_key_value[:, :HD], cosine, sine)
+    dq_raw, query_term = norm_back(dq_normed, q_raw, q_scale, column_query, 1)
+    dk_raw, key_term = norm_back(dk_normed, k_raw, k_scale, column_key, 1)
+    d_projected = jnp.concatenate(
+        [
+            dq_raw.reshape(q_width, rows_here).astype(bf16),
+            dk_raw.reshape(kv_width, rows_here).astype(bf16),
+            d_key_value[:, HD:].reshape(kv_width, rows_here).astype(bf16),
+        ],
+        axis=0,
+    )
+    d_normed = contract(d_projected, w_qkv, (0, 1))
+    d_norm_one, attn_gain_term = norm_back(d_normed, inputs, scale_one, gain_attn)
+    d_inputs = d_h_one + d_norm_one
+    grad_gate_up = None
+    for chunk in range(CHUNKS):
+        grad_gate_up = place_gate_up(here, chunk, links.reduce(*products[chunk]), grad_gate_up)
+    (grad_down,) = place_pieces(
+        here, links.reduce(*down_products(here, ffn_plane, *hidden_plane)), (width,), True
+    )
+
+    def deal(value, size, axis):
+        def share(core, y):
+            return lax.dynamic_slice_in_dim(value, (core * 2 + y) * size, size, axis)
+
+        return links.deal_plane(
+            share(links.core, links.y),
+            share(links.core, 1 - links.y),
+            share(1 - links.core, links.y),
+            share(1 - links.core, 1 - links.y),
+        )
+
+    attention_terms = attention_products(
+        here,
+        normed_plane,
+        deal(d_projected, d_projected.shape[0] // 4, 0),
+        attn_plane,
+        deal(d_attn, width // 4, 1),
+    )
+    grad_qkv, grad_out = place_pieces(
+        here, links.reduce(*attention_terms), (d_projected.shape[0] // 4, width // 4), False
+    )
+    gain_terms = jnp.concatenate(
+        [
+            jnp.sum(attn_gain_term, axis=0),
+            jnp.sum(ffn_gain_term, axis=0),
+            jnp.sum(query_term, axis=(0, 2)),
+            jnp.sum(key_term, axis=(0, 2)),
+        ]
+    )
+    gain_sums = links.total(gain_terms.reshape(-1, 128)).reshape(-1)
+    gain_grads = []
+    at = 0
+    for gain in (attn_gain, ffn_gain, query_gain, key_gain):
+        size = gain.shape[0]
+        gain_grads.append(lax.dynamic_slice_in_dim(gain_sums, at + links.side * size, size))
+        at += 2 * size
+    return (
+        output[None],
+        d_inputs[None],
+        grad_qkv,
+        grad_out,
+        grad_gate_up,
+        grad_down,
+        *gain_grads,
+    )
 
 
 def on_device(
@@ -484,8 +1208,9 @@
 
 
 def solution(mesh):
+    block = mesh.shape["fsdp"] == 2 and mesh.shape["ctx"] == 16
     return jax.shard_map(
-        on_device,
+        on_block if block else on_device,
         mesh=mesh,
         in_specs=(
             P("fsdp", "ctx", None),

time: 1360 us -> 680 us (0.50)
  waiting for transfers between devices: 991 us -> 289 us
  Pallas kernels: 46.5 us -> 166 us
  starting transfers between devices: 19.9 us -> 136 us
  matrix products: 86.8 us -> 10.8 us
  blocking collectives: 74.4 us -> 0 us
  local copies, waits for them, and re-layouts: 90.9 us -> 41.7 us
  between operations: 17 us -> 2.36 us
    reduce_scatter x4 -> x0, waiting for transfers between devices: 361 us -> none  [the longest x1 215 us: on_device(): lax.psum_scatter(jnp.einsum('tr,tgf->rgf', columns, d_gate_up, preferred_...]
    all_gather x4 -> x0, waiting for transfers between devices: 308 us -> none  [the longest x1 163 us: on_device(): lax.all_gather(gate_up_weight, 'fsdp', axis=0, tiled=True)]
    ppermute x0 -> x102, waiting for transfers between devices: none -> 289 us  [the longest x30 133 us: over_y(): return lax.ppermute(value, 'ctx', self.route(lambda z, y, c: (z, 1 - y, c)))]
    psum x1 -> x0, waiting for transfers between devices: 253 us -> none  [on_device(): lax.psum(grad_gate_up, 'ctx').astype(jnp.float32)]
    pallas_call x0 -> x12, Pallas kernels: none -> 119 us  [call_with_here(): pl.pallas_call(kernel, grid_spec=pltpu.PrefetchScalarGridSpec(num_scalar_...]
    ppermute x0 -> x102, starting transfers between devices: none -> 112 us  [the longest x9 47.5 us: over_z(): return lax.ppermute(value, 'ctx', self.route(lambda z, y, c: (z ^ 1, y, c)))]
    dot_general x12 -> x4, matrix products: 86.8 us -> 10.8 us  [the longest x2 5.55 us: contract(): lax.dot_general(left, right, ((axes[:1], axes[1:]), ((), ())), preferred_...]
    all_to_all x3 -> x4, waiting for transfers between devices: 66.4 us -> 0.01 us  [the longest x1 0.01 us: on_block(): got = lax.all_to_all(sent, 'ctx', 0, 0, tiled=True)]
  transfers between devices with their start and end apart: 12 -> 106, of which waited for: 10 -> 31; matrix products, arithmetic and copies ran while one was open for 8% -> 8% of each run, Pallas kernels for 2% -> 23%
where the time goes in v3:
time: 680 us; the launch traced here: 671 us
  waiting for transfers between devices  289 us (42%)
  Pallas kernels  166 us (24%)
  starting transfers between devices  136 us (20%)
  local copies, waits for them, and re-layouts  41.7 us (6%)
  other arithmetic  26.5 us (4%)
  matrix products  10.8 us (2%)
    ppermute x30, waiting for transfers between devices, over_y(): return lax.ppermute(value, 'ctx', self.route(lambda z, y, c: (z, 1 - y, c)))  133 us
    pallas_call x12, Pallas kernels, call_with_here(): pl.pallas_call(kernel, grid_spec=pltpu.PrefetchScalarGridSpec(num_scalar_...  119 us
    ppermute x11, waiting for transfers between devices, over_x(): return lax.ppermute(value, 'fsdp', [(0, 1), (1, 0)])  88.1 us
    ppermute x9, starting transfers between devices, over_z(): return lax.ppermute(value, 'ctx', self.route(lambda z, y, c: (z ^ 1, y, c)))  47.5 us
    pallas_call x2, Pallas kernels, kernel_call(): pl.pallas_call(kernel, out_shape=outs, in_specs=[smem] * len(tables) + [v...  46.9 us
    ppermute x9, waiting for transfers between devices, over_z(): return lax.ppermute(value, 'ctx', self.route(lambda z, y, c: (z ^ 1, y, c)))  41.3 us
    ppermute x30, starting transfers between devices, over_y(): return lax.ppermute(value, 'ctx', self.route(lambda z, y, c: (z, 1 - y, c)))  36.2 us
    unnamed x209, local copies, waits for them, and re-layouts  26.9 us
  transfers between devices with their start and end apart: 106, of which 31 were waited for; matrix products, arithmetic and copies ran while one was open for 8% of the time, Pallas kernels for 23%

profile of v3, /device:TPU:0, one launch (start us, length us, event | category | flops | bytes accessed | tf_op | source)
XLA Modules:
  0.0 671.4 jit_solution(14169839361833104147)
XLA Ops:
  19.3 8.9 %copy.35 = bf16[512,2,4608]{2,0,1:T(8,128)(2,1)} copy(bf16[512,2,4608]{2,1,0:T(2,128)(2,1)} %param.15) | data formatting | bytes 18874368 | tf_op args[3]
  60.7 28.7 %collective-permute-done.5.refs_0_ = bf16[128,1024]{1,0:T(8,128)(2,1)S(1)} collective-permute-done((bf16[128,1024]{1,0:T(8,128)(2,1)S(1)}, bf16[128,1024]{1,0:T(8,128)(2,1)S(1)}, u32[]{:S(2)}, u32[]{:S(2)}) %collective-permute-start.5) | collective-permute-done | bytes 262176 | tf_op jit(solution)/shard_map/ppermute | solution.py:258
  102.9 15.7 %collective-permute-done.14.refs_8_ = bf16[2304,256]{1,0:T(8,128)(2,1)} collective-permute-done((bf16[2304,256]{1,0:T(8,128)(2,1)}, bf16[2304,256]{1,0:T(8,128)(2,1)}, u32[]{:S(2)}, u32[]{:S(2)}) %collective-permute-start.14) | collective-permute-done | bytes 1179680 | tf_op jit(solution)/shard_map/ppermute | solution.py:258
  120.3 22.2 %collective-permute-done.10.refs_3_ = bf16[2,128,2304]{2,1,0:T(8,128)(2,1)} collective-permute-done((bf16[2,128,2304]{2,1,0:T(8,128)(2,1)S(1)}, bf16[2,128,2304]{2,1,0:T(8,128)(2,1)}, u32[]{:S(2)}, u32[]{:S(2)}) %collective-permute-start.10) | collective-permute-done | bytes 1179680 | tf_op jit(solution)/shard_map/ppermute | solution.py:258
  145.5 22.0 %shard_map.196 = (bf16[16,64,256]{2,1,0:T(8,128)(2,1)}, bf16[4096,64]{1,0:T(8,128)(2,1)S(1)}, bf16[64,4096]{1,0:T(8,128)(2,1)S(1)}, bf16[4096,64]{1,0:T(8,128)(2...) custom-call(s32[32]{0:T(128)S(1)} %broadcast_add_fusion.q_slot, ...), custom_call_target="tpu_custom_call" | custom-call | tf_op jit(solution)/shard_map/pallas_call | solution.py:215
  204.5 20.2 %shard_map.198 = (bf16[256,1152]{1,0:T(8,128)(2,1)}, bf16[256,1152]{1,0:T(8,128)(2,1)}, bf16[256,1152]{1,0:T(8,128)(2,1)}, bf16[256,1152]{1,0:T(8,128)(2,1)}, bf...) custom-call(s32[4]{0:T(128)} %pad_add_fusion.here, ...), custom_call_target="tpu_custom_call" | custom-call | tf_op jit(solution)/shard_map/pallas_call | solution.py:314
  224.7 20.4 %shard_map.199 = (bf16[256,1152]{1,0:T(8,128)(2,1)}, bf16[256,1152]{1,0:T(8,128)(2,1)}, bf16[256,1152]{1,0:T(8,128)(2,1)}, bf16[256,1152]{1,0:T(8,128)(2,1)}, bf...) custom-call(s32[4]{0:T(128)} %pad_add_fusion.here, ...), custom_call_target="tpu_custom_call" | custom-call | tf_op jit(solution)/shard_map/pallas_call | solution.py:314
  267.4 13.5 %collective-permute-done.46.refs_2_ = bf16[256,1024]{1,0:T(8,128)(2,1)} collective-permute-done((bf16[256,1024]{1,0:T(8,128)(2,1)}, bf16[256,1024]{1,0:T(8,128)(2,1)}, u32[]{:S(2)}, u32[]{:S(2)}) %collective-permute-start.46) | collective-permute-done | bytes 524320 | tf_op jit(solution)/shard_map/ppermute | solution.py:249
  283.1 10.4 %collective-permute-done.49.refs_6_ = bf16[256,1152]{1,0:T(8,128)(2,1)S(1)} collective-permute-done((bf16[256,1152]{1,0:T(8,128)(2,1)}, bf16[256,1152]{1,0:T(8,128)(2,1)S(1)}, u32[]{:S(2)}, u32[]{:S(2)}) %collective-permute-start.49) | collective-permute-done | bytes 589856 | tf_op jit(solution)/shard_map/ppermute | solution.py:249
  299.8 24.9 %shard_map.200 = bf16[16,192,256]{2,1,0:T(8,128)(2,1)} custom-call(s32[32]{0:T(128)S(1)} %broadcast_add_fusion.q_slot, s32[32]{0:T(128)S(1)} %get-tuple-element.103.kv_slot, s32[16]{0:T(128)S(1)} %get-tuple-element.147.first, s32[16]{0:T(128)S(1)} %get-tuple-element.148.last, bf16[16,64,256]{2,1,0:T(8,128)(2,1)S(1)} %all-to-all-done.2.d_ref, ...), custom_call_target="tpu_custom_call" | custom-call | tf_op jit(solution)/shard_map/pallas_call | solution.py:215
  350.7 12.8 %collective-permute-done.63.refs_6_ = bf16[256,1152]{1,0:T(8,128)(2,1)S(1)} collective-permute-done((bf16[256,1152]{1,0:T(8,128)(2,1)}, bf16[256,1152]{1,0:T(8,128)(2,1)S(1)}, u32[]{:S(2)}, u32[]{:S(2)}) %collective-permute-start.63) | collective-permute-done | bytes 589856 | tf_op jit(solution)/shard_map/ppermute | solution.py:249
  363.5 12.2 %collective-permute-done.65.refs_7_ = bf16[256,1152]{1,0:T(8,128)(2,1)S(1)} collective-permute-done((bf16[256,1152]{1,0:T(8,128)(2,1)}, bf16[256,1152]{1,0:T(8,128)(2,1)S(1)}, u32[]{:S(2)}, u32[]{:S(2)}) %collective-permute-start.65) | collective-permute-done | bytes 589856 | tf_op jit(solution)/shard_map/ppermute | solution.py:249
  386.5 13.1 %collective-permute-done.22.refs_2_ = bf16[256,1024]{1,0:T(8,128)(2,1)} collective-permute-done((bf16[256,1024]{1,0:T(8,128)(2,1)}, bf16[256,1024]{1,0:T(8,128)(2,1)}, u32[]{:S(2)}, u32[]{:S(2)}) %collective-permute-start.22) | collective-permute-done | bytes 524320 | tf_op jit(solution)/shard_map/ppermute | solution.py:249
  405.4 13.8 %collective-permute-done.66 = bf16[512,1152]{1,0:T(8,128)(2,1)S(1)} collective-permute-done((bf16[512,1152]{1,0:T(8,128)(2,1)}, bf16[512,1152]{1,0:T(8,128)(2,1)S(1)}, u32[]{:S(2)}, u32[]{:S(2)}) %collective-permute-start.66) | collective-permute-done | bytes 1179680 | tf_op jit(solution)/shard_map/ppermute | solution.py:258
  455.8 11.4 %collective-permute-done.89 = bf16[288,1024]{1,0:T(8,128)(2,1)S(1)} collective-permute-done((bf16[288,1024]{1,0:T(8,128)(2,1)S(1)}, bf16[288,1024]{1,0:T(8,128)(2,1)S(1)}, u32[]{:S(2)}, u32[]{:S(2)}) %collective-permute-start.89) | collective-permute-done | bytes 589856 | tf_op jit(solution)/shard_map/ppermute | solution.py:255
  469.5 9.1 %collective-permute-done.54 = bf16[256,1152]{1,0:T(8,128)(2,1)S(1)} collective-permute-done((bf16[256,1152]{1,0:T(8,128)(2,1)S(1)}, bf16[256,1152]{1,0:T(8,128)(2,1)S(1)}, u32[]{:S(2)}, u32[]{:S(2)}) %collective-permute-start.54) | collective-permute-done | bytes 589856 | tf_op jit(solution)/shard_map/ppermute | solution.py:255
  481.6 36.6 %collective-permute-start.93 = (bf16[288,1024]{1,0:T(8,128)(2,1)S(1)}, bf16[288,1024]{1,0:T(8,128)(2,1)}, u32[]{:S(2)}, u32[]{:S(2)}) collective-permute-start(bf16[288,1024]{1,0:T(8,128)(2,1)S(1)} %add_convert_fusion.refs_0_), channel_id=1, source_target_pairs={{0,8},{2,10},{4,12},{6,14},{8,0},{10,2},{12,4},{14,6},{16,24},{18,... | collective-permute-start | bytes 1769480 | tf_op jit(solution)/shard_map/ppermute | solution.py:252
  533.9 13.0 %collective-permute-done.100 = f32[17,128]{1,0:T(8,128)S(1)} collective-permute-done((f32[17,128]{1,0:T(8,128)S(1)}, f32[17,128]{1,0:T(8,128)S(1)}, u32[]{:S(2)}, u32[]{:S(2)}) %collective-permute-start.100) | collective-permute-done | bytes 8736 | tf_op jit(solution)/shard_map/ppermute | solution.py:252
  555.5 8.9 %collective-permute-done.36 = bf16[256,768]{1,0:T(8,128)(2,1)S(1)} collective-permute-done((bf16[256,768]{1,0:T(8,128)(2,1)S(1)}, bf16[256,768]{1,0:T(8,128)(2,1)S(1)}, u32[]{:S(2)}, u32[]{:S(2)}) %collective-permute-start.36) | collective-permute-done | bytes 393248 | tf_op jit(solution)/shard_map/ppermute | solution.py:252
  570.0 13.9 %collective-permute-done.72.refs_4_ = bf16[256,1152]{1,0:T(8,128)(2,1)} collective-permute-done((bf16[256,1152]{1,0:T(8,128)(2,1)S(1)}, bf16[256,1152]{1,0:T(8,128)(2,1)}, u32[]{:S(2)}, u32[]{:S(2)}) %collective-permute-start.72) | collective-permute-done | bytes 589856 | tf_op jit(solution)/shard_map/ppermute | solution.py:252
  590.7 10.3 %collective-permute-done.60.refs_6_ = bf16[256,1152]{1,0:T(8,128)(2,1)} collective-permute-done((bf16[256,1152]{1,0:T(8,128)(2,1)}, bf16[256,1152]{1,0:T(8,128)(2,1)}, u32[]{:S(2)}, u32[]{:S(2)}) %collective-permute-start.60) | collective-permute-done | bytes 589856 | tf_op jit(solution)/shard_map/ppermute | solution.py:249
  600.9 11.8 %collective-permute-done.74.refs_6_ = bf16[256,1152]{1,0:T(8,128)(2,1)} collective-permute-done((bf16[256,1152]{1,0:T(8,128)(2,1)}, bf16[256,1152]{1,0:T(8,128)(2,1)}, u32[]{:S(2)}, u32[]{:S(2)}) %collective-permute-start.74) | collective-permute-done | bytes 589856 | tf_op jit(solution)/shard_map/ppermute | solution.py:249
  642.1 9.9 %shard_map.205.refs_8_ = f32[512,2,4608]{2,1,0:T(2,128)} custom-call(s32[4]{0:T(128)} %pad_add_fusion.here, bf16[256,1152]{1,0:T(8,128)(2,1)} %copy-done.22, bf16[256,1152]{1,0:T(8,128)(2,1)} %copy-done.37, bf16[256,1152]{1,0:T(8,128)(2,1)} %collective-permute-done.70.refs_2_, bf16[256,1152]{1,0:T(8,128)(2,1)} %collective-permute-done.71.refs_3_, ...), custom_call_target="tpu_custom_call" | custom-call | tf_op jit(solution)/shard_map/pallas_call | solution.py:314
  652.8 9.9 %shard_map.206 = f32[512,2,4608]{2,1,0:T(2,128)} custom-call(s32[4]{0:T(128)} %pad_add_fusion.here, bf16[256,1152]{1,0:T(8,128)(2,1)} %copy-done.28, bf16[256,1152]{1,0:T(8,128)(2,1)} %copy-done.48, bf16[256,1152]{1,0:T(8,128)(2,1)} %copy-done.49, bf16[256,1152]{1,0:T(8,128)(2,1)} %copy-done.50, ...), custom_call_target="tpu_custom_call", output_to_operand_aliasing={{}: (9, {})} | custom-call | tf_op jit(solution)/shard_map/pallas_call | solution.py:314
  (513 shorter events, 295.6 us)
Async XLA Ops:
  46.5 97.8 %all-to-all-start = ((bf16[16,192,256]{2,1,0:T(8,128)(2,1)}), bf16[16,192,256]{2,1,0:T(8,128)(2,1)S(1)}, u32[]{:S(2)}, u32[]{:S(2)}) async-start(bf16[16,192,256]{2,1,0:T(8,128)(2,1)} %pad_maximum_fusion), calls=%async_computation | async-start | bytes 3145728 | tf_op jit(solution)/shard_map/all_to_all | solution.py:813
  90.9 51.6 %collective-permute-start.10 = (bf16[2,128,2304]{2,1,0:T(8,128)(2,1)S(1)}, bf16[2,128,2304]{2,1,0:T(8,128)(2,1)}, u32[]{:S(2)}, u32[]{:S(2)}) collective-permute-start(bf16[2,128,2304]{2,1,0:T(8,128)(2,1)S(1)} %get-tuple-element.57), channel_id=1, source_target_pairs={{0,1},{1,0},{2,3},{3,2},{4,5},{5,4},{6,7},{7,6},{8,9},{9,8},{10,11... | collective-permute-start | bytes 3538952 | tf_op jit(solution)/shard_map/ppermute | solution.py:258
  100.8 75.4 %collective-permute-start.18 = (bf16[2,128,2304]{2,1,0:T(8,128)(2,1)}, bf16[2,128,2304]{2,1,0:T(8,128)(2,1)}, u32[]{:S(2)}, u32[]{:S(2)}) collective-permute-start(bf16[2,128,2304]{2,1,0:T(8,128)(2,1)} %collective-permute-done.9.refs_3_), channel_id=1, source_target_pairs={{0,2},{2,0},{4,6},{6,4},{8,10},{10,8},{12,14},{14,12},{16,18},{18,... | collective-permute-start | bytes 3538952 | tf_op jit(solution)/shard_map/ppermute | solution.py:246
  101.3 74.2 %collective-permute-start.19 = (bf16[2,128,2304]{2,1,0:T(8,128)(2,1)}, bf16[2,128,2304]{2,1,0:T(8,128)(2,1)}, u32[]{:S(2)}, u32[]{:S(2)}) collective-permute-start(bf16[2,128,2304]{2,1,0:T(8,128)(2,1)} %collective-permute-done.9.refs_3_), channel_id=1, source_target_pairs={{0,4},{2,6},{4,0},{6,2},{8,12},{10,14},{12,8},{14,10},{16,20},{18,... | collective-permute-start | bytes 3538952 | tf_op jit(solution)/shard_map/ppermute | solution.py:249
  118.6 57.5 %collective-permute-start.16 = (bf16[2304,256]{1,0:T(8,128)(2,1)}, bf16[2304,256]{1,0:T(8,128)(2,1)}, u32[]{:S(2)}, u32[]{:S(2)}) collective-permute-start(bf16[2304,256]{1,0:T(8,128)(2,1)} %collective-permute-done.14.refs_8_), channel_id=1, source_target_pairs={{0,4},{2,6},{4,0},{6,2},{8,12},{10,14},{12,8},{14,10},{16,20},{18,... | collective-permute-start | bytes 3538952 | tf_op jit(solution)/shard_map/ppermute | solution.py:249
  144.2 44.7 %collective-permute-start.15 = (bf16[2304,256]{1,0:T(8,128)(2,1)}, bf16[2304,256]{1,0:T(8,128)(2,1)}, u32[]{:S(2)}, u32[]{:S(2)}) collective-permute-start(bf16[2304,256]{1,0:T(8,128)(2,1)} %collective-permute-done.14.refs_8_), channel_id=1, source_target_pairs={{0,2},{2,0},{4,6},{6,4},{8,10},{10,8},{12,14},{14,12},{16,18},{18,... | collective-permute-start | bytes 3538952 | tf_op jit(solution)/shard_map/ppermute | solution.py:246
  176.2 48.5 %collective-permute-start.11 = (bf16[2,128,2304]{2,1,0:T(8,128)(2,1)}, bf16[2,128,2304]{2,1,0:T(8,128)(2,1)}, u32[]{:S(2)}, u32[]{:S(2)}) collective-permute-start(bf16[2,128,2304]{2,1,0:T(8,128)(2,1)} %collective-permute-done.10.refs_3_), channel_id=1, source_target_pairs={{0,2},{2,0},{4,6},{6,4},{8,10},{10,8},{12,14},{14,12},{16,18},{18,... | collective-permute-start | bytes 3538952 | tf_op jit(solution)/shard_map/ppermute | solution.py:246
  194.5 55.7 %collective-permute-start.76 = (bf16[256,1024]{1,0:T(8,128)(2,1)S(1)}, bf16[256,1024]{1,0:T(8,128)(2,1)}, u32[]{:S(2)}, u32[]{:S(2)}) collective-permute-start(bf16[256,1024]{1,0:T(8,128)(2,1)S(1)} %bitcast.134), channel_id=1, source_target_pairs={{0,2},{2,0},{4,6},{6,4},{8,10},{10,8},{12,14},{14,12},{16,18},{18,... | collective-permute-start | bytes 1572872 | tf_op jit(solution)/shard_map/ppermute | solution.py:246
  203.4 47.3 %collective-permute-start.78 = (bf16[256,1024]{1,0:T(8,128)(2,1)}, bf16[256,1024]{1,0:T(8,128)(2,1)}, u32[]{:S(2)}, u32[]{:S(2)}) collective-permute-start(bf16[256,1024]{1,0:T(8,128)(2,1)} %collective-permute-done.77.refs_2_), channel_id=1, source_target_pairs={{0,2},{2,0},{4,6},{6,4},{8,10},{10,8},{12,14},{14,12},{16,18},{18,... | collective-permute-start | bytes 1572872 | tf_op jit(solution)/shard_map/ppermute | solution.py:246
  267.2 63.2 %collective-permute-start.64 = (bf16[256,1152]{1,0:T(8,128)(2,1)}, bf16[256,1152]{1,0:T(8,128)(2,1)}, u32[]{:S(2)}, u32[]{:S(2)}) collective-permute-start(bf16[256,1152]{1,0:T(8,128)(2,1)} %get-tuple-element.84), channel_id=1, source_target_pairs={{0,2},{2,0},{4,6},{6,4},{8,10},{10,8},{12,14},{14,12},{16,18},{18,... | collective-permute-start | bytes 1769480 | tf_op jit(solution)/shard_map/ppermute | solution.py:246
  280.9 59.9 %collective-permute-start.47 = (bf16[256,1024]{1,0:T(8,128)(2,1)}, bf16[256,1024]{1,0:T(8,128)(2,1)}, u32[]{:S(2)}, u32[]{:S(2)}) collective-permute-start(bf16[256,1024]{1,0:T(8,128)(2,1)} %collective-permute-done.46.refs_2_), channel_id=1, source_target_pairs={{0,2},{2,0},{4,6},{6,4},{8,10},{10,8},{12,14},{14,12},{16,18},{18,... | collective-permute-start | bytes 1572872 | tf_op jit(solution)/shard_map/ppermute | solution.py:246
  280.9 61.4 %collective-permute-start.51 = (bf16[256,1152]{1,0:T(8,128)(2,1)}, bf16[256,1152]{1,0:T(8,128)(2,1)}, u32[]{:S(2)}, u32[]{:S(2)}) collective-permute-start(bf16[256,1152]{1,0:T(8,128)(2,1)} %collective-permute-done.50), channel_id=1, source_target_pairs={{0,4},{2,6},{4,0},{6,2},{8,12},{10,14},{12,8},{14,10},{16,20},{18,... | collective-permute-start | bytes 1769480 | tf_op jit(solution)/shard_map/ppermute | solution.py:249
  283.0 47.9 %collective-permute-start.82 = (bf16[576,256]{1,0:T(8,128)(2,1)}, bf16[576,256]{1,0:T(8,128)(2,1)}, u32[]{:S(2)}, u32[]{:S(2)}) collective-permute-start(bf16[576,256]{1,0:T(8,128)(2,1)} %collective-permute-done.81), channel_id=1, source_target_pairs={{0,4},{2,6},{4,0},{6,2},{8,12},{10,14},{12,8},{14,10},{16,20},{18,... | collective-permute-start | bytes 884744 | tf_op jit(solution)/shard_map/ppermute | solution.py:249
  324.8 107.5 %all-to-all-start.3 = ((bf16[16,192,256]{2,1,0:T(8,128)(2,1)}), bf16[16,192,256]{2,1,0:T(8,128)(2,1)S(1)}, u32[]{:S(2)}, u32[]{:S(2)}) async-start(bf16[16,192,256]{2,1,0:T(8,128)(2,1)} %shard_map.200), calls=%async_computation.3 | async-start | bytes 3145728 | tf_op jit(solution)/shard_map/all_to_all | solution.py:873
  340.8 58.7 %collective-permute-start.87 = (bf16[576,1024]{1,0:T(8,128)(2,1)}, bf16[576,1024]{1,0:T(8,128)(2,1)}, u32[]{:S(2)}, u32[]{:S(2)}) collective-permute-start(bf16[576,1024]{1,0:T(8,128)(2,1)} %get-tuple-element.97), channel_id=1, source_target_pairs={{0,1},{1,0},{2,3},{3,2},{4,5},{5,4},{6,7},{7,6},{8,9},{9,8},{10,11... | collective-permute-start | bytes 3538952 | tf_op jit(solution)/shard_map/ppermute | solution.py:258
  350.1 52.6 %collective-permute-start.52 = (bf16[512,1152]{1,0:T(8,128)(2,1)}, bf16[512,1152]{1,0:T(8,128)(2,1)}, u32[]{:S(2)}, u32[]{:S(2)}) collective-permute-start(bf16[512,1152]{1,0:T(8,128)(2,1)} %get-tuple-element.80), channel_id=1, source_target_pairs={{0,1},{1,0},{2,3},{3,2},{4,5},{5,4},{6,7},{7,6},{8,9},{9,8},{10,11... | collective-permute-start | bytes 3538952 | tf_op jit(solution)/shard_map/ppermute | solution.py:258
  386.5 53.7 %collective-permute-start.21 = (bf16[256,1024]{1,0:T(8,128)(2,1)}, bf16[256,1024]{1,0:T(8,128)(2,1)}, u32[]{:S(2)}, u32[]{:S(2)}) collective-permute-start(bf16[256,1024]{1,0:T(8,128)(2,1)} %fusion.2.refs_0_), channel_id=1, source_target_pairs={{0,2},{2,0},{4,6},{6,4},{8,10},{10,8},{12,14},{14,12},{16,18},{18,... | collective-permute-start | bytes 1572872 | tf_op jit(solution)/shard_map/ppermute | solution.py:246
  467.8 50.4 %collective-permute-start.27 = (bf16[512,256]{1,0:T(8,128)(2,1)S(1)}, bf16[512,256]{1,0:T(8,128)(2,1)S(1)}, u32[]{:S(2)}, u32[]{:S(2)}) collective-permute-start(bf16[512,256]{1,0:T(8,128)(2,1)S(1)} %collective-permute-done.26), channel_id=1, source_target_pairs={{0,4},{2,6},{4,0},{6,2},{8,12},{10,14},{12,8},{14,10},{16,20},{18,... | collective-permute-start | bytes 786440 | tf_op jit(solution)/shard_map/ppermute | solution.py:249
  478.6 49.2 %collective-permute-start.68 = (bf16[256,1152]{1,0:T(8,128)(2,1)S(1)}, bf16[256,1152]{1,0:T(8,128)(2,1)S(1)}, u32[]{:S(2)}, u32[]{:S(2)}) collective-permute-start(bf16[256,1152]{1,0:T(8,128)(2,1)S(1)} %add_convert_fusion.5), channel_id=1, source_target_pairs={{0,24},{2,26},{4,28},{6,30},{8,16},{10,18},{12,20},{14,22},{16,8},... | collective-permute-start | bytes 1769480 | tf_op jit(solution)/shard_map/ppermute | solution.py:255
  481.0 46.9 %collective-permute-start.90 = (bf16[288,1024]{1,0:T(8,128)(2,1)S(1)}, bf16[288,1024]{1,0:T(8,128)(2,1)S(1)}, u32[]{:S(2)}, u32[]{:S(2)}) collective-permute-start(bf16[288,1024]{1,0:T(8,128)(2,1)S(1)} %add_convert_fusion.refs_0_), channel_id=1, source_target_pairs={{0,2},{2,0},{4,6},{6,4},{8,10},{10,8},{12,14},{14,12},{16,18},{18,... | collective-permute-start | bytes 1769480 | tf_op jit(solution)/shard_map/ppermute | solution.py:246
  481.0 48.4 %collective-permute-start.91 = (bf16[288,1024]{1,0:T(8,128)(2,1)S(1)}, bf16[288,1024]{1,0:T(8,128)(2,1)}, u32[]{:S(2)}, u32[]{:S(2)}) collective-permute-start(bf16[288,1024]{1,0:T(8,128)(2,1)S(1)} %add_convert_fusion.refs_0_), channel_id=1, source_target_pairs={{0,4},{2,6},{4,0},{6,2},{8,12},{10,14},{12,8},{14,10},{16,20},{18,... | collective-permute-start | bytes 1769480 | tf_op jit(solution)/shard_map/ppermute | solution.py:249
  481.6 51.8 %collective-permute-start.93 = (bf16[288,1024]{1,0:T(8,128)(2,1)S(1)}, bf16[288,1024]{1,0:T(8,128)(2,1)}, u32[]{:S(2)}, u32[]{:S(2)}) collective-permute-start(bf16[288,1024]{1,0:T(8,128)(2,1)S(1)} %add_convert_fusion.refs_0_), channel_id=1, source_target_pairs={{0,8},{2,10},{4,12},{6,14},{8,0},{10,2},{12,4},{14,6},{16,24},{18,... | collective-permute-start | bytes 1769480 | tf_op jit(solution)/shard_map/ppermute | solution.py:252
  617.8 44.9 %collective-permute-start.38 = (bf16[256,768]{1,0:T(8,128)(2,1)S(1)}, bf16[256,768]{1,0:T(8,128)(2,1)S(1)}, u32[]{:S(2)}, u32[]{:S(2)}) collective-permute-start(bf16[256,768]{1,0:T(8,128)(2,1)S(1)} %add_convert_fusion.12.refs_0_), channel_id=1, source_target_pairs={{0,2},{2,0},{4,6},{6,4},{8,10},{10,8},{12,14},{14,12},{16,18},{18,... | collective-permute-start | bytes 1179656 | tf_op jit(solution)/shard_map/ppermute | solution.py:246
  618.4 44.4 %collective-permute-start.42 = (bf16[256,768]{1,0:T(8,128)(2,1)}, bf16[256,768]{1,0:T(8,128)(2,1)S(1)}, u32[]{:S(2)}, u32[]{:S(2)}) collective-permute-start(bf16[256,768]{1,0:T(8,128)(2,1)} %collective-permute-done.41.refs_4_), channel_id=1, source_target_pairs={{0,2},{2,0},{4,6},{6,4},{8,10},{10,8},{12,14},{14,12},{16,18},{18,... | collective-permute-start | bytes 1179656 | tf_op jit(solution)/shard_map/ppermute | solution.py:246
  (186 other events, 3367.5 us)

commit v4 on v3

--- a/solution.py
+++ b/solution.py
@@ -219,6 +219,9 @@
         out_specs=[vmem] * len(outs),
         scratch_shapes=scratch,
         compiler_params=pltpu.CompilerParams(vmem_limit_bytes=48 * 1024 * 1024),
+        cost_estimate=pl.CostEstimate(
+            flops=1, bytes_accessed=24 * 3_000_000, transcendentals=0
+        ),
     )(*tables, *arrays)
 
 
@@ -310,7 +313,13 @@
 PARAMS = pltpu.CompilerParams(vmem_limit_bytes=56 * 1024 * 1024)
 
 
-def call_with_here(kernel, here, grid, arrays, specs, outs, out_specs, scratch=(), aliases=None):
+def cost(micros):
+    return pl.CostEstimate(flops=1, bytes_accessed=micros * 3_000_000, transcendentals=0)
+
+
+def call_with_here(
+    kernel, here, grid, arrays, specs, outs, out_specs, scratch=(), aliases=None, micros=5
+):
     return pl.pallas_call(
         kernel,
         grid_spec=pltpu.PrefetchScalarGridSpec(
@@ -323,12 +332,83 @@
         out_shape=outs,
         input_output_aliases=aliases or {},
         compiler_params=PARAMS,
+        cost_estimate=cost(micros),
     )(here, *arrays)
 
 
 def whole(array):
     rank = len(array.shape)
     return pl.BlockSpec(array.shape, lambda i, here: (0,) * rank)
+
+
+def project_kernel(here, *refs):
+    x_ref, gain_ref, own_ref = refs[:3]
+    pieces, q_gain, k_gain, cos_ref, sin_ref = refs[3:7], refs[7], refs[8], refs[9], refs[10]
+    sent, weight, q_ref, k_ref, q_scale, k_scale, normed_ref, scale_ref = refs[11:]
+    core, y, side = here[1], here[2], here[3]
+    rows = own_ref.shape[0]
+    part = rows // 4
+    f32, bf16 = jnp.float32, jnp.bfloat16
+    weight[pl.ds(pl.multiple_of(side * rows, rows), rows), :] = own_ref[...]
+    for p in range(4):
+        at = (1 - side) * rows + (((p % 2) ^ core) * 2 + ((p // 2) ^ y)) * part
+        weight[pl.ds(pl.multiple_of(at, part), part), :] = pieces[p][...]
+    x = x_ref[...].astype(f32)
+    scale = rms_scale(x)
+    scale_ref[...] = scale
+    normed = (x * scale * gain_ref[...]).astype(bf16)
+    normed_ref[...] = normed
+    cosine, sine = cos_ref[...], sin_ref[...]
+    half = HD // 2
+
+    def turned(raw, gain, raw_ref, kept_scale, head):
+        raw_ref[head * HD : (head + 1) * HD, :] = raw
+        scale = rms_scale(raw, 0)
+        kept_scale[head : head + 1, :] = scale
+        value = raw * scale * gain
+        first, second = value[:half], value[half:]
+        return jnp.concatenate(
+            [first * cosine - second * sine, second * cosine + first * sine], axis=0
+        ).astype(bf16)
+
+    per_group = HEADS // KV_HEADS
+    for at in range(0, weight.shape[1], 2 * BLK):
+        block = jnp.dot(normed, weight[:, at : at + 2 * BLK], preferred_element_type=f32)
+        turned_block = block.T
+        for n in range(2 * BLK // HD):
+            head = at // HD + n
+            raw = turned_block[n * HD : (n + 1) * HD, :]
+            if head < HEADS:
+                sent[head, 0:HD, :] = turned(raw, q_gain[...], q_ref, q_scale, head)
+                continue
+            head -= HEADS
+            if head < KV_HEADS:
+                value, row = turned(raw, k_gain[...], k_ref, k_scale, head), HD
+            else:
+                value, row, head = raw.astype(bf16), 2 * HD, head - KV_HEADS
+            for copy in range(per_group):
+                sent[head * per_group + copy, row : row + HD, :] = value
+
+
+def project(here, x, gain, own, pieces, q_gain, k_gain, cosine, sine):
+    tokens, width = x.shape
+    f32, bf16 = jnp.float32, jnp.bfloat16
+    shape = jax.ShapeDtypeStruct
+    arrays = [x, gain, own, *pieces, q_gain, k_gain, cosine, sine]
+    outs = [
+        shape((HEADS, 3 * HD, tokens), bf16),
+        shape((width, own.shape[1]), bf16),
+        shape((HEADS * HD, tokens), f32),
+        shape((KV_HEADS * HD, tokens), f32),
+        shape((HEADS, tokens), f32),
+        shape((KV_HEADS, tokens), f32),
+        shape((tokens, width), bf16),
+        shape((tokens, 1), f32),
+    ]
+    return call_with_here(
+        project_kernel, here, (1,), arrays, [whole(a) for a in arrays], outs,
+        [whole(o) for o in outs], micros=8,
+    )
 
 
 def place_rows(here, own, pieces):
@@ -661,6 +741,7 @@
         [jax.ShapeDtypeStruct((2 * rows, 2, 2 * wide * CHUNKS), jnp.float32)],
         [pl.BlockSpec((step, 2, 2 * wide), lambda i, here: (i, 0, chunk))],
         aliases=aliases,
+        micros=10,
     )
     return out
 
@@ -769,48 +850,56 @@
     gain_ffn = gain_of(rows, rows)
     gain_query = gain_of(2 * rows, HD // 2)
     gain_key = gain_of(2 * rows + HD // 2, HD // 2)
+    ff_chunk = gate_up_weight.shape[2] // CHUNKS
+
+    def gate_up_piece(chunk):
+        return jnp.transpose(
+            lax.dynamic_slice(
+                gate_up_weight,
+                (links.quarter * part_rows, 0, chunk * ff_chunk),
+                (part_rows, 2, ff_chunk),
+            ),
+            (1, 0, 2),
+        )
+
     qkv_there = links.over_x(quarter_rows(qkv_weight))
-    qkv_pieces = links.spread_plane(qkv_there)
-    gate_up = jnp.transpose(gate_up_weight, (1, 0, 2))
-    ff_chunk = gate_up.shape[2] // CHUNKS
-    out_there = links.over_x(after(quarter_rows(out_weight), qkv_there))
-
-    def gate_up_piece(chunk):
-        return lax.dynamic_slice(
-            gate_up, (0, links.quarter * part_rows, chunk * ff_chunk), (2, part_rows, ff_chunk)
-        )
-
-    first_there = links.over_x(after(gate_up_piece(0), qkv_there))
-    down_there = links.over_x(
-        after(
-            lax.dynamic_slice_in_dim(down_weight, links.quarter * (width // 4), width // 4, 1),
-            out_there,
-        )
-    )
-    second_there = links.over_x(after(gate_up_piece(1), first_there))
-    out_pieces = links.spread_plane(out_there)
-    gate_up_pieces = [links.spread_plane(first_there), links.spread_plane(second_there)]
-    down_pieces = links.spread_plane(down_there)
-    w_out = place_rows(here, out_weight, out_pieces)
-    scale_one = rms_scale(inputs)
-    normed = (inputs * scale_one * gain_attn).astype(jnp.bfloat16)
-    w_qkv = place_rows(here, qkv_weight, qkv_pieces)
-    projected = lax.dot_general(
-        w_qkv, normed, (((0,), (1,)), ((), ())), preferred_element_type=f32
-    )
-    q_raw = projected[:q_width].reshape(HEADS, HD, rows_here)
-    k_raw = projected[q_width : q_width + kv_width].reshape(KV_HEADS, HD, rows_here)
-    values_here = projected[q_width + kv_width :].reshape(KV_HEADS, HD, rows_here).astype(bf16)
-    q_scale = rms_scale(q_raw, 1)
-    k_scale = rms_scale(k_raw, 1)
+    out_piece = quarter_rows(out_weight)
+    first_piece, second_piece = gate_up_piece(0), gate_up_piece(1)
+    down_piece = lax.dynamic_slice_in_dim(
+        down_weight, links.quarter * (width // 4), width // 4, 1
+    )
+    d_ffn = cotangent[0]
+    qkv_there = after(qkv_there, out_piece, first_piece, second_piece, down_piece)
+    out_there = links.over_x(after(out_piece, qkv_there))
+    first_there = links.over_x(after(first_piece, qkv_there))
+    gate_up = jnp.transpose(after(gate_up_weight, qkv_there), (1, 0, 2))
+    qkv_beside = links.over_y(qkv_there)
+    qkv_pieces = (
+        qkv_there,
+        links.over_core(qkv_there),
+        qkv_beside,
+        links.over_core(after(qkv_beside, gate_up)),
+    )
+    ffn_plane = links.spread_plane(after(d_ffn, qkv_beside))
+    tokens_here = tokens[0]
+    sent, w_qkv, q_raw, k_raw, q_scale, k_scale, normed, scale_one = project(
+        here, tokens_here, gain_attn[None], qkv_weight, qkv_pieces,
+        gain_query[:, None], gain_key[:, None], cosine[0], sine[0],
+    )
+    q_raw = q_raw.reshape(HEADS, HD, rows_here)
+    k_raw = k_raw.reshape(KV_HEADS, HD, rows_here)
+    q_scale, k_scale = q_scale[:, None], k_scale[:, None]
     column_query, column_key = gain_query[:, None], gain_key[:, None]
-    queries = rope(q_raw * q_scale * column_query, cosine, sine).astype(bf16)
-    keys_here = rope(k_raw * k_scale * column_key, cosine, sine).astype(bf16)
-    sent = jnp.concatenate(
-        [queries, jnp.repeat(keys_here, per_group, 0), jnp.repeat(values_here, per_group, 0)], axis=1
-    )
-    sent = jnp.concatenate([sent] * parts, axis=0)
     got = lax.all_to_all(sent, "ctx", 0, 0, tiled=True)
+    out_there = after(out_there, sent)
+    first_there = after(first_there, sent)
+    down_there = links.over_x(after(down_piece, first_there))
+    first_beside = links.over_y(first_there)
+    out_beside = links.over_y(out_there)
+    normed_plane = links.spread_plane(after(normed, sent))
+    second_there = links.over_x(after(second_piece, down_there))
+    down_beside = links.over_y(down_there)
+    got = after(got, down_there)
     q_place, q_start = q_place[None], q_start[None]
     shape = jax.ShapeDtypeStruct
     attn_sent, *held = kernel_call(
@@ -832,22 +921,31 @@
     attn_in = lax.dynamic_slice_in_dim(
         lax.all_to_all(attn_sent, "ctx", 0, 0, tiled=True), part * HEADS, HEADS
     ).reshape(q_width, rows_here)
-    normed_plane = links.spread_plane(after(normed, got))
-    d_ffn = cotangent[0]
-    ffn_plane = links.spread_plane(after(d_ffn, got))
+    second_there = after(second_there, attn_sent)
+
+    def spread(there, beside):
+        return (there, links.over_core(there), beside, links.over_core(after(beside, attn_sent)))
+
+    out_pieces = spread(out_there, out_beside)
+    w_out = place_rows(here, out_weight, out_pieces)
+    gate_up_pieces = [spread(first_there, first_beside), links.spread_plane(second_there)]
+    down_pieces = spread(down_there, down_beside)
     attn_plane = links.spread_plane(attn_in)
     h_one = inputs + contract(attn_in, w_out, (0, 0))
     scale_two = rms_scale(h_one)
     normed_two = (h_one * scale_two * gain_ffn).astype(bf16)
     two_plane = links.spread_plane(normed_two)
     sums = [h_one, jnp.zeros_like(h_one)]
-    products, hidden_plane = [], []
+    wide_shares, hidden_plane = [], []
     for chunk in range(CHUNKS):
         d_wide, hidden, sums = ffn(
             here, chunk, normed_two, d_ffn, gate_up, gate_up_pieces[chunk],
             down_weight, down_pieces, sums,
         )
-        products.append(wide_products(here, two_plane, links.deal_plane(*d_wide)))
+        shares = links.deal_plane(*d_wide)
+        if chunk == 0:
+            sums = [after(sums[0], shares[1]), sums[1]]
+        wide_shares.append(shares)
         hidden_plane.append(links.deal_plane(*hidden))
     output = sums[0].astype(bf16)
     d_norm_two, ffn_gain_term = norm_back(sums[1], h_one, scale_two, gain_ffn)
@@ -858,6 +956,9 @@
     ).astype(bf16)
     d_heads = jnp.concatenate([d_heads.reshape(HEADS, HD, rows_here)] * parts, axis=0)
     d_got = lax.all_to_all(d_heads, "ctx", 0, 0, tiled=True)
+    first_shares = [after(v, d_heads) for v in wide_shares[0]]
+    first_products = wide_products(here, two_plane, first_shares)
+    d_got = after(d_got, first_products[0])
     (d_sent,) = kernel_call(
         attend_back_kernel,
         tables,
@@ -871,6 +972,8 @@
         ],
     )
     d_back = lax.all_to_all(d_sent, "ctx", 0, 0, tiled=True)
+    second_shares = [after(v, d_sent) for v in wide_shares[1]]
+    products = [first_products, wide_products(here, two_plane, second_shares)]
     d_query = lax.dynamic_slice_in_dim(d_back[:, :HD], part * HEADS, HEADS).astype(f32)
     d_key_value = jnp.sum(
         d_back[:, HD:].reshape(parts, KV_HEADS, per_group, 2 * HD, rows_here).astype(f32),

time: 680 us -> 656 us (0.965)
  starting transfers between devices: 136 us -> 104 us
  waiting for transfers between devices: 289 us -> 296 us
    ppermute x30, waiting for transfers between devices: 133 us -> 170 us  [over_y(): return lax.ppermute(value, 'ctx', self.route(lambda z, y, c: (z, 1 - y, c)))]
    ppermute x9, starting transfers between devices: 47.5 us -> 16.2 us  [over_z(): return lax.ppermute(value, 'ctx', self.route(lambda z, y, c: (z ^ 1, y, c)))]
    ppermute x5, waiting for transfers between devices: 24.7 us -> 6.87 us  [mirror_z(): lax.ppermute(value, 'ctx', self.route(lambda z, y, c: (self.depth - 1 - z...]
    ppermute x11, waiting for transfers between devices: 88.1 us -> 72.3 us  [over_x(): return lax.ppermute(value, 'fsdp', [(0, 1), (1, 0)])]
    unnamed x209 -> x178, local copies, waits for them, and re-layouts: 26.9 us -> 17.4 us
    optimization_barrier x0 -> x1, local copies, waits for them, and re-layouts: none -> 8.85 us  [after(): return lax.optimization_barrier((value, *others))[0]]
  transfers between devices with their start and end apart: 106 -> 106, of which waited for: 31 -> 35; matrix products, arithmetic and copies ran while one was open for 8% -> 9% of each run, Pallas kernels for 23% -> 25%
where the time goes in v4:
time: 656 us; the launch traced here: 647 us
  waiting for transfers between devices  296 us (45%)
  Pallas kernels  165 us (25%)
  starting transfers between devices  104 us (16%)
  local copies, waits for them, and re-layouts  43.2 us (7%)
  other arithmetic  30.1 us (5%)
    ppermute x30, waiting for transfers between devices, over_y(): return lax.ppermute(value, 'ctx', self.route(lambda z, y, c: (z, 1 - y, c)))  170 us
    pallas_call x12, Pallas kernels, call_with_here(): pl.pallas_call(kernel, grid_spec=pltpu.PrefetchScalarGridSpec(num_scalar_...  119 us
    ppermute x11, waiting for transfers between devices, over_x(): return lax.ppermute(value, 'fsdp', [(0, 1), (1, 0)])  72.3 us
    pallas_call x2, Pallas kernels, kernel_call(): pl.pallas_call(kernel, out_shape=outs, in_specs=[smem] * len(tables) + [v...  46.9 us
    ppermute x9, waiting for transfers between devices, over_z(): return lax.ppermute(value, 'ctx', self.route(lambda z, y, c: (z ^ 1, y, c)))  42.4 us
    ppermute x30, starting transfers between devices, over_y(): return lax.ppermute(value, 'ctx', self.route(lambda z, y, c: (z, 1 - y, c)))  34.4 us
    unnamed x178, local copies, waits for them, and re-layouts  17.4 us
    ppermute x9, starting transfers between devices, over_z(): return lax.ppermute(value, 'ctx', self.route(lambda z, y, c: (z ^ 1, y, c)))  16.2 us
  transfers between devices with their start and end apart: 106, of which 35 were waited for; matrix products, arithmetic and copies ran while one was open for 9% of the time, Pallas kernels for 25%

profile of v4, /device:TPU:0, one launch (start us, length us, event | category | flops | bytes accessed | tf_op | source)
XLA Modules:
  0.0 646.9 jit_solution(688480812883878160)
XLA Ops:
  23.8 8.9 %copy.65 = bf16[512,2,4608]{2,0,1:T(8,128)(2,1)} copy(bf16[512,2,4608]{2,1,0:T(2,128)(2,1)} %param.15) | data formatting | bytes 18874368 | tf_op jit(solution)/shard_map/optimization_barrier | solution.py:304
  50.4 27.0 %collective-permute-done.6.refs_8_ = bf16[2304,256]{1,0:T(8,128)(2,1)} collective-permute-done((bf16[2304,256]{1,0:T(8,128)(2,1)S(1)}, bf16[2304,256]{1,0:T(8,128)(2,1)}, u32[]{:S(2)}, u32[]{:S(2)}) %collective-permute-start.6) | collective-permute-done | bytes 1179680 | tf_op jit(solution)/shard_map/ppermute | solution.py:261
  82.1 22.0 %shard_map.196 = (bf16[16,64,256]{2,1,0:T(8,128)(2,1)}, bf16[4096,64]{1,0:T(8,128)(2,1)S(1)}, bf16[64,4096]{1,0:T(8,128)(2,1)S(1)}, bf16[4096,64]{1,0:T(8,128)(2...) custom-call(s32[32]{0:T(128)S(1)} %broadcast_add_fusion.q_slot, ...), custom_call_target="tpu_custom_call" | custom-call | flops 1 | bytes 72000000 | tf_op jit(solution)/shard_map/pallas_call | solution.py:215
  120.3 48.2 %collective-permute-done.9.refs_2_ = bf16[128,1024]{1,0:T(8,128)(2,1)S(1)} collective-permute-done((bf16[128,1024]{1,0:T(8,128)(2,1)S(1)}, bf16[128,1024]{1,0:T(8,128)(2,1)S(1)}, u32[]{:S(2)}, u32[]{:S(2)}) %collective-permute-start.9) | collective-permute-done | bytes 262176 | tf_op jit(solution)/shard_map/ppermute | solution.py:252
  182.4 20.1 %shard_map.198 = (bf16[256,1152]{1,0:T(8,128)(2,1)}, bf16[256,1152]{1,0:T(8,128)(2,1)}, bf16[256,1152]{1,0:T(8,128)(2,1)}, bf16[256,1152]{1,0:T(8,128)(2,1)}, bf...) custom-call(s32[4]{0:T(128)} %pad_add_fusion.here, ...), custom_call_target="tpu_custom_call" | custom-call | flops 1 | bytes 15000000 | tf_op jit(solution)/shard_map/pallas_call | solution.py:323
  206.2 20.4 %shard_map.199 = (bf16[256,1152]{1,0:T(8,128)(2,1)}, bf16[256,1152]{1,0:T(8,128)(2,1)}, bf16[256,1152]{1,0:T(8,128)(2,1)}, bf16[256,1152]{1,0:T(8,128)(2,1)}, bf...) custom-call(s32[4]{0:T(128)} %pad_add_fusion.here, ...), custom_call_target="tpu_custom_call" | custom-call | flops 1 | bytes 15000000 | tf_op jit(solution)/shard_map/pallas_call | solution.py:323
  241.8 16.1 %collective-permute-done.77.refs_2_ = bf16[256,1024]{1,0:T(8,128)(2,1)} collective-permute-done((bf16[256,1024]{1,0:T(8,128)(2,1)}, bf16[256,1024]{1,0:T(8,128)(2,1)}, u32[]{:S(2)}, u32[]{:S(2)}) %collective-permute-start.77) | collective-permute-done | bytes 524320 | tf_op jit(solution)/shard_map/ppermute | solution.py:252
  258.4 12.0 %collective-permute-done.25.refs_6_ = bf16[256,1152]{1,0:T(8,128)(2,1)S(1)} collective-permute-done((bf16[256,1152]{1,0:T(8,128)(2,1)}, bf16[256,1152]{1,0:T(8,128)(2,1)S(1)}, u32[]{:S(2)}, u32[]{:S(2)}) %collective-permute-start.25) | collective-permute-done | bytes 589856 | tf_op jit(solution)/shard_map/ppermute | solution.py:252
  270.9 12.2 %collective-permute-done.27.refs_7_ = bf16[256,1152]{1,0:T(8,128)(2,1)S(1)} collective-permute-done((bf16[256,1152]{1,0:T(8,128)(2,1)}, bf16[256,1152]{1,0:T(8,128)(2,1)S(1)}, u32[]{:S(2)}, u32[]{:S(2)}) %collective-permute-start.27) | collective-permute-done | bytes 589856 | tf_op jit(solution)/shard_map/ppermute | solution.py:252
  295.3 24.9 %shard_map.201 = bf16[16,192,256]{2,1,0:T(8,128)(2,1)} custom-call(s32[32]{0:T(128)S(1)} %broadcast_add_fusion.q_slot, s32[32]{0:T(128)S(1)} %get-tuple-element.159.kv_slot, s32[16]{0:T(128)S(1)} %get-tuple-element.203.first, s32[16]{0:T(128)S(1)} %get-tuple-element.204.last, bf16[16,64,256]{2,1,0:T(8,128)(2,1)S(1)} %all-to-all-done.2.d_ref, ...), custom_call_target="tpu_custom_call" | custom-call | flops 1 | bytes 72000000 | tf_op jit(solution)/shard_map/pallas_call | solution.py:215
  330.4 16.9 %collective-permute-done.82.refs_7_ = bf16[576,256]{1,0:T(8,128)(2,1)S(1)} collective-permute-done((bf16[576,256]{1,0:T(8,128)(2,1)}, bf16[576,256]{1,0:T(8,128)(2,1)S(1)}, u32[]{:S(2)}, u32[]{:S(2)}) %collective-permute-start.82) | collective-permute-done | bytes 294944 | tf_op jit(solution)/shard_map/ppermute | solution.py:252
  347.3 10.5 %collective-permute-done.84.refs_10_ = bf16[576,256]{1,0:T(8,128)(2,1)S(1)} collective-permute-done((bf16[576,256]{1,0:T(8,128)(2,1)}, bf16[576,256]{1,0:T(8,128)(2,1)S(1)}, u32[]{:S(2)}, u32[]{:S(2)}) %collective-permute-start.84) | collective-permute-done | bytes 294944 | tf_op jit(solution)/shard_map/ppermute | solution.py:252
  383.3 17.0 %collective-permute-done.87 = bf16[576,1024]{1,0:T(8,128)(2,1)} collective-permute-done((bf16[576,1024]{1,0:T(8,128)(2,1)}, bf16[576,1024]{1,0:T(8,128)(2,1)}, u32[]{:S(2)}, u32[]{:S(2)}) %collective-permute-start.87) | collective-permute-done | bytes 1179680 | tf_op jit(solution)/shard_map/ppermute | solution.py:261
  405.3 9.6 %collective-permute-done.29.refs_2_ = bf16[256,1024]{1,0:T(8,128)(2,1)} collective-permute-done((bf16[256,1024]{1,0:T(8,128)(2,1)}, bf16[256,1024]{1,0:T(8,128)(2,1)}, u32[]{:S(2)}, u32[]{:S(2)}) %collective-permute-start.29) | collective-permute-done | bytes 524320 | tf_op jit(solution)/shard_map/ppermute | solution.py:252
  443.9 11.5 %collective-permute-done.56 = bf16[512,1152]{1,0:T(8,128)(2,1)} collective-permute-done((bf16[512,1152]{1,0:T(8,128)(2,1)}, bf16[512,1152]{1,0:T(8,128)(2,1)}, u32[]{:S(2)}, u32[]{:S(2)}) %collective-permute-start.56) | collective-permute-done | bytes 1179680 | tf_op jit(solution)/shard_map/ppermute | solution.py:261
  459.1 8.1 %collective-permute-done.41.refs_15_ = bf16[256,256]{1,0:T(8,128)(2,1)S(1)} collective-permute-done((bf16[256,256]{1,0:T(8,128)(2,1)S(1)}, bf16[256,256]{1,0:T(8,128)(2,1)S(1)}, u32[]{:S(2)}, u32[]{:S(2)}) %collective-permute-start.41) | collective-permute-done | bytes 131104 | tf_op jit(solution)/shard_map/ppermute | solution.py:252
  485.8 12.4 %collective-permute-done.99 = f32[17,128]{1,0:T(8,128)S(1)} collective-permute-done((f32[17,128]{1,0:T(8,128)S(1)}, f32[17,128]{1,0:T(8,128)S(1)}, u32[]{:S(2)}, u32[]{:S(2)}) %collective-permute-start.99) | collective-permute-done | bytes 8736 | tf_op jit(solution)/shard_map/ppermute | solution.py:261
  503.5 9.2 %collective-permute-start.100 = (f32[17,128]{1,0:T(8,128)S(1)}, f32[17,128]{1,0:T(8,128)S(1)}, u32[]{:S(2)}, u32[]{:S(2)}) collective-permute-start(f32[17,128]{1,0:T(8,128)S(1)} %add.356), channel_id=1, source_target_pairs={{0,8},{2,10},{4,12},{6,14},{8,0},{10,2},{12,4},{14,6},{16,24},{18,... | collective-permute-start | bytes 26120 | tf_op jit(solution)/shard_map/ppermute | solution.py:255
  518.2 9.0 %collective-permute-done.93.refs_4_ = bf16[288,1024]{1,0:T(8,128)(2,1)S(1)} collective-permute-done((bf16[288,1024]{1,0:T(8,128)(2,1)S(1)}, bf16[288,1024]{1,0:T(8,128)(2,1)S(1)}, u32[]{:S(2)}, u32[]{:S(2)}) %collective-permute-start.93) | collective-permute-done | bytes 589856 | tf_op jit(solution)/shard_map/ppermute | solution.py:255
  528.9 16.9 %collective-permute-done.43 = bf16[256,768]{1,0:T(8,128)(2,1)S(1)} collective-permute-done((bf16[256,768]{1,0:T(8,128)(2,1)S(1)}, bf16[256,768]{1,0:T(8,128)(2,1)S(1)}, u32[]{:S(2)}, u32[]{:S(2)}) %collective-permute-start.43) | collective-permute-done | bytes 393248 | tf_op jit(solution)/shard_map/ppermute | solution.py:255
  554.3 8.5 %collective-permute-done.95.refs_6_ = bf16[288,1024]{1,0:T(8,128)(2,1)} collective-permute-done((bf16[288,1024]{1,0:T(8,128)(2,1)S(1)}, bf16[288,1024]{1,0:T(8,128)(2,1)}, u32[]{:S(2)}, u32[]{:S(2)}) %collective-permute-start.95) | collective-permute-done | bytes 589856 | tf_op jit(solution)/shard_map/ppermute | solution.py:252
  565.2 10.8 %collective-permute-done.62.refs_4_ = bf16[256,1152]{1,0:T(8,128)(2,1)} collective-permute-done((bf16[256,1152]{1,0:T(8,128)(2,1)S(1)}, bf16[256,1152]{1,0:T(8,128)(2,1)}, u32[]{:S(2)}, u32[]{:S(2)}) %collective-permute-start.62) | collective-permute-done | bytes 589856 | tf_op jit(solution)/shard_map/ppermute | solution.py:255
  609.7 9.9 %shard_map.205.refs_8_ = f32[512,2,4608]{2,1,0:T(2,128)} custom-call(s32[4]{0:T(128)} %pad_add_fusion.here, bf16[256,1152]{1,0:T(8,128)(2,1)} %copy-done.16, bf16[256,1152]{1,0:T(8,128)(2,1)} %copy-done.31, bf16[256,1152]{1,0:T(8,128)(2,1)} %copy-done.32, bf16[256,1152]{1,0:T(8,128)(2,1)} %copy-done.37, bf16[256,1152]{1,0:T(8,128)(2,1)} %copy-done.33, ...), custom_call_target="tpu_custom_call" | custom-call | flops 1 | bytes 30000000 | tf_op jit(solution)/shard_map/pallas_call | solution.py:323
  628.4 9.9 %shard_map.206 = f32[512,2,4608]{2,1,0:T(2,128)} custom-call(s32[4]{0:T(128)} %pad_add_fusion.here, bf16[256,1152]{1,0:T(8,128)(2,1)} %copy-done.23, bf16[256,1152]{1,0:T(8,128)(2,1)} %copy-done.45, bf16[256,1152]{1,0:T(8,128)(2,1)} %collective-permute-done.60.refs_2_, bf16[256,1152]{1,0:T(8,128)(2,1)} %copy-done.47, ...), custom_call_target="tpu_custom_call", output_to_operand_aliasing={{}: (9, {})} | custom-call | flops 1 | bytes 30000000 | tf_op jit(solution)/shard_map/pallas_call | solution.py:323
  (478 shorter events, 273.0 us)
Async XLA Ops:
  42.9 38.1 %all-to-all-start = ((bf16[16,192,256]{2,1,0:T(8,128)(2,1)}), bf16[16,192,256]{2,1,0:T(8,128)(2,1)S(1)}, u32[]{:S(2)}, u32[]{:S(2)}) async-start(bf16[16,192,256]{2,1,0:T(8,128)(2,1)} %get-tuple-element.85), calls=%async_computation | async-start | bytes 3145728 | tf_op jit(solution)/shard_map/all_to_all | solution.py:893
  78.1 90.3 %collective-permute-start.16 = (bf16[2304,256]{1,0:T(8,128)(2,1)}, bf16[2304,256]{1,0:T(8,128)(2,1)}, u32[]{:S(2)}, u32[]{:S(2)}) collective-permute-start(bf16[2304,256]{1,0:T(8,128)(2,1)} %collective-permute-done.6.refs_8_), channel_id=1, source_target_pairs={{0,4},{2,6},{4,0},{6,2},{8,12},{10,14},{12,8},{14,10},{16,20},{18,... | collective-permute-start | bytes 3538952 | tf_op jit(solution)/shard_map/ppermute | solution.py:252
  79.8 89.2 %collective-permute-start.19 = (bf16[2,128,2304]{2,1,0:T(8,128)(2,1)}, bf16[2,128,2304]{2,1,0:T(8,128)(2,1)}, u32[]{:S(2)}, u32[]{:S(2)}) collective-permute-start(bf16[2,128,2304]{2,1,0:T(8,128)(2,1)} %collective-permute-done.5.refs_3_), channel_id=1, source_target_pairs={{0,4},{2,6},{4,0},{6,2},{8,12},{10,14},{12,8},{14,10},{16,20},{18,... | collective-permute-start | bytes 3538952 | tf_op jit(solution)/shard_map/ppermute | solution.py:252
  80.8 96.3 %collective-permute-start.18 = (bf16[2,128,2304]{2,1,0:T(8,128)(2,1)}, bf16[2,128,2304]{2,1,0:T(8,128)(2,1)}, u32[]{:S(2)}, u32[]{:S(2)}) collective-permute-start(bf16[2,128,2304]{2,1,0:T(8,128)(2,1)} %collective-permute-done.5.refs_3_), channel_id=1, source_target_pairs={{0,2},{2,0},{4,6},{6,4},{8,10},{10,8},{12,14},{14,12},{16,18},{18,... | collective-permute-start | bytes 3538952 | tf_op jit(solution)/shard_map/ppermute | solution.py:249
  107.0 70.3 %collective-permute-start.13 = (bf16[2,128,2304]{2,1,0:T(8,128)(2,1)}, bf16[2,128,2304]{2,1,0:T(8,128)(2,1)}, u32[]{:S(2)}, u32[]{:S(2)}) collective-permute-start(bf16[2,128,2304]{2,1,0:T(8,128)(2,1)} %collective-permute-done.11.refs_3_), channel_id=1, source_target_pairs={{0,4},{2,6},{4,0},{6,2},{8,12},{10,14},{12,8},{14,10},{16,20},{18,... | collective-permute-start | bytes 3538952 | tf_op jit(solution)/shard_map/ppermute | solution.py:252
  110.1 67.5 %all-to-all-start.1 = ((bf16[16,64,256]{2,1,0:T(8,128)(2,1)}), bf16[16,64,256]{2,1,0:T(8,128)(2,1)}, u32[]{:S(2)}, u32[]{:S(2)}) async-start(bf16[16,64,256]{2,1,0:T(8,128)(2,1)} %get-tuple-element.90), calls=%async_computation.1 | async-start | bytes 1048576 | tf_op jit(solution)/shard_map/all_to_all | solution.py:922
  118.3 50.2 %collective-permute-start.9 = (bf16[128,1024]{1,0:T(8,128)(2,1)S(1)}, bf16[128,1024]{1,0:T(8,128)(2,1)S(1)}, u32[]{:S(2)}, u32[]{:S(2)}) collective-permute-start(bf16[128,1024]{1,0:T(8,128)(2,1)S(1)} %collective-permute-done.7.refs_0_), channel_id=1, source_target_pairs={{0,4},{2,6},{4,0},{6,2},{8,12},{10,14},{12,8},{14,10},{16,20},{18,... | collective-permute-start | bytes 786440 | tf_op jit(solution)/shard_map/ppermute | solution.py:252
  202.7 38.6 %collective-permute-start.76 = (bf16[256,1024]{1,0:T(8,128)(2,1)}, bf16[256,1024]{1,0:T(8,128)(2,1)}, u32[]{:S(2)}, u32[]{:S(2)}) collective-permute-start(bf16[256,1024]{1,0:T(8,128)(2,1)} %bitcast.20.refs_1_.refs_0_), channel_id=1, source_target_pairs={{0,2},{2,0},{4,6},{6,4},{8,10},{10,8},{12,14},{14,12},{16,18},{18,... | collective-permute-start | bytes 1572872 | tf_op jit(solution)/shard_map/ppermute | solution.py:249
  203.1 38.2 %collective-permute-start.23 = (bf16[256,1024]{1,0:T(8,128)(2,1)}, bf16[256,1024]{1,0:T(8,128)(2,1)}, u32[]{:S(2)}, u32[]{:S(2)}) collective-permute-start(bf16[256,1024]{1,0:T(8,128)(2,1)} %multiply_convert_fusion.refs_0_), channel_id=1, source_target_pairs={{0,4},{2,6},{4,0},{6,2},{8,12},{10,14},{12,8},{14,10},{16,20},{18,... | collective-permute-start | bytes 1572872 | tf_op jit(solution)/shard_map/ppermute | solution.py:252
  231.5 60.3 %all-to-all-start.2 = ((bf16[16,64,256]{2,1,0:T(8,128)(2,1)}), bf16[16,64,256]{2,1,0:T(8,128)(2,1)S(1)}, u32[]{:S(2)}, u32[]{:S(2)}) async-start(bf16[16,64,256]{2,1,0:T(8,128)(2,1)} %bitcast.128), calls=%async_computation.2 | async-start | bytes 1048576 | tf_op jit(solution)/shard_map/all_to_all | solution.py:958
  239.5 43.6 %collective-permute-start.27 = (bf16[256,1152]{1,0:T(8,128)(2,1)}, bf16[256,1152]{1,0:T(8,128)(2,1)S(1)}, u32[]{:S(2)}, u32[]{:S(2)}) collective-permute-start(bf16[256,1152]{1,0:T(8,128)(2,1)} %collective-permute-done.26), channel_id=1, source_target_pairs={{0,4},{2,6},{4,0},{6,2},{8,12},{10,14},{12,8},{14,10},{16,20},{18,... | collective-permute-start | bytes 1769480 | tf_op jit(solution)/shard_map/ppermute | solution.py:252
  257.9 66.8 %collective-permute-start.78 = (bf16[256,1024]{1,0:T(8,128)(2,1)}, bf16[256,1024]{1,0:T(8,128)(2,1)}, u32[]{:S(2)}, u32[]{:S(2)}) collective-permute-start(bf16[256,1024]{1,0:T(8,128)(2,1)} %collective-permute-done.77.refs_2_), channel_id=1, source_target_pairs={{0,2},{2,0},{4,6},{6,4},{8,10},{10,8},{12,14},{14,12},{16,18},{18,... | collective-permute-start | bytes 1572872 | tf_op jit(solution)/shard_map/ppermute | solution.py:249
  257.9 68.4 %collective-permute-start.81 = (bf16[576,256]{1,0:T(8,128)(2,1)}, bf16[576,256]{1,0:T(8,128)(2,1)}, u32[]{:S(2)}, u32[]{:S(2)}) collective-permute-start(bf16[576,256]{1,0:T(8,128)(2,1)} %get-tuple-element.147), channel_id=1, source_target_pairs={{0,2},{2,0},{4,6},{6,4},{8,10},{10,8},{12,14},{14,12},{16,18},{18,... | collective-permute-start | bytes 884744 | tf_op jit(solution)/shard_map/ppermute | solution.py:249
  270.5 57.8 %collective-permute-start.79 = (bf16[576,256]{1,0:T(8,128)(2,1)}, bf16[576,256]{1,0:T(8,128)(2,1)S(1)}, u32[]{:S(2)}, u32[]{:S(2)}) collective-permute-start(bf16[576,256]{1,0:T(8,128)(2,1)} %get-tuple-element.145), channel_id=1, source_target_pairs={{0,2},{2,0},{4,6},{6,4},{8,10},{10,8},{12,14},{14,12},{16,18},{18,... | collective-permute-start | bytes 884744 | tf_op jit(solution)/shard_map/ppermute | solution.py:249
  270.5 57.8 %collective-permute-start.80 = (bf16[576,256]{1,0:T(8,128)(2,1)}, bf16[576,256]{1,0:T(8,128)(2,1)}, u32[]{:S(2)}, u32[]{:S(2)}) collective-permute-start(bf16[576,256]{1,0:T(8,128)(2,1)} %get-tuple-element.146), channel_id=1, source_target_pairs={{0,4},{2,6},{4,0},{6,2},{8,12},{10,14},{12,8},{14,10},{16,20},{18,... | collective-permute-start | bytes 884744 | tf_op jit(solution)/shard_map/ppermute | solution.py:252
  283.1 45.3 %collective-permute-start.85 = (bf16[576,256]{1,0:T(8,128)(2,1)}, bf16[576,256]{1,0:T(8,128)(2,1)}, u32[]{:S(2)}, u32[]{:S(2)}) collective-permute-start(bf16[576,256]{1,0:T(8,128)(2,1)} %get-tuple-element.151), channel_id=1, source_target_pairs={{0,2},{2,0},{4,6},{6,4},{8,10},{10,8},{12,14},{14,12},{16,18},{18,... | collective-permute-start | bytes 884744 | tf_op jit(solution)/shard_map/ppermute | solution.py:249
  320.2 109.9 %all-to-all-start.3 = ((bf16[16,192,256]{2,1,0:T(8,128)(2,1)}), bf16[16,192,256]{2,1,0:T(8,128)(2,1)S(1)}, u32[]{:S(2)}, u32[]{:S(2)}) async-start(bf16[16,192,256]{2,1,0:T(8,128)(2,1)} %shard_map.201), calls=%async_computation.3 | async-start | bytes 3145728 | tf_op jit(solution)/shard_map/all_to_all | solution.py:974
  324.8 52.8 %collective-permute-start.66 = (bf16[512,1152]{1,0:T(8,128)(2,1)}, bf16[512,1152]{1,0:T(8,128)(2,1)S(1)}, u32[]{:S(2)}, u32[]{:S(2)}) collective-permute-start(bf16[512,1152]{1,0:T(8,128)(2,1)} %get-tuple-element.113), channel_id=1, source_target_pairs={{0,1},{1,0},{2,3},{3,2},{4,5},{5,4},{6,7},{7,6},{8,9},{9,8},{10,11... | collective-permute-start | bytes 3538952 | tf_op jit(solution)/shard_map/ppermute | solution.py:261
  377.2 37.8 %collective-permute-start.55 = (bf16[256,1152]{1,0:T(8,128)(2,1)}, bf16[256,1152]{1,0:T(8,128)(2,1)}, u32[]{:S(2)}, u32[]{:S(2)}) collective-permute-start(bf16[256,1152]{1,0:T(8,128)(2,1)} %collective-permute-done.54), channel_id=1, source_target_pairs={{0,4},{2,6},{4,0},{6,2},{8,12},{10,14},{12,8},{14,10},{16,20},{18,... | collective-permute-start | bytes 1769480 | tf_op jit(solution)/shard_map/ppermute | solution.py:252
  380.2 45.0 %collective-permute-start.67 = (bf16[256,1152]{1,0:T(8,128)(2,1)}, bf16[256,1152]{1,0:T(8,128)(2,1)}, u32[]{:S(2)}, u32[]{:S(2)}) collective-permute-start(bf16[256,1152]{1,0:T(8,128)(2,1)} %add_convert_fusion.6), channel_id=1, source_target_pairs={{0,8},{2,10},{4,12},{6,14},{8,0},{10,2},{12,4},{14,6},{16,24},{18,... | collective-permute-start | bytes 1769480 | tf_op jit(solution)/shard_map/ppermute | solution.py:255
  435.8 43.9 %collective-permute-start.68 = (bf16[256,1152]{1,0:T(8,128)(2,1)S(1)}, bf16[256,1152]{1,0:T(8,128)(2,1)S(1)}, u32[]{:S(2)}, u32[]{:S(2)}) collective-permute-start(bf16[256,1152]{1,0:T(8,128)(2,1)S(1)} %add_convert_fusion.5), channel_id=1, source_target_pairs={{0,24},{2,26},{4,28},{6,30},{8,16},{10,18},{12,20},{14,22},{16,8},... | collective-permute-start | bytes 1769480 | tf_op jit(solution)/shard_map/ppermute | solution.py:258
  595.7 42.6 %collective-permute-start.45 = (bf16[256,768]{1,0:T(8,128)(2,1)}, bf16[256,768]{1,0:T(8,128)(2,1)S(1)}, u32[]{:S(2)}, u32[]{:S(2)}) collective-permute-start(bf16[256,768]{1,0:T(8,128)(2,1)} %add_convert_fusion.12.refs_0_), channel_id=1, source_target_pairs={{0,2},{2,0},{4,6},{6,4},{8,10},{10,8},{12,14},{14,12},{16,18},{18,... | collective-permute-start | bytes 1179656 | tf_op jit(solution)/shard_map/ppermute | solution.py:249
  596.2 42.2 %collective-permute-start.49 = (bf16[256,768]{1,0:T(8,128)(2,1)}, bf16[256,768]{1,0:T(8,128)(2,1)S(1)}, u32[]{:S(2)}, u32[]{:S(2)}) collective-permute-start(bf16[256,768]{1,0:T(8,128)(2,1)} %collective-permute-done.48.refs_4_), channel_id=1, source_target_pairs={{0,2},{2,0},{4,6},{6,4},{8,10},{10,8},{12,14},{14,12},{16,18},{18,... | collective-permute-start | bytes 1179656 | tf_op jit(solution)/shard_map/ppermute | solution.py:249
  600.9 37.4 %collective-permute-start.47 = (bf16[256,768]{1,0:T(8,128)(2,1)S(1)}, bf16[256,768]{1,0:T(8,128)(2,1)S(1)}, u32[]{:S(2)}, u32[]{:S(2)}) collective-permute-start(bf16[256,768]{1,0:T(8,128)(2,1)S(1)} %collective-permute-done.46.refs_2_), channel_id=1, source_target_pairs={{0,2},{2,0},{4,6},{6,4},{8,10},{10,8},{12,14},{14,12},{16,18},{18,... | collective-permute-start | bytes 1179656 | tf_op jit(solution)/shard_map/ppermute | solution.py:249
  (171 other events, 2557.6 us)

commit v5 on v4

--- a/solution.py
+++ b/solution.py
@@ -265,31 +265,21 @@
         beside = self.over_y(value)
         return (value, across, beside, self.over_core(beside))
 
-    def deal_plane(self, keep, keep_far, give, give_far):
-        got, got_far = self.over_core(give), self.over_core(give_far)
-        return (keep, got, self.over_y(keep_far), self.over_y(got_far))
+    def deal_plane(self, near, give, far):
+        beside = self.over_y(far)
+        return (near, self.over_core(give), beside, self.over_core(beside))
 
     def sum_depth(self, kept, got):
-        rows = kept.shape[0] // 2
-
         def half(index):
-            return add(
-                lax.dynamic_slice_in_dim(kept, index * rows, rows),
-                lax.dynamic_slice_in_dim(got, index * rows, rows),
-            )
+            return add(pick(kept, index, 0), pick(got, index, 0))
 
         given = self.over_z(half(1 - self.half))
         part = add(half(self.half), given)
         full = add(part, self.mirror_z(part))
-        return (full, self.over_z(full))
+        return jnp.stack([full, self.over_z(full)])
 
     def reduce(self, sent, kept):
-        return [self.spread_plane(v) for v in self.sum_depth(kept, self.over_x(sent))]
-
-    def total(self, value):
-        for swap in (self.over_core, self.over_y, self.over_x, self.over_z, self.mirror_z):
-            value = value + swap(value)
-        return value
+        return self.spread_plane(self.sum_depth(kept, self.over_x(sent)))
 
 
 def pick(value, index, axis):
@@ -344,7 +334,8 @@
 def project_kernel(here, *refs):
     x_ref, gain_ref, own_ref = refs[:3]
     pieces, q_gain, k_gain, cos_ref, sin_ref = refs[3:7], refs[7], refs[8], refs[9], refs[10]
-    sent, weight, q_ref, k_ref, q_scale, k_scale, normed_ref, scale_ref = refs[11:]
+    d_ref = refs[11]
+    sent, weight, q_ref, k_ref, q_scale, k_scale, early_ref, scale_ref = refs[12:]
     core, y, side = here[1], here[2], here[3]
     rows = own_ref.shape[0]
     part = rows // 4
@@ -357,7 +348,8 @@
     scale = rms_scale(x)
     scale_ref[...] = scale
     normed = (x * scale * gain_ref[...]).astype(bf16)
-    normed_ref[...] = normed
+    early_ref[0] = d_ref[...]
+    early_ref[1] = normed
     cosine, sine = cos_ref[...], sin_ref[...]
     half = HD // 2
 
@@ -390,11 +382,11 @@
                 sent[head * per_group + copy, row : row + HD, :] = value
 
 
-def project(here, x, gain, own, pieces, q_gain, k_gain, cosine, sine):
+def project(here, x, gain, own, pieces, q_gain, k_gain, cosine, sine, d_ffn):
     tokens, width = x.shape
     f32, bf16 = jnp.float32, jnp.bfloat16
     shape = jax.ShapeDtypeStruct
-    arrays = [x, gain, own, *pieces, q_gain, k_gain, cosine, sine]
+    arrays = [x, gain, own, *pieces, q_gain, k_gain, cosine, sine, d_ffn]
     outs = [
         shape((HEADS, 3 * HD, tokens), bf16),
         shape((width, own.shape[1]), bf16),
@@ -402,7 +394,7 @@
         shape((KV_HEADS * HD, tokens), f32),
         shape((HEADS, tokens), f32),
         shape((KV_HEADS, tokens), f32),
-        shape((tokens, width), bf16),
+        shape((2, tokens, width), bf16),
         shape((tokens, 1), f32),
     ]
     return call_with_here(
@@ -411,49 +403,65 @@
     )
 
 
-def place_rows(here, own, pieces):
-    rows, columns = own.shape
+def layer(array, index):
+    return pl.BlockSpec((1, *array.shape[1:]), lambda i, here: (index, 0, 0))
+
+
+def attend_out_kernel(here, *refs):
+    attn_ref, x_ref, gain_ref, own_ref = refs[:4]
+    pieces = refs[4:12]
+    weight, h_ref, scale_ref, late_ref = refs[12:]
+    core, y, side = here[1], here[2], here[3]
+    rows = own_ref.shape[0]
     part = rows // 4
-
-    def kernel(here, own_ref, *refs):
-        out_ref = refs[-1]
-        s = pl.program_id(0)
-
-        @pl.when(s < 4)
-        def _():
-            out_ref[...] = own_ref[...]
-
-        for p in range(4):
-
-            @pl.when(s == 4 + p)
-            def _(p=p):
-                out_ref[...] = refs[p][...]
-
-    def target(s, here):
-        p = s - 4
-        other = (1 - here[3]) * 4 + ((p % 2) ^ here[1]) * 2 + ((p // 2) ^ here[2])
-        return (jnp.where(s < 4, here[3] * 4 + s, other), 0)
-
-    (out,) = call_with_here(
-        kernel,
-        here,
-        (8,),
-        [own, *pieces],
-        [pl.BlockSpec((part, columns), lambda s, here: (jnp.minimum(s, 3), 0))]
-        + [whole(p) for p in pieces],
-        [jax.ShapeDtypeStruct((2 * rows, columns), own.dtype)],
-        [pl.BlockSpec((part, columns), target)],
-    )
-    return out
+    weight[pl.ds(pl.multiple_of(side * rows, rows), rows), :] = own_ref[...]
+    for p in range(4):
+        at = (1 - side) * rows + (((p % 2) ^ core) * 2 + ((p // 2) ^ y)) * part
+        for n in range(2):
+            piece = pieces[2 * p + n]
+            wide = piece.shape[1]
+            weight[pl.ds(pl.multiple_of(at, part), part), n * wide : (n + 1) * wide] = piece[...]
+    attn = attn_ref[...].T
+    late_ref[0] = attn
+    h_one = x_ref[...].astype(jnp.float32) + jnp.dot(
+        attn, weight[...], preferred_element_type=jnp.float32
+    )
+    scale = rms_scale(h_one)
+    h_ref[...] = h_one
+    scale_ref[...] = scale
+    late_ref[1] = (h_one * scale * gain_ref[...]).astype(jnp.bfloat16)
+
+
+def attend_out(here, attn, x, gain, own, pieces):
+    tokens, width = x.shape
+    f32, bf16 = jnp.float32, jnp.bfloat16
+    shape = jax.ShapeDtypeStruct
+    part = own.shape[0] // 4
+    half = width // 2
+    first = pieces[0].shape[1] // half - 2
+    arrays = [attn, x, gain, own]
+    specs = [whole(a) for a in arrays]
+    for piece in pieces:
+        for n in range(2):
+            arrays.append(piece)
+            specs.append(pl.BlockSpec((part, half), lambda i, here, n=n: (0, first + n)))
+    outs = [
+        shape((width, width), bf16),
+        shape((tokens, width), f32),
+        shape((tokens, 1), f32),
+        shape((2, tokens, width), bf16),
+    ]
+    return call_with_here(
+        attend_out_kernel, here, (1,), arrays, specs, outs, [whole(o) for o in outs], micros=5
+    )
 
 
 def ffn_kernel(chunk, here, *refs):
     two_ref, d_ref, own_ref = refs[:3]
-    gate_pieces, down_ref, down_pieces = refs[3:7], refs[7], refs[8:12]
-    before_out, before_two = refs[12:14]
-    keep, give, hidden_keep, hidden_give = refs[14:16], refs[16:18], refs[18:20], refs[20:22]
-    out_ref, d_two_ref = refs[22:24]
-    weight, down, hidden_t = refs[24:27]
+    gate_pieces, up_pieces, down_ref, down_pieces = refs[3:7], refs[7:11], refs[11], refs[12:16]
+    before_out, before_two = refs[16:18]
+    near, give, far, out_ref, d_two_ref = refs[18:23]
+    weight, down, hidden_rows = refs[23:26]
     core, y, side = here[1], here[2], here[3]
     t = pl.program_id(0)
     f32, bf16 = jnp.float32, jnp.bfloat16
@@ -471,7 +479,8 @@
     weight[:, pl.ds(pl.multiple_of(side * own_rows, own_rows), own_rows), :] = own_ref[...]
     for p in range(4):
         at = pl.multiple_of((1 - side) * own_rows + quarter(p) * part, part)
-        weight[:, pl.ds(at, part), :] = gate_pieces[p][...]
+        weight[0, pl.ds(at, part), :] = gate_pieces[p][...]
+        weight[1, pl.ds(at, part), :] = up_pieces[p][...]
 
     @pl.when(side == chunk)
     def _():
@@ -484,7 +493,7 @@
             at = pl.multiple_of(quarter(p) * wide, wide)
             down[:, pl.ds(at, wide)] = down_pieces[p][...]
 
-    two = two_ref[...]
+    two = two_ref[0]
     d_ffn = d_ref[...]
     tile = own_ref.shape[2]
     first = (tile // 2) // 256 * 256
@@ -502,40 +511,45 @@
         d_two_ref[...] += contract(d_gate, weight[0, :, at], (1, 1)) + contract(
             d_upper, weight[1, :, at], (1, 1)
         )
-        hidden_t[at, :] = hidden.T
+        hidden_rows[:, at] = hidden
         mine = jnp.where(core == 0, d_gate, d_upper)
         other = jnp.where(core == 0, d_upper, d_gate)
-        for far in range(2):
-
-            @pl.when((t == y) == (far == 0))
-            def _(far=far):
-                keep[far][:, at] = mine
-                give[far][:, at] = other
+
+        @pl.when(t == y)
+        def _(mine=mine, other=other, at=at):
+            near[:, at] = mine
+            give[:, at] = other
+
+        @pl.when(t != y)
+        def _(mine=mine, other=other, at=at):
+            far[0, :, at] = mine
+            far[1, :, at] = other
 
     share = tile // 2
-    for far in range(2):
-        at = pl.multiple_of((y ^ far) * share, share)
-
-        @pl.when(t == core)
-        def _(far=far, at=at):
-            hidden_keep[far][...] = hidden_t[pl.ds(at, share), :]
-
-        @pl.when(t != core)
-        def _(far=far, at=at):
-            hidden_give[far][...] = hidden_t[pl.ds(at, share), :]
-
-
-def ffn(here, chunk, two, d_ffn, own, pieces, down, down_pieces, before):
-    tokens, width = two.shape
+    lower, upper = hidden_rows[:, :share], hidden_rows[:, share:]
+    close = jnp.where(y == 0, lower, upper)
+    distant = jnp.where(y == 0, upper, lower)
+    at = slice(tile, tile + share)
+
+    @pl.when(t == core)
+    def _():
+        near[:, at] = close
+        far[0, :, at] = distant
+
+    @pl.when(t != core)
+    def _():
+        give[:, at] = close
+        far[1, :, at] = distant
+
+
+def ffn(here, chunk, late, d_ffn, own, pieces, down, down_pieces, before):
+    _, tokens, width = late.shape
     tile = own.shape[2] // 4
-    share = tile // 2
+    padded = (tile + tile // 2 + BLK - 1) // BLK * BLK
     shape = jax.ShapeDtypeStruct
     f32, bf16 = jnp.float32, jnp.bfloat16
-    outs = (
-        [shape((tokens, tile), bf16)] * 4
-        + [shape((share, tokens), bf16)] * 4
-        + [shape((tokens, width), f32)] * 2
-    )
+    outs = [shape((tokens, padded), bf16)] * 2 + [shape((2, tokens, padded), bf16)]
+    outs += [shape((tokens, width), f32)] * 2
 
     def own_down(t, here):
         return (jnp.where(here[3] == chunk, t, 0), 0)
@@ -543,10 +557,12 @@
     def other_down(t, here):
         return (jnp.where(here[3] == chunk, 0, t), 0)
 
+    part = own.shape[1] // 4
     specs = (
-        [whole(two), whole(d_ffn)]
+        [layer(late, 1), whole(d_ffn)]
         + [pl.BlockSpec((2, own.shape[1], tile), lambda t, here: (0, 0, 2 * chunk + t))]
-        + [pl.BlockSpec((2, own.shape[1] // 4, tile), lambda t, here: (0, 0, t))] * 4
+        + [pl.BlockSpec((part, tile), lambda t, here: (0, t))] * 4
+        + [pl.BlockSpec((part, tile), lambda t, here: (0, 2 + t))] * 4
         + [pl.BlockSpec((tile, width), own_down)]
         + [pl.BlockSpec((tile, width // 4), other_down)] * 4
         + [whole(before[0]), whole(before[1])]
@@ -555,185 +571,310 @@
         functools.partial(ffn_kernel, chunk),
         here,
         (2,),
-        [two, d_ffn, own, *pieces, down, *down_pieces, *before],
+        [late, d_ffn, own, *pieces, *pieces, down, *down_pieces, *before],
         specs,
         outs,
         [whole(o) for o in outs],
         [
             pltpu.VMEM((2, width, tile), bf16),
             pltpu.VMEM((tile, width), bf16),
-            pltpu.VMEM((tile, tokens), bf16),
+            pltpu.VMEM((tokens, tile), bf16),
         ],
-    )
-    return got[:4], got[4:8], got[8:]
+        micros=20,
+    )
+    return got[:3], got[3:]
+
+
+def dealt(shares):
+    return list(shares), [whole(shares[0]), whole(shares[1]), layer(shares[2], 0), layer(shares[3], 1)]
+
+
+def flat(ref):
+    return ref[...] if len(ref.shape) == 2 else ref[0]
 
 
 def wide_product_kernel(here, *refs):
     planes, terms = refs[:4], refs[4:8]
     sent, kept, left, right = refs[8:]
-    tokens = planes[0].shape[0]
+    tokens = planes[0].shape[1]
+    columns = right.shape[1]
     for i in range(4):
-        left[:, i * tokens : (i + 1) * tokens] = planes[i][...].T
-        right[i * tokens : (i + 1) * tokens, :] = terms[i][...]
+        left[:, i * tokens : (i + 1) * tokens] = planes[i][0].T
+        right[i * tokens : (i + 1) * tokens, :] = flat(terms[i])[:, :columns]
     side = here[3]
-    rows = kept.shape[0]
-    step = 256
-    for at in range(0, rows, step):
+    _, step, _ = kept.shape
+    for half in range(2):
         for owner, out_ref in ((1 - side, sent), (side, kept)):
-            place = pl.multiple_of(owner * rows + at, step)
-            out_ref[at : at + step, :] = jnp.dot(
+            place = pl.multiple_of(owner * 2 * step + half * step, step)
+            out_ref[half] = jnp.dot(
                 left[pl.ds(place, step), :], right[...], preferred_element_type=jnp.float32
             ).astype(out_ref.dtype)
 
 
-def wide_products(here, planes, terms):
-    tokens, rows = planes[0].shape
-    columns = terms[0].shape[1]
+def wide_products(here, late_plane, shares, columns):
+    _, tokens, rows = late_plane[0].shape
     outs = [
-        jax.ShapeDtypeStruct((rows // 2, columns), jnp.bfloat16),
-        jax.ShapeDtypeStruct((rows // 2, columns), jnp.float32),
+        jax.ShapeDtypeStruct((2, rows // 4, columns), jnp.bfloat16),
+        jax.ShapeDtypeStruct((2, rows // 4, columns), jnp.float32),
     ]
-    arrays = [*planes, *terms]
+    arrays, specs = dealt(shares)
     return call_with_here(
         wide_product_kernel,
         here,
         (1,),
-        arrays,
-        [whole(a) for a in arrays],
+        [*late_plane, *arrays],
+        [layer(a, 1) for a in late_plane] + specs,
         outs,
         [whole(o) for o in outs],
         [
             pltpu.VMEM((rows, 4 * tokens), jnp.bfloat16),
             pltpu.VMEM((4 * tokens, columns), jnp.bfloat16),
         ],
+        micros=8,
     )
 
 
 def down_product_kernel(here, *refs):
     planes, terms = refs[:4], (refs[4:8], refs[8:12])
     sent, kept, left, right = refs[12:]
-    tokens = planes[0].shape[0]
+    tokens = planes[0].shape[1]
+    rows = left.shape[0]
     for i in range(4):
-        right[i * tokens : (i + 1) * tokens, :] = planes[i][...]
+        right[i * tokens : (i + 1) * tokens, :] = planes[i][0]
     for chunk in range(2):
         for i in range(4):
-            left[:, i * tokens : (i + 1) * tokens] = terms[chunk][i][...]
-        product = jnp.dot(left[...], right[...], preferred_element_type=jnp.float32)
-
-        @pl.when(here[3] == chunk)
-        def _(product=product):
-            kept[...] = product
-
-        @pl.when(here[3] != chunk)
-        def _(product=product):
-            sent[...] = product.astype(sent.dtype)
-
-
-def down_products(here, planes, first, second):
-    tokens, columns = planes[0].shape
-    rows = first[0].shape[0]
+            share = flat(terms[chunk][i])
+            at = share.shape[1] // BLK * BLK - (rows + BLK - 1) // BLK * BLK
+            left[:, i * tokens : (i + 1) * tokens] = share[:, at : at + rows].T
+        for half in range(2):
+            product = jnp.dot(
+                left[half * rows // 2 : (half + 1) * rows // 2, :],
+                right[...],
+                preferred_element_type=jnp.float32,
+            )
+
+            @pl.when(here[3] == chunk)
+            def _(product=product, half=half):
+                kept[half] = product
+
+            @pl.when(here[3] != chunk)
+            def _(product=product, half=half):
+                sent[half] = product.astype(sent.dtype)
+
+
+def down_products(here, early_plane, first, second, rows):
+    _, tokens, columns = early_plane[0].shape
     outs = [
-        jax.ShapeDtypeStruct((rows, columns), jnp.bfloat16),
-        jax.ShapeDtypeStruct((rows, columns), jnp.float32),
+        jax.ShapeDtypeStruct((2, rows // 2, columns), jnp.bfloat16),
+        jax.ShapeDtypeStruct((2, rows // 2, columns), jnp.float32),
     ]
-    arrays = [*planes, *first, *second]
+    first, first_specs = dealt(first)
+    second, second_specs = dealt(second)
     return call_with_here(
         down_product_kernel,
         here,
         (1,),
-        arrays,
-        [whole(a) for a in arrays],
+        [*early_plane, *first, *second],
+        [layer(a, 0) for a in early_plane] + first_specs + second_specs,
         outs,
         [whole(o) for o in outs],
         [
             pltpu.VMEM((rows, 4 * tokens), jnp.bfloat16),
             pltpu.VMEM((4 * tokens, columns), jnp.bfloat16),
         ],
+        micros=8,
+    )
+
+
+GAIN_ROWS = 16
+
+
+def attention_back_kernel(here, *refs):
+    d_ref, q_ref, k_ref, q_scale, k_scale, q_gain, k_gain, cos_ref, sin_ref = refs[:9]
+    weight, x_ref, scale_ref, gain_ref, d_h_ref, d_attn_ref = refs[9:15]
+    near, give, far, d_x_ref, gains_ref = refs[15:20]
+    turned, natural = refs[20:]
+    f32, bf16 = jnp.float32, jnp.bfloat16
+    core, y = here[1], here[2]
+    cosine, sine = cos_ref[...], sin_ref[...]
+    half = HD // 2
+    per_group = HEADS // KV_HEADS
+    tokens = x_ref.shape[0]
+
+    def back(grad, raw, scale, gain):
+        first, second = grad[:half], grad[half:]
+        normed = jnp.concatenate(
+            [first * cosine + second * sine, second * cosine - first * sine], axis=0
+        )
+        return norm_back(normed, raw, scale, gain, 0)
+
+    q_term = jnp.zeros((HD, tokens), f32)
+    k_term = jnp.zeros((HD, tokens), f32)
+    for head in range(HEADS):
+        at = slice(head * HD, (head + 1) * HD)
+        grad, term = back(
+            d_ref[head, :HD, :].astype(f32), q_ref[at, :], q_scale[head : head + 1, :], q_gain[...]
+        )
+        turned[at, :] = grad.astype(bf16)
+        q_term = q_term + term
+    for head in range(KV_HEADS):
+        at = slice(head * HD, (head + 1) * HD)
+        both = d_ref[head * per_group, HD:, :].astype(f32)
+        for other in range(1, per_group):
+            both = both + d_ref[head * per_group + other, HD:, :].astype(f32)
+        grad, term = back(both[:HD], k_ref[at, :], k_scale[head : head + 1, :], k_gain[...])
+        place = HEADS * HD + head * HD
+        turned[place : place + HD, :] = grad.astype(bf16)
+        k_term = k_term + term
+        place += KV_HEADS * HD
+        turned[place : place + HD, :] = both[HD:].astype(bf16)
+    rows = turned.shape[0] // 4
+    columns = d_attn_ref.shape[1] // 4
+    shares = (
+        (near, None, core, y), (give, None, 1 - core, y), (far, 0, core, 1 - y), (far, 1, 1 - core, 1 - y),
+    )
+    for out_ref, index, to_core, to_y in shares:
+        share = to_core * 2 + to_y
+        first = turned[pl.ds(pl.multiple_of(share * rows, rows), rows), :]
+        second = d_attn_ref[:, pl.ds(pl.multiple_of(share * columns, columns), columns)]
+        if index is None:
+            out_ref[:rows, :] = first
+            out_ref[rows:, :] = second
+        else:
+            out_ref[index, :rows, :] = first
+            out_ref[index, rows:, :] = second
+    for at in range(0, turned.shape[0], 256):
+        natural[:, at : at + 256] = turned[at : at + 256, :].T
+    d_normed = contract(natural[...], weight[...], (1, 1))
+    x = x_ref[...].astype(f32)
+    d_norm, gain_term = norm_back(d_normed, x, scale_ref[...], gain_ref[...])
+    d_x_ref[...] = d_h_ref[...] + d_norm
+    gains_ref[...] = jnp.zeros_like(gains_ref)
+    gains_ref[0:1, :] = jnp.sum(gain_term, axis=0, keepdims=True)
+    gains_ref[1:2, 0:HD] = jnp.sum(q_term.T, axis=0, keepdims=True)
+    gains_ref[2:3, 0:HD] = jnp.sum(k_term.T, axis=0, keepdims=True)
+
+
+def attention_back(here, arrays):
+    f32, bf16 = jnp.float32, jnp.bfloat16
+    shape = jax.ShapeDtypeStruct
+    weight, x = arrays[9], arrays[10]
+    tokens, width = x.shape
+    rows = weight.shape[1] // 4 + tokens
+    assert width // 4 == tokens
+    outs = [
+        shape((rows, tokens), bf16),
+        shape((rows, tokens), bf16),
+        shape((2, rows, tokens), bf16),
+        shape((tokens, width), f32),
+        shape((8, width), f32),
+    ]
+    return call_with_here(
+        attention_back_kernel, here, (1,), arrays, [whole(a) for a in arrays], outs,
+        [whole(o) for o in outs],
+        [pltpu.VMEM((weight.shape[1], tokens), bf16), pltpu.VMEM((tokens, weight.shape[1]), bf16)],
+        micros=12,
     )
 
 
 def attention_product_kernel(here, *refs):
-    normed, projected, attn, d_attn = refs[:4], refs[4:8], refs[8:12], refs[12:16]
-    sent, kept, left, right, left_out, right_out = refs[16:]
-    tokens = normed[0].shape[0]
+    normed, attn, terms, gains_ref, ffn_gain_ref = refs[:4], refs[4:8], refs[8:12], refs[12], refs[13]
+    sent, kept, left, right, left_out, right_out = refs[14:]
+    tokens = normed[0].shape[1]
+    cut = right.shape[1]
     for i in range(4):
         at = slice(i * tokens, (i + 1) * tokens)
-        left[:, at] = normed[i][...].T
-        right[at, :] = projected[i][...].T
-        left_out[:, at] = attn[i][...]
-        right_out[at, :] = d_attn[i][...]
-    rows = kept.shape[0]
-    cut = right.shape[1]
+        left[:, at] = normed[i][0].T
+        left_out[:, at] = attn[i][0].T
+        share = flat(terms[i])
+        right[at, :] = share[:cut].T
+        right_out[at, :] = share[cut:]
+    step = left.shape[0] // 4
     for owner, out_ref in ((1 - here[3], sent), (here[3], kept)):
-        at = pl.ds(pl.multiple_of(owner * rows, rows), rows)
-        out_ref[:, :cut] = jnp.dot(
-            left[at, :], right[...], preferred_element_type=jnp.float32
-        ).astype(out_ref.dtype)
-        out_ref[:, cut:] = jnp.dot(
-            left_out[at, :], right_out[...], preferred_element_type=jnp.float32
-        ).astype(out_ref.dtype)
-
-
-def attention_products(here, normed, projected, attn, d_attn):
-    tokens, rows = normed[0].shape
-    cut, rest = projected[0].shape[0], d_attn[0].shape[1]
-    outs = [
-        jax.ShapeDtypeStruct((rows // 2, cut + rest), jnp.bfloat16),
-        jax.ShapeDtypeStruct((rows // 2, cut + rest), jnp.float32),
-    ]
-    arrays = [*normed, *projected, *attn, *d_attn]
+        for half in range(2):
+            at = pl.ds(pl.multiple_of(owner * 2 * step + half * step, step), step)
+            out_ref[half, :step, :cut] = jnp.dot(
+                left[at, :], right[...], preferred_element_type=jnp.float32
+            ).astype(out_ref.dtype)
+            out_ref[half, :step, cut:] = jnp.dot(
+                left_out[at, :], right_out[...], preferred_element_type=jnp.float32
+            ).astype(out_ref.dtype)
+        rows = gains_ref.shape[1] // 2
+        mine = pl.ds(pl.multiple_of(owner * rows, rows), rows)
+        wide = out_ref.shape[2] - rows
+        block = jnp.concatenate(
+            [
+                jnp.concatenate([gains_ref[0:1, mine], gains_ref[1:2, 0:wide]], axis=1),
+                jnp.concatenate([ffn_gain_ref[:, mine], gains_ref[2:3, 0:wide]], axis=1),
+                jnp.zeros((GAIN_ROWS - 2, out_ref.shape[2]), jnp.float32),
+            ],
+            axis=0,
+        )
+        out_ref[0, step:, :] = block.astype(out_ref.dtype)
+        out_ref[1, step:, :] = jnp.zeros((GAIN_ROWS, out_ref.shape[2]), out_ref.dtype)
+
+
+def attention_products(here, early_plane, late_plane, shares, gains, ffn_gain):
+    _, tokens, width = early_plane[0].shape
+    cut = shares[0].shape[0] - tokens
+    shape = (2, width // 4 + GAIN_ROWS, cut + tokens)
+    outs = [jax.ShapeDtypeStruct(shape, jnp.bfloat16), jax.ShapeDtypeStruct(shape, jnp.float32)]
+    arrays, specs = dealt(shares)
     return call_with_here(
         attention_product_kernel,
         here,
         (1,),
-        arrays,
-        [whole(a) for a in arrays],
+        [*early_plane, *late_plane, *arrays, gains, ffn_gain],
+        [layer(a, 1) for a in early_plane]
+        + [layer(a, 0) for a in late_plane]
+        + specs
+        + [whole(gains), whole(ffn_gain)],
         outs,
         [whole(o) for o in outs],
         [
-            pltpu.VMEM((rows, 4 * tokens), jnp.bfloat16),
+            pltpu.VMEM((width, 4 * tokens), jnp.bfloat16),
             pltpu.VMEM((4 * tokens, cut), jnp.bfloat16),
-            pltpu.VMEM((rows, 4 * tokens), jnp.bfloat16),
-            pltpu.VMEM((4 * tokens, rest), jnp.bfloat16),
+            pltpu.VMEM((width, 4 * tokens), jnp.bfloat16),
+            pltpu.VMEM((4 * tokens, tokens), jnp.bfloat16),
         ],
-    )
-
-
-def place_gate_up_kernel(blocks, here, *refs):
-    out_ref = refs[-1]
-    pieces = refs[:8]
-    wide = pieces[0].shape[1]
-    far_half = (pl.program_id(0) // blocks) ^ here[0]
-    for case in range(8):
-        half, core, y = case // 4, case // 2 % 2, case % 2
-
-        @pl.when((far_half == half) & (here[1] == core) & (here[2] == y))
-        def _(half=half, core=core, y=y):
+        micros=8,
+    )
+
+
+def place_gate_up_kernel(here, *refs):
+    mine, across, beside, diagonal, out_ref = *refs[:4], refs[-1]
+    pieces = (mine, across, beside, diagonal)
+    wide = mine.shape[2]
+    for case in range(4):
+        core, y = case // 2, case % 2
+
+        @pl.when((here[1] == core) & (here[2] == y))
+        def _(core=core, y=y):
             for kind in range(2):
                 for column in range(2):
-                    value = pieces[half * 4 + (y ^ column) * 2 + (core ^ kind)][...]
+                    value = pieces[(y ^ column) * 2 + (core ^ kind)][0]
                     out_ref[:, kind, column * wide : (column + 1) * wide] = value.astype(
                         jnp.float32
                     )
 
 
 def place_gate_up(here, chunk, pieces, before):
-    rows, wide = pieces[0][0].shape
+    _, rows, wide = pieces[0].shape
     step = 64
     blocks = rows // step
 
-    def source(half):
-        return lambda i, here: (jnp.clip(i - blocks * (here[0] ^ half), 0, blocks - 1), 0)
-
-    arrays = [v for plane in pieces for v in plane]
-    specs = [pl.BlockSpec((step, wide), source(n // 4)) for n in range(8)]
+    def source(i, here):
+        return ((i // blocks) ^ here[0], i % blocks, 0)
+
+    arrays = list(pieces)
+    specs = [pl.BlockSpec((1, step, wide), source)] * 4
     aliases = {}
     if before is not None:
         arrays.append(before)
         specs.append(pl.BlockSpec(memory_space=pl.ANY))
-        aliases = {9: 0}
+        aliases = {5: 0}
     (out,) = call_with_here(
-        functools.partial(place_gate_up_kernel, blocks),
+        place_gate_up_kernel,
         here,
         (2 * blocks,),
         arrays,
@@ -746,38 +887,73 @@
     return out
 
 
-def place_pieces(here, pieces, cuts, by_rows):
-    rows = pieces[0][0].shape[0]
-    flat = [v for plane in pieces for v in plane]
+def place_down(here, pieces):
+    _, rows, columns = pieces[0].shape
 
     def kernel(here, *refs):
         for s in range(8):
 
             @pl.when(pl.program_id(0) == s)
             def _(s=s):
-                at = 0
-                for out_ref in refs[8:]:
-                    wide = out_ref.shape[1]
-                    out_ref[...] = refs[s][:, at : at + wide].astype(jnp.float32)
-                    at += wide
+                refs[4][...] = refs[s % 4][s // 4].astype(jnp.float32)
 
     def target(s, here):
         half = (s // 4) ^ here[0]
         y = ((s // 2) % 2) ^ here[2]
         core = (s % 2) ^ here[1]
-        if by_rows:
-            return ((core * 2 + y) * 2 + half, 0)
-        return (half, core * 2 + y)
-
-    across, along = (1, 8) if by_rows else (4, 2)
+        return ((core * 2 + y) * 2 + half, 0)
+
+    (out,) = call_with_here(
+        kernel,
+        here,
+        (8,),
+        list(pieces),
+        [whole(v) for v in pieces],
+        [jax.ShapeDtypeStruct((rows * 8, columns), jnp.float32)],
+        [pl.BlockSpec((rows, columns), target)],
+    )
+    return out
+
+
+def place_attention(here, pieces, cut):
+    _, rows, columns = pieces[0].shape
+    rows -= GAIN_ROWS
+
+    def kernel(here, *refs):
+        qkv_ref, out_ref, gains_ref = refs[4:]
+        for s in range(8):
+
+            @pl.when(pl.program_id(0) == s)
+            def _(s=s):
+                value = refs[s % 4][s // 4]
+                qkv_ref[...] = value[:rows, :cut].astype(jnp.float32)
+                out_ref[...] = value[:rows, cut:].astype(jnp.float32)
+                gains = value[rows:].astype(jnp.float32)
+                gains_ref[...] = gains if s == 0 else gains_ref[...] + gains
+
+    def target(s, here):
+        half = (s // 4) ^ here[0]
+        return (half, ((s % 2) ^ here[1]) * 2 + (((s // 2) % 2) ^ here[2]))
+
+    shape = jax.ShapeDtypeStruct
+    f32 = jnp.float32
+    gain_shape = (GAIN_ROWS, columns)
     return call_with_here(
         kernel,
         here,
         (8,),
-        flat,
-        [whole(v) for v in flat],
-        [jax.ShapeDtypeStruct((rows * along, wide * across), jnp.float32) for wide in cuts],
-        [pl.BlockSpec((rows, wide), target) for wide in cuts],
+        list(pieces),
+        [whole(v) for v in pieces],
+        [
+            shape((2 * rows, 4 * cut), f32),
+            shape((2 * rows, 4 * (columns - cut)), f32),
+            shape(gain_shape, f32),
+        ],
+        [
+            pl.BlockSpec((rows, cut), target),
+            pl.BlockSpec((rows, columns - cut), target),
+            pl.BlockSpec(gain_shape, lambda s, here: (0, 0)),
+        ],
     )
 
 
@@ -853,24 +1029,22 @@
     ff_chunk = gate_up_weight.shape[2] // CHUNKS
 
     def gate_up_piece(chunk):
-        return jnp.transpose(
-            lax.dynamic_slice(
-                gate_up_weight,
-                (links.quarter * part_rows, 0, chunk * ff_chunk),
-                (part_rows, 2, ff_chunk),
-            ),
-            (1, 0, 2),
+        piece = lax.dynamic_slice(
+            gate_up_weight,
+            (links.quarter * part_rows, 0, chunk * ff_chunk),
+            (part_rows, 2, ff_chunk),
         )
+        return [piece[:, 0], piece[:, 1]]
 
     qkv_there = links.over_x(quarter_rows(qkv_weight))
-    out_piece = quarter_rows(out_weight)
-    first_piece, second_piece = gate_up_piece(0), gate_up_piece(1)
+    first_piece = jnp.concatenate([*gate_up_piece(0), quarter_rows(out_weight)], axis=1)
+    second_piece = jnp.concatenate(gate_up_piece(1), axis=1)
     down_piece = lax.dynamic_slice_in_dim(
         down_weight, links.quarter * (width // 4), width // 4, 1
     )
     d_ffn = cotangent[0]
-    qkv_there = after(qkv_there, out_piece, first_piece, second_piece, down_piece)
-    out_there = links.over_x(after(out_piece, qkv_there))
+    tokens_here = tokens[0]
+    qkv_there = after(qkv_there, first_piece)
     first_there = links.over_x(after(first_piece, qkv_there))
     gate_up = jnp.transpose(after(gate_up_weight, qkv_there), (1, 0, 2))
     qkv_beside = links.over_y(qkv_there)
@@ -880,23 +1054,15 @@
         qkv_beside,
         links.over_core(after(qkv_beside, gate_up)),
     )
-    ffn_plane = links.spread_plane(after(d_ffn, qkv_beside))
-    tokens_here = tokens[0]
-    sent, w_qkv, q_raw, k_raw, q_scale, k_scale, normed, scale_one = project(
+    sent, w_qkv, q_raw, k_raw, q_scale, k_scale, early, scale_one = project(
         here, tokens_here, gain_attn[None], qkv_weight, qkv_pieces,
-        gain_query[:, None], gain_key[:, None], cosine[0], sine[0],
-    )
-    q_raw = q_raw.reshape(HEADS, HD, rows_here)
-    k_raw = k_raw.reshape(KV_HEADS, HD, rows_here)
-    q_scale, k_scale = q_scale[:, None], k_scale[:, None]
-    column_query, column_key = gain_query[:, None], gain_key[:, None]
+        gain_query[:, None], gain_key[:, None], cosine[0], sine[0], d_ffn,
+    )
     got = lax.all_to_all(sent, "ctx", 0, 0, tiled=True)
-    out_there = after(out_there, sent)
+    early_beside = links.over_y(early)
     first_there = after(first_there, sent)
     down_there = links.over_x(after(down_piece, first_there))
     first_beside = links.over_y(first_there)
-    out_beside = links.over_y(out_there)
-    normed_plane = links.spread_plane(after(normed, sent))
     second_there = links.over_x(after(second_piece, down_there))
     down_beside = links.over_y(down_there)
     got = after(got, down_there)
@@ -924,29 +1090,30 @@
     second_there = after(second_there, attn_sent)
 
     def spread(there, beside):
-        return (there, links.over_core(there), beside, links.over_core(after(beside, attn_sent)))
-
-    out_pieces = spread(out_there, out_beside)
-    w_out = place_rows(here, out_weight, out_pieces)
-    gate_up_pieces = [spread(first_there, first_beside), links.spread_plane(second_there)]
+        there, beside = after(there, attn_sent), after(beside, attn_sent)
+        return (there, links.over_core(there), beside, links.over_core(beside))
+
+    first_pieces = spread(first_there, first_beside)
     down_pieces = spread(down_there, down_beside)
-    attn_plane = links.spread_plane(attn_in)
-    h_one = inputs + contract(attn_in, w_out, (0, 0))
-    scale_two = rms_scale(h_one)
-    normed_two = (h_one * scale_two * gain_ffn).astype(bf16)
-    two_plane = links.spread_plane(normed_two)
+    second_pieces = links.spread_plane(second_there)
+    w_out, h_one, scale_two, late = attend_out(
+        here, attn_in, tokens_here, gain_ffn[None], out_weight, first_pieces
+    )
+    late_plane = links.spread_plane(late)
     sums = [h_one, jnp.zeros_like(h_one)]
-    wide_shares, hidden_plane = [], []
-    for chunk in range(CHUNKS):
-        d_wide, hidden, sums = ffn(
-            here, chunk, normed_two, d_ffn, gate_up, gate_up_pieces[chunk],
-            down_weight, down_pieces, sums,
+    shares = []
+    for chunk, pieces in enumerate((first_pieces, second_pieces)):
+        dealt_here, sums = ffn(
+            here, chunk, late, d_ffn, gate_up, pieces, down_weight, down_pieces, sums
         )
-        shares = links.deal_plane(*d_wide)
+        shares.append(links.deal_plane(*dealt_here))
         if chunk == 0:
-            sums = [after(sums[0], shares[1]), sums[1]]
-        wide_shares.append(shares)
-        hidden_plane.append(links.deal_plane(*hidden))
+            early = after(early, sums[0])
+            early_plane = (
+                early, links.over_core(early), early_beside,
+                links.over_core(after(early_beside, sums[0])),
+            )
+    columns = ff_chunk // 2
     output = sums[0].astype(bf16)
     d_norm_two, ffn_gain_term = norm_back(sums[1], h_one, scale_two, gain_ffn)
     d_h_one = d_ffn.astype(f32) + d_norm_two
@@ -956,8 +1123,8 @@
     ).astype(bf16)
     d_heads = jnp.concatenate([d_heads.reshape(HEADS, HD, rows_here)] * parts, axis=0)
     d_got = lax.all_to_all(d_heads, "ctx", 0, 0, tiled=True)
-    first_shares = [after(v, d_heads) for v in wide_shares[0]]
-    first_products = wide_products(here, two_plane, first_shares)
+    first_shares = [after(v, d_heads) for v in shares[0]]
+    first_products = wide_products(here, late_plane, first_shares, columns)
     d_got = after(d_got, first_products[0])
     (d_sent,) = kernel_call(
         attend_back_kernel,
@@ -972,71 +1139,34 @@
         ],
     )
     d_back = lax.all_to_all(d_sent, "ctx", 0, 0, tiled=True)
-    second_shares = [after(v, d_sent) for v in wide_shares[1]]
-    products = [first_products, wide_products(here, two_plane, second_shares)]
-    d_query = lax.dynamic_slice_in_dim(d_back[:, :HD], part * HEADS, HEADS).astype(f32)
-    d_key_value = jnp.sum(
-        d_back[:, HD:].reshape(parts, KV_HEADS, per_group, 2 * HD, rows_here).astype(f32),
-        axis=(0, 2),
-    )
-    dq_normed = rope_back(d_query, cosine, sine)
-    dk_normed = rope_back(d_key_value[:, :HD], cosine, sine)
-    dq_raw, query_term = norm_back(dq_normed, q_raw, q_scale, column_query, 1)
-    dk_raw, key_term = norm_back(dk_normed, k_raw, k_scale, column_key, 1)
-    d_projected = jnp.concatenate(
+    second_shares = [after(v, d_sent) for v in shares[1]]
+    second_products = wide_products(here, late_plane, second_shares, columns)
+    *d_shares, d_inputs, gain_sums = attention_back(
+        here,
         [
-            dq_raw.reshape(q_width, rows_here).astype(bf16),
-            dk_raw.reshape(kv_width, rows_here).astype(bf16),
-            d_key_value[:, HD:].reshape(kv_width, rows_here).astype(bf16),
+            d_back, q_raw, k_raw, q_scale, k_scale, gain_query[:, None], gain_key[:, None],
+            cosine[0], sine[0], w_qkv, tokens_here, scale_one, gain_attn[None], d_h_one, d_attn,
         ],
-        axis=0,
-    )
-    d_normed = contract(d_projected, w_qkv, (0, 1))
-    d_norm_one, attn_gain_term = norm_back(d_normed, inputs, scale_one, gain_attn)
-    d_inputs = d_h_one + d_norm_one
+    )
     grad_gate_up = None
-    for chunk in range(CHUNKS):
-        grad_gate_up = place_gate_up(here, chunk, links.reduce(*products[chunk]), grad_gate_up)
-    (grad_down,) = place_pieces(
-        here, links.reduce(*down_products(here, ffn_plane, *hidden_plane)), (width,), True
-    )
-
-    def deal(value, size, axis):
-        def share(core, y):
-            return lax.dynamic_slice_in_dim(value, (core * 2 + y) * size, size, axis)
-
-        return links.deal_plane(
-            share(links.core, links.y),
-            share(links.core, 1 - links.y),
-            share(1 - links.core, links.y),
-            share(1 - links.core, 1 - links.y),
-        )
-
+    for chunk, products in enumerate((first_products, second_products)):
+        grad_gate_up = place_gate_up(here, chunk, links.reduce(*products), grad_gate_up)
+    grad_down = place_down(
+        here, links.reduce(*down_products(here, early_plane, *shares, columns // 2))
+    )
     attention_terms = attention_products(
-        here,
-        normed_plane,
-        deal(d_projected, d_projected.shape[0] // 4, 0),
-        attn_plane,
-        deal(d_attn, width // 4, 1),
-    )
-    grad_qkv, grad_out = place_pieces(
-        here, links.reduce(*attention_terms), (d_projected.shape[0] // 4, width // 4), False
-    )
-    gain_terms = jnp.concatenate(
-        [
-            jnp.sum(attn_gain_term, axis=0),
-            jnp.sum(ffn_gain_term, axis=0),
-            jnp.sum(query_term, axis=(0, 2)),
-            jnp.sum(key_term, axis=(0, 2)),
-        ]
-    )
-    gain_sums = links.total(gain_terms.reshape(-1, 128)).reshape(-1)
-    gain_grads = []
-    at = 0
-    for gain in (attn_gain, ffn_gain, query_gain, key_gain):
-        size = gain.shape[0]
-        gain_grads.append(lax.dynamic_slice_in_dim(gain_sums, at + links.side * size, size))
-        at += 2 * size
+        here, early_plane, late_plane, links.deal_plane(*d_shares), gain_sums,
+        jnp.sum(ffn_gain_term, axis=0, keepdims=True),
+    )
+    cut = qkv_weight.shape[1] // 4
+    grad_qkv, grad_out, gain_sums = place_attention(here, links.reduce(*attention_terms), cut)
+    at = links.side * (HD // 2)
+    gain_grads = [
+        gain_sums[0, :rows],
+        gain_sums[1, :rows],
+        lax.dynamic_slice_in_dim(gain_sums[0, rows : rows + HD], at, HD // 2),
+        lax.dynamic_slice_in_dim(gain_sums[1, rows : rows + HD], at, HD // 2),
+    ]
     return (
         output[None],
         d_inputs[None],

time: 656 us -> 604 us (0.921)
  waiting for transfers between devices: 296 us -> 270 us
  starting transfers between devices: 104 us -> 81.6 us
  Pallas kernels: 165 us -> 176 us
  other arithmetic: 30.1 us -> 22.9 us
    ppermute x30 -> x13, waiting for transfers between devices: 170 us -> 126 us  [over_y(): return lax.ppermute(value, 'ctx', self.route(lambda z, y, c: (z, 1 - y, c)))]
    ppermute x30 -> x13, starting transfers between devices: 34.4 us -> 21.7 us  [over_y(): return lax.ppermute(value, 'ctx', self.route(lambda z, y, c: (z, 1 - y, c)))]
    all_to_all x1, waiting for transfers between devices: 0.01 us -> 11.8 us  [on_block(): lax.all_to_all(attn_sent, 'ctx', 0, 0, tiled=True)]
    pallas_call x12 -> x13, Pallas kernels: 119 us -> 130 us  [call_with_here(): pl.pallas_call(kernel, grid_spec=pltpu.PrefetchScalarGridSpec(num_scalar_...]
    ppermute x5 -> x4, waiting for transfers between devices: 6.87 us -> 16.2 us  [mirror_z(): lax.ppermute(value, 'ctx', self.route(lambda z, y, c: (self.depth - 1 - z...]
    slice x1 -> x3, local copies, waits for them, and re-layouts: 0.03 us -> 8.4 us  [the longest x1 6.28 us: gate_up_piece(): return [piece[:, 0], piece[:, 1]]]
    ppermute x9 -> x8, waiting for transfers between devices: 42.4 us -> 36 us  [over_z(): return lax.ppermute(value, 'ctx', self.route(lambda z, y, c: (z ^ 1, y, c)))]
    unnamed x178 -> x82, local copies, waits for them, and re-layouts: 17.4 us -> 13.5 us
  transfers between devices with their start and end apart: 106 -> 64, of which waited for: 35 -> 26; matrix products, arithmetic and copies ran while one was open for 9% -> 8% of each run, Pallas kernels for 25% -> 29%
where the time goes in v5:
time: 604 us; the launch traced here: 594 us
  waiting for transfers between devices  270 us (45%)
  Pallas kernels  176 us (29%)
  starting transfers between devices  81.6 us (14%)
  local copies, waits for them, and re-layouts  40.5 us (7%)
  other arithmetic  22.9 us (4%)
    pallas_call x13, Pallas kernels, call_with_here(): pl.pallas_call(kernel, grid_spec=pltpu.PrefetchScalarGridSpec(num_scalar_...  130 us
    ppermute x13, waiting for transfers between devices, over_y(): return lax.ppermute(value, 'ctx', self.route(lambda z, y, c: (z, 1 - y, c)))  126 us
    ppermute x9, waiting for transfers between devices, over_x(): return lax.ppermute(value, 'fsdp', [(0, 1), (1, 0)])  73.7 us
    pallas_call x2, Pallas kernels, kernel_call(): pl.pallas_call(kernel, out_shape=outs, in_specs=[smem] * len(tables) + [v...  46.9 us
    ppermute x8, waiting for transfers between devices, over_z(): return lax.ppermute(value, 'ctx', self.route(lambda z, y, c: (z ^ 1, y, c)))  36 us
    ppermute x13, starting transfers between devices, over_y(): return lax.ppermute(value, 'ctx', self.route(lambda z, y, c: (z, 1 - y, c)))  21.7 us
    ppermute x8, starting transfers between devices, over_z(): return lax.ppermute(value, 'ctx', self.route(lambda z, y, c: (z ^ 1, y, c)))  18.4 us
    ppermute x4, waiting for transfers between devices, mirror_z(): lax.ppermute(value, 'ctx', self.route(lambda z, y, c: (self.depth - 1 - z...  16.2 us
  transfers between devices with their start and end apart: 64, of which 26 were waited for; matrix products, arithmetic and copies ran while one was open for 8% of the time, Pallas kernels for 29%

profile of v5, /device:TPU:0, one launch (start us, length us, event | category | flops | bytes accessed | tf_op | source)
XLA Modules:
  0.0 594.3 jit_solution(5465105345500173181)
XLA Ops:
  23.8 8.9 %copy.71 = bf16[512,2,4608]{2,0,1:T(8,128)(2,1)} copy(bf16[512,2,4608]{2,1,0:T(2,128)(2,1)} %param.15) | data formatting | bytes 18874368 | tf_op jit(solution)/shard_map/optimization_barrier | solution.py:294
  57.5 22.6 %collective-permute-done.6.refs_12_ = bf16[2304,256]{1,0:T(8,128)(2,1)} collective-permute-done((bf16[2304,256]{1,0:T(8,128)(2,1)S(1)}, bf16[2304,256]{1,0:T(8,128)(2,1)}, u32[]{:S(2)}, u32[]{:S(2)}) %collective-permute-start.6) | collective-permute-done | bytes 1179680 | tf_op jit(solution)/shard_map/ppermute | solution.py:261
  83.5 22.0 %shard_map.196 = (bf16[16,64,256]{2,1,0:T(8,128)(2,1)}, bf16[4096,64]{1,0:T(8,128)(2,1)S(1)}, bf16[64,4096]{1,0:T(8,128)(2,1)S(1)}, bf16[4096,64]{1,0:T(8,128)(2...) custom-call(s32[32]{0:T(128)S(1)} %broadcast_add_fusion.q_slot, ...), custom_call_target="tpu_custom_call" | custom-call | flops 1 | bytes 72000000 | tf_op jit(solution)/shard_map/pallas_call | solution.py:215
  108.7 16.8 %collective-permute-done.15.refs_14_ = bf16[2304,256]{1,0:T(8,128)(2,1)} collective-permute-done((bf16[2304,256]{1,0:T(8,128)(2,1)}, bf16[2304,256]{1,0:T(8,128)(2,1)}, u32[]{:S(2)}, u32[]{:S(2)}) %collective-permute-start.15) | collective-permute-done | bytes 1179680 | tf_op jit(solution)/shard_map/ppermute | solution.py:252
  133.7 11.8 %all-to-all-done.1 = bf16[16,64,256]{2,1,0:T(8,128)(2,1)S(1)} async-done(((bf16[16,64,256]{2,1,0:T(8,128)(2,1)}), bf16[16,64,256]{2,1,0:T(8,128)(2,1)S(1)}, u32[]{:S(2)}, u32[]{:S(2)}) %all-to-all-start.1) | async-done | bytes 524320 | tf_op jit(solution)/shard_map/all_to_all | solution.py:1088
  152.2 20.3 %shard_map.198 = (bf16[256,1792]{1,0:T(8,128)(2,1)}, bf16[256,1792]{1,0:T(8,128)(2,1)}, bf16[2,256,1792]{2,1,0:T(8,128)(2,1)}, f32[256,1024]{1,0:T(8,128)}, f32[256,1024]{1,0:T(8,128)}) custom-call(s32[4]{0:T(128)} %pad_add_fusion.here, bf16[2,256,1024]{2,1,0:T(8,128)(2,1)} %get-tuple-element.91.refs_0_.refs_4_, bf16[256,1024]{1,0:T(8,128)(2,1)} %bitcast.90, ...), custom_call_target="tpu_custom_call" | custom-call | flops 1 | bytes 60000000 | tf_op jit(solution)/shard_map/pallas_call | solution.py:313
  177.9 21.0 %shard_map.199 = (bf16[256,1792]{1,0:T(8,128)(2,1)}, bf16[256,1792]{1,0:T(8,128)(2,1)}, bf16[2,256,1792]{2,1,0:T(8,128)(2,1)}, f32[256,1024]{1,0:T(8,128)}, f32[256,1024]{1,0:T(8,128)}) custom-call(s32[4]{0:T(128)} %pad_add_fusion.here, bf16[2,256,1024]{2,1,0:T(8,128)(2,1)} %get-tuple-element.91.refs_0_.refs_4_, bf16[256,1024]{1,0:T(8,128)(2,1)} %bitcast.91, ...), custom_call_target="tpu_custom_call" | custom-call | flops 1 | bytes 60000000 | tf_op jit(solution)/shard_map/pallas_call | solution.py:313
  201.2 14.6 %collective-permute-done.21.refs_6_ = bf16[2,256,1792]{2,1,0:T(8,128)(2,1)} collective-permute-done((bf16[2,256,1792]{2,1,0:T(8,128)(2,1)}, bf16[2,256,1792]{2,1,0:T(8,128)(2,1)}, u32[]{:S(2)}, u32[]{:S(2)}) %collective-permute-start.21) | collective-permute-done | bytes 1835040 | tf_op jit(solution)/shard_map/ppermute | solution.py:252
  217.3 20.0 %collective-permute-done.18.refs_2_.refs_6_ = bf16[2,256,1024]{2,1,0:T(8,128)(2,1)} collective-permute-done((bf16[2,256,1024]{2,1,0:T(8,128)(2,1)}, bf16[2,256,1024]{2,1,0:T(8,128)(2,1)}, u32[]{:S(2)}, u32[]{:S(2)}) %collective-permute-start.18) | collective-permute-done | bytes 1048608 | tf_op jit(solution)/shard_map/ppermute | solution.py:252
  247.1 8.2 %shard_map.200 = (bf16[2,256,1152]{2,1,0:T(8,128)(2,1)}, f32[2,256,1152]{2,1,0:T(8,128)}) custom-call(s32[4]{0:T(128)} %pad_add_fusion.here, bf16[2,256,1024]{2,1,0:T(8,128)(2,1)} %get-tuple-element.91.refs_0_.refs_4_, bf16[2,256,1024]{2,1,0:T(8,128)(2,1)} %collective-permute-done.17.refs_1_.refs_5_, ...), custom_call_target="tpu_custom_call" | custom-call | flops 1 | bytes 24000000 | tf_op jit(solution)/shard_map/pallas_call | solution.py:313
  261.4 24.9 %shard_map.201 = bf16[16,192,256]{2,1,0:T(8,128)(2,1)} custom-call(s32[32]{0:T(128)S(1)} %broadcast_add_fusion.q_slot, s32[32]{0:T(128)S(1)} %get-tuple-element.153.kv_slot, s32[16]{0:T(128)S(1)} %get-tuple-element.176.first, s32[16]{0:T(128)S(1)} %get-tuple-element.177.last, bf16[16,64,256]{2,1,0:T(8,128)(2,1)S(1)} %all-to-all-done.2.d_ref, ...), custom_call_target="tpu_custom_call" | custom-call | flops 1 | bytes 72000000 | tf_op jit(solution)/shard_map/pallas_call | solution.py:215
  293.5 39.5 %collective-permute-done.24.refs_2_ = bf16[2,256,1024]{2,1,0:T(8,128)(2,1)} collective-permute-done((bf16[2,256,1024]{2,1,0:T(8,128)(2,1)}, bf16[2,256,1024]{2,1,0:T(8,128)(2,1)}, u32[]{:S(2)}, u32[]{:S(2)}) %collective-permute-start.24) | collective-permute-done | bytes 1048608 | tf_op jit(solution)/shard_map/ppermute | solution.py:252
  334.6 8.5 %shard_map.202 = (bf16[768,256]{1,0:T(8,128)(2,1)}, bf16[768,256]{1,0:T(8,128)(2,1)}, bf16[2,768,256]{2,1,0:T(8,128)(2,1)}, f32[256,1024]{1,0:T(8,128)}, f32[8,1024]{1,0:T(8,128)}) custom-call(s32[4]{0:T(128)} %pad_add_fusion.here, bf16[16,192,256]{2,1,0:T(8,128)(2,1)} %copy-done.10, f32[1024,256]{1,0:T(8,128)} %get-tuple-element.119.refs_1_, ...), custom_call_target="tpu_custom_call" | custom-call | flops 1 | bytes 36000000 | tf_op jit(solution)/shard_map/pallas_call | solution.py:313
  347.8 9.5 %shard_map.208 = (bf16[2,288,1024]{2,1,0:T(8,128)(2,1)}, f32[2,288,1024]{2,1,0:T(8,128)}) custom-call(s32[4]{0:T(128)} %pad_add_fusion.here, bf16[2,256,1024]{2,1,0:T(8,128)(2,1)} %get-tuple-element.127.refs_0_, bf16[2,256,1024]{2,1,0:T(8,128)(2,1)} %collective-permute-done.23.refs_1_, bf16[2,256,1024]{2,1,0:T(8,128)(2,1)} %collective-permute-done.24.refs_2_, ...), custom_call_target="tpu_custom_call" | custom-call | flops 1 | bytes 24000000 | tf_op jit(solution)/shard_map/pallas_call | solution.py:313
  371.7 14.9 %collective-permute-done.53 = bf16[2,288,1024]{2,1,0:T(8,128)(2,1)} collective-permute-done((bf16[2,288,1024]{2,1,0:T(8,128)(2,1)}, bf16[2,288,1024]{2,1,0:T(8,128)(2,1)}, u32[]{:S(2)}, u32[]{:S(2)}) %collective-permute-start.53) | collective-permute-done | bytes 1179680 | tf_op jit(solution)/shard_map/ppermute | solution.py:261
  388.3 21.9 %collective-permute-done.39 = bf16[2,256,1152]{2,1,0:T(8,128)(2,1)} collective-permute-done((bf16[2,256,1152]{2,1,0:T(8,128)(2,1)}, bf16[2,256,1152]{2,1,0:T(8,128)(2,1)}, u32[]{:S(2)}, u32[]{:S(2)}) %collective-permute-start.39) | collective-permute-done | bytes 1179680 | tf_op jit(solution)/shard_map/ppermute | solution.py:261
  441.9 13.1 %collective-permute-done.55 = bf16[288,1024]{1,0:T(8,128)(2,1)S(1)} collective-permute-done((bf16[288,1024]{1,0:T(8,128)(2,1)S(1)}, bf16[288,1024]{1,0:T(8,128)(2,1)S(1)}, u32[]{:S(2)}, u32[]{:S(2)}) %collective-permute-start.55) | collective-permute-done | bytes 589856 | tf_op jit(solution)/shard_map/ppermute | solution.py:258
  455.2 10.6 %collective-permute-start.56 = (bf16[288,1024]{1,0:T(8,128)(2,1)S(1)}, bf16[288,1024]{1,0:T(8,128)(2,1)S(1)}, u32[]{:S(2)}, u32[]{:S(2)}) collective-permute-start(bf16[288,1024]{1,0:T(8,128)(2,1)S(1)} %add_convert_fusion), channel_id=1, source_target_pairs={{0,8},{2,10},{4,12},{6,14},{8,0},{10,2},{12,4},{14,6},{16,24},{18,... | collective-permute-start | bytes 1769480 | tf_op jit(solution)/shard_map/ppermute | solution.py:255
  478.0 11.0 %collective-permute-done.56 = bf16[288,1024]{1,0:T(8,128)(2,1)S(1)} collective-permute-done((bf16[288,1024]{1,0:T(8,128)(2,1)S(1)}, bf16[288,1024]{1,0:T(8,128)(2,1)S(1)}, u32[]{:S(2)}, u32[]{:S(2)}) %collective-permute-start.56) | collective-permute-done | bytes 589856 | tf_op jit(solution)/shard_map/ppermute | solution.py:255
  498.2 9.9 %collective-permute-done.42 = bf16[256,1152]{1,0:T(8,128)(2,1)S(1)} collective-permute-done((bf16[256,1152]{1,0:T(8,128)(2,1)S(1)}, bf16[256,1152]{1,0:T(8,128)(2,1)S(1)}, u32[]{:S(2)}, u32[]{:S(2)}) %collective-permute-start.42) | collective-permute-done | bytes 589856 | tf_op jit(solution)/shard_map/ppermute | solution.py:255
  518.0 21.9 %collective-permute-done.44.refs_2_ = bf16[2,256,1152]{2,1,0:T(8,128)(2,1)} collective-permute-done((bf16[2,256,1152]{2,1,0:T(8,128)(2,1)S(1)}, bf16[2,256,1152]{2,1,0:T(8,128)(2,1)}, u32[]{:S(2)}, u32[]{:S(2)}) %collective-permute-start.44) | collective-permute-done | bytes 1179680 | tf_op jit(solution)/shard_map/ppermute | solution.py:252
  541.6 12.7 %collective-permute-done.34.refs_2_ = bf16[2,272,768]{2,1,0:T(8,128)(2,1)} collective-permute-done((bf16[2,272,768]{2,1,0:T(8,128)(2,1)}, bf16[2,272,768]{2,1,0:T(8,128)(2,1)}, u32[]{:S(2)}, u32[]{:S(2)}) %collective-permute-start.34) | collective-permute-done | bytes 835616 | tf_op jit(solution)/shard_map/ppermute | solution.py:252
  556.4 9.9 %shard_map.206.refs_4_ = f32[512,2,4608]{2,1,0:T(2,128)} custom-call(s32[4]{0:T(128)} %pad_add_fusion.here, bf16[2,256,1152]{2,1,0:T(8,128)(2,1)} %copy-done.12, bf16[2,256,1152]{2,1,0:T(8,128)(2,1)} %copy-done.25, bf16[2,256,1152]{2,1,0:T(8,128)(2,1)} %copy-done.24, bf16[2,256,1152]{2,1,0:T(8,128)(2,1)} %copy-done.26), custom_call_target="tpu_custom_call" | custom-call | flops 1 | bytes 30000000 | tf_op jit(solution)/shard_map/pallas_call | solution.py:313
  574.3 9.7 %shard_map.207 = f32[512,2,4608]{2,1,0:T(2,128)} custom-call(s32[4]{0:T(128)} %pad_add_fusion.here, bf16[2,256,1152]{2,1,0:T(8,128)(2,1)} %copy-done.13, bf16[2,256,1152]{2,1,0:T(8,128)(2,1)} %collective-permute-done.43.refs_1_, bf16[2,256,1152]{2,1,0:T(8,128)(2,1)} %collective-permute-done.44.refs_2_, ...), custom_call_target="tpu_custom_call", output_to_operand_aliasing={{}: (5, {})} | custom-call | flops 1 | bytes 30000000 | tf_op jit(solution)/shard_map/pallas_call | solution.py:313
  (275 shorter events, 208.7 us)
Async XLA Ops:
  43.2 39.1 %all-to-all-start = ((bf16[16,192,256]{2,1,0:T(8,128)(2,1)}), bf16[16,192,256]{2,1,0:T(8,128)(2,1)S(1)}, u32[]{:S(2)}, u32[]{:S(2)}) async-start(bf16[16,192,256]{2,1,0:T(8,128)(2,1)} %get-tuple-element.83), calls=%async_computation | async-start | bytes 3145728 | tf_op jit(solution)/shard_map/all_to_all | solution.py:1061
  55.4 52.8 %collective-permute-start.8 = (bf16[128,5632]{1,0:T(8,128)(2,1)}, bf16[128,5632]{1,0:T(8,128)(2,1)}, u32[]{:S(2)}, u32[]{:S(2)}) collective-permute-start(bf16[128,5632]{1,0:T(8,128)(2,1)} %collective-permute-done.5.refs_4_.refs_5_.refs_3_.refs_7_), channel_id=1, source_target_pairs={{0,4},{2,6},{4,0},{6,2},{8,12},{10,14},{12,8},{14,10},{16,20},{18,... | collective-permute-start | bytes 4325384 | tf_op jit(solution)/shard_map/ppermute | solution.py:252
  80.1 45.5 %collective-permute-start.15 = (bf16[2304,256]{1,0:T(8,128)(2,1)}, bf16[2304,256]{1,0:T(8,128)(2,1)}, u32[]{:S(2)}, u32[]{:S(2)}) collective-permute-start(bf16[2304,256]{1,0:T(8,128)(2,1)} %collective-permute-done.6.refs_12_), channel_id=1, source_target_pairs={{0,4},{2,6},{4,0},{6,2},{8,12},{10,14},{12,8},{14,10},{16,20},{18,... | collective-permute-start | bytes 3538952 | tf_op jit(solution)/shard_map/ppermute | solution.py:252
  81.2 49.8 %collective-permute-start.10 = (bf16[128,4608]{1,0:T(8,128)(2,1)}, bf16[128,4608]{1,0:T(8,128)(2,1)}, u32[]{:S(2)}, u32[]{:S(2)}) collective-permute-start(bf16[128,4608]{1,0:T(8,128)(2,1)} %pad_maximum_fusion.1), channel_id=1, source_target_pairs={{0,1},{1,0},{2,3},{3,2},{4,5},{5,4},{6,7},{7,6},{8,9},{9,8},{10,11... | collective-permute-start | bytes 3538952 | tf_op jit(solution)/shard_map/ppermute | solution.py:261
  131.0 42.4 %collective-permute-start.12 = (bf16[128,4608]{1,0:T(8,128)(2,1)}, bf16[128,4608]{1,0:T(8,128)(2,1)}, u32[]{:S(2)}, u32[]{:S(2)}) collective-permute-start(bf16[128,4608]{1,0:T(8,128)(2,1)} %collective-permute-done.10.refs_3_.refs_7_), channel_id=1, source_target_pairs={{0,4},{2,6},{4,0},{6,2},{8,12},{10,14},{12,8},{14,10},{16,20},{18,... | collective-permute-start | bytes 3538952 | tf_op jit(solution)/shard_map/ppermute | solution.py:252
  172.5 43.3 %collective-permute-start.21 = (bf16[2,256,1792]{2,1,0:T(8,128)(2,1)}, bf16[2,256,1792]{2,1,0:T(8,128)(2,1)}, u32[]{:S(2)}, u32[]{:S(2)}) collective-permute-start(bf16[2,256,1792]{2,1,0:T(8,128)(2,1)} %get-tuple-element.107), channel_id=1, source_target_pairs={{0,4},{2,6},{4,0},{6,2},{8,12},{10,14},{12,8},{14,10},{16,20},{18,... | collective-permute-start | bytes 5505032 | tf_op jit(solution)/shard_map/ppermute | solution.py:252
  173.4 63.8 %collective-permute-start.18 = (bf16[2,256,1024]{2,1,0:T(8,128)(2,1)}, bf16[2,256,1024]{2,1,0:T(8,128)(2,1)}, u32[]{:S(2)}, u32[]{:S(2)}) collective-permute-start(bf16[2,256,1024]{2,1,0:T(8,128)(2,1)} %get-tuple-element.91.refs_0_.refs_4_), channel_id=1, source_target_pairs={{0,4},{2,6},{4,0},{6,2},{8,12},{10,14},{12,8},{14,10},{16,20},{18,... | collective-permute-start | bytes 3145736 | tf_op jit(solution)/shard_map/ppermute | solution.py:252
  175.1 71.0 %collective-permute-start.17 = (bf16[2,256,1024]{2,1,0:T(8,128)(2,1)}, bf16[2,256,1024]{2,1,0:T(8,128)(2,1)}, u32[]{:S(2)}, u32[]{:S(2)}) collective-permute-start(bf16[2,256,1024]{2,1,0:T(8,128)(2,1)} %get-tuple-element.91.refs_0_.refs_4_), channel_id=1, source_target_pairs={{0,2},{2,0},{4,6},{6,4},{8,10},{10,8},{12,14},{14,12},{16,18},{18,... | collective-permute-start | bytes 3145736 | tf_op jit(solution)/shard_map/ppermute | solution.py:249
  243.8 48.5 %collective-permute-start.37 = (bf16[2,256,1792]{2,1,0:T(8,128)(2,1)}, bf16[2,256,1792]{2,1,0:T(8,128)(2,1)}, u32[]{:S(2)}, u32[]{:S(2)}) collective-permute-start(bf16[2,256,1792]{2,1,0:T(8,128)(2,1)} %get-tuple-element.141), channel_id=1, source_target_pairs={{0,4},{2,6},{4,0},{6,2},{8,12},{10,14},{12,8},{14,10},{16,20},{18,... | collective-permute-start | bytes 5505032 | tf_op jit(solution)/shard_map/ppermute | solution.py:252
  286.3 47.2 %all-to-all-start.3 = ((bf16[16,192,256]{2,1,0:T(8,128)(2,1)}), bf16[16,192,256]{2,1,0:T(8,128)(2,1)S(1)}, u32[]{:S(2)}, u32[]{:S(2)}) async-start(bf16[16,192,256]{2,1,0:T(8,128)(2,1)} %shard_map.201), calls=%async_computation.3 | async-start | bytes 3145728 | tf_op jit(solution)/shard_map/all_to_all | solution.py:1141
  290.4 42.6 %collective-permute-start.24 = (bf16[2,256,1024]{2,1,0:T(8,128)(2,1)}, bf16[2,256,1024]{2,1,0:T(8,128)(2,1)}, u32[]{:S(2)}, u32[]{:S(2)}) collective-permute-start(bf16[2,256,1024]{2,1,0:T(8,128)(2,1)} %get-tuple-element.127.refs_0_), channel_id=1, source_target_pairs={{0,4},{2,6},{4,0},{6,2},{8,12},{10,14},{12,8},{14,10},{16,20},{18,... | collective-permute-start | bytes 3145736 | tf_op jit(solution)/shard_map/ppermute | solution.py:252
  292.3 54.2 %collective-permute-start.38 = (bf16[2,256,1792]{2,1,0:T(8,128)(2,1)}, bf16[2,256,1792]{2,1,0:T(8,128)(2,1)S(1)}, u32[]{:S(2)}, u32[]{:S(2)}) collective-permute-start(bf16[2,256,1792]{2,1,0:T(8,128)(2,1)} %collective-permute-done.37.refs_6_.refs_10_), channel_id=1, source_target_pairs={{0,2},{2,0},{4,6},{6,4},{8,10},{10,8},{12,14},{14,12},{16,18},{18,... | collective-permute-start | bytes 5505032 | tf_op jit(solution)/shard_map/ppermute | solution.py:249
  292.3 50.8 %collective-permute-start.46 = (bf16[2,256,1152]{2,1,0:T(8,128)(2,1)}, bf16[2,256,1152]{2,1,0:T(8,128)(2,1)}, u32[]{:S(2)}, u32[]{:S(2)}) collective-permute-start(bf16[2,256,1152]{2,1,0:T(8,128)(2,1)} %get-tuple-element.110), channel_id=1, source_target_pairs={{0,1},{1,0},{2,3},{3,2},{4,5},{5,4},{6,7},{7,6},{8,9},{9,8},{10,11... | collective-permute-start | bytes 3538952 | tf_op jit(solution)/shard_map/ppermute | solution.py:261
  293.3 51.5 %collective-permute-start.23 = (bf16[2,256,1024]{2,1,0:T(8,128)(2,1)}, bf16[2,256,1024]{2,1,0:T(8,128)(2,1)}, u32[]{:S(2)}, u32[]{:S(2)}) collective-permute-start(bf16[2,256,1024]{2,1,0:T(8,128)(2,1)} %get-tuple-element.127.refs_0_), channel_id=1, source_target_pairs={{0,2},{2,0},{4,6},{6,4},{8,10},{10,8},{12,14},{14,12},{16,18},{18,... | collective-permute-start | bytes 3145736 | tf_op jit(solution)/shard_map/ppermute | solution.py:249
  366.4 43.8 %collective-permute-start.39 = (bf16[2,256,1152]{2,1,0:T(8,128)(2,1)}, bf16[2,256,1152]{2,1,0:T(8,128)(2,1)}, u32[]{:S(2)}, u32[]{:S(2)}) collective-permute-start(bf16[2,256,1152]{2,1,0:T(8,128)(2,1)} %get-tuple-element.145), channel_id=1, source_target_pairs={{0,1},{1,0},{2,3},{3,2},{4,5},{5,4},{6,7},{7,6},{8,9},{9,8},{10,11... | collective-permute-start | bytes 3538952 | tf_op jit(solution)/shard_map/ppermute | solution.py:261
  367.6 44.2 %collective-permute-start.28 = (bf16[2,768,256]{2,1,0:T(8,128)(2,1)}, bf16[2,768,256]{2,1,0:T(8,128)(2,1)}, u32[]{:S(2)}, u32[]{:S(2)}) collective-permute-start(bf16[2,768,256]{2,1,0:T(8,128)(2,1)} %collective-permute-done.27.refs_10_), channel_id=1, source_target_pairs={{0,2},{2,0},{4,6},{6,4},{8,10},{10,8},{12,14},{14,12},{16,18},{18,... | collective-permute-start | bytes 2359304 | tf_op jit(solution)/shard_map/ppermute | solution.py:249
  369.2 51.2 %collective-permute-start.48 = (bf16[256,1152]{1,0:T(8,128)(2,1)S(1)}, bf16[256,1152]{1,0:T(8,128)(2,1)S(1)}, u32[]{:S(2)}, u32[]{:S(2)}) collective-permute-start(bf16[256,1152]{1,0:T(8,128)(2,1)S(1)} %fusion.1), channel_id=1, source_target_pairs={{0,24},{2,26},{4,28},{6,30},{8,16},{10,18},{12,20},{14,22},{16,8},... | collective-permute-start | bytes 1769480 | tf_op jit(solution)/shard_map/ppermute | solution.py:258
  371.6 40.2 %collective-permute-start.26 = (bf16[768,256]{1,0:T(8,128)(2,1)S(1)}, bf16[768,256]{1,0:T(8,128)(2,1)}, u32[]{:S(2)}, u32[]{:S(2)}) collective-permute-start(bf16[768,256]{1,0:T(8,128)(2,1)S(1)} %copy-done.40), channel_id=1, source_target_pairs={{0,2},{2,0},{4,6},{6,4},{8,10},{10,8},{12,14},{14,12},{16,18},{18,... | collective-permute-start | bytes 1179656 | tf_op jit(solution)/shard_map/ppermute | solution.py:249
  429.0 47.3 %collective-permute-start.41 = (bf16[256,1152]{1,0:T(8,128)(2,1)S(1)}, bf16[256,1152]{1,0:T(8,128)(2,1)S(1)}, u32[]{:S(2)}, u32[]{:S(2)}) collective-permute-start(bf16[256,1152]{1,0:T(8,128)(2,1)S(1)} %fusion.2), channel_id=1, source_target_pairs={{0,24},{2,26},{4,28},{6,30},{8,16},{10,18},{12,20},{14,22},{16,8},... | collective-permute-start | bytes 1769480 | tf_op jit(solution)/shard_map/ppermute | solution.py:258
  440.3 69.6 %collective-permute-start.51 = (bf16[2,256,1152]{2,1,0:T(8,128)(2,1)S(1)}, bf16[2,256,1152]{2,1,0:T(8,128)(2,1)S(1)}, u32[]{:S(2)}, u32[]{:S(2)}) collective-permute-start(bf16[2,256,1152]{2,1,0:T(8,128)(2,1)S(1)} %pad_maximum_fusion.3.refs_0_), channel_id=1, source_target_pairs={{0,4},{2,6},{4,0},{6,2},{8,12},{10,14},{12,8},{14,10},{16,20},{18,... | collective-permute-start | bytes 3538952 | tf_op jit(solution)/shard_map/ppermute | solution.py:252
  478.0 38.2 %collective-permute-start.50 = (bf16[2,256,1152]{2,1,0:T(8,128)(2,1)S(1)}, bf16[2,256,1152]{2,1,0:T(8,128)(2,1)S(1)}, u32[]{:S(2)}, u32[]{:S(2)}) collective-permute-start(bf16[2,256,1152]{2,1,0:T(8,128)(2,1)S(1)} %pad_maximum_fusion.3.refs_0_), channel_id=1, source_target_pairs={{0,2},{2,0},{4,6},{6,4},{8,10},{10,8},{12,14},{14,12},{16,18},{18,... | collective-permute-start | bytes 3538952 | tf_op jit(solution)/shard_map/ppermute | solution.py:249
  516.2 38.1 %collective-permute-start.34 = (bf16[2,272,768]{2,1,0:T(8,128)(2,1)}, bf16[2,272,768]{2,1,0:T(8,128)(2,1)}, u32[]{:S(2)}, u32[]{:S(2)}) collective-permute-start(bf16[2,272,768]{2,1,0:T(8,128)(2,1)} %pad_maximum_fusion.5.refs_0_), channel_id=1, source_target_pairs={{0,4},{2,6},{4,0},{6,2},{8,12},{10,14},{12,8},{14,10},{16,20},{18,... | collective-permute-start | bytes 2506760 | tf_op jit(solution)/shard_map/ppermute | solution.py:252
  517.8 48.6 %collective-permute-start.59 = (bf16[2,288,1024]{2,1,0:T(8,128)(2,1)}, bf16[2,288,1024]{2,1,0:T(8,128)(2,1)}, u32[]{:S(2)}, u32[]{:S(2)}) collective-permute-start(bf16[2,288,1024]{2,1,0:T(8,128)(2,1)} %collective-permute-done.58.refs_2_), channel_id=1, source_target_pairs={{0,2},{2,0},{4,6},{6,4},{8,10},{10,8},{12,14},{14,12},{16,18},{18,... | collective-permute-start | bytes 3538952 | tf_op jit(solution)/shard_map/ppermute | solution.py:249
  541.4 42.6 %collective-permute-start.33 = (bf16[2,272,768]{2,1,0:T(8,128)(2,1)}, bf16[2,272,768]{2,1,0:T(8,128)(2,1)}, u32[]{:S(2)}, u32[]{:S(2)}) collective-permute-start(bf16[2,272,768]{2,1,0:T(8,128)(2,1)} %pad_maximum_fusion.5.refs_0_), channel_id=1, source_target_pairs={{0,2},{2,0},{4,6},{6,4},{8,10},{10,8},{12,14},{14,12},{16,18},{18,... | collective-permute-start | bytes 2506760 | tf_op jit(solution)/shard_map/ppermute | solution.py:249
  (81 other events, 1432.1 us)

commit v6 on v5

--- a/solution.py
+++ b/solution.py
@@ -13,6 +13,11 @@
 BLK = 128
 TILE = 256
 CHUNKS = 2
+PROJECT = 0
+ATTEND = 0
+OUT = 0
+FFN = (0, 0)
+ATTEND_BACK = 25
 
 
 EPSILON = 1e-05
@@ -209,7 +214,13 @@
         )
 
 
-def kernel_call(kernel, tables, arrays, outs, scratch):
+def cost(micros):
+    return pl.CostEstimate(
+        flops=1 + micros * 1_000_000_000, bytes_accessed=1, transcendentals=0
+    )
+
+
+def kernel_call(kernel, tables, arrays, outs, scratch, micros):
     smem = pl.BlockSpec(memory_space=pltpu.SMEM)
     vmem = pl.BlockSpec(memory_space=pltpu.VMEM)
     return pl.pallas_call(
@@ -219,9 +230,7 @@
         out_specs=[vmem] * len(outs),
         scratch_shapes=scratch,
         compiler_params=pltpu.CompilerParams(vmem_limit_bytes=48 * 1024 * 1024),
-        cost_estimate=pl.CostEstimate(
-            flops=1, bytes_accessed=24 * 3_000_000, transcendentals=0
-        ),
+        cost_estimate=cost(micros),
     )(*tables, *arrays)
 
 
@@ -265,9 +274,9 @@
         beside = self.over_y(value)
         return (value, across, beside, self.over_core(beside))
 
-    def deal_plane(self, near, give, far):
-        beside = self.over_y(far)
-        return (near, self.over_core(give), beside, self.over_core(beside))
+    def deal_plane(self, near, far, give, give_far):
+        got, got_far = self.over_core(give), self.over_core(give_far)
+        return (near, got, self.over_y(far), self.over_y(got_far))
 
     def sum_depth(self, kept, got):
         def half(index):
@@ -278,8 +287,8 @@
         full = add(part, self.mirror_z(part))
         return jnp.stack([full, self.over_z(full)])
 
-    def reduce(self, sent, kept):
-        return self.spread_plane(self.sum_depth(kept, self.over_x(sent)))
+    def reduce(self, got, kept):
+        return self.spread_plane(self.sum_depth(kept, got))
 
 
 def pick(value, index, axis):
@@ -301,10 +310,6 @@
 
 
 PARAMS = pltpu.CompilerParams(vmem_limit_bytes=56 * 1024 * 1024)
-
-
-def cost(micros):
-    return pl.CostEstimate(flops=1, bytes_accessed=micros * 3_000_000, transcendentals=0)
 
 
 def call_with_here(
@@ -399,7 +404,7 @@
     ]
     return call_with_here(
         project_kernel, here, (1,), arrays, [whole(a) for a in arrays], outs,
-        [whole(o) for o in outs], micros=8,
+        [whole(o) for o in outs], micros=PROJECT,
     )
 
 
@@ -410,7 +415,7 @@
 def attend_out_kernel(here, *refs):
     attn_ref, x_ref, gain_ref, own_ref = refs[:4]
     pieces = refs[4:12]
-    weight, h_ref, scale_ref, late_ref = refs[12:]
+    weight, h_ref, scale_ref, two_ref, two_t_ref = refs[12:]
     core, y, side = here[1], here[2], here[3]
     rows = own_ref.shape[0]
     part = rows // 4
@@ -422,14 +427,15 @@
             wide = piece.shape[1]
             weight[pl.ds(pl.multiple_of(at, part), part), n * wide : (n + 1) * wide] = piece[...]
     attn = attn_ref[...].T
-    late_ref[0] = attn
     h_one = x_ref[...].astype(jnp.float32) + jnp.dot(
         attn, weight[...], preferred_element_type=jnp.float32
     )
     scale = rms_scale(h_one)
     h_ref[...] = h_one
     scale_ref[...] = scale
-    late_ref[1] = (h_one * scale * gain_ref[...]).astype(jnp.bfloat16)
+    two = (h_one * scale * gain_ref[...]).astype(jnp.bfloat16)
+    two_ref[...] = two
+    two_t_ref[...] = two.T
 
 
 def attend_out(here, attn, x, gain, own, pieces):
@@ -449,56 +455,104 @@
         shape((width, width), bf16),
         shape((tokens, width), f32),
         shape((tokens, 1), f32),
-        shape((2, tokens, width), bf16),
+        shape((tokens, width), bf16),
+        shape((width, tokens), bf16),
     ]
     return call_with_here(
-        attend_out_kernel, here, (1,), arrays, specs, outs, [whole(o) for o in outs], micros=5
+        attend_out_kernel, here, (1,), arrays, specs, outs, [whole(o) for o in outs], micros=OUT
     )
 
 
 def ffn_kernel(chunk, here, *refs):
     two_ref, d_ref, own_ref = refs[:3]
-    gate_pieces, up_pieces, down_ref, down_pieces = refs[3:7], refs[7:11], refs[11], refs[12:16]
-    before_out, before_two = refs[16:18]
-    near, give, far, out_ref, d_two_ref = refs[18:23]
-    weight, down, hidden_rows = refs[23:26]
+    pieces, down_ref, down_pieces = refs[3:7], refs[7], refs[8:12]
+    if chunk == 0:
+        before_refs, refs = refs[12:13], refs[13:]
+        near, far, give, give_far, out_ref, d_two_ref = refs[:6]
+        refs = refs[6:]
+    else:
+        before_refs, gain_ref, refs = refs[12:17], refs[17], refs[18:]
+        near, far, give, give_far = refs[:4]
+        out_ref, d_h_ref, d_attn_ref, heads_ref, gain_term_ref = refs[4:9]
+        refs = refs[9:]
+    weight, down, hidden_rows, out_sum, two_sum = refs[:5]
+    held, weight_sem, down_sem, before_sem = refs[5:-3], refs[-3], refs[-2], refs[-1]
     core, y, side = here[1], here[2], here[3]
-    t = pl.program_id(0)
     f32, bf16 = jnp.float32, jnp.bfloat16
-    own_rows = own_ref.shape[1]
+    own_rows, columns = own_ref.shape[1], own_ref.shape[2] // CHUNKS
     part = own_rows // 4
-
-    @pl.when(t == 0)
-    def _():
-        out_ref[...] = before_out[...]
-        d_two_ref[...] = before_two[...]
+    tile = columns // FFN_TILES
+    half = columns // 2
 
     def quarter(p):
         return ((p % 2) ^ core) * 2 + ((p // 2) ^ y)
 
-    weight[:, pl.ds(pl.multiple_of(side * own_rows, own_rows), own_rows), :] = own_ref[...]
-    for p in range(4):
-        at = pl.multiple_of((1 - side) * own_rows + quarter(p) * part, part)
-        weight[0, pl.ds(at, part), :] = gate_pieces[p][...]
-        weight[1, pl.ds(at, part), :] = up_pieces[p][...]
-
-    @pl.when(side == chunk)
-    def _():
-        down[...] = down_ref[...]
-
-    @pl.when(side != chunk)
-    def _():
+    def copies(n):
+        at = slice(n * tile, (n + 1) * tile)
+        mine = pl.ds(pl.multiple_of(side * own_rows, own_rows), own_rows)
+        found = [
+            pltpu.make_async_copy(
+                own_ref.at[:, :, chunk * columns + n * tile : chunk * columns + (n + 1) * tile],
+                weight.at[:, mine, at],
+                weight_sem.at[n, 0],
+            )
+        ]
+        for p in range(4):
+            rows = pl.ds(pl.multiple_of((1 - side) * own_rows + quarter(p) * part, part), part)
+            for kind in range(2):
+                begin = kind * columns + n * tile
+                found.append(
+                    pltpu.make_async_copy(
+                        pieces[p].at[:, begin : begin + tile],
+                        weight.at[kind, rows, at],
+                        weight_sem.at[n, 1 + 2 * p + kind],
+                    )
+                )
+        return found
+
+    def own_down(n):
+        at = slice(n * tile, (n + 1) * tile)
+        return [pltpu.make_async_copy(down_ref.at[at, :], down.at[at, :], down_sem.at[n, 0])]
+
+    def other_down(n):
+        at = slice(n * tile, (n + 1) * tile)
+        found = []
         for p in range(4):
             wide = down_pieces[p].shape[1]
-            at = pl.multiple_of(quarter(p) * wide, wide)
-            down[:, pl.ds(at, wide)] = down_pieces[p][...]
-
-    two = two_ref[0]
+            lanes = pl.ds(pl.multiple_of(quarter(p) * wide, wide), wide)
+            found.append(
+                pltpu.make_async_copy(
+                    down_pieces[p].at[at, :], down.at[at, lanes], down_sem.at[n, p]
+                )
+            )
+        return found
+
+    def each(action, n):
+        for copy in copies(n):
+            action(copy)
+
+        @pl.when(side == chunk)
+        def _():
+            for copy in own_down(n):
+                action(copy)
+
+        @pl.when(side != chunk)
+        def _():
+            for copy in other_down(n):
+                action(copy)
+
+    before = [
+        pltpu.make_async_copy(ref, held[n], before_sem.at[n]) for n, ref in enumerate(before_refs)
+    ]
+    for n in range(FFN_TILES):
+        each(lambda copy: copy.start(), n)
+    for copy in before:
+        copy.start()
+    two = two_ref[...]
     d_ffn = d_ref[...]
-    tile = own_ref.shape[2]
-    first = (tile // 2) // 256 * 256
-    for begin, end in ((0, first), (first, tile)):
-        at = slice(begin, end)
+    for n in range(FFN_TILES):
+        each(lambda copy: copy.wait(), n)
+        at = slice(n * tile, (n + 1) * tile)
         gate = jnp.dot(two, weight[0, :, at], preferred_element_type=f32)
         upper = jnp.dot(two, weight[1, :, at], preferred_element_type=f32)
         d_hidden = contract(d_ffn, down[at, :], (1, 1))
@@ -507,90 +561,120 @@
         hidden = (silu * upper).astype(bf16)
         d_gate = (d_hidden * upper * sigma * (1.0 + gate * (1.0 - sigma))).astype(bf16)
         d_upper = (d_hidden * silu).astype(bf16)
-        out_ref[...] += jnp.dot(hidden, down[at, :], preferred_element_type=f32)
-        d_two_ref[...] += contract(d_gate, weight[0, :, at], (1, 1)) + contract(
+        out_term = jnp.dot(hidden, down[at, :], preferred_element_type=f32)
+        two_term = contract(d_gate, weight[0, :, at], (1, 1)) + contract(
             d_upper, weight[1, :, at], (1, 1)
         )
+        out_sum[...] = out_term if n == 0 else out_sum[...] + out_term
+        two_sum[...] = two_term if n == 0 else two_sum[...] + two_term
         hidden_rows[:, at] = hidden
         mine = jnp.where(core == 0, d_gate, d_upper)
         other = jnp.where(core == 0, d_upper, d_gate)
-
-        @pl.when(t == y)
-        def _(mine=mine, other=other, at=at):
-            near[:, at] = mine
-            give[:, at] = other
-
-        @pl.when(t != y)
-        def _(mine=mine, other=other, at=at):
-            far[0, :, at] = mine
-            far[1, :, at] = other
-
-    share = tile // 2
-    lower, upper = hidden_rows[:, :share], hidden_rows[:, share:]
-    close = jnp.where(y == 0, lower, upper)
-    distant = jnp.where(y == 0, upper, lower)
-    at = slice(tile, tile + share)
-
-    @pl.when(t == core)
-    def _():
-        near[:, at] = close
-        far[0, :, at] = distant
-
-    @pl.when(t != core)
-    def _():
-        give[:, at] = close
-        far[1, :, at] = distant
-
-
-def ffn(here, chunk, late, d_ffn, own, pieces, down, down_pieces, before):
-    _, tokens, width = late.shape
-    tile = own.shape[2] // 4
-    padded = (tile + tile // 2 + BLK - 1) // BLK * BLK
+        for column in range(2):
+            begin, end = max(n * tile, column * half), min((n + 1) * tile, (column + 1) * half)
+            if begin >= end:
+                continue
+            source = slice(begin - n * tile, end - n * tile)
+            target = slice(begin - column * half, end - column * half)
+            first, second = mine[:, source], other[:, source]
+
+            @pl.when(y == column)
+            def _(first=first, second=second, target=target):
+                near[:, target] = first
+                give[:, target] = second
+
+            @pl.when(y != column)
+            def _(first=first, second=second, target=target):
+                far[:, target] = first
+                give_far[:, target] = second
+
+    share = half // 2
+    target = slice(half, half + share)
+    for owner in range(2):
+        lower = hidden_rows[:, owner * half : owner * half + share]
+        upper = hidden_rows[:, owner * half + share : (owner + 1) * half]
+        close = jnp.where(y == 0, lower, upper)
+        distant = jnp.where(y == 0, upper, lower)
+
+        @pl.when(core == owner)
+        def _(close=close, distant=distant):
+            near[:, target] = close
+            far[:, target] = distant
+
+        @pl.when(core != owner)
+        def _(close=close, distant=distant):
+            give[:, target] = close
+            give_far[:, target] = distant
+
+    for copy in before:
+        copy.wait()
+    if chunk == 0:
+        out_ref[...] = held[0][...] + out_sum[...]
+        d_two_ref[...] = two_sum[...]
+    else:
+        out_before, two_before, h_one, scale, w_out = held
+        out_ref[...] = (out_before[...] + out_sum[...]).astype(bf16)
+        d_norm, gain_term = norm_back(
+            two_before[...] + two_sum[...], h_one[...], scale[...], gain_ref[...]
+        )
+        gain_term_ref[...] = jnp.sum(gain_term, axis=0, keepdims=True)
+        d_h_one = d_ffn.astype(f32) + d_norm
+        d_h_ref[...] = d_h_one
+        d_attn = d_h_one.astype(bf16)
+        d_attn_ref[...] = d_attn
+        heads_ref[...] = contract(w_out[...], d_attn, (1, 1)).astype(bf16)
+
+
+FFN_TILES = 3
+
+
+def ffn(here, chunk, two, d_ffn, own, pieces, down, down_pieces, before, gain=None):
+    tokens, width = two.shape
+    columns = own.shape[2] // CHUNKS
+    padded = (columns // 2 + columns // 4 + BLK - 1) // BLK * BLK
     shape = jax.ShapeDtypeStruct
     f32, bf16 = jnp.float32, jnp.bfloat16
-    outs = [shape((tokens, padded), bf16)] * 2 + [shape((2, tokens, padded), bf16)]
-    outs += [shape((tokens, width), f32)] * 2
-
-    def own_down(t, here):
-        return (jnp.where(here[3] == chunk, t, 0), 0)
-
-    def other_down(t, here):
-        return (jnp.where(here[3] == chunk, 0, t), 0)
-
-    part = own.shape[1] // 4
-    specs = (
-        [layer(late, 1), whole(d_ffn)]
-        + [pl.BlockSpec((2, own.shape[1], tile), lambda t, here: (0, 0, 2 * chunk + t))]
-        + [pl.BlockSpec((part, tile), lambda t, here: (0, t))] * 4
-        + [pl.BlockSpec((part, tile), lambda t, here: (0, 2 + t))] * 4
-        + [pl.BlockSpec((tile, width), own_down)]
-        + [pl.BlockSpec((tile, width // 4), other_down)] * 4
-        + [whole(before[0]), whole(before[1])]
-    )
+    outs = [shape((tokens, padded), bf16)] * 4
+    if chunk == 0:
+        outs += [shape((tokens, width), f32)] * 2
+    else:
+        outs += [
+            shape((tokens, width), bf16),
+            shape((tokens, width), f32),
+            shape((tokens, width), bf16),
+            shape((width, tokens), bf16),
+            shape((1, width), f32),
+        ]
+    far_away = pl.BlockSpec(memory_space=pl.ANY)
+    arrays = [two, d_ffn, own, *pieces, down, *down_pieces, *before]
+    specs = [whole(two), whole(d_ffn)] + [far_away] * (len(arrays) - 2)
+    if gain is not None:
+        arrays.append(gain)
+        specs.append(whole(gain))
     got = call_with_here(
         functools.partial(ffn_kernel, chunk),
         here,
-        (2,),
-        [late, d_ffn, own, *pieces, *pieces, down, *down_pieces, *before],
+        (1,),
+        arrays,
         specs,
         outs,
         [whole(o) for o in outs],
         [
-            pltpu.VMEM((2, width, tile), bf16),
-            pltpu.VMEM((tile, width), bf16),
-            pltpu.VMEM((tokens, tile), bf16),
+            pltpu.VMEM((2, width, columns), bf16),
+            pltpu.VMEM((columns, width), bf16),
+            pltpu.VMEM((tokens, columns), bf16),
+            pltpu.VMEM((tokens, width), f32),
+            pltpu.VMEM((tokens, width), f32),
+        ]
+        + [pltpu.VMEM(v.shape, v.dtype) for v in before]
+        + [
+            pltpu.SemaphoreType.DMA((FFN_TILES, 9)),
+            pltpu.SemaphoreType.DMA((FFN_TILES, 4)),
+            pltpu.SemaphoreType.DMA((len(before),)),
         ],
-        micros=20,
-    )
-    return got[:3], got[3:]
-
-
-def dealt(shares):
-    return list(shares), [whole(shares[0]), whole(shares[1]), layer(shares[2], 0), layer(shares[3], 1)]
-
-
-def flat(ref):
-    return ref[...] if len(ref.shape) == 2 else ref[0]
+        micros=FFN[chunk],
+    )
+    return got[:4], got[4:]
 
 
 def wide_product_kernel(here, *refs):
@@ -599,8 +683,8 @@
     tokens = planes[0].shape[1]
     columns = right.shape[1]
     for i in range(4):
-        left[:, i * tokens : (i + 1) * tokens] = planes[i][0].T
-        right[i * tokens : (i + 1) * tokens, :] = flat(terms[i])[:, :columns]
+        left[:, i * tokens : (i + 1) * tokens] = planes[i][...]
+        right[i * tokens : (i + 1) * tokens, :] = terms[i][:, :columns]
     side = here[3]
     _, step, _ = kept.shape
     for half in range(2):
@@ -611,19 +695,20 @@
             ).astype(out_ref.dtype)
 
 
-def wide_products(here, late_plane, shares, columns):
-    _, tokens, rows = late_plane[0].shape
+def wide_products(here, two_plane, shares, columns):
+    rows, tokens = two_plane[0].shape
     outs = [
         jax.ShapeDtypeStruct((2, rows // 4, columns), jnp.bfloat16),
         jax.ShapeDtypeStruct((2, rows // 4, columns), jnp.float32),
     ]
-    arrays, specs = dealt(shares)
+    arrays = [*two_plane, *shares]
     return call_with_here(
         wide_product_kernel,
         here,
         (1,),
-        [*late_plane, *arrays],
-        [layer(a, 1) for a in late_plane] + specs,
+        arrays,
+        [whole(a) for a in two_plane]
+        + [pl.BlockSpec((tokens, columns), lambda i, here: (0, 0))] * 4,
         outs,
         [whole(o) for o in outs],
         [
@@ -643,7 +728,7 @@
         right[i * tokens : (i + 1) * tokens, :] = planes[i][0]
     for chunk in range(2):
         for i in range(4):
-            share = flat(terms[chunk][i])
+            share = terms[chunk][i]
             at = share.shape[1] // BLK * BLK - (rows + BLK - 1) // BLK * BLK
             left[:, i * tokens : (i + 1) * tokens] = share[:, at : at + rows].T
         for half in range(2):
@@ -668,14 +753,12 @@
         jax.ShapeDtypeStruct((2, rows // 2, columns), jnp.bfloat16),
         jax.ShapeDtypeStruct((2, rows // 2, columns), jnp.float32),
     ]
-    first, first_specs = dealt(first)
-    second, second_specs = dealt(second)
     return call_with_here(
         down_product_kernel,
         here,
         (1,),
         [*early_plane, *first, *second],
-        [layer(a, 0) for a in early_plane] + first_specs + second_specs,
+        [layer(a, 0) for a in early_plane] + [whole(a) for a in (*first, *second)],
         outs,
         [whole(o) for o in outs],
         [
@@ -692,8 +775,8 @@
 def attention_back_kernel(here, *refs):
     d_ref, q_ref, k_ref, q_scale, k_scale, q_gain, k_gain, cos_ref, sin_ref = refs[:9]
     weight, x_ref, scale_ref, gain_ref, d_h_ref, d_attn_ref = refs[9:15]
-    near, give, far, d_x_ref, gains_ref = refs[15:20]
-    turned, natural = refs[20:]
+    near, far, give, give_far, d_x_ref, gains_ref = refs[15:21]
+    turned, natural = refs[21:]
     f32, bf16 = jnp.float32, jnp.bfloat16
     core, y = here[1], here[2]
     cosine, sine = cos_ref[...], sin_ref[...]
@@ -730,19 +813,11 @@
         turned[place : place + HD, :] = both[HD:].astype(bf16)
     rows = turned.shape[0] // 4
     columns = d_attn_ref.shape[1] // 4
-    shares = (
-        (near, None, core, y), (give, None, 1 - core, y), (far, 0, core, 1 - y), (far, 1, 1 - core, 1 - y),
-    )
-    for out_ref, index, to_core, to_y in shares:
+    shares = ((near, core, y), (far, core, 1 - y), (give, 1 - core, y), (give_far, 1 - core, 1 - y))
+    for out_ref, to_core, to_y in shares:
         share = to_core * 2 + to_y
-        first = turned[pl.ds(pl.multiple_of(share * rows, rows), rows), :]
-        second = d_attn_ref[:, pl.ds(pl.multiple_of(share * columns, columns), columns)]
-        if index is None:
-            out_ref[:rows, :] = first
-            out_ref[rows:, :] = second
-        else:
-            out_ref[index, :rows, :] = first
-            out_ref[index, rows:, :] = second
+        out_ref[:rows, :] = turned[pl.ds(pl.multiple_of(share * rows, rows), rows), :]
+        out_ref[rows:, :] = d_attn_ref[:, pl.ds(pl.multiple_of(share * columns, columns), columns)]
     for at in range(0, turned.shape[0], 256):
         natural[:, at : at + 256] = turned[at : at + 256, :].T
     d_normed = contract(natural[...], weight[...], (1, 1))
@@ -763,9 +838,7 @@
     rows = weight.shape[1] // 4 + tokens
     assert width // 4 == tokens
     outs = [
-        shape((rows, tokens), bf16),
-        shape((rows, tokens), bf16),
-        shape((2, rows, tokens), bf16),
+        *[shape((rows, tokens), bf16)] * 4,
         shape((tokens, width), f32),
         shape((8, width), f32),
     ]
@@ -785,8 +858,8 @@
     for i in range(4):
         at = slice(i * tokens, (i + 1) * tokens)
         left[:, at] = normed[i][0].T
-        left_out[:, at] = attn[i][0].T
-        share = flat(terms[i])
+        left_out[:, at] = attn[i][...]
+        share = terms[i]
         right[at, :] = share[:cut].T
         right_out[at, :] = share[cut:]
     step = left.shape[0] // 4
@@ -814,21 +887,18 @@
         out_ref[1, step:, :] = jnp.zeros((GAIN_ROWS, out_ref.shape[2]), out_ref.dtype)
 
 
-def attention_products(here, early_plane, late_plane, shares, gains, ffn_gain):
+def attention_products(here, early_plane, attn_plane, shares, gains, ffn_gain):
     _, tokens, width = early_plane[0].shape
     cut = shares[0].shape[0] - tokens
     shape = (2, width // 4 + GAIN_ROWS, cut + tokens)
     outs = [jax.ShapeDtypeStruct(shape, jnp.bfloat16), jax.ShapeDtypeStruct(shape, jnp.float32)]
-    arrays, specs = dealt(shares)
     return call_with_here(
         attention_product_kernel,
         here,
         (1,),
-        [*early_plane, *late_plane, *arrays, gains, ffn_gain],
+        [*early_plane, *attn_plane, *shares, gains, ffn_gain],
         [layer(a, 1) for a in early_plane]
-        + [layer(a, 0) for a in late_plane]
-        + specs
-        + [whole(gains), whole(ffn_gain)],
+        + [whole(a) for a in (*attn_plane, *shares, gains, ffn_gain)],
         outs,
         [whole(o) for o in outs],
         [
@@ -1013,7 +1083,8 @@
     def quarter_rows(weight):
         return lax.dynamic_slice_in_dim(weight, links.quarter * part_rows, part_rows)
 
-    gains_here = jnp.concatenate([attn_gain, ffn_gain, query_gain, key_gain])
+    qkv_piece = quarter_rows(qkv_weight)
+    gains_here = jnp.concatenate([after(attn_gain, qkv_piece), ffn_gain, query_gain, key_gain])
     gains_there = links.over_x(gains_here)
 
     def gain_of(at, size):
@@ -1036,7 +1107,7 @@
         )
         return [piece[:, 0], piece[:, 1]]
 
-    qkv_there = links.over_x(quarter_rows(qkv_weight))
+    qkv_there = links.over_x(qkv_piece)
     first_piece = jnp.concatenate([*gate_up_piece(0), quarter_rows(out_weight)], axis=1)
     second_piece = jnp.concatenate(gate_up_piece(1), axis=1)
     down_piece = lax.dynamic_slice_in_dim(
@@ -1083,48 +1154,49 @@
             shape((1, q_rows), f32),
         ],
         [pltpu.VMEM((HD, kv_rows), bf16)],
+        ATTEND,
     )
     attn_in = lax.dynamic_slice_in_dim(
         lax.all_to_all(attn_sent, "ctx", 0, 0, tiled=True), part * HEADS, HEADS
     ).reshape(q_width, rows_here)
     second_there = after(second_there, attn_sent)
 
-    def spread(there, beside):
-        there, beside = after(there, attn_sent), after(beside, attn_sent)
+    def spread(there, beside, time):
+        there, beside = after(there, time), after(beside, time)
         return (there, links.over_core(there), beside, links.over_core(beside))
 
-    first_pieces = spread(first_there, first_beside)
-    down_pieces = spread(down_there, down_beside)
+    first_pieces = spread(first_there, first_beside, attn_sent)
+    down_pieces = spread(down_there, down_beside, attn_in)
     second_pieces = links.spread_plane(second_there)
-    w_out, h_one, scale_two, late = attend_out(
-        here, attn_in, tokens_here, gain_ffn[None], out_weight, first_pieces
-    )
-    late_plane = links.spread_plane(late)
-    sums = [h_one, jnp.zeros_like(h_one)]
-    shares = []
-    for chunk, pieces in enumerate((first_pieces, second_pieces)):
-        dealt_here, sums = ffn(
-            here, chunk, late, d_ffn, gate_up, pieces, down_weight, down_pieces, sums
-        )
-        shares.append(links.deal_plane(*dealt_here))
-        if chunk == 0:
-            early = after(early, sums[0])
-            early_plane = (
-                early, links.over_core(early), early_beside,
-                links.over_core(after(early_beside, sums[0])),
-            )
+    w_out, h_one, scale_two, two, two_t = attend_out(
+        here, after(attn_in, early_beside), tokens_here, gain_ffn[None], out_weight, first_pieces
+    )
+    attn_beside = links.over_y(attn_in)
+    two_beside = links.over_y(two_t)
+    dealt_here, (out_sum, two_sum) = ffn(
+        here, 0, two, d_ffn, gate_up, first_pieces, down_weight, down_pieces, [h_one]
+    )
+    two_plane = (two_t, links.over_core(two_t), two_beside, links.over_core(two_beside))
+    near, far, give, give_far = dealt_here
+    got_far = links.over_core(give_far)
+    first_shares = (near, links.over_core(give), links.over_y(far), links.over_y(got_far))
+    out_sum = after(out_sum, got_far)
+    dealt_here, (output, d_h_one, d_attn, d_heads, ffn_gain_term) = ffn(
+        here, 1, two, d_ffn, gate_up, second_pieces, down_weight, down_pieces,
+        [out_sum, two_sum, h_one, scale_two, w_out], gain_ffn[None],
+    )
+    second_shares = links.deal_plane(*dealt_here)
+
+    def plane(value, beside, time):
+        value, beside = after(value, time), after(beside, time)
+        return (value, links.over_core(value), beside, links.over_core(beside))
+
     columns = ff_chunk // 2
-    output = sums[0].astype(bf16)
-    d_norm_two, ffn_gain_term = norm_back(sums[1], h_one, scale_two, gain_ffn)
-    d_h_one = d_ffn.astype(f32) + d_norm_two
-    d_attn = d_h_one.astype(bf16)
-    d_heads = lax.dot_general(
-        w_out, d_attn, (((1,), (1,)), ((), ())), preferred_element_type=f32
-    ).astype(bf16)
-    d_heads = jnp.concatenate([d_heads.reshape(HEADS, HD, rows_here)] * parts, axis=0)
+    d_heads = d_heads.reshape(HEADS, HD, rows_here)
     d_got = lax.all_to_all(d_heads, "ctx", 0, 0, tiled=True)
-    first_shares = [after(v, d_heads) for v in shares[0]]
-    first_products = wide_products(here, late_plane, first_shares, columns)
+    first_products = wide_products(
+        here, two_plane, [after(v, d_heads) for v in first_shares], columns
+    )
     d_got = after(d_got, first_products[0])
     (d_sent,) = kernel_call(
         attend_back_kernel,
@@ -1137,10 +1209,21 @@
             pltpu.VMEM((kv_rows, HD), f32),
             pltpu.VMEM((kv_rows, HD), f32),
         ],
-    )
+        ATTEND_BACK,
+    )
+    first_got = links.over_x(first_products[0])
+    d_sent = after(d_sent, first_got)
     d_back = lax.all_to_all(d_sent, "ctx", 0, 0, tiled=True)
-    second_shares = [after(v, d_sent) for v in shares[1]]
-    second_products = wide_products(here, late_plane, second_shares, columns)
+    second_products = wide_products(
+        here, two_plane, [after(v, d_sent) for v in second_shares], columns
+    )
+    early_plane = plane(early, early_beside, d_sent)
+    attn_plane = plane(attn_in, attn_beside, d_sent)
+    down_terms = down_products(
+        here, early_plane, first_shares, second_shares, columns // 2
+    )
+    second_got = links.over_x(after(second_products[0], first_got))
+    down_got = links.over_x(after(down_terms[0], second_got))
     *d_shares, d_inputs, gain_sums = attention_back(
         here,
         [
@@ -1149,17 +1232,18 @@
         ],
     )
     grad_gate_up = None
-    for chunk, products in enumerate((first_products, second_products)):
-        grad_gate_up = place_gate_up(here, chunk, links.reduce(*products), grad_gate_up)
-    grad_down = place_down(
-        here, links.reduce(*down_products(here, early_plane, *shares, columns // 2))
-    )
+    for chunk, (got, kept) in enumerate(
+        ((first_got, first_products[1]), (second_got, second_products[1]))
+    ):
+        grad_gate_up = place_gate_up(here, chunk, links.reduce(got, kept), grad_gate_up)
+    grad_down = place_down(here, links.reduce(down_got, down_terms[1]))
     attention_terms = attention_products(
-        here, early_plane, late_plane, links.deal_plane(*d_shares), gain_sums,
-        jnp.sum(ffn_gain_term, axis=0, keepdims=True),
+        here, early_plane, attn_plane, links.deal_plane(*d_shares), gain_sums, ffn_gain_term
     )
     cut = qkv_weight.shape[1] // 4
-    grad_qkv, grad_out, gain_sums = place_attention(here, links.reduce(*attention_terms), cut)
+    grad_qkv, grad_out, gain_sums = place_attention(
+        here, links.reduce(links.over_x(attention_terms[0]), attention_terms[1]), cut
+    )
     at = links.side * (HD // 2)
     gain_grads = [
         gain_sums[0, :rows],
@@ -1275,6 +1359,7 @@
             shape((1, q_rows), f32),
         ],
         [pltpu.VMEM((HD, kv_rows), bf16)],
+        ATTEND,
     )
     attn_in = lax.dynamic_slice_in_dim(
         lax.all_to_all(attn_sent, "ctx", 0, 0, tiled=True), part * HEADS, HEADS
@@ -1357,6 +1442,7 @@
             pltpu.VMEM((kv_rows, HD), f32),
             pltpu.VMEM((kv_rows, HD), f32),
         ],
+        ATTEND_BACK,
     )
     d_back = lax.all_to_all(d_sent, "ctx", 0, 0, tiled=True)
     d_query = lax.dynamic_slice_in_dim(d_back[:, :HD], part * HEADS, HEADS).astype(f32)

time: 604 us -> 554 us (0.917)
  waiting for transfers between devices: 270 us -> 216 us
  starting transfers between devices: 81.6 us -> 98.4 us
  Pallas kernels: 176 us -> 168 us
    ppermute x13 -> x17, waiting for transfers between devices: 126 us -> 95.7 us  [over_y(): return lax.ppermute(value, 'ctx', self.route(lambda z, y, c: (z, 1 - y, c)))]
    pallas_call x13, Pallas kernels: 130 us -> 121 us  [call_with_here(): pl.pallas_call(kernel, grid_spec=pltpu.PrefetchScalarGridSpec(num_scalar_...]
    ppermute x8, starting transfers between devices: 18.4 us -> 26.7 us  [over_z(): return lax.ppermute(value, 'ctx', self.route(lambda z, y, c: (z ^ 1, y, c)))]
    ppermute x4, waiting for transfers between devices: 16.2 us -> 8.02 us  [mirror_z(): lax.ppermute(value, 'ctx', self.route(lambda z, y, c: (self.depth - 1 - z...]
    unnamed x82 -> x84, local copies, waits for them, and re-layouts: 13.5 us -> 14.9 us
    ppermute x13 -> x17, starting transfers between devices: 21.7 us -> 21.4 us  [over_y(): return lax.ppermute(value, 'ctx', self.route(lambda z, y, c: (z, 1 - y, c)))]
  transfers between devices with their start and end apart: 64 -> 70, of which waited for: 26 -> 23; matrix products, arithmetic and copies ran while one was open for 8% -> 8% of each run, Pallas kernels for 29% -> 30%
where the time goes in v6:
time: 554 us; the launch traced here: 546 us
  waiting for transfers between devices  216 us (39%)
  Pallas kernels  168 us (30%)
  starting transfers between devices  98.4 us (18%)
  local copies, waits for them, and re-layouts  40.6 us (7%)
  other arithmetic  21.4 us (4%)
    pallas_call x13, Pallas kernels, call_with_here(): pl.pallas_call(kernel, grid_spec=pltpu.PrefetchScalarGridSpec(num_scalar_...  121 us
    ppermute x17, waiting for transfers between devices, over_y(): return lax.ppermute(value, 'ctx', self.route(lambda z, y, c: (z, 1 - y, c)))  95.7 us
    ppermute x9, waiting for transfers between devices, over_x(): return lax.ppermute(value, 'fsdp', [(0, 1), (1, 0)])  68.2 us
    pallas_call x2, Pallas kernels, kernel_call(): pl.pallas_call(kernel, out_shape=outs, in_specs=[smem] * len(tables) + [v...  46.9 us
    ppermute x8, waiting for transfers between devices, over_z(): return lax.ppermute(value, 'ctx', self.route(lambda z, y, c: (z ^ 1, y, c)))  31.7 us
    ppermute x8, starting transfers between devices, over_z(): return lax.ppermute(value, 'ctx', self.route(lambda z, y, c: (z ^ 1, y, c)))  26.7 us
    ppermute x17, starting transfers between devices, over_y(): return lax.ppermute(value, 'ctx', self.route(lambda z, y, c: (z, 1 - y, c)))  21.4 us
    unnamed x84, local copies, waits for them, and re-layouts  14.9 us
  transfers between devices with their start and end apart: 70, of which 23 were waited for; matrix products, arithmetic and copies ran while one was open for 8% of the time, Pallas kernels for 30%

profile of v6, /device:TPU:0, one launch (start us, length us, event | category | flops | bytes accessed | tf_op | source)
XLA Modules:
  0.0 545.9 jit_solution(13846204366945331786)
XLA Ops:
  20.4 8.9 %copy.71 = bf16[512,2,4608]{2,0,1:T(8,128)(2,1)} copy(bf16[512,2,4608]{2,1,0:T(2,128)(2,1)} %param.15) | data formatting | bytes 18874368 | tf_op jit(solution)/shard_map/optimization_barrier | solution.py:303
  50.5 16.0 %collective-permute-done.5.refs_4_.refs_5_.refs_3_ = bf16[128,5632]{1,0:T(8,128)(2,1)} collective-permute-done((bf16[128,5632]{1,0:T(8,128)(2,1)}, bf16[128,5632]{1,0:T(8,128)(2,1)}, u32[]{:S(2)}, u32[]{:S(2)}) %collective-permute-start.5) | collective-permute-done | bytes 1441824 | tf_op jit(solution)/shard_map/ppermute | solution.py:270
  71.0 23.2 %collective-permute-done.6.refs_8_ = bf16[2304,256]{1,0:T(8,128)(2,1)} collective-permute-done((bf16[2304,256]{1,0:T(8,128)(2,1)S(1)}, bf16[2304,256]{1,0:T(8,128)(2,1)}, u32[]{:S(2)}, u32[]{:S(2)}) %collective-permute-start.6) | collective-permute-done | bytes 1179680 | tf_op jit(solution)/shard_map/ppermute | solution.py:270
  98.6 22.0 %shard_map.196 = (bf16[16,64,256]{2,1,0:T(8,128)(2,1)}, bf16[4096,64]{1,0:T(8,128)(2,1)S(1)}, bf16[64,4096]{1,0:T(8,128)(2,1)S(1)}, bf16[4096,64]{1,0:T(8,128)(2...) custom-call(s32[32]{0:T(128)S(1)} %broadcast_add_fusion.q_slot, ...), custom_call_target="tpu_custom_call" | custom-call | flops 1 | bytes 1 | tf_op jit(solution)/shard_map/pallas_call | solution.py:226
  131.5 11.9 %all-to-all-done.1 = bf16[16,64,256]{2,1,0:T(8,128)(2,1)S(1)} async-done(((bf16[16,64,256]{2,1,0:T(8,128)(2,1)}), bf16[16,64,256]{2,1,0:T(8,128)(2,1)S(1)}, u32[]{:S(2)}, u32[]{:S(2)}) %all-to-all-start.1) | async-done | bytes 524320 | tf_op jit(solution)/shard_map/all_to_all | solution.py:1160
  143.9 16.3 %collective-permute-done.7.refs_2_ = bf16[2,256,1024]{2,1,0:T(8,128)(2,1)} collective-permute-done((bf16[2,256,1024]{2,1,0:T(8,128)(2,1)}, bf16[2,256,1024]{2,1,0:T(8,128)(2,1)}, u32[]{:S(2)}, u32[]{:S(2)}) %collective-permute-start.7) | collective-permute-done | bytes 1048608 | tf_op jit(solution)/shard_map/ppermute | solution.py:261
  168.2 16.8 %shard_map.198 = (bf16[256,1792]{1,0:T(8,128)(2,1)}, bf16[256,1792]{1,0:T(8,128)(2,1)}, bf16[256,1792]{1,0:T(8,128)(2,1)}, bf16[256,1792]{1,0:T(8,128)(2,1)}, f32[256,1024]{1,0:T(8,128)}, /*index=5*/f32[256,1024]{1,0:T(8,128)}) custom-call(s32[4]{0:T(128)} %pad_add_fusion.here, bf16[256,1024]{1,0:T(8,128)(2,1)} %get-tuple-element.109.refs_0_, ...), custom_call_target="tpu_custom_call" | custom-call | flops 1 | bytes 1 | tf_op jit(solution)/shard_map/pallas_call | solution.py:318
  190.9 12.7 %collective-permute-done.20.refs_2_ = bf16[1024,256]{1,0:T(8,128)(2,1)} collective-permute-done((bf16[1024,256]{1,0:T(8,128)(2,1)}, bf16[1024,256]{1,0:T(8,128)(2,1)}, u32[]{:S(2)}, u32[]{:S(2)}) %collective-permute-start.20) | collective-permute-done | bytes 524320 | tf_op jit(solution)/shard_map/ppermute | solution.py:261
  204.6 16.9 %shard_map.199 = (bf16[256,1792]{1,0:T(8,128)(2,1)}, bf16[256,1792]{1,0:T(8,128)(2,1)}, bf16[256,1792]{1,0:T(8,128)(2,1)}, bf16[256,1792]{1,0:T(8,128)(2,1)}, bf...) custom-call(s32[4]{0:T(128)} %pad_add_fusion.here, ...), custom_call_target="tpu_custom_call" | custom-call | flops 1 | bytes 1 | tf_op jit(solution)/shard_map/pallas_call | solution.py:318
  227.8 19.1 %collective-permute-done.24.refs_7_ = bf16[256,1792]{1,0:T(8,128)(2,1)} collective-permute-done((bf16[256,1792]{1,0:T(8,128)(2,1)}, bf16[256,1792]{1,0:T(8,128)(2,1)}, u32[]{:S(2)}, u32[]{:S(2)}) %collective-permute-start.24) | collective-permute-done | bytes 917536 | tf_op jit(solution)/shard_map/ppermute | solution.py:261
  260.4 24.9 %shard_map.201 = bf16[16,192,256]{2,1,0:T(8,128)(2,1)} custom-call(s32[32]{0:T(128)S(1)} %broadcast_add_fusion.q_slot, s32[32]{0:T(128)S(1)} %get-tuple-element.181.kv_slot, s32[16]{0:T(128)S(1)} %get-tuple-element.202.first, s32[16]{0:T(128)S(1)} %get-tuple-element.203.last, bf16[16,64,256]{2,1,0:T(8,128)(2,1)S(1)} %all-to-all-done.2.d_ref, ...), custom_call_target="tpu_custom_call" | custom-call | flops 24999999488 | bytes 1 | tf_op jit(solution)/shard_map/pallas_call | solution.py:226
  291.2 7.6 %shard_map.205 = (bf16[2,256,1152]{2,1,0:T(8,128)(2,1)}, f32[2,256,1152]{2,1,0:T(8,128)}) custom-call(s32[4]{0:T(128)} %pad_add_fusion.here, bf16[1024,256]{1,0:T(8,128)(2,1)} %get-tuple-element.123.refs_0_, bf16[1024,256]{1,0:T(8,128)(2,1)} %collective-permute-done.19.refs_1_, bf16[1024,256]{1,0:T(8,128)(2,1)} %collective-permute-done.20.refs_2_, ...), custom_call_target="tpu_custom_call" | custom-call | flops 8000000000 | bytes 1 | tf_op jit(solution)/shard_map/pallas_call | solution.py:318
  304.9 9.7 %shard_map.208 = (bf16[2,288,1024]{2,1,0:T(8,128)(2,1)}, f32[2,288,1024]{2,1,0:T(8,128)}) custom-call(s32[4]{0:T(128)} %pad_add_fusion.here, bf16[2,256,1024]{2,1,0:T(8,128)(2,1)} %get-tuple-element.150.refs_0_, bf16[2,256,1024]{2,1,0:T(8,128)(2,1)} %collective-permute-done.26.refs_1_, bf16[2,256,1024]{2,1,0:T(8,128)(2,1)} %collective-permute-done.7.refs_2_, ...), custom_call_target="tpu_custom_call" | custom-call | flops 8000000000 | bytes 1 | tf_op jit(solution)/shard_map/pallas_call | solution.py:318
  314.6 12.8 %collective-permute-done.46 = bf16[2,256,1152]{2,1,0:T(8,128)(2,1)} collective-permute-done((bf16[2,256,1152]{2,1,0:T(8,128)(2,1)}, bf16[2,256,1152]{2,1,0:T(8,128)(2,1)}, u32[]{:S(2)}, u32[]{:S(2)}) %collective-permute-start.46) | collective-permute-done | bytes 1179680 | tf_op jit(solution)/shard_map/ppermute | solution.py:270
  338.8 16.3 %collective-permute-done.59 = bf16[2,288,1024]{2,1,0:T(8,128)(2,1)} collective-permute-done((bf16[2,288,1024]{2,1,0:T(8,128)(2,1)}, bf16[2,288,1024]{2,1,0:T(8,128)(2,1)}, u32[]{:S(2)}, u32[]{:S(2)}) %collective-permute-start.59) | collective-permute-done | bytes 1179680 | tf_op jit(solution)/shard_map/ppermute | solution.py:270
  358.6 8.4 %shard_map.202 = (bf16[768,256]{1,0:T(8,128)(2,1)}, bf16[768,256]{1,0:T(8,128)(2,1)}, bf16[768,256]{1,0:T(8,128)(2,1)}, bf16[768,256]{1,0:T(8,128)(2,1)}, f32[256,1024]{1,0:T(8,128)}, /*index=5*/f32[8,1024]{1,0:T(8,128)}) custom-call(s32[4]{0:T(128)} %pad_add_fusion.here, bf16[16,192,256]{2,1,0:T(8,128)(2,1)} %all-to-all-done.3.refs_0_, ...), custom_call_target="tpu_custom_call" | custom-call | flops 12000000000 | bytes 1 | tf_op jit(solution)/shard_map/pallas_call | solution.py:318
  410.7 13.9 %collective-permute-start.49 = (bf16[256,1152]{1,0:T(8,128)(2,1)S(1)}, bf16[256,1152]{1,0:T(8,128)(2,1)S(1)}, u32[]{:S(2)}, u32[]{:S(2)}) collective-permute-start(bf16[256,1152]{1,0:T(8,128)(2,1)S(1)} %add_convert_fusion.6), channel_id=1, source_target_pairs={{0,8},{2,10},{4,12},{6,14},{8,0},{10,2},{12,4},{14,6},{16,24},{18,... | collective-permute-start | bytes 1769480 | tf_op jit(solution)/shard_map/ppermute | solution.py:264
  427.6 8.0 %collective-permute-start.62 = (bf16[288,1024]{1,0:T(8,128)(2,1)S(1)}, bf16[288,1024]{1,0:T(8,128)(2,1)S(1)}, u32[]{:S(2)}, u32[]{:S(2)}) collective-permute-start(bf16[288,1024]{1,0:T(8,128)(2,1)S(1)} %add_convert_fusion), channel_id=1, source_target_pairs={{0,8},{2,10},{4,12},{6,14},{8,0},{10,2},{12,4},{14,6},{16,24},{18,... | collective-permute-start | bytes 1769480 | tf_op jit(solution)/shard_map/ppermute | solution.py:264
  450.8 9.8 %collective-permute-done.62 = bf16[288,1024]{1,0:T(8,128)(2,1)S(1)} collective-permute-done((bf16[288,1024]{1,0:T(8,128)(2,1)S(1)}, bf16[288,1024]{1,0:T(8,128)(2,1)S(1)}, u32[]{:S(2)}, u32[]{:S(2)}) %collective-permute-start.62) | collective-permute-done | bytes 589856 | tf_op jit(solution)/shard_map/ppermute | solution.py:264
  475.7 17.1 %collective-permute-done.64.refs_2_ = bf16[2,288,1024]{2,1,0:T(8,128)(2,1)} collective-permute-done((bf16[2,288,1024]{2,1,0:T(8,128)(2,1)}, bf16[2,288,1024]{2,1,0:T(8,128)(2,1)}, u32[]{:S(2)}, u32[]{:S(2)}) %collective-permute-start.64) | collective-permute-done | bytes 1179680 | tf_op jit(solution)/shard_map/ppermute | solution.py:261
  494.3 10.0 %shard_map.206.refs_4_ = f32[512,2,4608]{2,1,0:T(2,128)} custom-call(s32[4]{0:T(128)} %pad_add_fusion.here, bf16[2,256,1152]{2,1,0:T(8,128)(2,1)} %pad_maximum_fusion.3.refs_0_, bf16[2,256,1152]{2,1,0:T(8,128)(2,1)} %collective-permute-done.56.refs_1_, bf16[2,256,1152]{2,1,0:T(8,128)(2,1)} %collective-permute-done.57.refs_2_, ...), custom_call_target="tpu_custom_call" | custom-call | flops 10000000000 | bytes 1 | tf_op jit(solution)/shard_map/pallas_call | solution.py:318
  504.4 9.4 %collective-permute-done.40.refs_2_ = bf16[2,272,768]{2,1,0:T(8,128)(2,1)S(1)} collective-permute-done((bf16[2,272,768]{2,1,0:T(8,128)(2,1)S(1)}, bf16[2,272,768]{2,1,0:T(8,128)(2,1)S(1)}, u32[]{:S(2)}, u32[]{:S(2)}) %collective-permute-start.40) | collective-permute-done | bytes 835616 | tf_op jit(solution)/shard_map/ppermute | solution.py:261
  513.8 9.7 %shard_map.207 = f32[512,2,4608]{2,1,0:T(2,128)} custom-call(s32[4]{0:T(128)} %pad_add_fusion.here, bf16[2,256,1152]{2,1,0:T(8,128)(2,1)} %copy-done.10, bf16[2,256,1152]{2,1,0:T(8,128)(2,1)} %collective-permute-done.50.refs_1_, bf16[2,256,1152]{2,1,0:T(8,128)(2,1)} %copy-done.18, ...), custom_call_target="tpu_custom_call", output_to_operand_aliasing={{}: (5, {})} | custom-call | flops 10000000000 | bytes 1 | tf_op jit(solution)/shard_map/pallas_call | solution.py:318
  525.6 7.9 %shard_map.209 = f32[2304,1024]{1,0:T(8,128)} custom-call(s32[4]{0:T(128)} %pad_add_fusion.here, bf16[2,288,1024]{2,1,0:T(8,128)(2,1)} %pad_maximum_fusion.4.refs_0_, bf16[2,288,1024]{2,1,0:T(8,128)(2,1)} %copy-done.32, bf16[2,288,1024]{2,1,0:T(8,128)(2,1)} %collective-permute-done.64.refs_2_, bf16[2,288,1024]{2,1,0:T(8,128)(2,1)} %copy-done.33), custom_call_target="tpu_custom_call" | custom-call | flops 5000000000 | bytes 1 | tf_op jit(solution)/shard_map/pallas_call | solution.py:318
  (281 shorter events, 214.8 us)
Async XLA Ops:
  32.2 34.3 %collective-permute-start.5 = (bf16[128,5632]{1,0:T(8,128)(2,1)}, bf16[128,5632]{1,0:T(8,128)(2,1)}, u32[]{:S(2)}, u32[]{:S(2)}) collective-permute-start(bf16[128,5632]{1,0:T(8,128)(2,1)} %pad_maximum_fusion), channel_id=1, source_target_pairs={{0,1},{1,0},{2,3},{3,2},{4,5},{5,4},{6,7},{7,6},{8,9},{9,8},{10,11... | collective-permute-start | bytes 4325384 | tf_op jit(solution)/shard_map/ppermute | solution.py:270
  42.2 55.2 %all-to-all-start = ((bf16[16,192,256]{2,1,0:T(8,128)(2,1)}), bf16[16,192,256]{2,1,0:T(8,128)(2,1)S(1)}, u32[]{:S(2)}, u32[]{:S(2)}) async-start(bf16[16,192,256]{2,1,0:T(8,128)(2,1)} %get-tuple-element.99), calls=%async_computation | async-start | bytes 3145728 | tf_op jit(solution)/shard_map/all_to_all | solution.py:1132
  68.3 62.7 %collective-permute-start.9 = (bf16[128,5632]{1,0:T(8,128)(2,1)}, bf16[128,5632]{1,0:T(8,128)(2,1)}, u32[]{:S(2)}, u32[]{:S(2)}) collective-permute-start(bf16[128,5632]{1,0:T(8,128)(2,1)} %collective-permute-done.5.refs_4_.refs_5_.refs_3_), channel_id=1, source_target_pairs={{0,4},{2,6},{4,0},{6,2},{8,12},{10,14},{12,8},{14,10},{16,20},{18,... | collective-permute-start | bytes 4325384 | tf_op jit(solution)/shard_map/ppermute | solution.py:261
  94.2 49.2 %collective-permute-start.11 = (bf16[128,4608]{1,0:T(8,128)(2,1)}, bf16[128,4608]{1,0:T(8,128)(2,1)}, u32[]{:S(2)}, u32[]{:S(2)}) collective-permute-start(bf16[128,4608]{1,0:T(8,128)(2,1)} %pad_maximum_fusion.1), channel_id=1, source_target_pairs={{0,1},{1,0},{2,3},{3,2},{4,5},{5,4},{6,7},{7,6},{8,9},{9,8},{10,11... | collective-permute-start | bytes 3538952 | tf_op jit(solution)/shard_map/ppermute | solution.py:270
  95.9 35.6 %collective-permute-start.16 = (bf16[2304,256]{1,0:T(8,128)(2,1)}, bf16[2304,256]{1,0:T(8,128)(2,1)}, u32[]{:S(2)}, u32[]{:S(2)}) collective-permute-start(bf16[2304,256]{1,0:T(8,128)(2,1)} %collective-permute-done.6.refs_8_), channel_id=1, source_target_pairs={{0,4},{2,6},{4,0},{6,2},{8,12},{10,14},{12,8},{14,10},{16,20},{18,... | collective-permute-start | bytes 3538952 | tf_op jit(solution)/shard_map/ppermute | solution.py:261
  188.0 39.1 %collective-permute-start.22 = (bf16[256,1792]{1,0:T(8,128)(2,1)}, bf16[256,1792]{1,0:T(8,128)(2,1)}, u32[]{:S(2)}, u32[]{:S(2)}) collective-permute-start(bf16[256,1792]{1,0:T(8,128)(2,1)} %get-tuple-element.126), channel_id=1, source_target_pairs={{0,2},{2,0},{4,6},{6,4},{8,10},{10,8},{12,14},{14,12},{16,18},{18,... | collective-permute-start | bytes 2752520 | tf_op jit(solution)/shard_map/ppermute | solution.py:258
  188.8 38.8 %collective-permute-start.23 = (bf16[256,1792]{1,0:T(8,128)(2,1)}, bf16[256,1792]{1,0:T(8,128)(2,1)}, u32[]{:S(2)}, u32[]{:S(2)}) collective-permute-start(bf16[256,1792]{1,0:T(8,128)(2,1)} %get-tuple-element.128), channel_id=1, source_target_pairs={{0,4},{2,6},{4,0},{6,2},{8,12},{10,14},{12,8},{14,10},{16,20},{18,... | collective-permute-start | bytes 2752520 | tf_op jit(solution)/shard_map/ppermute | solution.py:261
  190.5 56.4 %collective-permute-start.24 = (bf16[256,1792]{1,0:T(8,128)(2,1)}, bf16[256,1792]{1,0:T(8,128)(2,1)}, u32[]{:S(2)}, u32[]{:S(2)}) collective-permute-start(bf16[256,1792]{1,0:T(8,128)(2,1)} %collective-permute-done.18), channel_id=1, source_target_pairs={{0,4},{2,6},{4,0},{6,2},{8,12},{10,14},{12,8},{14,10},{16,20},{18,... | collective-permute-start | bytes 2752520 | tf_op jit(solution)/shard_map/ppermute | solution.py:261
  203.6 43.6 %collective-permute-start.19 = (bf16[1024,256]{1,0:T(8,128)(2,1)}, bf16[1024,256]{1,0:T(8,128)(2,1)}, u32[]{:S(2)}, u32[]{:S(2)}) collective-permute-start(bf16[1024,256]{1,0:T(8,128)(2,1)} %get-tuple-element.123.refs_0_), channel_id=1, source_target_pairs={{0,2},{2,0},{4,6},{6,4},{8,10},{10,8},{12,14},{14,12},{16,18},{18,... | collective-permute-start | bytes 1572872 | tf_op jit(solution)/shard_map/ppermute | solution.py:258
  203.6 43.6 %collective-permute-start.21 = (bf16[1024,256]{1,0:T(8,128)(2,1)}, bf16[1024,256]{1,0:T(8,128)(2,1)}, u32[]{:S(2)}, u32[]{:S(2)}) collective-permute-start(bf16[1024,256]{1,0:T(8,128)(2,1)} %collective-permute-done.20.refs_2_), channel_id=1, source_target_pairs={{0,2},{2,0},{4,6},{6,4},{8,10},{10,8},{12,14},{14,12},{16,18},{18,... | collective-permute-start | bytes 1572872 | tf_op jit(solution)/shard_map/ppermute | solution.py:258
  221.5 35.4 %all-to-all-start.2 = ((bf16[16,64,256]{2,1,0:T(8,128)(2,1)}), bf16[16,64,256]{2,1,0:T(8,128)(2,1)S(1)}, u32[]{:S(2)}, u32[]{:S(2)}) async-start(bf16[16,64,256]{2,1,0:T(8,128)(2,1)} %bitcast.100), calls=%async_computation.2 | async-start | bytes 1048576 | tf_op jit(solution)/shard_map/all_to_all | solution.py:1196
  227.7 62.9 %collective-permute-start.42 = (bf16[256,1792]{1,0:T(8,128)(2,1)}, bf16[256,1792]{1,0:T(8,128)(2,1)}, u32[]{:S(2)}, u32[]{:S(2)}) collective-permute-start(bf16[256,1792]{1,0:T(8,128)(2,1)} %get-tuple-element.166), channel_id=1, source_target_pairs={{0,2},{2,0},{4,6},{6,4},{8,10},{10,8},{12,14},{14,12},{16,18},{18,... | collective-permute-start | bytes 2752520 | tf_op jit(solution)/shard_map/ppermute | solution.py:258
  246.9 43.7 %collective-permute-start.43 = (bf16[256,1792]{1,0:T(8,128)(2,1)}, bf16[256,1792]{1,0:T(8,128)(2,1)}, u32[]{:S(2)}, u32[]{:S(2)}) collective-permute-start(bf16[256,1792]{1,0:T(8,128)(2,1)} %get-tuple-element.168), channel_id=1, source_target_pairs={{0,4},{2,6},{4,0},{6,2},{8,12},{10,14},{12,8},{14,10},{16,20},{18,... | collective-permute-start | bytes 2752520 | tf_op jit(solution)/shard_map/ppermute | solution.py:261
  255.2 35.4 %collective-permute-start.45 = (bf16[256,1792]{1,0:T(8,128)(2,1)}, bf16[256,1792]{1,0:T(8,128)(2,1)}, u32[]{:S(2)}, u32[]{:S(2)}) collective-permute-start(bf16[256,1792]{1,0:T(8,128)(2,1)} %collective-permute-done.44), channel_id=1, source_target_pairs={{0,4},{2,6},{4,0},{6,2},{8,12},{10,14},{12,8},{14,10},{16,20},{18,... | collective-permute-start | bytes 2752520 | tf_op jit(solution)/shard_map/ppermute | solution.py:261
  285.3 73.3 %all-to-all-start.3 = ((bf16[16,192,256]{2,1,0:T(8,128)(2,1)}), bf16[16,192,256]{2,1,0:T(8,128)(2,1)}, u32[]{:S(2)}, u32[]{:S(2)}) async-start(bf16[16,192,256]{2,1,0:T(8,128)(2,1)} %shard_map.201), calls=%async_computation.3 | async-start | bytes 3145728 | tf_op jit(solution)/shard_map/all_to_all | solution.py:1216
  328.8 51.9 %collective-permute-start.28 = (bf16[1024,256]{1,0:T(8,128)(2,1)S(1)}, bf16[1024,256]{1,0:T(8,128)(2,1)}, u32[]{:S(2)}, u32[]{:S(2)}) collective-permute-start(bf16[1024,256]{1,0:T(8,128)(2,1)S(1)} %bitcast.95), channel_id=1, source_target_pairs={{0,2},{2,0},{4,6},{6,4},{8,10},{10,8},{12,14},{14,12},{16,18},{18,... | collective-permute-start | bytes 1572872 | tf_op jit(solution)/shard_map/ppermute | solution.py:258
  328.9 52.9 %collective-permute-start.30 = (bf16[1024,256]{1,0:T(8,128)(2,1)}, bf16[1024,256]{1,0:T(8,128)(2,1)}, u32[]{:S(2)}, u32[]{:S(2)}) collective-permute-start(bf16[1024,256]{1,0:T(8,128)(2,1)} %collective-permute-done.29.refs_6_), channel_id=1, source_target_pairs={{0,2},{2,0},{4,6},{6,4},{8,10},{10,8},{12,14},{14,12},{16,18},{18,... | collective-permute-start | bytes 1572872 | tf_op jit(solution)/shard_map/ppermute | solution.py:258
  333.5 33.5 %collective-permute-start.54 = (bf16[256,1152]{1,0:T(8,128)(2,1)S(1)}, bf16[256,1152]{1,0:T(8,128)(2,1)}, u32[]{:S(2)}, u32[]{:S(2)}) collective-permute-start(bf16[256,1152]{1,0:T(8,128)(2,1)S(1)} %fusion.1), channel_id=1, source_target_pairs={{0,24},{2,26},{4,28},{6,30},{8,16},{10,18},{12,20},{14,22},{16,8},... | collective-permute-start | bytes 1769480 | tf_op jit(solution)/shard_map/ppermute | solution.py:267
  380.7 43.9 %collective-permute-start.55 = (bf16[256,1152]{1,0:T(8,128)(2,1)S(1)}, bf16[256,1152]{1,0:T(8,128)(2,1)S(1)}, u32[]{:S(2)}, u32[]{:S(2)}) collective-permute-start(bf16[256,1152]{1,0:T(8,128)(2,1)S(1)} %add_convert_fusion.3), channel_id=1, source_target_pairs={{0,8},{2,10},{4,12},{6,14},{8,0},{10,2},{12,4},{14,6},{16,24},{18,... | collective-permute-start | bytes 1769480 | tf_op jit(solution)/shard_map/ppermute | solution.py:264
  383.7 43.7 %collective-permute-start.61 = (bf16[288,1024]{1,0:T(8,128)(2,1)S(1)}, bf16[288,1024]{1,0:T(8,128)(2,1)S(1)}, u32[]{:S(2)}, u32[]{:S(2)}) collective-permute-start(bf16[288,1024]{1,0:T(8,128)(2,1)S(1)} %fusion), channel_id=1, source_target_pairs={{0,24},{2,26},{4,28},{6,30},{8,16},{10,18},{12,20},{14,22},{16,8},... | collective-permute-start | bytes 1769480 | tf_op jit(solution)/shard_map/ppermute | solution.py:267
  425.7 37.1 %collective-permute-start.57 = (bf16[2,256,1152]{2,1,0:T(8,128)(2,1)}, bf16[2,256,1152]{2,1,0:T(8,128)(2,1)}, u32[]{:S(2)}, u32[]{:S(2)}) collective-permute-start(bf16[2,256,1152]{2,1,0:T(8,128)(2,1)} %pad_maximum_fusion.3.refs_0_), channel_id=1, source_target_pairs={{0,4},{2,6},{4,0},{6,2},{8,12},{10,14},{12,8},{14,10},{16,20},{18,... | collective-permute-start | bytes 3538952 | tf_op jit(solution)/shard_map/ppermute | solution.py:261
  439.0 33.9 %collective-permute-start.51 = (bf16[2,256,1152]{2,1,0:T(8,128)(2,1)S(1)}, bf16[2,256,1152]{2,1,0:T(8,128)(2,1)S(1)}, u32[]{:S(2)}, u32[]{:S(2)}) collective-permute-start(bf16[2,256,1152]{2,1,0:T(8,128)(2,1)S(1)} %pad_maximum_fusion.2.refs_0_), channel_id=1, source_target_pairs={{0,4},{2,6},{4,0},{6,2},{8,12},{10,14},{12,8},{14,10},{16,20},{18,... | collective-permute-start | bytes 3538952 | tf_op jit(solution)/shard_map/ppermute | solution.py:261
  475.0 38.8 %collective-permute-start.52 = (bf16[2,256,1152]{2,1,0:T(8,128)(2,1)S(1)}, bf16[2,256,1152]{2,1,0:T(8,128)(2,1)}, u32[]{:S(2)}, u32[]{:S(2)}) collective-permute-start(bf16[2,256,1152]{2,1,0:T(8,128)(2,1)S(1)} %collective-permute-done.51.refs_2_), channel_id=1, source_target_pairs={{0,2},{2,0},{4,6},{6,4},{8,10},{10,8},{12,14},{14,12},{16,18},{18,... | collective-permute-start | bytes 3538952 | tf_op jit(solution)/shard_map/ppermute | solution.py:258
  475.2 48.4 %collective-permute-start.63 = (bf16[2,288,1024]{2,1,0:T(8,128)(2,1)}, bf16[2,288,1024]{2,1,0:T(8,128)(2,1)S(1)}, u32[]{:S(2)}, u32[]{:S(2)}) collective-permute-start(bf16[2,288,1024]{2,1,0:T(8,128)(2,1)} %pad_maximum_fusion.4.refs_0_), channel_id=1, source_target_pairs={{0,2},{2,0},{4,6},{6,4},{8,10},{10,8},{12,14},{14,12},{16,18},{18,... | collective-permute-start | bytes 3538952 | tf_op jit(solution)/shard_map/ppermute | solution.py:258
  (88 other events, 1409.2 us)

commit v7 on v6

--- a/solution.py
+++ b/solution.py
@@ -14,7 +14,7 @@
 TILE = 256
 CHUNKS = 2
 PROJECT = 0
-ATTEND = 0
+ATTEND = 22
 OUT = 0
 FFN = (0, 0)
 ATTEND_BACK = 25
@@ -278,17 +278,15 @@
         got, got_far = self.over_core(give), self.over_core(give_far)
         return (near, got, self.over_y(far), self.over_y(got_far))
 
-    def sum_depth(self, kept, got):
+    def sum_depth(self, kept, got, time=None):
         def half(index):
             return add(pick(kept, index, 0), pick(got, index, 0))
 
         given = self.over_z(half(1 - self.half))
         part = add(half(self.half), given)
-        full = add(part, self.mirror_z(part))
+        other = self.mirror_z(part)
+        full = add(part, other if time is None else after(other, time))
         return jnp.stack([full, self.over_z(full)])
-
-    def reduce(self, got, kept):
-        return self.spread_plane(self.sum_depth(kept, got))
 
 
 def pick(value, index, axis):
@@ -339,8 +337,7 @@
 def project_kernel(here, *refs):
     x_ref, gain_ref, own_ref = refs[:3]
     pieces, q_gain, k_gain, cos_ref, sin_ref = refs[3:7], refs[7], refs[8], refs[9], refs[10]
-    d_ref = refs[11]
-    sent, weight, q_ref, k_ref, q_scale, k_scale, early_ref, scale_ref = refs[12:]
+    sent, weight, q_ref, k_ref, q_scale, k_scale, normed_ref, scale_ref = refs[11:]
     core, y, side = here[1], here[2], here[3]
     rows = own_ref.shape[0]
     part = rows // 4
@@ -353,8 +350,7 @@
     scale = rms_scale(x)
     scale_ref[...] = scale
     normed = (x * scale * gain_ref[...]).astype(bf16)
-    early_ref[0] = d_ref[...]
-    early_ref[1] = normed
+    normed_ref[...] = normed.T
     cosine, sine = cos_ref[...], sin_ref[...]
     half = HD // 2
 
@@ -387,11 +383,11 @@
                 sent[head * per_group + copy, row : row + HD, :] = value
 
 
-def project(here, x, gain, own, pieces, q_gain, k_gain, cosine, sine, d_ffn):
+def project(here, x, gain, own, pieces, q_gain, k_gain, cosine, sine):
     tokens, width = x.shape
     f32, bf16 = jnp.float32, jnp.bfloat16
     shape = jax.ShapeDtypeStruct
-    arrays = [x, gain, own, *pieces, q_gain, k_gain, cosine, sine, d_ffn]
+    arrays = [x, gain, own, *pieces, q_gain, k_gain, cosine, sine]
     outs = [
         shape((HEADS, 3 * HD, tokens), bf16),
         shape((width, own.shape[1]), bf16),
@@ -399,7 +395,7 @@
         shape((KV_HEADS * HD, tokens), f32),
         shape((HEADS, tokens), f32),
         shape((KV_HEADS, tokens), f32),
-        shape((2, tokens, width), bf16),
+        shape((width, tokens), bf16),
         shape((tokens, 1), f32),
     ]
     return call_with_here(
@@ -414,16 +410,16 @@
 
 def attend_out_kernel(here, *refs):
     attn_ref, x_ref, gain_ref, own_ref = refs[:4]
-    pieces = refs[4:12]
-    weight, h_ref, scale_ref, two_ref, two_t_ref = refs[12:]
+    pieces = refs[4:20]
+    weight, h_ref, scale_ref, two_ref, two_t_ref = refs[20:]
     core, y, side = here[1], here[2], here[3]
     rows = own_ref.shape[0]
     part = rows // 4
     weight[pl.ds(pl.multiple_of(side * rows, rows), rows), :] = own_ref[...]
     for p in range(4):
         at = (1 - side) * rows + (((p % 2) ^ core) * 2 + ((p // 2) ^ y)) * part
-        for n in range(2):
-            piece = pieces[2 * p + n]
+        for n in range(4):
+            piece = pieces[4 * p + n]
             wide = piece.shape[1]
             weight[pl.ds(pl.multiple_of(at, part), part), n * wide : (n + 1) * wide] = piece[...]
     attn = attn_ref[...].T
@@ -443,14 +439,15 @@
     f32, bf16 = jnp.float32, jnp.bfloat16
     shape = jax.ShapeDtypeStruct
     part = own.shape[0] // 4
-    half = width // 2
-    first = pieces[0].shape[1] // half - 2
+    cuts = 4
+    part_width = width // cuts
+    first = pieces[0].shape[1] // part_width - cuts
     arrays = [attn, x, gain, own]
     specs = [whole(a) for a in arrays]
     for piece in pieces:
-        for n in range(2):
+        for n in range(cuts):
             arrays.append(piece)
-            specs.append(pl.BlockSpec((part, half), lambda i, here, n=n: (0, first + n)))
+            specs.append(pl.BlockSpec((part, part_width), lambda i, here, n=n: (0, first + n)))
     outs = [
         shape((width, width), bf16),
         shape((tokens, width), f32),
@@ -465,7 +462,8 @@
 
 def ffn_kernel(chunk, here, *refs):
     two_ref, d_ref, own_ref = refs[:3]
-    pieces, down_ref, down_pieces = refs[3:7], refs[7], refs[8:12]
+    pieces, down_ref, down_pieces = (refs[3:7], refs[7:11]), refs[11], refs[12:16]
+    refs = refs[4:]
     if chunk == 0:
         before_refs, refs = refs[12:13], refs[13:]
         near, far, give, give_far, out_ref, d_two_ref = refs[:6]
@@ -500,10 +498,10 @@
         for p in range(4):
             rows = pl.ds(pl.multiple_of((1 - side) * own_rows + quarter(p) * part, part), part)
             for kind in range(2):
-                begin = kind * columns + n * tile
+                begin = n * tile + (columns if kind == 1 and chunk == 1 else 0)
                 found.append(
                     pltpu.make_async_copy(
-                        pieces[p].at[:, begin : begin + tile],
+                        pieces[kind][p].at[:, begin : begin + tile],
                         weight.at[kind, rows, at],
                         weight_sem.at[n, 1 + 2 * p + kind],
                     )
@@ -646,7 +644,7 @@
             shape((1, width), f32),
         ]
     far_away = pl.BlockSpec(memory_space=pl.ANY)
-    arrays = [two, d_ffn, own, *pieces, down, *down_pieces, *before]
+    arrays = [two, d_ffn, own, *pieces[0], *pieces[1], down, *down_pieces, *before]
     specs = [whole(two), whole(d_ffn)] + [far_away] * (len(arrays) - 2)
     if gain is not None:
         arrays.append(gain)
@@ -722,10 +720,10 @@
 def down_product_kernel(here, *refs):
     planes, terms = refs[:4], (refs[4:8], refs[8:12])
     sent, kept, left, right = refs[12:]
-    tokens = planes[0].shape[1]
+    tokens = planes[0].shape[0]
     rows = left.shape[0]
     for i in range(4):
-        right[i * tokens : (i + 1) * tokens, :] = planes[i][0]
+        right[i * tokens : (i + 1) * tokens, :] = planes[i][...]
     for chunk in range(2):
         for i in range(4):
             share = terms[chunk][i]
@@ -747,8 +745,8 @@
                 sent[half] = product.astype(sent.dtype)
 
 
-def down_products(here, early_plane, first, second, rows):
-    _, tokens, columns = early_plane[0].shape
+def down_products(here, d_plane, first, second, rows):
+    tokens, columns = d_plane[0].shape
     outs = [
         jax.ShapeDtypeStruct((2, rows // 2, columns), jnp.bfloat16),
         jax.ShapeDtypeStruct((2, rows // 2, columns), jnp.float32),
@@ -757,8 +755,8 @@
         down_product_kernel,
         here,
         (1,),
-        [*early_plane, *first, *second],
-        [layer(a, 0) for a in early_plane] + [whole(a) for a in (*first, *second)],
+        [*d_plane, *first, *second],
+        [whole(a) for a in (*d_plane, *first, *second)],
         outs,
         [whole(o) for o in outs],
         [
@@ -851,14 +849,14 @@
 
 
 def attention_product_kernel(here, *refs):
-    normed, attn, terms, gains_ref, ffn_gain_ref = refs[:4], refs[4:8], refs[8:12], refs[12], refs[13]
-    sent, kept, left, right, left_out, right_out = refs[14:]
-    tokens = normed[0].shape[1]
+    planes, terms, gains_ref, ffn_gain_ref = refs[:4], refs[4:8], refs[8], refs[9]
+    sent, kept, left, right, left_out, right_out = refs[10:]
+    tokens = planes[0].shape[2]
     cut = right.shape[1]
     for i in range(4):
         at = slice(i * tokens, (i + 1) * tokens)
-        left[:, at] = normed[i][0].T
-        left_out[:, at] = attn[i][...]
+        left[:, at] = planes[i][0]
+        left_out[:, at] = planes[i][1]
         share = terms[i]
         right[at, :] = share[:cut].T
         right_out[at, :] = share[cut:]
@@ -887,8 +885,8 @@
         out_ref[1, step:, :] = jnp.zeros((GAIN_ROWS, out_ref.shape[2]), out_ref.dtype)
 
 
-def attention_products(here, early_plane, attn_plane, shares, gains, ffn_gain):
-    _, tokens, width = early_plane[0].shape
+def attention_products(here, pair_plane, shares, gains, ffn_gain):
+    _, width, tokens = pair_plane[0].shape
     cut = shares[0].shape[0] - tokens
     shape = (2, width // 4 + GAIN_ROWS, cut + tokens)
     outs = [jax.ShapeDtypeStruct(shape, jnp.bfloat16), jax.ShapeDtypeStruct(shape, jnp.float32)]
@@ -896,9 +894,8 @@
         attention_product_kernel,
         here,
         (1,),
-        [*early_plane, *attn_plane, *shares, gains, ffn_gain],
-        [layer(a, 1) for a in early_plane]
-        + [whole(a) for a in (*attn_plane, *shares, gains, ffn_gain)],
+        [*pair_plane, *shares, gains, ffn_gain],
+        [whole(a) for a in (*pair_plane, *shares, gains, ffn_gain)],
         outs,
         [whole(o) for o in outs],
         [
@@ -1108,35 +1105,33 @@
         return [piece[:, 0], piece[:, 1]]
 
     qkv_there = links.over_x(qkv_piece)
-    first_piece = jnp.concatenate([*gate_up_piece(0), quarter_rows(out_weight)], axis=1)
-    second_piece = jnp.concatenate(gate_up_piece(1), axis=1)
+    first_gate, first_up = gate_up_piece(0)
+    first_piece = jnp.concatenate([first_gate, quarter_rows(out_weight)], axis=1)
+    second_gate, second_up = gate_up_piece(1)
+    second_piece = jnp.concatenate([second_gate, second_up], axis=1)
     down_piece = lax.dynamic_slice_in_dim(
         down_weight, links.quarter * (width // 4), width // 4, 1
     )
     d_ffn = cotangent[0]
+    d_beside = links.over_y(d_ffn)
     tokens_here = tokens[0]
-    qkv_there = after(qkv_there, first_piece)
+    qkv_there = after(qkv_there, first_piece, d_beside)
     first_there = links.over_x(after(first_piece, qkv_there))
-    gate_up = jnp.transpose(after(gate_up_weight, qkv_there), (1, 0, 2))
-    qkv_beside = links.over_y(qkv_there)
-    qkv_pieces = (
-        qkv_there,
-        links.over_core(qkv_there),
-        qkv_beside,
-        links.over_core(after(qkv_beside, gate_up)),
-    )
-    sent, w_qkv, q_raw, k_raw, q_scale, k_scale, early, scale_one = project(
-        here, tokens_here, gain_attn[None], qkv_weight, qkv_pieces,
-        gain_query[:, None], gain_key[:, None], cosine[0], sine[0], d_ffn,
+    up_there = links.over_x(after(first_up, first_there))
+    qkv_pieces = links.spread_plane(qkv_there)
+    sent, w_qkv, q_raw, k_raw, q_scale, k_scale, normed, scale_one = project(
+        here, after(tokens_here, first_there), gain_attn[None], qkv_weight, qkv_pieces,
+        gain_query[:, None], gain_key[:, None], cosine[0], sine[0],
     )
     got = lax.all_to_all(sent, "ctx", 0, 0, tiled=True)
-    early_beside = links.over_y(early)
-    first_there = after(first_there, sent)
-    down_there = links.over_x(after(down_piece, first_there))
+    gate_up = jnp.transpose(after(gate_up_weight, sent), (1, 0, 2))
+    up_there = after(up_there, sent)
+    down_there = links.over_x(after(down_piece, up_there))
     first_beside = links.over_y(first_there)
+    up_beside = links.over_y(up_there)
     second_there = links.over_x(after(second_piece, down_there))
     down_beside = links.over_y(down_there)
-    got = after(got, down_there)
+    got = after(got, down_there, gate_up)
     q_place, q_start = q_place[None], q_start[None]
     shape = jax.ShapeDtypeStruct
     attn_sent, *held = kernel_call(
@@ -1156,6 +1151,7 @@
         [pltpu.VMEM((HD, kv_rows), bf16)],
         ATTEND,
     )
+    attn_sent = after(attn_sent, up_beside)
     attn_in = lax.dynamic_slice_in_dim(
         lax.all_to_all(attn_sent, "ctx", 0, 0, tiled=True), part * HEADS, HEADS
     ).reshape(q_width, rows_here)
@@ -1166,23 +1162,24 @@
         return (there, links.over_core(there), beside, links.over_core(beside))
 
     first_pieces = spread(first_there, first_beside, attn_sent)
+    up_pieces = spread(up_there, up_beside, attn_in)
     down_pieces = spread(down_there, down_beside, attn_in)
     second_pieces = links.spread_plane(second_there)
     w_out, h_one, scale_two, two, two_t = attend_out(
-        here, after(attn_in, early_beside), tokens_here, gain_ffn[None], out_weight, first_pieces
-    )
-    attn_beside = links.over_y(attn_in)
+        here, attn_in, tokens_here, gain_ffn[None], out_weight, first_pieces
+    )
+    d_plane = spread(d_ffn, d_beside, attn_sent)
+    two = after(two, d_plane[1], d_plane[3])
     two_beside = links.over_y(two_t)
     dealt_here, (out_sum, two_sum) = ffn(
-        here, 0, two, d_ffn, gate_up, first_pieces, down_weight, down_pieces, [h_one]
-    )
-    two_plane = (two_t, links.over_core(two_t), two_beside, links.over_core(two_beside))
+        here, 0, two, d_ffn, gate_up, (first_pieces, up_pieces), down_weight, down_pieces, [h_one]
+    )
     near, far, give, give_far = dealt_here
     got_far = links.over_core(give_far)
     first_shares = (near, links.over_core(give), links.over_y(far), links.over_y(got_far))
     out_sum = after(out_sum, got_far)
     dealt_here, (output, d_h_one, d_attn, d_heads, ffn_gain_term) = ffn(
-        here, 1, two, d_ffn, gate_up, second_pieces, down_weight, down_pieces,
+        here, 1, two, d_ffn, gate_up, (second_pieces, second_pieces), down_weight, down_pieces,
         [out_sum, two_sum, h_one, scale_two, w_out], gain_ffn[None],
     )
     second_shares = links.deal_plane(*dealt_here)
@@ -1191,13 +1188,15 @@
         value, beside = after(value, time), after(beside, time)
         return (value, links.over_core(value), beside, links.over_core(beside))
 
+    two_plane = plane(two_t, two_beside, d_heads)
     columns = ff_chunk // 2
     d_heads = d_heads.reshape(HEADS, HD, rows_here)
+    pair = jnp.stack([after(normed, d_heads), attn_in])
     d_got = lax.all_to_all(d_heads, "ctx", 0, 0, tiled=True)
     first_products = wide_products(
         here, two_plane, [after(v, d_heads) for v in first_shares], columns
     )
-    d_got = after(d_got, first_products[0])
+    d_got = after(d_got, first_products[0], pair)
     (d_sent,) = kernel_call(
         attend_back_kernel,
         tables,
@@ -1212,18 +1211,15 @@
         ATTEND_BACK,
     )
     first_got = links.over_x(first_products[0])
-    d_sent = after(d_sent, first_got)
+    d_sent = after(d_sent, first_got, *second_shares[2:])
     d_back = lax.all_to_all(d_sent, "ctx", 0, 0, tiled=True)
     second_products = wide_products(
         here, two_plane, [after(v, d_sent) for v in second_shares], columns
     )
-    early_plane = plane(early, early_beside, d_sent)
-    attn_plane = plane(attn_in, attn_beside, d_sent)
     down_terms = down_products(
-        here, early_plane, first_shares, second_shares, columns // 2
+        here, d_plane, first_shares, second_shares, columns // 2
     )
     second_got = links.over_x(after(second_products[0], first_got))
-    down_got = links.over_x(after(down_terms[0], second_got))
     *d_shares, d_inputs, gain_sums = attention_back(
         here,
         [
@@ -1231,19 +1227,24 @@
             cosine[0], sine[0], w_qkv, tokens_here, scale_one, gain_attn[None], d_h_one, d_attn,
         ],
     )
-    grad_gate_up = None
-    for chunk, (got, kept) in enumerate(
-        ((first_got, first_products[1]), (second_got, second_products[1]))
-    ):
-        grad_gate_up = place_gate_up(here, chunk, links.reduce(got, kept), grad_gate_up)
-    grad_down = place_down(here, links.reduce(down_got, down_terms[1]))
+    second_got = after(second_got, d_shares[0])
+    down_got = links.over_x(after(down_terms[0], second_got))
+    pair_plane = plane(pair, links.over_y(after(pair, d_sent)), d_shares[0])
+    first_pair = links.sum_depth(first_products[1], first_got, d_shares[0])
+    second_pair = links.sum_depth(second_products[1], second_got)
+    down_pair = links.sum_depth(down_terms[1], down_got)
+    grad_gate_up = place_gate_up(here, 0, links.spread_plane(first_pair), None)
+    second_spread = links.spread_plane(second_pair)
+    down_spread = links.spread_plane(after(down_pair, grad_gate_up))
     attention_terms = attention_products(
-        here, early_plane, attn_plane, links.deal_plane(*d_shares), gain_sums, ffn_gain_term
+        here, pair_plane, links.deal_plane(*d_shares), gain_sums, ffn_gain_term
     )
     cut = qkv_weight.shape[1] // 4
-    grad_qkv, grad_out, gain_sums = place_attention(
-        here, links.reduce(links.over_x(attention_terms[0]), attention_terms[1]), cut
-    )
+    attention_pair = links.sum_depth(attention_terms[1], links.over_x(attention_terms[0]))
+    grad_gate_up = place_gate_up(here, 1, second_spread, grad_gate_up)
+    attention_spread = links.spread_plane(after(attention_pair, grad_gate_up))
+    grad_down = place_down(here, down_spread)
+    grad_qkv, grad_out, gain_sums = place_attention(here, attention_spread, cut)
     at = links.side * (HD // 2)
     gain_grads = [
         gain_sums[0, :rows],

time: 554 us -> 568 us (1.025)
  waiting for transfers between devices: 216 us -> 234 us
    ppermute x9 -> x10, waiting for transfers between devices: 68.2 us -> 33.1 us  [over_x(): return lax.ppermute(value, 'fsdp', [(0, 1), (1, 0)])]
    ppermute x8, waiting for transfers between devices: 31.7 us -> 62.9 us  [over_z(): return lax.ppermute(value, 'ctx', self.route(lambda z, y, c: (z ^ 1, y, c)))]
    ppermute x4, waiting for transfers between devices: 8.02 us -> 30.1 us  [mirror_z(): lax.ppermute(value, 'ctx', self.route(lambda z, y, c: (self.depth - 1 - z...]
    ppermute x28 -> x30, waiting for transfers between devices: 0.07 us -> 8.8 us  [over_core(): return lax.ppermute(value, 'ctx', self.route(lambda z, y, c: (z, y, 1 - c)))]
    ppermute x17 -> x18, waiting for transfers between devices: 95.7 us -> 91.4 us  [over_y(): return lax.ppermute(value, 'ctx', self.route(lambda z, y, c: (z, 1 - y, c)))]
    unnamed x84 -> x76, local copies, waits for them, and re-layouts: 14.9 us -> 17.8 us
    ppermute x17 -> x18, starting transfers between devices: 21.4 us -> 20.1 us  [over_y(): return lax.ppermute(value, 'ctx', self.route(lambda z, y, c: (z, 1 - y, c)))]
    ppermute x9 -> x10, starting transfers between devices: 13.1 us -> 13.1 us  [over_x(): return lax.ppermute(value, 'fsdp', [(0, 1), (1, 0)])]
  transfers between devices with their start and end apart: 70 -> 74, of which waited for: 23 -> 27; matrix products, arithmetic and copies ran while one was open for 8% -> 8% of each run, Pallas kernels for 30% -> 27%
where the time goes in v7:
time: 568 us; the launch traced here: 559 us
  waiting for transfers between devices  234 us (41%)
  Pallas kernels  166 us (29%)
  starting transfers between devices  94.7 us (17%)
  local copies, waits for them, and re-layouts  45.4 us (8%)
  other arithmetic  16.6 us (3%)
    pallas_call x13, Pallas kernels, call_with_here(): pl.pallas_call(kernel, grid_spec=pltpu.PrefetchScalarGridSpec(num_scalar_...  120 us
    ppermute x18, waiting for transfers between devices, over_y(): return lax.ppermute(value, 'ctx', self.route(lambda z, y, c: (z, 1 - y, c)))  91.4 us
    ppermute x8, waiting for transfers between devices, over_z(): return lax.ppermute(value, 'ctx', self.route(lambda z, y, c: (z ^ 1, y, c)))  62.9 us
    pallas_call x2, Pallas kernels, kernel_call(): pl.pallas_call(kernel, out_shape=outs, in_specs=[smem] * len(tables) + [v...  46.9 us
    ppermute x10, waiting for transfers between devices, over_x(): return lax.ppermute(value, 'fsdp', [(0, 1), (1, 0)])  33.1 us
    ppermute x4, waiting for transfers between devices, mirror_z(): lax.ppermute(value, 'ctx', self.route(lambda z, y, c: (self.depth - 1 - z...  30.1 us
    ppermute x8, starting transfers between devices, over_z(): return lax.ppermute(value, 'ctx', self.route(lambda z, y, c: (z ^ 1, y, c)))  23.6 us
    ppermute x18, starting transfers between devices, over_y(): return lax.ppermute(value, 'ctx', self.route(lambda z, y, c: (z, 1 - y, c)))  20.1 us
  transfers between devices with their start and end apart: 74, of which 27 were waited for; matrix products, arithmetic and copies ran while one was open for 8% of the time, Pallas kernels for 27%

profile of v7, /device:TPU:0, one launch (start us, length us, event | category | flops | bytes accessed | tf_op | source)
XLA Modules:
  0.0 559.3 jit_solution(2945539885997307244)
XLA Ops:
  25.0 10.2 %collective-permute-done.5.refs_5_ = bf16[128,2048]{1,0:T(8,128)(2,1)} collective-permute-done((bf16[128,2048]{1,0:T(8,128)(2,1)}, bf16[128,2048]{1,0:T(8,128)(2,1)}, u32[]{:S(2)}, u32[]{:S(2)}) %collective-permute-start.5) | collective-permute-done | bytes 524320 | tf_op jit(solution)/shard_map/ppermute | solution.py:261
  62.6 12.0 %collective-permute-done.7.refs_7_ = bf16[128,2304]{1,0:T(8,128)(2,1)} collective-permute-done((bf16[128,2304]{1,0:T(8,128)(2,1)}, bf16[128,2304]{1,0:T(8,128)(2,1)}, u32[]{:S(2)}, u32[]{:S(2)}) %collective-permute-start.7) | collective-permute-done | bytes 589856 | tf_op jit(solution)/shard_map/ppermute | solution.py:270
  79.0 8.8 %copy.71 = bf16[512,2,4608]{2,0,1:T(8,128)(2,1)} copy(bf16[512,2,4608]{2,1,0:T(2,128)(2,1)} %param.15) | data formatting | bytes 18874368 | tf_op jit(solution)/shard_map/optimization_barrier | solution.py:301
  88.2 14.1 %collective-permute-done.8.refs_12_ = bf16[2304,256]{1,0:T(8,128)(2,1)} collective-permute-done((bf16[2304,256]{1,0:T(8,128)(2,1)}, bf16[2304,256]{1,0:T(8,128)(2,1)}, u32[]{:S(2)}, u32[]{:S(2)}) %collective-permute-start.8) | collective-permute-done | bytes 1179680 | tf_op jit(solution)/shard_map/ppermute | solution.py:270
  105.3 22.0 %shard_map.196 = (bf16[16,64,256]{2,1,0:T(8,128)(2,1)}, bf16[4096,64]{1,0:T(8,128)(2,1)S(1)}, bf16[64,4096]{1,0:T(8,128)(2,1)S(1)}, bf16[4096,64]{1,0:T(8,128)(2...) custom-call(s32[32]{0:T(128)S(1)} %broadcast_add_fusion.q_slot, ...), custom_call_target="tpu_custom_call" | custom-call | flops 22000001024 | bytes 1 | tf_op jit(solution)/shard_map/pallas_call | solution.py:226
  163.2 16.8 %shard_map.198 = (bf16[256,1792]{1,0:T(8,128)(2,1)}, bf16[256,1792]{1,0:T(8,128)(2,1)}, bf16[256,1792]{1,0:T(8,128)(2,1)}, bf16[256,1792]{1,0:T(8,128)(2,1)}, f32[256,1024]{1,0:T(8,128)}, /*index=5*/f32[256,1024]{1,0:T(8,128)}) custom-call(s32[4]{0:T(128)} %pad_add_fusion.here, bf16[256,1024]{1,0:T(8,128)(2,1)} %get-tuple-element.124.refs_0_, ...), custom_call_target="tpu_custom_call" | custom-call | flops 1 | bytes 1 | tf_op jit(solution)/shard_map/pallas_call | solution.py:316
  186.6 16.9 %shard_map.199 = (bf16[256,1792]{1,0:T(8,128)(2,1)}, bf16[256,1792]{1,0:T(8,128)(2,1)}, bf16[256,1792]{1,0:T(8,128)(2,1)}, bf16[256,1792]{1,0:T(8,128)(2,1)}, bf...) custom-call(s32[4]{0:T(128)} %pad_add_fusion.here, ...), custom_call_target="tpu_custom_call" | custom-call | flops 1 | bytes 1 | tf_op jit(solution)/shard_map/pallas_call | solution.py:316
  203.9 11.8 %collective-permute-done.26.refs_2_ = bf16[1024,256]{1,0:T(8,128)(2,1)} collective-permute-done((bf16[1024,256]{1,0:T(8,128)(2,1)}, bf16[1024,256]{1,0:T(8,128)(2,1)}, u32[]{:S(2)}, u32[]{:S(2)}) %collective-permute-start.26) | collective-permute-done | bytes 524320 | tf_op jit(solution)/shard_map/ppermute | solution.py:261
  224.7 14.9 %collective-permute-done.30.refs_7_ = bf16[256,1792]{1,0:T(8,128)(2,1)} collective-permute-done((bf16[256,1792]{1,0:T(8,128)(2,1)}, bf16[256,1792]{1,0:T(8,128)(2,1)}, u32[]{:S(2)}, u32[]{:S(2)}) %collective-permute-start.30) | collective-permute-done | bytes 917536 | tf_op jit(solution)/shard_map/ppermute | solution.py:261
  252.0 24.9 %shard_map.201 = bf16[16,192,256]{2,1,0:T(8,128)(2,1)} custom-call(s32[32]{0:T(128)S(1)} %broadcast_add_fusion.q_slot, s32[32]{0:T(128)S(1)} %get-tuple-element.205.kv_slot, s32[16]{0:T(128)S(1)} %get-tuple-element.226.first, s32[16]{0:T(128)S(1)} %get-tuple-element.227.last, bf16[16,64,256]{2,1,0:T(8,128)(2,1)S(1)} %all-to-all-done.2.d_ref, ...), custom_call_target="tpu_custom_call" | custom-call | flops 24999999488 | bytes 1 | tf_op jit(solution)/shard_map/pallas_call | solution.py:226
  299.5 25.4 %collective-permute-done.54 = bf16[256,1152]{1,0:T(8,128)(2,1)S(1)} collective-permute-done((bf16[256,1152]{1,0:T(8,128)(2,1)S(1)}, bf16[256,1152]{1,0:T(8,128)(2,1)S(1)}, u32[]{:S(2)}, u32[]{:S(2)}) %collective-permute-start.54) | collective-permute-done | bytes 589856 | tf_op jit(solution)/shard_map/ppermute | solution.py:264
  328.6 8.5 %shard_map.202 = (bf16[768,256]{1,0:T(8,128)(2,1)}, bf16[768,256]{1,0:T(8,128)(2,1)}, bf16[768,256]{1,0:T(8,128)(2,1)}, bf16[768,256]{1,0:T(8,128)(2,1)}, f32[256,1024]{1,0:T(8,128)}, /*index=5*/f32[8,1024]{1,0:T(8,128)}) custom-call(s32[4]{0:T(128)} %pad_add_fusion.here, bf16[16,192,256]{2,1,0:T(8,128)(2,1)} %all-to-all-done.3.refs_0_, ...), custom_call_target="tpu_custom_call" | custom-call | flops 12000000000 | bytes 1 | tf_op jit(solution)/shard_map/pallas_call | solution.py:316
  343.2 12.2 %collective-permute-start.56 = (bf16[256,1152]{1,0:T(8,128)(2,1)S(1)}, bf16[256,1152]{1,0:T(8,128)(2,1)S(1)}, u32[]{:S(2)}, u32[]{:S(2)}) collective-permute-start(bf16[256,1152]{1,0:T(8,128)(2,1)S(1)} %add_convert_fusion.3), channel_id=1, source_target_pairs={{0,8},{2,10},{4,12},{6,14},{8,0},{10,2},{12,4},{14,6},{16,24},{18,... | collective-permute-start | bytes 1769480 | tf_op jit(solution)/shard_map/ppermute | solution.py:264
  357.6 10.5 %collective-permute-done.56 = bf16[256,1152]{1,0:T(8,128)(2,1)S(1)} collective-permute-done((bf16[256,1152]{1,0:T(8,128)(2,1)S(1)}, bf16[256,1152]{1,0:T(8,128)(2,1)S(1)}, u32[]{:S(2)}, u32[]{:S(2)}) %collective-permute-start.56) | collective-permute-done | bytes 589856 | tf_op jit(solution)/shard_map/ppermute | solution.py:264
  369.8 9.8 %shard_map.208 = (bf16[2,288,1024]{2,1,0:T(8,128)(2,1)}, f32[2,288,1024]{2,1,0:T(8,128)}) custom-call(s32[4]{0:T(128)} %pad_add_fusion.here, bf16[256,1024]{1,0:T(8,128)(2,1)} %bitcast.95, bf16[256,1024]{1,0:T(8,128)(2,1)} %collective-permute-done.13.refs_1_, bf16[256,1024]{1,0:T(8,128)(2,1)} %collective-permute-done.1.refs_2_, ...), custom_call_target="tpu_custom_call" | custom-call | flops 8000000000 | bytes 1 | tf_op jit(solution)/shard_map/pallas_call | solution.py:316
  385.1 8.7 %collective-permute-done.39.refs_6_ = bf16[768,256]{1,0:T(8,128)(2,1)S(1)} collective-permute-done((bf16[768,256]{1,0:T(8,128)(2,1)S(1)}, bf16[768,256]{1,0:T(8,128)(2,1)S(1)}, u32[]{:S(2)}, u32[]{:S(2)}) %collective-permute-start.39) | collective-permute-done | bytes 393248 | tf_op jit(solution)/shard_map/ppermute | solution.py:261
  431.3 8.9 %collective-permute-done.50 = bf16[256,1152]{1,0:T(8,128)(2,1)S(1)} collective-permute-done((bf16[256,1152]{1,0:T(8,128)(2,1)S(1)}, bf16[256,1152]{1,0:T(8,128)(2,1)S(1)}, u32[]{:S(2)}, u32[]{:S(2)}) %collective-permute-start.50) | collective-permute-done | bytes 589856 | tf_op jit(solution)/shard_map/ppermute | solution.py:264
  452.7 11.6 %collective-permute-done.65 = bf16[288,1024]{1,0:T(8,128)(2,1)S(1)} collective-permute-done((bf16[288,1024]{1,0:T(8,128)(2,1)S(1)}, bf16[288,1024]{1,0:T(8,128)(2,1)S(1)}, u32[]{:S(2)}, u32[]{:S(2)}) %collective-permute-start.65) | collective-permute-done | bytes 589856 | tf_op jit(solution)/shard_map/ppermute | solution.py:267
  464.6 8.5 %collective-permute-done.44 = bf16[272,768]{1,0:T(8,128)(2,1)S(1)} collective-permute-done((bf16[272,768]{1,0:T(8,128)(2,1)S(1)}, bf16[272,768]{1,0:T(8,128)(2,1)S(1)}, u32[]{:S(2)}, u32[]{:S(2)}) %collective-permute-start.44) | collective-permute-done | bytes 417824 | tf_op jit(solution)/shard_map/ppermute | solution.py:267
  473.2 10.1 %collective-permute-done.66 = bf16[288,1024]{1,0:T(8,128)(2,1)S(1)} collective-permute-done((bf16[288,1024]{1,0:T(8,128)(2,1)S(1)}, bf16[288,1024]{1,0:T(8,128)(2,1)S(1)}, u32[]{:S(2)}, u32[]{:S(2)}) %collective-permute-start.66) | collective-permute-done | bytes 589856 | tf_op jit(solution)/shard_map/ppermute | solution.py:264
  485.6 9.7 %shard_map.205.refs_4_ = f32[512,2,4608]{2,1,0:T(2,128)} custom-call(s32[4]{0:T(128)} %pad_add_fusion.here, bf16[2,256,1152]{2,1,0:T(8,128)(2,1)} %copy-done.20, bf16[2,256,1152]{2,1,0:T(8,128)(2,1)} %copy-done.31, bf16[2,256,1152]{2,1,0:T(8,128)(2,1)} %collective-permute-done.58.refs_2_, bf16[2,256,1152]{2,1,0:T(8,128)(2,1)} %collective-permute-done.59.refs_3_), custom_call_target="tpu_custom_call" | custom-call | flops 10000000000 | bytes 1 | tf_op jit(solution)/shard_map/pallas_call | solution.py:316
  499.2 9.7 %shard_map.206 = f32[512,2,4608]{2,1,0:T(2,128)} custom-call(s32[4]{0:T(128)} %pad_add_fusion.here, bf16[2,256,1152]{2,1,0:T(8,128)(2,1)} %copy-done.12, bf16[2,256,1152]{2,1,0:T(8,128)(2,1)} %copy-done.18, bf16[2,256,1152]{2,1,0:T(8,128)(2,1)} %copy-done.17, bf16[2,256,1152]{2,1,0:T(8,128)(2,1)} %copy-done.19, ...), custom_call_target="tpu_custom_call", output_to_operand_aliasing={{}: (5, {})} | custom-call | flops 10000000000 | bytes 1 | tf_op jit(solution)/shard_map/pallas_call | solution.py:316
  509.2 15.1 %collective-permute-done.68.refs_2_ = bf16[2,288,1024]{2,1,0:T(8,128)(2,1)} collective-permute-done((bf16[2,288,1024]{2,1,0:T(8,128)(2,1)S(1)}, bf16[2,288,1024]{2,1,0:T(8,128)(2,1)}, u32[]{:S(2)}, u32[]{:S(2)}) %collective-permute-start.68) | collective-permute-done | bytes 1179680 | tf_op jit(solution)/shard_map/ppermute | solution.py:261
  524.8 16.0 %collective-permute-done.61.refs_2_ = bf16[2,272,768]{2,1,0:T(8,128)(2,1)} collective-permute-done((bf16[2,272,768]{2,1,0:T(8,128)(2,1)S(1)}, bf16[2,272,768]{2,1,0:T(8,128)(2,1)}, u32[]{:S(2)}, u32[]{:S(2)}) %collective-permute-start.61) | collective-permute-done | bytes 835616 | tf_op jit(solution)/shard_map/ppermute | solution.py:261
  (281 shorter events, 240.3 us)
Async XLA Ops:
  49.5 55.8 %all-to-all-start = ((bf16[16,192,256]{2,1,0:T(8,128)(2,1)}), bf16[16,192,256]{2,1,0:T(8,128)(2,1)}, u32[]{:S(2)}, u32[]{:S(2)}) async-start(bf16[16,192,256]{2,1,0:T(8,128)(2,1)} %get-tuple-element.111), calls=%async_computation | async-start | bytes 3145728 | tf_op jit(solution)/shard_map/all_to_all | solution.py:1126
  77.4 58.6 %collective-permute-start.11 = (bf16[128,3328]{1,0:T(8,128)(2,1)S(1)}, bf16[128,3328]{1,0:T(8,128)(2,1)}, u32[]{:S(2)}, u32[]{:S(2)}) collective-permute-start(bf16[128,3328]{1,0:T(8,128)(2,1)S(1)} %collective-permute-done.2.refs_4_.refs_5_.refs_6_.refs_7_.refs_3_), channel_id=1, source_target_pairs={{0,4},{2,6},{4,0},{6,2},{8,12},{10,14},{12,8},{14,10},{16,20},{18,... | collective-permute-start | bytes 2555912 | tf_op jit(solution)/shard_map/ppermute | solution.py:261
  87.9 42.2 %collective-permute-start.9 = (bf16[128,2304]{1,0:T(8,128)(2,1)}, bf16[128,2304]{1,0:T(8,128)(2,1)}, u32[]{:S(2)}, u32[]{:S(2)}) collective-permute-start(bf16[128,2304]{1,0:T(8,128)(2,1)} %collective-permute-done.7.refs_7_), channel_id=1, source_target_pairs={{0,4},{2,6},{4,0},{6,2},{8,12},{10,14},{12,8},{14,10},{16,20},{18,... | collective-permute-start | bytes 1769480 | tf_op jit(solution)/shard_map/ppermute | solution.py:261
  102.4 47.4 %collective-permute-start.15 = (bf16[128,4608]{1,0:T(8,128)(2,1)}, bf16[128,4608]{1,0:T(8,128)(2,1)}, u32[]{:S(2)}, u32[]{:S(2)}) collective-permute-start(bf16[128,4608]{1,0:T(8,128)(2,1)} %pad_maximum_fusion), channel_id=1, source_target_pairs={{0,1},{1,0},{2,3},{3,2},{4,5},{5,4},{6,7},{7,6},{8,9},{9,8},{10,11... | collective-permute-start | bytes 3538952 | tf_op jit(solution)/shard_map/ppermute | solution.py:270
  103.9 37.8 %collective-permute-start.20 = (bf16[2304,256]{1,0:T(8,128)(2,1)}, bf16[2304,256]{1,0:T(8,128)(2,1)}, u32[]{:S(2)}, u32[]{:S(2)}) collective-permute-start(bf16[2304,256]{1,0:T(8,128)(2,1)} %collective-permute-done.8.refs_12_), channel_id=1, source_target_pairs={{0,4},{2,6},{4,0},{6,2},{8,12},{10,14},{12,8},{14,10},{16,20},{18,... | collective-permute-start | bytes 3538952 | tf_op jit(solution)/shard_map/ppermute | solution.py:261
  180.6 39.6 %collective-permute-start.28 = (bf16[256,1792]{1,0:T(8,128)(2,1)}, bf16[256,1792]{1,0:T(8,128)(2,1)}, u32[]{:S(2)}, u32[]{:S(2)}) collective-permute-start(bf16[256,1792]{1,0:T(8,128)(2,1)} %get-tuple-element.145), channel_id=1, source_target_pairs={{0,2},{2,0},{4,6},{6,4},{8,10},{10,8},{12,14},{14,12},{16,18},{18,... | collective-permute-start | bytes 2752520 | tf_op jit(solution)/shard_map/ppermute | solution.py:258
  181.0 39.8 %collective-permute-start.29 = (bf16[256,1792]{1,0:T(8,128)(2,1)}, bf16[256,1792]{1,0:T(8,128)(2,1)}, u32[]{:S(2)}, u32[]{:S(2)}) collective-permute-start(bf16[256,1792]{1,0:T(8,128)(2,1)} %get-tuple-element.147), channel_id=1, source_target_pairs={{0,4},{2,6},{4,0},{6,2},{8,12},{10,14},{12,8},{14,10},{16,20},{18,... | collective-permute-start | bytes 2752520 | tf_op jit(solution)/shard_map/ppermute | solution.py:261
  181.8 33.9 %collective-permute-start.26 = (bf16[1024,256]{1,0:T(8,128)(2,1)}, bf16[1024,256]{1,0:T(8,128)(2,1)}, u32[]{:S(2)}, u32[]{:S(2)}) collective-permute-start(bf16[1024,256]{1,0:T(8,128)(2,1)} %get-tuple-element.141.refs_0_), channel_id=1, source_target_pairs={{0,4},{2,6},{4,0},{6,2},{8,12},{10,14},{12,8},{14,10},{16,20},{18,... | collective-permute-start | bytes 1572872 | tf_op jit(solution)/shard_map/ppermute | solution.py:261
  183.0 56.6 %collective-permute-start.30 = (bf16[256,1792]{1,0:T(8,128)(2,1)}, bf16[256,1792]{1,0:T(8,128)(2,1)}, u32[]{:S(2)}, u32[]{:S(2)}) collective-permute-start(bf16[256,1792]{1,0:T(8,128)(2,1)} %collective-permute-done.24), channel_id=1, source_target_pairs={{0,4},{2,6},{4,0},{6,2},{8,12},{10,14},{12,8},{14,10},{16,20},{18,... | collective-permute-start | bytes 2752520 | tf_op jit(solution)/shard_map/ppermute | solution.py:261
  203.5 36.1 %collective-permute-start.25 = (bf16[1024,256]{1,0:T(8,128)(2,1)}, bf16[1024,256]{1,0:T(8,128)(2,1)}, u32[]{:S(2)}, u32[]{:S(2)}) collective-permute-start(bf16[1024,256]{1,0:T(8,128)(2,1)} %get-tuple-element.141.refs_0_), channel_id=1, source_target_pairs={{0,2},{2,0},{4,6},{6,4},{8,10},{10,8},{12,14},{14,12},{16,18},{18,... | collective-permute-start | bytes 1572872 | tf_op jit(solution)/shard_map/ppermute | solution.py:258
  215.7 32.8 %all-to-all-start.2 = ((bf16[16,64,256]{2,1,0:T(8,128)(2,1)}), bf16[16,64,256]{2,1,0:T(8,128)(2,1)S(1)}, u32[]{:S(2)}, u32[]{:S(2)}) async-start(bf16[16,64,256]{2,1,0:T(8,128)(2,1)} %bitcast.104), calls=%async_computation.2 | async-start | bytes 1048576 | tf_op jit(solution)/shard_map/all_to_all | solution.py:1195
  220.8 56.1 %collective-permute-start.32 = (bf16[256,1792]{1,0:T(8,128)(2,1)}, bf16[256,1792]{1,0:T(8,128)(2,1)}, u32[]{:S(2)}, u32[]{:S(2)}) collective-permute-start(bf16[256,1792]{1,0:T(8,128)(2,1)} %get-tuple-element.161), channel_id=1, source_target_pairs={{0,4},{2,6},{4,0},{6,2},{8,12},{10,14},{12,8},{14,10},{16,20},{18,... | collective-permute-start | bytes 2752520 | tf_op jit(solution)/shard_map/ppermute | solution.py:261
  247.1 32.5 %collective-permute-start.31 = (bf16[2,256,1152]{2,1,0:T(8,128)(2,1)}, bf16[2,256,1152]{2,1,0:T(8,128)(2,1)}, u32[]{:S(2)}, u32[]{:S(2)}) collective-permute-start(bf16[2,256,1152]{2,1,0:T(8,128)(2,1)} %get-tuple-element.150), channel_id=1, source_target_pairs={{0,1},{1,0},{2,3},{3,2},{4,5},{5,4},{6,7},{7,6},{8,9},{9,8},{10,11... | collective-permute-start | bytes 3538952 | tf_op jit(solution)/shard_map/ppermute | solution.py:270
  279.5 49.1 %all-to-all-start.3 = ((bf16[16,192,256]{2,1,0:T(8,128)(2,1)}), bf16[16,192,256]{2,1,0:T(8,128)(2,1)}, u32[]{:S(2)}, u32[]{:S(2)}) async-start(bf16[16,192,256]{2,1,0:T(8,128)(2,1)} %shard_map.201), calls=%async_computation.3 | async-start | bytes 3145728 | tf_op jit(solution)/shard_map/all_to_all | solution.py:1215
  288.2 36.7 %collective-permute-start.54 = (bf16[256,1152]{1,0:T(8,128)(2,1)S(1)}, bf16[256,1152]{1,0:T(8,128)(2,1)S(1)}, u32[]{:S(2)}, u32[]{:S(2)}) collective-permute-start(bf16[256,1152]{1,0:T(8,128)(2,1)S(1)} %fusion.7), channel_id=1, source_target_pairs={{0,8},{2,10},{4,12},{6,14},{8,0},{10,2},{12,4},{14,6},{16,24},{18,... | collective-permute-start | bytes 1769480 | tf_op jit(solution)/shard_map/ppermute | solution.py:264
  297.5 57.9 %collective-permute-start.47 = (bf16[2,256,1152]{2,1,0:T(8,128)(2,1)}, bf16[2,256,1152]{2,1,0:T(8,128)(2,1)}, u32[]{:S(2)}, u32[]{:S(2)}) collective-permute-start(bf16[2,256,1152]{2,1,0:T(8,128)(2,1)} %get-tuple-element.192), channel_id=1, source_target_pairs={{0,1},{1,0},{2,3},{3,2},{4,5},{5,4},{6,7},{7,6},{8,9},{9,8},{10,11... | collective-permute-start | bytes 3538952 | tf_op jit(solution)/shard_map/ppermute | solution.py:270
  298.0 57.4 %collective-permute-start.36 = (bf16[2,1024,256]{2,1,0:T(8,128)(2,1)}, bf16[2,1024,256]{2,1,0:T(8,128)(2,1)}, u32[]{:S(2)}, u32[]{:S(2)}) collective-permute-start(bf16[2,1024,256]{2,1,0:T(8,128)(2,1)} %pad_maximum_fusion.4.refs_0_), channel_id=1, source_target_pairs={{0,4},{2,6},{4,0},{6,2},{8,12},{10,14},{12,8},{14,10},{16,20},{18,... | collective-permute-start | bytes 3145736 | tf_op jit(solution)/shard_map/ppermute | solution.py:261
  355.4 49.6 %collective-permute-start.35 = (bf16[2,1024,256]{2,1,0:T(8,128)(2,1)}, bf16[2,1024,256]{2,1,0:T(8,128)(2,1)}, u32[]{:S(2)}, u32[]{:S(2)}) collective-permute-start(bf16[2,1024,256]{2,1,0:T(8,128)(2,1)} %pad_maximum_fusion.4.refs_0_), channel_id=1, source_target_pairs={{0,2},{2,0},{4,6},{6,4},{8,10},{10,8},{12,14},{14,12},{16,18},{18,... | collective-permute-start | bytes 3145736 | tf_op jit(solution)/shard_map/ppermute | solution.py:258
  355.4 49.6 %collective-permute-start.37 = (bf16[2,1024,256]{2,1,0:T(8,128)(2,1)}, bf16[2,1024,256]{2,1,0:T(8,128)(2,1)}, u32[]{:S(2)}, u32[]{:S(2)}) collective-permute-start(bf16[2,1024,256]{2,1,0:T(8,128)(2,1)} %collective-permute-done.36.refs_2_), channel_id=1, source_target_pairs={{0,2},{2,0},{4,6},{6,4},{8,10},{10,8},{12,14},{14,12},{16,18},{18,... | collective-permute-start | bytes 3145736 | tf_op jit(solution)/shard_map/ppermute | solution.py:258
  393.9 48.2 %collective-permute-start.58 = (bf16[2,256,1152]{2,1,0:T(8,128)(2,1)S(1)}, bf16[2,256,1152]{2,1,0:T(8,128)(2,1)}, u32[]{:S(2)}, u32[]{:S(2)}) collective-permute-start(bf16[2,256,1152]{2,1,0:T(8,128)(2,1)S(1)} %pad_maximum_fusion.2.refs_0_), channel_id=1, source_target_pairs={{0,4},{2,6},{4,0},{6,2},{8,12},{10,14},{12,8},{14,10},{16,20},{18,... | collective-permute-start | bytes 3538952 | tf_op jit(solution)/shard_map/ppermute | solution.py:261
  427.8 36.5 %collective-permute-start.65 = (bf16[288,1024]{1,0:T(8,128)(2,1)S(1)}, bf16[288,1024]{1,0:T(8,128)(2,1)S(1)}, u32[]{:S(2)}, u32[]{:S(2)}) collective-permute-start(bf16[288,1024]{1,0:T(8,128)(2,1)S(1)} %fusion), channel_id=1, source_target_pairs={{0,24},{2,26},{4,28},{6,30},{8,16},{10,18},{12,20},{14,22},{16,8},... | collective-permute-start | bytes 1769480 | tf_op jit(solution)/shard_map/ppermute | solution.py:267
  440.3 43.3 %collective-permute-start.52 = (bf16[2,256,1152]{2,1,0:T(8,128)(2,1)S(1)}, bf16[2,256,1152]{2,1,0:T(8,128)(2,1)S(1)}, u32[]{:S(2)}, u32[]{:S(2)}) collective-permute-start(bf16[2,256,1152]{2,1,0:T(8,128)(2,1)S(1)} %pad_maximum_fusion.1.refs_0_), channel_id=1, source_target_pairs={{0,4},{2,6},{4,0},{6,2},{8,12},{10,14},{12,8},{14,10},{16,20},{18,... | collective-permute-start | bytes 3538952 | tf_op jit(solution)/shard_map/ppermute | solution.py:261
  442.1 42.5 %collective-permute-start.57 = (bf16[2,256,1152]{2,1,0:T(8,128)(2,1)S(1)}, bf16[2,256,1152]{2,1,0:T(8,128)(2,1)S(1)}, u32[]{:S(2)}, u32[]{:S(2)}) collective-permute-start(bf16[2,256,1152]{2,1,0:T(8,128)(2,1)S(1)} %pad_maximum_fusion.2.refs_0_), channel_id=1, source_target_pairs={{0,2},{2,0},{4,6},{6,4},{8,10},{10,8},{12,14},{14,12},{16,18},{18,... | collective-permute-start | bytes 3538952 | tf_op jit(solution)/shard_map/ppermute | solution.py:258
  442.1 43.5 %collective-permute-start.59 = (bf16[2,256,1152]{2,1,0:T(8,128)(2,1)}, bf16[2,256,1152]{2,1,0:T(8,128)(2,1)}, u32[]{:S(2)}, u32[]{:S(2)}) collective-permute-start(bf16[2,256,1152]{2,1,0:T(8,128)(2,1)} %collective-permute-done.58.refs_2_), channel_id=1, source_target_pairs={{0,2},{2,0},{4,6},{6,4},{8,10},{10,8},{12,14},{14,12},{16,18},{18,... | collective-permute-start | bytes 3538952 | tf_op jit(solution)/shard_map/ppermute | solution.py:258
  (87 other events, 1379.1 us)

commit v8 on v7

--- a/solution.py
+++ b/solution.py
@@ -16,7 +16,7 @@
 PROJECT = 0
 ATTEND = 22
 OUT = 0
-FFN = (0, 0)
+FFN = (15, 18)
 ATTEND_BACK = 25
 
 
@@ -268,6 +268,9 @@
 
     def over_x(self, value):
         return lax.ppermute(value, "fsdp", [(0, 1), (1, 0)])
+
+    def to_side(self, value, side):
+        return lax.ppermute(value, "fsdp", [(1 - side, side)])
 
     def spread_plane(self, value):
         across = self.over_core(value)
@@ -466,13 +469,13 @@
     refs = refs[4:]
     if chunk == 0:
         before_refs, refs = refs[12:13], refs[13:]
-        near, far, give, give_far, out_ref, d_two_ref = refs[:6]
-        refs = refs[6:]
+        near, far, give, give_far, hidden_ref, out_ref, d_two_ref = refs[:7]
+        refs = refs[7:]
     else:
         before_refs, gain_ref, refs = refs[12:17], refs[17], refs[18:]
-        near, far, give, give_far = refs[:4]
-        out_ref, d_h_ref, d_attn_ref, heads_ref, gain_term_ref = refs[4:9]
-        refs = refs[9:]
+        near, far, give, give_far, hidden_ref = refs[:5]
+        out_ref, d_h_ref, d_attn_ref, heads_ref, gain_term_ref = refs[5:10]
+        refs = refs[10:]
     weight, down, hidden_rows, out_sum, two_sum = refs[:5]
     held, weight_sem, down_sem, before_sem = refs[5:-3], refs[-3], refs[-2], refs[-1]
     core, y, side = here[1], here[2], here[3]
@@ -586,24 +589,9 @@
                 far[:, target] = first
                 give_far[:, target] = second
 
-    share = half // 2
-    target = slice(half, half + share)
-    for owner in range(2):
-        lower = hidden_rows[:, owner * half : owner * half + share]
-        upper = hidden_rows[:, owner * half + share : (owner + 1) * half]
-        close = jnp.where(y == 0, lower, upper)
-        distant = jnp.where(y == 0, upper, lower)
-
-        @pl.when(core == owner)
-        def _(close=close, distant=distant):
-            near[:, target] = close
-            far[:, target] = distant
-
-        @pl.when(core != owner)
-        def _(close=close, distant=distant):
-            give[:, target] = close
-            give_far[:, target] = distant
-
+    lower, upper = hidden_rows[:, :half], hidden_rows[:, half:]
+    hidden_ref[0] = jnp.where(core == 0, lower, upper)
+    hidden_ref[1] = jnp.where(core == 0, upper, lower)
     for copy in before:
         copy.wait()
     if chunk == 0:
@@ -629,10 +617,9 @@
 def ffn(here, chunk, two, d_ffn, own, pieces, down, down_pieces, before, gain=None):
     tokens, width = two.shape
     columns = own.shape[2] // CHUNKS
-    padded = (columns // 2 + columns // 4 + BLK - 1) // BLK * BLK
     shape = jax.ShapeDtypeStruct
     f32, bf16 = jnp.float32, jnp.bfloat16
-    outs = [shape((tokens, padded), bf16)] * 4
+    outs = [shape((tokens, columns // 2), bf16)] * 4 + [shape((2, tokens, columns // 2), bf16)]
     if chunk == 0:
         outs += [shape((tokens, width), f32)] * 2
     else:
@@ -672,17 +659,16 @@
         ],
         micros=FFN[chunk],
     )
-    return got[:4], got[4:]
+    return got[:4], got[4], got[5:]
 
 
 def wide_product_kernel(here, *refs):
     planes, terms = refs[:4], refs[4:8]
     sent, kept, left, right = refs[8:]
     tokens = planes[0].shape[1]
-    columns = right.shape[1]
     for i in range(4):
         left[:, i * tokens : (i + 1) * tokens] = planes[i][...]
-        right[i * tokens : (i + 1) * tokens, :] = terms[i][:, :columns]
+        right[i * tokens : (i + 1) * tokens, :] = terms[i][...]
     side = here[3]
     _, step, _ = kept.shape
     for half in range(2):
@@ -721,42 +707,37 @@
     planes, terms = refs[:4], (refs[4:8], refs[8:12])
     sent, kept, left, right = refs[12:]
     tokens = planes[0].shape[0]
-    rows = left.shape[0]
     for i in range(4):
         right[i * tokens : (i + 1) * tokens, :] = planes[i][...]
     for chunk in range(2):
-        for i in range(4):
-            share = terms[chunk][i]
-            at = share.shape[1] // BLK * BLK - (rows + BLK - 1) // BLK * BLK
-            left[:, i * tokens : (i + 1) * tokens] = share[:, at : at + rows].T
-        for half in range(2):
-            product = jnp.dot(
-                left[half * rows // 2 : (half + 1) * rows // 2, :],
-                right[...],
-                preferred_element_type=jnp.float32,
-            )
-
-            @pl.when(here[3] == chunk)
-            def _(product=product, half=half):
-                kept[half] = product
-
-            @pl.when(here[3] != chunk)
-            def _(product=product, half=half):
-                sent[half] = product.astype(sent.dtype)
-
-
-def down_products(here, d_plane, first, second, rows):
+
+        @pl.when(here[3] == chunk)
+        def _(chunk=chunk):
+            for i in range(4):
+                left[:, i * tokens : (i + 1) * tokens] = terms[chunk][i][0].T
+
+    _, step, _ = kept.shape
+    for half in range(2):
+        for owner, out_ref in ((1 - here[2], sent), (here[2], kept)):
+            place = pl.multiple_of(owner * 2 * step + half * step, step)
+            out_ref[half] = jnp.dot(
+                left[pl.ds(place, step), :], right[...], preferred_element_type=jnp.float32
+            ).astype(out_ref.dtype)
+
+
+def down_products(here, d_plane, first, second):
     tokens, columns = d_plane[0].shape
+    rows = first[0].shape[2]
     outs = [
-        jax.ShapeDtypeStruct((2, rows // 2, columns), jnp.bfloat16),
-        jax.ShapeDtypeStruct((2, rows // 2, columns), jnp.float32),
+        jax.ShapeDtypeStruct((2, rows // 4, columns), jnp.bfloat16),
+        jax.ShapeDtypeStruct((2, rows // 4, columns), jnp.float32),
     ]
     return call_with_here(
         down_product_kernel,
         here,
         (1,),
         [*d_plane, *first, *second],
-        [whole(a) for a in (*d_plane, *first, *second)],
+        [whole(a) for a in d_plane] + [layer(a, i % 2) for i, a in enumerate((*first, *second))],
         outs,
         [whole(o) for o in outs],
         [
@@ -1113,14 +1094,13 @@
         down_weight, links.quarter * (width // 4), width // 4, 1
     )
     d_ffn = cotangent[0]
-    d_beside = links.over_y(d_ffn)
     tokens_here = tokens[0]
-    qkv_there = after(qkv_there, first_piece, d_beside)
-    first_there = links.over_x(after(first_piece, qkv_there))
+    qkv_there = after(qkv_there, first_piece)
+    first_there = links.over_x(after(first_piece, qkv_piece))
     up_there = links.over_x(after(first_up, first_there))
     qkv_pieces = links.spread_plane(qkv_there)
     sent, w_qkv, q_raw, k_raw, q_scale, k_scale, normed, scale_one = project(
-        here, after(tokens_here, first_there), gain_attn[None], qkv_weight, qkv_pieces,
+        here, after(tokens_here, first_there, first_up), gain_attn[None], qkv_weight, qkv_pieces,
         gain_query[:, None], gain_key[:, None], cosine[0], sine[0],
     )
     got = lax.all_to_all(sent, "ctx", 0, 0, tiled=True)
@@ -1168,17 +1148,15 @@
     w_out, h_one, scale_two, two, two_t = attend_out(
         here, attn_in, tokens_here, gain_ffn[None], out_weight, first_pieces
     )
-    d_plane = spread(d_ffn, d_beside, attn_sent)
-    two = after(two, d_plane[1], d_plane[3])
     two_beside = links.over_y(two_t)
-    dealt_here, (out_sum, two_sum) = ffn(
+    dealt_here, first_hidden, (out_sum, two_sum) = ffn(
         here, 0, two, d_ffn, gate_up, (first_pieces, up_pieces), down_weight, down_pieces, [h_one]
     )
     near, far, give, give_far = dealt_here
     got_far = links.over_core(give_far)
     first_shares = (near, links.over_core(give), links.over_y(far), links.over_y(got_far))
     out_sum = after(out_sum, got_far)
-    dealt_here, (output, d_h_one, d_attn, d_heads, ffn_gain_term) = ffn(
+    dealt_here, second_hidden, (output, d_h_one, d_attn, d_heads, ffn_gain_term) = ffn(
         here, 1, two, d_ffn, gate_up, (second_pieces, second_pieces), down_weight, down_pieces,
         [out_sum, two_sum, h_one, scale_two, w_out], gain_ffn[None],
     )
@@ -1188,15 +1166,16 @@
         value, beside = after(value, time), after(beside, time)
         return (value, links.over_core(value), beside, links.over_core(beside))
 
-    two_plane = plane(two_t, two_beside, d_heads)
     columns = ff_chunk // 2
-    d_heads = d_heads.reshape(HEADS, HD, rows_here)
+    d_there = links.over_x(after(d_ffn, attn_sent))
+    first_hidden_there = links.to_side(first_hidden, 0)
+    second_hidden_there = links.to_side(second_hidden, 1)
+    d_heads = after(d_heads, two_beside, first_shares[2], first_hidden_there).reshape(HEADS, HD, rows_here)
     pair = jnp.stack([after(normed, d_heads), attn_in])
     d_got = lax.all_to_all(d_heads, "ctx", 0, 0, tiled=True)
-    first_products = wide_products(
-        here, two_plane, [after(v, d_heads) for v in first_shares], columns
-    )
-    d_got = after(d_got, first_products[0], pair)
+    two_plane = plane(two_t, two_beside, d_got)
+    first_products = wide_products(here, two_plane, first_shares, columns)
+    d_got = after(d_got, first_products[0], pair, second_hidden_there, d_there)
     (d_sent,) = kernel_call(
         attend_back_kernel,
         tables,
@@ -1216,8 +1195,14 @@
     second_products = wide_products(
         here, two_plane, [after(v, d_sent) for v in second_shares], columns
     )
+    def hidden_plane(hidden, there):
+        return (hidden, links.over_core(after(hidden, d_sent)), there, links.over_core(there))
+
+    d_plane = (d_ffn, links.over_core(after(d_ffn, d_got)), d_there, links.over_core(d_there))
     down_terms = down_products(
-        here, d_plane, first_shares, second_shares, columns // 2
+        here, d_plane,
+        hidden_plane(first_hidden, first_hidden_there),
+        hidden_plane(second_hidden, second_hidden_there),
     )
     second_got = links.over_x(after(second_products[0], first_got))
     *d_shares, d_inputs, gain_sums = attention_back(
@@ -1227,23 +1212,29 @@
             cosine[0], sine[0], w_qkv, tokens_here, scale_one, gain_attn[None], d_h_one, d_attn,
         ],
     )
-    second_got = after(second_got, d_shares[0])
-    down_got = links.over_x(after(down_terms[0], second_got))
+    near, far, give, give_far = d_shares
+    got, got_far = links.over_core(give), links.over_core(give_far)
+    attention_shares = (near, got, links.over_y(far), links.over_y(got_far))
+    second_got = after(second_got, got_far)
+    down_got = after(links.over_y(down_terms[0]), got_far)
     pair_plane = plane(pair, links.over_y(after(pair, d_sent)), d_shares[0])
-    first_pair = links.sum_depth(first_products[1], first_got, d_shares[0])
+    first_pair = links.sum_depth(first_products[1], after(first_got, d_back), got_far)
     second_pair = links.sum_depth(second_products[1], second_got)
     down_pair = links.sum_depth(down_terms[1], down_got)
-    grad_gate_up = place_gate_up(here, 0, links.spread_plane(first_pair), None)
+    first_placed = place_gate_up(here, 0, links.spread_plane(first_pair), None)
     second_spread = links.spread_plane(second_pair)
-    down_spread = links.spread_plane(after(down_pair, grad_gate_up))
+    down_spread = links.spread_plane(down_pair)
     attention_terms = attention_products(
-        here, pair_plane, links.deal_plane(*d_shares), gain_sums, ffn_gain_term
+        here, pair_plane, attention_shares, gain_sums, ffn_gain_term
     )
     cut = qkv_weight.shape[1] // 4
     attention_pair = links.sum_depth(attention_terms[1], links.over_x(attention_terms[0]))
-    grad_gate_up = place_gate_up(here, 1, second_spread, grad_gate_up)
-    attention_spread = links.spread_plane(after(attention_pair, grad_gate_up))
+    grad_gate_up = place_gate_up(here, 1, second_spread, first_placed)
     grad_down = place_down(here, down_spread)
+    beside = after(links.over_y(attention_pair), first_placed, grad_down)
+    attention_spread = (
+        attention_pair, links.over_core(attention_pair), beside, links.over_core(beside)
+    )
     grad_qkv, grad_out, gain_sums = place_attention(here, attention_spread, cut)
     at = links.side * (HD // 2)
     gain_grads = [

time: 568 us -> 587 us (1.033)
  starting transfers between devices: 94.7 us -> 130 us
  waiting for transfers between devices: 234 us -> 219 us
    ppermute x8, starting transfers between devices: 23.6 us -> 53.2 us  [over_z(): return lax.ppermute(value, 'ctx', self.route(lambda z, y, c: (z ^ 1, y, c)))]
    ppermute x10, waiting for transfers between devices: 33.1 us -> 60.2 us  [over_x(): return lax.ppermute(value, 'fsdp', [(0, 1), (1, 0)])]
    ppermute x18, waiting for transfers between devices: 91.4 us -> 66.5 us  [over_y(): return lax.ppermute(value, 'ctx', self.route(lambda z, y, c: (z, 1 - y, c)))]
    ppermute x8, waiting for transfers between devices: 62.9 us -> 39.5 us  [over_z(): return lax.ppermute(value, 'ctx', self.route(lambda z, y, c: (z ^ 1, y, c)))]
    all_to_all x1, waiting for transfers between devices: 0.01 us -> 12.3 us  [on_block(): d_got = lax.all_to_all(d_heads, 'ctx', 0, 0, tiled=True)]
    ppermute x4, waiting for transfers between devices: 30.1 us -> 20.4 us  [mirror_z(): lax.ppermute(value, 'ctx', self.route(lambda z, y, c: (self.depth - 1 - z...]
    unnamed x76 -> x98, local copies, waits for them, and re-layouts: 17.8 us -> 17.5 us
  transfers between devices with their start and end apart: 74 -> 80, of which waited for: 27 -> 28; matrix products, arithmetic and copies ran while one was open for 8% -> 8% of each run, Pallas kernels for 27% -> 26%
where the time goes in v8:
time: 587 us; the launch traced here: 579 us
  waiting for transfers between devices  219 us (37%)
  Pallas kernels  164 us (28%)
  starting transfers between devices  130 us (22%)
  local copies, waits for them, and re-layouts  42.1 us (7%)
  other arithmetic  21.9 us (4%)
    pallas_call x13, Pallas kernels, call_with_here(): pl.pallas_call(kernel, grid_spec=pltpu.PrefetchScalarGridSpec(num_scalar_...  117 us
    ppermute x18, waiting for transfers between devices, over_y(): return lax.ppermute(value, 'ctx', self.route(lambda z, y, c: (z, 1 - y, c)))  66.5 us
    ppermute x10, waiting for transfers between devices, over_x(): return lax.ppermute(value, 'fsdp', [(0, 1), (1, 0)])  60.2 us
    ppermute x8, starting transfers between devices, over_z(): return lax.ppermute(value, 'ctx', self.route(lambda z, y, c: (z ^ 1, y, c)))  53.2 us
    pallas_call x2, Pallas kernels, kernel_call(): pl.pallas_call(kernel, out_shape=outs, in_specs=[smem] * len(tables) + [v...  46.9 us
    ppermute x8, waiting for transfers between devices, over_z(): return lax.ppermute(value, 'ctx', self.route(lambda z, y, c: (z ^ 1, y, c)))  39.5 us
    ppermute x18, starting transfers between devices, over_y(): return lax.ppermute(value, 'ctx', self.route(lambda z, y, c: (z, 1 - y, c)))  23.2 us
    ppermute x4, waiting for transfers between devices, mirror_z(): lax.ppermute(value, 'ctx', self.route(lambda z, y, c: (self.depth - 1 - z...  20.4 us
  transfers between devices with their start and end apart: 80, of which 28 were waited for; matrix products, arithmetic and copies ran while one was open for 8% of the time, Pallas kernels for 26%

profile of v8, /device:TPU:0, one launch (start us, length us, event | category | flops | bytes accessed | tf_op | source)
XLA Modules:
  0.0 578.6 jit_solution(13664720032950490278)
XLA Ops:
  23.5 12.5 %collective-permute-done.1 = bf16[1088]{0:T(1024)(128)(2,1)S(1)} collective-permute-done((bf16[1088]{0:T(1024)(128)(2,1)S(1)}, bf16[1088]{0:T(1024)(128)(2,1)S(1)}, u32[]{:S(2)}, u32[]{:S(2)}) %collective-permute-start.1) | collective-permute-done | bytes 2208 | tf_op jit(solution)/shard_map/ppermute | solution.py:270
  58.0 12.0 %collective-permute-done.6.refs_7_ = bf16[128,2304]{1,0:T(8,128)(2,1)} collective-permute-done((bf16[128,2304]{1,0:T(8,128)(2,1)}, bf16[128,2304]{1,0:T(8,128)(2,1)}, u32[]{:S(2)}, u32[]{:S(2)}) %collective-permute-start.6) | collective-permute-done | bytes 589856 | tf_op jit(solution)/shard_map/ppermute | solution.py:270
  74.8 8.8 %copy.71 = bf16[512,2,4608]{2,0,1:T(8,128)(2,1)} copy(bf16[512,2,4608]{2,1,0:T(2,128)(2,1)} %param.15) | data formatting | bytes 18874368 | tf_op jit(solution)/shard_map/optimization_barrier | solution.py:304
  83.7 14.1 %collective-permute-done.7.refs_12_ = bf16[2304,256]{1,0:T(8,128)(2,1)} collective-permute-done((bf16[2304,256]{1,0:T(8,128)(2,1)}, bf16[2304,256]{1,0:T(8,128)(2,1)}, u32[]{:S(2)}, u32[]{:S(2)}) %collective-permute-start.7) | collective-permute-done | bytes 1179680 | tf_op jit(solution)/shard_map/ppermute | solution.py:270
  100.7 22.0 %shard_map.196 = (bf16[16,64,256]{2,1,0:T(8,128)(2,1)}, bf16[4096,64]{1,0:T(8,128)(2,1)S(1)}, bf16[64,4096]{1,0:T(8,128)(2,1)S(1)}, bf16[4096,64]{1,0:T(8,128)(2...) custom-call(s32[32]{0:T(128)S(1)} %broadcast_add_fusion.q_slot, ...), custom_call_target="tpu_custom_call" | custom-call | flops 22000001024 | bytes 1 | tf_op jit(solution)/shard_map/pallas_call | solution.py:226
  151.6 14.4 %collective-permute-done.14.refs_5_.refs_9_ = bf16[128,4608]{1,0:T(8,128)(2,1)} collective-permute-done((bf16[128,4608]{1,0:T(8,128)(2,1)}, bf16[128,4608]{1,0:T(8,128)(2,1)}, u32[]{:S(2)}, u32[]{:S(2)}) %collective-permute-start.14) | collective-permute-done | bytes 1179680 | tf_op jit(solution)/shard_map/ppermute | solution.py:261
  168.2 15.9 %shard_map.198 = (bf16[256,1152]{1,0:T(8,128)(2,1)}, bf16[256,1152]{1,0:T(8,128)(2,1)}, bf16[256,1152]{1,0:T(8,128)(2,1)}, bf16[256,1152]{1,0:T(8,128)(2,1)}, bf...) custom-call(s32[4]{0:T(128)} %pad_add_fusion.here, ...), custom_call_target="tpu_custom_call" | custom-call | flops 15000000512 | bytes 1 | tf_op jit(solution)/shard_map/pallas_call | solution.py:319
  189.7 16.2 %shard_map.199 = (bf16[256,1152]{1,0:T(8,128)(2,1)}, bf16[256,1152]{1,0:T(8,128)(2,1)}, bf16[256,1152]{1,0:T(8,128)(2,1)}, bf16[256,1152]{1,0:T(8,128)(2,1)}, bf...) custom-call(s32[4]{0:T(128)} %pad_add_fusion.here, ...), custom_call_target="tpu_custom_call" | custom-call | flops 18000001024 | bytes 1 | tf_op jit(solution)/shard_map/pallas_call | solution.py:319
  223.7 12.3 %all-to-all-done.2.d_ref = bf16[16,64,256]{2,1,0:T(8,128)(2,1)S(1)} async-done(((bf16[16,64,256]{2,1,0:T(8,128)(2,1)}), bf16[16,64,256]{2,1,0:T(8,128)(2,1)S(1)}, u32[]{:S(2)}, u32[]{:S(2)}) %all-to-all-start.2) | async-done | bytes 524320 | tf_op jit(solution)/shard_map/all_to_all | solution.py:1175
  255.5 20.4 %collective-permute-done.30.refs_2_ = bf16[256,1024]{1,0:T(8,128)(2,1)} collective-permute-done((bf16[256,1024]{1,0:T(8,128)(2,1)}, bf16[256,1024]{1,0:T(8,128)(2,1)}, u32[]{:S(2)}, u32[]{:S(2)}) %collective-permute-start.30) | collective-permute-done | bytes 524320 | tf_op jit(solution)/shard_map/ppermute | solution.py:270
  275.9 24.9 %shard_map.201 = bf16[16,192,256]{2,1,0:T(8,128)(2,1)} custom-call(s32[32]{0:T(128)S(1)} %broadcast_add_fusion.q_slot, s32[32]{0:T(128)S(1)} %get-tuple-element.205.kv_slot, s32[16]{0:T(128)S(1)} %get-tuple-element.226.first, s32[16]{0:T(128)S(1)} %get-tuple-element.227.last, bf16[16,64,256]{2,1,0:T(8,128)(2,1)S(1)} %all-to-all-done.2.d_ref, ...), custom_call_target="tpu_custom_call" | custom-call | flops 24999999488 | bytes 1 | tf_op jit(solution)/shard_map/pallas_call | solution.py:226
  324.8 8.7 %shard_map.205 = (bf16[2,288,1024]{2,1,0:T(8,128)(2,1)}, f32[2,288,1024]{2,1,0:T(8,128)}) custom-call(s32[4]{0:T(128)} %pad_add_fusion.here, bf16[256,1024]{1,0:T(8,128)(2,1)} %bitcast.20.refs_1_.refs_0_, bf16[256,1024]{1,0:T(8,128)(2,1)} %copy-done.43, bf16[256,1024]{1,0:T(8,128)(2,1)} %collective-permute-done.30.refs_2_, ...), custom_call_target="tpu_custom_call" | custom-call | flops 8000000000 | bytes 1 | tf_op jit(solution)/shard_map/pallas_call | solution.py:319
  339.8 8.5 %shard_map.202 = (bf16[768,256]{1,0:T(8,128)(2,1)}, bf16[768,256]{1,0:T(8,128)(2,1)}, bf16[768,256]{1,0:T(8,128)(2,1)}, bf16[768,256]{1,0:T(8,128)(2,1)}, f32[256,1024]{1,0:T(8,128)}, /*index=5*/f32[8,1024]{1,0:T(8,128)}) custom-call(s32[4]{0:T(128)} %pad_add_fusion.here, bf16[16,192,256]{2,1,0:T(8,128)(2,1)} %copy-done.13, ...), custom_call_target="tpu_custom_call" | custom-call | flops 12000000000 | bytes 1 | tf_op jit(solution)/shard_map/pallas_call | solution.py:319
  355.9 21.7 %collective-permute-done.60 = bf16[2,288,1024]{2,1,0:T(8,128)(2,1)} collective-permute-done((bf16[2,288,1024]{2,1,0:T(8,128)(2,1)}, bf16[2,288,1024]{2,1,0:T(8,128)(2,1)}, u32[]{:S(2)}, u32[]{:S(2)}) %collective-permute-start.60) | collective-permute-done | bytes 1179680 | tf_op jit(solution)/shard_map/ppermute | solution.py:261
  387.5 8.5 %collective-permute-done.61 = bf16[288,1024]{1,0:T(8,128)(2,1)} collective-permute-done((bf16[288,1024]{1,0:T(8,128)(2,1)}, bf16[288,1024]{1,0:T(8,128)(2,1)}, u32[]{:S(2)}, u32[]{:S(2)}) %collective-permute-start.61) | collective-permute-done | bytes 589856 | tf_op jit(solution)/shard_map/ppermute | solution.py:264
  417.5 14.4 %collective-permute-done.49 = bf16[256,1152]{1,0:T(8,128)(2,1)S(1)} collective-permute-done((bf16[256,1152]{1,0:T(8,128)(2,1)S(1)}, bf16[256,1152]{1,0:T(8,128)(2,1)S(1)}, u32[]{:S(2)}, u32[]{:S(2)}) %collective-permute-start.49) | collective-permute-done | bytes 589856 | tf_op jit(solution)/shard_map/ppermute | solution.py:267
  432.0 13.3 %collective-permute-start.50 = (bf16[256,1152]{1,0:T(8,128)(2,1)S(1)}, bf16[256,1152]{1,0:T(8,128)(2,1)S(1)}, u32[]{:S(2)}, u32[]{:S(2)}) collective-permute-start(bf16[256,1152]{1,0:T(8,128)(2,1)S(1)} %add_convert_fusion.6), channel_id=1, source_target_pairs={{0,8},{2,10},{4,12},{6,14},{8,0},{10,2},{12,4},{14,6},{16,24},{18,... | collective-permute-start | bytes 1769480 | tf_op jit(solution)/shard_map/ppermute | solution.py:264
  446.5 21.1 %collective-permute-start.63 = (bf16[288,1024]{1,0:T(8,128)(2,1)S(1)}, bf16[288,1024]{1,0:T(8,128)(2,1)S(1)}, u32[]{:S(2)}, u32[]{:S(2)}) collective-permute-start(bf16[288,1024]{1,0:T(8,128)(2,1)S(1)} %add_convert_fusion.3), channel_id=1, source_target_pairs={{0,8},{2,10},{4,12},{6,14},{8,0},{10,2},{12,4},{14,6},{16,24},{18,... | collective-permute-start | bytes 1769480 | tf_op jit(solution)/shard_map/ppermute | solution.py:264
  473.1 8.1 %collective-permute-start.72 = (bf16[256,1152]{1,0:T(8,128)(2,1)S(1)}, bf16[256,1152]{1,0:T(8,128)(2,1)S(1)}, u32[]{:S(2)}, u32[]{:S(2)}) collective-permute-start(bf16[256,1152]{1,0:T(8,128)(2,1)S(1)} %add_convert_fusion), channel_id=1, source_target_pairs={{0,8},{2,10},{4,12},{6,14},{8,0},{10,2},{12,4},{14,6},{16,24},{18,... | collective-permute-start | bytes 1769480 | tf_op jit(solution)/shard_map/ppermute | solution.py:264
  494.5 11.9 %collective-permute-done.72 = bf16[256,1152]{1,0:T(8,128)(2,1)S(1)} collective-permute-done((bf16[256,1152]{1,0:T(8,128)(2,1)S(1)}, bf16[256,1152]{1,0:T(8,128)(2,1)S(1)}, u32[]{:S(2)}, u32[]{:S(2)}) %collective-permute-start.72) | collective-permute-done | bytes 589856 | tf_op jit(solution)/shard_map/ppermute | solution.py:264
  512.1 8.5 %collective-permute-done.45 = bf16[272,768]{1,0:T(8,128)(2,1)S(1)} collective-permute-done((bf16[272,768]{1,0:T(8,128)(2,1)S(1)}, bf16[272,768]{1,0:T(8,128)(2,1)S(1)}, u32[]{:S(2)}, u32[]{:S(2)}) %collective-permute-start.45) | collective-permute-done | bytes 417824 | tf_op jit(solution)/shard_map/ppermute | solution.py:264
  521.3 15.9 %collective-permute-done.74.refs_2_ = bf16[2,256,1152]{2,1,0:T(8,128)(2,1)S(1)} collective-permute-done((bf16[2,256,1152]{2,1,0:T(8,128)(2,1)S(1)}, bf16[2,256,1152]{2,1,0:T(8,128)(2,1)S(1)}, u32[]{:S(2)}, u32[]{:S(2)}) %collective-permute-start.74) | collective-permute-done | bytes 1179680 | tf_op jit(solution)/shard_map/ppermute | solution.py:261
  537.7 10.0 %shard_map.204.refs_4_ = f32[512,2,4608]{2,1,0:T(2,128)} custom-call(s32[4]{0:T(128)} %pad_add_fusion.here, bf16[2,256,1152]{2,1,0:T(8,128)(2,1)} %pad_maximum_fusion.1.refs_0_, bf16[2,256,1152]{2,1,0:T(8,128)(2,1)} %collective-permute-done.51.refs_1_, bf16[2,256,1152]{2,1,0:T(8,128)(2,1)} %collective-permute-done.52.refs_2_, ...), custom_call_target="tpu_custom_call" | custom-call | flops 10000000000 | bytes 1 | tf_op jit(solution)/shard_map/pallas_call | solution.py:319
  558.4 9.7 %shard_map.209 = f32[512,2,4608]{2,1,0:T(2,128)} custom-call(s32[4]{0:T(128)} %pad_add_fusion.here, bf16[2,256,1152]{2,1,0:T(8,128)(2,1)} %copy-done.7, bf16[2,256,1152]{2,1,0:T(8,128)(2,1)} %copy-done.15, bf16[2,256,1152]{2,1,0:T(8,128)(2,1)} %copy-done.14, bf16[2,256,1152]{2,1,0:T(8,128)(2,1)} %copy-done.16, ...), custom_call_target="tpu_custom_call", output_to_operand_aliasing={{}: (5, {})} | custom-call | flops 10000000000 | bytes 1 | tf_op jit(solution)/shard_map/pallas_call | solution.py:319
  (315 shorter events, 242.8 us)
Async XLA Ops:
  47.0 53.7 %all-to-all-start = ((bf16[16,192,256]{2,1,0:T(8,128)(2,1)}), bf16[16,192,256]{2,1,0:T(8,128)(2,1)}, u32[]{:S(2)}, u32[]{:S(2)}) async-start(bf16[16,192,256]{2,1,0:T(8,128)(2,1)} %get-tuple-element.111), calls=%async_computation | async-start | bytes 3145728 | tf_op jit(solution)/shard_map/all_to_all | solution.py:1106
  72.8 57.9 %collective-permute-start.10 = (bf16[128,3328]{1,0:T(8,128)(2,1)S(1)}, bf16[128,3328]{1,0:T(8,128)(2,1)}, u32[]{:S(2)}, u32[]{:S(2)}) collective-permute-start(bf16[128,3328]{1,0:T(8,128)(2,1)S(1)} %collective-permute-done.refs_4_.refs_5_.refs_6_.refs_7_.refs_3_), channel_id=1, source_target_pairs={{0,4},{2,6},{4,0},{6,2},{8,12},{10,14},{12,8},{14,10},{16,20},{18,... | collective-permute-start | bytes 2555912 | tf_op jit(solution)/shard_map/ppermute | solution.py:261
  74.4 51.0 %collective-permute-start.8 = (bf16[128,2304]{1,0:T(8,128)(2,1)}, bf16[128,2304]{1,0:T(8,128)(2,1)}, u32[]{:S(2)}, u32[]{:S(2)}) collective-permute-start(bf16[128,2304]{1,0:T(8,128)(2,1)} %collective-permute-done.6.refs_7_), channel_id=1, source_target_pairs={{0,4},{2,6},{4,0},{6,2},{8,12},{10,14},{12,8},{14,10},{16,20},{18,... | collective-permute-start | bytes 1769480 | tf_op jit(solution)/shard_map/ppermute | solution.py:261
  97.8 33.6 %collective-permute-start.12 = (bf16[128,4608]{1,0:T(8,128)(2,1)}, bf16[128,4608]{1,0:T(8,128)(2,1)}, u32[]{:S(2)}, u32[]{:S(2)}) collective-permute-start(bf16[128,4608]{1,0:T(8,128)(2,1)} %pad_maximum_fusion), channel_id=1, source_target_pairs={{0,1},{1,0},{2,3},{3,2},{4,5},{5,4},{6,7},{7,6},{8,9},{9,8},{10,11... | collective-permute-start | bytes 3538952 | tf_op jit(solution)/shard_map/ppermute | solution.py:270
  99.3 38.5 %collective-permute-start.17 = (bf16[2304,256]{1,0:T(8,128)(2,1)}, bf16[2304,256]{1,0:T(8,128)(2,1)}, u32[]{:S(2)}, u32[]{:S(2)}) collective-permute-start(bf16[2304,256]{1,0:T(8,128)(2,1)} %collective-permute-done.7.refs_12_), channel_id=1, source_target_pairs={{0,4},{2,6},{4,0},{6,2},{8,12},{10,14},{12,8},{14,10},{16,20},{18,... | collective-permute-start | bytes 3538952 | tf_op jit(solution)/shard_map/ppermute | solution.py:261
  131.4 34.7 %collective-permute-start.14 = (bf16[128,4608]{1,0:T(8,128)(2,1)}, bf16[128,4608]{1,0:T(8,128)(2,1)}, u32[]{:S(2)}, u32[]{:S(2)}) collective-permute-start(bf16[128,4608]{1,0:T(8,128)(2,1)} %collective-permute-done.12.refs_3_.refs_7_), channel_id=1, source_target_pairs={{0,4},{2,6},{4,0},{6,2},{8,12},{10,14},{12,8},{14,10},{16,20},{18,... | collective-permute-start | bytes 3538952 | tf_op jit(solution)/shard_map/ppermute | solution.py:261
  236.6 39.3 %collective-permute-start.29 = (bf16[2,256,1152]{2,1,0:T(8,128)(2,1)}, bf16[2,256,1152]{2,1,0:T(8,128)(2,1)}, u32[]{:S(2)}, u32[]{:S(2)}) collective-permute-start(bf16[2,256,1152]{2,1,0:T(8,128)(2,1)} %get-tuple-element.186.refs_8_), channel_id=1, source_target_pairs={{0,1},{2,3},{4,5},{6,7},{8,9},{10,11},{12,13},{14,15},{16,17},{18,... | collective-permute-start | bytes 3538952 | tf_op jit(solution)/shard_map/ppermute | solution.py:273
  243.1 57.8 %collective-permute-start.32 = (bf16[256,1152]{1,0:T(8,128)(2,1)S(1)}, bf16[256,1152]{1,0:T(8,128)(2,1)S(1)}, u32[]{:S(2)}, u32[]{:S(2)}) collective-permute-start(bf16[256,1152]{1,0:T(8,128)(2,1)S(1)} %copy-done.36), channel_id=1, source_target_pairs={{0,4},{2,6},{4,0},{6,2},{8,12},{10,14},{12,8},{14,10},{16,20},{18,... | collective-permute-start | bytes 1769480 | tf_op jit(solution)/shard_map/ppermute | solution.py:261
  243.6 58.0 %collective-permute-start.34 = (bf16[256,1152]{1,0:T(8,128)(2,1)}, bf16[256,1152]{1,0:T(8,128)(2,1)S(1)}, u32[]{:S(2)}, u32[]{:S(2)}) collective-permute-start(bf16[256,1152]{1,0:T(8,128)(2,1)} %collective-permute-done.33), channel_id=1, source_target_pairs={{0,4},{2,6},{4,0},{6,2},{8,12},{10,14},{12,8},{14,10},{16,20},{18,... | collective-permute-start | bytes 1769480 | tf_op jit(solution)/shard_map/ppermute | solution.py:261
  253.6 48.9 %collective-permute-start.31 = (bf16[2,256,1152]{2,1,0:T(8,128)(2,1)}, bf16[2,256,1152]{2,1,0:T(8,128)(2,1)}, u32[]{:S(2)}, u32[]{:S(2)}) collective-permute-start(bf16[2,256,1152]{2,1,0:T(8,128)(2,1)} %get-tuple-element.145), channel_id=1, source_target_pairs={{0,1},{1,0},{2,3},{3,2},{4,5},{5,4},{6,7},{7,6},{8,9},{9,8},{10,11... | collective-permute-start | bytes 3538952 | tf_op jit(solution)/shard_map/ppermute | solution.py:270
  302.5 36.1 %all-to-all-start.3 = ((bf16[16,192,256]{2,1,0:T(8,128)(2,1)}), bf16[16,192,256]{2,1,0:T(8,128)(2,1)S(1)}, u32[]{:S(2)}, u32[]{:S(2)}) async-start(bf16[16,192,256]{2,1,0:T(8,128)(2,1)} %shard_map.201), calls=%async_computation.3 | async-start | bytes 3145728 | tf_op jit(solution)/shard_map/all_to_all | solution.py:1194
  318.3 64.9 %collective-permute-start.69 = (bf16[2,256,1152]{2,1,0:T(8,128)(2,1)}, bf16[2,256,1152]{2,1,0:T(8,128)(2,1)S(1)}, u32[]{:S(2)}, u32[]{:S(2)}) collective-permute-start(bf16[2,256,1152]{2,1,0:T(8,128)(2,1)} %get-tuple-element.201), channel_id=1, source_target_pairs={{0,1},{1,0},{2,3},{3,2},{4,5},{5,4},{6,7},{7,6},{8,9},{9,8},{10,11... | collective-permute-start | bytes 3538952 | tf_op jit(solution)/shard_map/ppermute | solution.py:270
  320.9 61.8 %collective-permute-start.36 = (bf16[2,1024,256]{2,1,0:T(8,128)(2,1)}, bf16[2,1024,256]{2,1,0:T(8,128)(2,1)}, u32[]{:S(2)}, u32[]{:S(2)}) collective-permute-start(bf16[2,1024,256]{2,1,0:T(8,128)(2,1)} %pad_maximum_fusion.4.refs_0_), channel_id=1, source_target_pairs={{0,4},{2,6},{4,0},{6,2},{8,12},{10,14},{12,8},{14,10},{16,20},{18,... | collective-permute-start | bytes 3145736 | tf_op jit(solution)/shard_map/ppermute | solution.py:261
  333.5 44.1 %collective-permute-start.60 = (bf16[2,288,1024]{2,1,0:T(8,128)(2,1)}, bf16[2,288,1024]{2,1,0:T(8,128)(2,1)}, u32[]{:S(2)}, u32[]{:S(2)}) collective-permute-start(bf16[2,288,1024]{2,1,0:T(8,128)(2,1)} %get-tuple-element.188), channel_id=1, source_target_pairs={{0,4},{2,6},{4,0},{6,2},{8,12},{10,14},{12,8},{14,10},{16,20},{18,... | collective-permute-start | bytes 3538952 | tf_op jit(solution)/shard_map/ppermute | solution.py:261
  351.2 34.3 %collective-permute-start.48 = (bf16[256,1152]{1,0:T(8,128)(2,1)}, bf16[256,1152]{1,0:T(8,128)(2,1)}, u32[]{:S(2)}, u32[]{:S(2)}) collective-permute-start(bf16[256,1152]{1,0:T(8,128)(2,1)} %fusion.5), channel_id=1, source_target_pairs={{0,8},{2,10},{4,12},{6,14},{8,0},{10,2},{12,4},{14,6},{16,24},{18,... | collective-permute-start | bytes 1769480 | tf_op jit(solution)/shard_map/ppermute | solution.py:264
  401.5 43.9 %collective-permute-start.70 = (bf16[256,1152]{1,0:T(8,128)(2,1)}, bf16[256,1152]{1,0:T(8,128)(2,1)S(1)}, u32[]{:S(2)}, u32[]{:S(2)}) collective-permute-start(bf16[256,1152]{1,0:T(8,128)(2,1)} %fusion.9), channel_id=1, source_target_pairs={{0,8},{2,10},{4,12},{6,14},{8,0},{10,2},{12,4},{14,6},{16,24},{18,... | collective-permute-start | bytes 1769480 | tf_op jit(solution)/shard_map/ppermute | solution.py:264
  407.5 38.8 %collective-permute-start.62 = (bf16[288,1024]{1,0:T(8,128)(2,1)S(1)}, bf16[288,1024]{1,0:T(8,128)(2,1)S(1)}, u32[]{:S(2)}, u32[]{:S(2)}) collective-permute-start(bf16[288,1024]{1,0:T(8,128)(2,1)S(1)} %fusion.1), channel_id=1, source_target_pairs={{0,24},{2,26},{4,28},{6,30},{8,16},{10,18},{12,20},{14,22},{16,8},... | collective-permute-start | bytes 1769480 | tf_op jit(solution)/shard_map/ppermute | solution.py:267
  417.4 51.4 %collective-permute-start.42 = (bf16[2,272,768]{2,1,0:T(8,128)(2,1)}, bf16[2,272,768]{2,1,0:T(8,128)(2,1)S(1)}, u32[]{:S(2)}, u32[]{:S(2)}) collective-permute-start(bf16[2,272,768]{2,1,0:T(8,128)(2,1)} %get-tuple-element.180), channel_id=1, source_target_pairs={{0,1},{1,0},{2,3},{3,2},{4,5},{5,4},{6,7},{7,6},{8,9},{9,8},{10,11... | collective-permute-start | bytes 2506760 | tf_op jit(solution)/shard_map/ppermute | solution.py:270
  432.0 35.6 %collective-permute-start.50 = (bf16[256,1152]{1,0:T(8,128)(2,1)S(1)}, bf16[256,1152]{1,0:T(8,128)(2,1)S(1)}, u32[]{:S(2)}, u32[]{:S(2)}) collective-permute-start(bf16[256,1152]{1,0:T(8,128)(2,1)S(1)} %add_convert_fusion.6), channel_id=1, source_target_pairs={{0,8},{2,10},{4,12},{6,14},{8,0},{10,2},{12,4},{14,6},{16,24},{18,... | collective-permute-start | bytes 1769480 | tf_op jit(solution)/shard_map/ppermute | solution.py:264
  446.5 37.9 %collective-permute-start.63 = (bf16[288,1024]{1,0:T(8,128)(2,1)S(1)}, bf16[288,1024]{1,0:T(8,128)(2,1)S(1)}, u32[]{:S(2)}, u32[]{:S(2)}) collective-permute-start(bf16[288,1024]{1,0:T(8,128)(2,1)S(1)} %add_convert_fusion.3), channel_id=1, source_target_pairs={{0,8},{2,10},{4,12},{6,14},{8,0},{10,2},{12,4},{14,6},{16,24},{18,... | collective-permute-start | bytes 1769480 | tf_op jit(solution)/shard_map/ppermute | solution.py:264
  468.8 39.6 %collective-permute-start.52 = (bf16[2,256,1152]{2,1,0:T(8,128)(2,1)}, bf16[2,256,1152]{2,1,0:T(8,128)(2,1)}, u32[]{:S(2)}, u32[]{:S(2)}) collective-permute-start(bf16[2,256,1152]{2,1,0:T(8,128)(2,1)} %pad_maximum_fusion.1.refs_0_), channel_id=1, source_target_pairs={{0,4},{2,6},{4,0},{6,2},{8,12},{10,14},{12,8},{14,10},{16,20},{18,... | collective-permute-start | bytes 3538952 | tf_op jit(solution)/shard_map/ppermute | solution.py:261
  481.2 40.0 %collective-permute-start.51 = (bf16[2,256,1152]{2,1,0:T(8,128)(2,1)}, bf16[2,256,1152]{2,1,0:T(8,128)(2,1)}, u32[]{:S(2)}, u32[]{:S(2)}) collective-permute-start(bf16[2,256,1152]{2,1,0:T(8,128)(2,1)} %pad_maximum_fusion.1.refs_0_), channel_id=1, source_target_pairs={{0,2},{2,0},{4,6},{6,4},{8,10},{10,8},{12,14},{14,12},{16,18},{18,... | collective-permute-start | bytes 3538952 | tf_op jit(solution)/shard_map/ppermute | solution.py:258
  485.6 35.0 %collective-permute-start.65 = (bf16[2,288,1024]{2,1,0:T(8,128)(2,1)}, bf16[2,288,1024]{2,1,0:T(8,128)(2,1)}, u32[]{:S(2)}, u32[]{:S(2)}) collective-permute-start(bf16[2,288,1024]{2,1,0:T(8,128)(2,1)} %pad_maximum_fusion.2.refs_0_), channel_id=1, source_target_pairs={{0,4},{2,6},{4,0},{6,2},{8,12},{10,14},{12,8},{14,10},{16,20},{18,... | collective-permute-start | bytes 3538952 | tf_op jit(solution)/shard_map/ppermute | solution.py:261
  521.2 35.0 %collective-permute-start.73 = (bf16[2,256,1152]{2,1,0:T(8,128)(2,1)S(1)}, bf16[2,256,1152]{2,1,0:T(8,128)(2,1)S(1)}, u32[]{:S(2)}, u32[]{:S(2)}) collective-permute-start(bf16[2,256,1152]{2,1,0:T(8,128)(2,1)S(1)} %pad_maximum_fusion.3.refs_0_), channel_id=1, source_target_pairs={{0,2},{2,0},{4,6},{6,4},{8,10},{10,8},{12,14},{14,12},{16,18},{18,... | collective-permute-start | bytes 3538952 | tf_op jit(solution)/shard_map/ppermute | solution.py:258
  (104 other events, 1463.2 us)

commit v9 on v8

--- a/solution.py
+++ b/solution.py
@@ -15,7 +15,7 @@
 CHUNKS = 2
 PROJECT = 0
 ATTEND = 22
-OUT = 0
+OUT = 5
 FFN = (15, 18)
 ATTEND_BACK = 25
 
@@ -241,7 +241,7 @@
         self.core = index % 2
         self.y = (index // 2) % 2
         self.side = lax.axis_index("fsdp")
-        self.half = ((index // 4 + 1) // 2) % 2
+        self.half = index // 4 % 2
         self.quarter = index % 2 * 2 + self.y
         self.here = jnp.stack([self.half, self.core, self.y, self.side]).astype(jnp.int32)
 
@@ -263,8 +263,8 @@
     def over_z(self, value):
         return lax.ppermute(value, "ctx", self.route(lambda z, y, c: (z ^ 1, y, c)))
 
-    def mirror_z(self, value):
-        return lax.ppermute(value, "ctx", self.route(lambda z, y, c: (self.depth - 1 - z, y, c)))
+    def over_two_z(self, value):
+        return lax.ppermute(value, "ctx", self.route(lambda z, y, c: (z ^ 2, y, c)))
 
     def over_x(self, value):
         return lax.ppermute(value, "fsdp", [(0, 1), (1, 0)])
@@ -286,9 +286,10 @@
             return add(pick(kept, index, 0), pick(got, index, 0))
 
         given = self.over_z(half(1 - self.half))
+        if time is not None:
+            given = after(given, time)
         part = add(half(self.half), given)
-        other = self.mirror_z(part)
-        full = add(part, other if time is None else after(other, time))
+        full = add(part, self.over_two_z(part))
         return jnp.stack([full, self.over_z(full)])
 
 
@@ -1087,7 +1088,8 @@
 
     qkv_there = links.over_x(qkv_piece)
     first_gate, first_up = gate_up_piece(0)
-    first_piece = jnp.concatenate([first_gate, quarter_rows(out_weight)], axis=1)
+    first_piece = first_gate
+    up_piece = jnp.concatenate([first_up, quarter_rows(out_weight)], axis=1)
     second_gate, second_up = gate_up_piece(1)
     second_piece = jnp.concatenate([second_gate, second_up], axis=1)
     down_piece = lax.dynamic_slice_in_dim(
@@ -1095,23 +1097,24 @@
     )
     d_ffn = cotangent[0]
     tokens_here = tokens[0]
-    qkv_there = after(qkv_there, first_piece)
-    first_there = links.over_x(after(first_piece, qkv_piece))
-    up_there = links.over_x(after(first_up, first_there))
+    qkv_there = after(qkv_there, first_piece, up_piece)
+    first_there = links.over_x(after(first_piece, qkv_there))
+    up_there = links.over_x(after(up_piece, first_there))
     qkv_pieces = links.spread_plane(qkv_there)
     sent, w_qkv, q_raw, k_raw, q_scale, k_scale, normed, scale_one = project(
-        here, after(tokens_here, first_there, first_up), gain_attn[None], qkv_weight, qkv_pieces,
+        here, after(tokens_here, first_there), gain_attn[None], qkv_weight, qkv_pieces,
         gain_query[:, None], gain_key[:, None], cosine[0], sine[0],
     )
     got = lax.all_to_all(sent, "ctx", 0, 0, tiled=True)
     gate_up = jnp.transpose(after(gate_up_weight, sent), (1, 0, 2))
     up_there = after(up_there, sent)
+    d_there = links.over_x(after(d_ffn, up_there))
     down_there = links.over_x(after(down_piece, up_there))
     first_beside = links.over_y(first_there)
     up_beside = links.over_y(up_there)
     second_there = links.over_x(after(second_piece, down_there))
     down_beside = links.over_y(down_there)
-    got = after(got, down_there, gate_up)
+    got = after(got, d_there, gate_up)
     q_place, q_start = q_place[None], q_start[None]
     shape = jax.ShapeDtypeStruct
     attn_sent, *held = kernel_call(
@@ -1131,7 +1134,7 @@
         [pltpu.VMEM((HD, kv_rows), bf16)],
         ATTEND,
     )
-    attn_sent = after(attn_sent, up_beside)
+    attn_sent = after(attn_sent, up_beside, first_beside)
     attn_in = lax.dynamic_slice_in_dim(
         lax.all_to_all(attn_sent, "ctx", 0, 0, tiled=True), part * HEADS, HEADS
     ).reshape(q_width, rows_here)
@@ -1141,16 +1144,20 @@
         there, beside = after(there, time), after(beside, time)
         return (there, links.over_core(there), beside, links.over_core(beside))
 
-    first_pieces = spread(first_there, first_beside, attn_sent)
-    up_pieces = spread(up_there, up_beside, attn_in)
+    first_pieces = spread(first_there, first_beside, attn_in)
+    up_pieces = spread(up_there, up_beside, attn_sent)
     down_pieces = spread(down_there, down_beside, attn_in)
-    second_pieces = links.spread_plane(second_there)
+    second_beside = links.over_y(second_there)
     w_out, h_one, scale_two, two, two_t = attend_out(
-        here, attn_in, tokens_here, gain_ffn[None], out_weight, first_pieces
+        here, attn_in, tokens_here, gain_ffn[None], out_weight, up_pieces
     )
     two_beside = links.over_y(two_t)
     dealt_here, first_hidden, (out_sum, two_sum) = ffn(
         here, 0, two, d_ffn, gate_up, (first_pieces, up_pieces), down_weight, down_pieces, [h_one]
+    )
+    second_beside = after(second_beside, out_sum)
+    second_pieces = (
+        second_there, links.over_core(second_there), second_beside, links.over_core(second_beside)
     )
     near, far, give, give_far = dealt_here
     got_far = links.over_core(give_far)
@@ -1167,7 +1174,6 @@
         return (value, links.over_core(value), beside, links.over_core(beside))
 
     columns = ff_chunk // 2
-    d_there = links.over_x(after(d_ffn, attn_sent))
     first_hidden_there = links.to_side(first_hidden, 0)
     second_hidden_there = links.to_side(second_hidden, 1)
     d_heads = after(d_heads, two_beside, first_shares[2], first_hidden_there).reshape(HEADS, HD, rows_here)
@@ -1175,7 +1181,15 @@
     d_got = lax.all_to_all(d_heads, "ctx", 0, 0, tiled=True)
     two_plane = plane(two_t, two_beside, d_got)
     first_products = wide_products(here, two_plane, first_shares, columns)
-    d_got = after(d_got, first_products[0], pair, second_hidden_there, d_there)
+    d_plane = (d_ffn, links.over_core(after(d_ffn, attn_sent)), d_there, links.over_core(d_there))
+    first_across, first_diagonal = (
+        links.over_core(after(first_hidden, d_heads)), links.over_core(first_hidden_there)
+    )
+    second_across = links.over_core(second_hidden)
+    d_got = after(
+        d_got, first_products[0], pair, second_hidden_there,
+        d_plane[1], d_plane[3], first_across, first_diagonal, second_across,
+    )
     (d_sent,) = kernel_call(
         attend_back_kernel,
         tables,
@@ -1195,16 +1209,13 @@
     second_products = wide_products(
         here, two_plane, [after(v, d_sent) for v in second_shares], columns
     )
-    def hidden_plane(hidden, there):
-        return (hidden, links.over_core(after(hidden, d_sent)), there, links.over_core(there))
-
-    d_plane = (d_ffn, links.over_core(after(d_ffn, d_got)), d_there, links.over_core(d_there))
     down_terms = down_products(
         here, d_plane,
-        hidden_plane(first_hidden, first_hidden_there),
-        hidden_plane(second_hidden, second_hidden_there),
-    )
-    second_got = links.over_x(after(second_products[0], first_got))
+        (first_hidden, first_across, first_hidden_there, first_diagonal),
+        (second_hidden, second_across, second_hidden_there, links.over_core(second_hidden_there)),
+    )
+    pair_beside = links.over_y(after(pair, d_sent))
+    d_back = after(d_back, down_terms[0], pair_beside, second_products[0])
     *d_shares, d_inputs, gain_sums = attention_back(
         here,
         [
@@ -1214,21 +1225,26 @@
     )
     near, far, give, give_far = d_shares
     got, got_far = links.over_core(give), links.over_core(give_far)
-    attention_shares = (near, got, links.over_y(far), links.over_y(got_far))
+    second_got = links.over_x(after(second_products[0], first_got))
+    attention_shares = (
+        near, got, links.over_y(after(far, second_got)), links.over_y(got_far)
+    )
     second_got = after(second_got, got_far)
-    down_got = after(links.over_y(down_terms[0]), got_far)
-    pair_plane = plane(pair, links.over_y(after(pair, d_sent)), d_shares[0])
+    down_got = links.over_y(after(down_terms[0], *attention_shares[2:]))
+    pair_plane = plane(pair, pair_beside, d_shares[0])
+    attention_terms = attention_products(
+        here, pair_plane, attention_shares, gain_sums, ffn_gain_term
+    )
+    attention_got = links.over_x(attention_terms[0])
+    down_got = after(down_got, attention_got)
     first_pair = links.sum_depth(first_products[1], after(first_got, d_back), got_far)
     second_pair = links.sum_depth(second_products[1], second_got)
     down_pair = links.sum_depth(down_terms[1], down_got)
     first_placed = place_gate_up(here, 0, links.spread_plane(first_pair), None)
-    second_spread = links.spread_plane(second_pair)
+    second_spread = links.spread_plane(after(second_pair, first_placed))
     down_spread = links.spread_plane(down_pair)
-    attention_terms = attention_products(
-        here, pair_plane, attention_shares, gain_sums, ffn_gain_term
-    )
     cut = qkv_weight.shape[1] // 4
-    attention_pair = links.sum_depth(attention_terms[1], links.over_x(attention_terms[0]))
+    attention_pair = links.sum_depth(attention_terms[1], attention_got)
     grad_gate_up = place_gate_up(here, 1, second_spread, first_placed)
     grad_down = place_down(here, down_spread)
     beside = after(links.over_y(attention_pair), first_placed, grad_down)

time: 587 us -> 617 us (1.051)
  the two profiles are of different devices: /device:TPU:0 before, /device:TPU:25 now
where the time goes in v9:
time: 617 us; the launch traced here: 609 us
  waiting for transfers between devices  275 us (45%)
  Pallas kernels  164 us (27%)
  starting transfers between devices  102 us (17%)
  local copies, waits for them, and re-layouts  45.4 us (7%)
  other arithmetic  20.7 us (3%)
    pallas_call x13, Pallas kernels, call_with_here(): pl.pallas_call(kernel, grid_spec=pltpu.PrefetchScalarGridSpec(num_scalar_...  117 us
    ppermute x18, waiting for transfers between devices, over_y(): return lax.ppermute(value, 'ctx', self.route(lambda z, y, c: (z, 1 - y, c)))  90 us
    ppermute x10, waiting for transfers between devices, over_x(): return lax.ppermute(value, 'fsdp', [(0, 1), (1, 0)])  68.1 us
    ppermute x8, waiting for transfers between devices, over_z(): return lax.ppermute(value, 'ctx', self.route(lambda z, y, c: (z ^ 1, y, c)))  50.3 us
    pallas_call x2, Pallas kernels, kernel_call(): pl.pallas_call(kernel, out_shape=outs, in_specs=[smem] * len(tables) + [v...  46.9 us
    ppermute x34, starting transfers between devices, over_core(): return lax.ppermute(value, 'ctx', self.route(lambda z, y, c: (z, y, 1 - c)))  35.9 us
    ppermute x4, waiting for transfers between devices, over_two_z(): return lax.ppermute(value, 'ctx', self.route(lambda z, y, c: (z ^ 2, y, c)))  33.9 us
    unnamed x110, local copies, waits for them, and re-layouts  17.3 us
  transfers between devices with their start and end apart: 80, of which 32 were waited for; matrix products, arithmetic and copies ran while one was open for 7% of the time, Pallas kernels for 25%

profile of v9, /device:TPU:25, one launch (start us, length us, event | category | flops | bytes accessed | tf_op | source)
XLA Modules:
  0.0 608.9 jit_solution(16958348575919396171)
XLA Ops:
  53.5 16.0 %collective-permute-done.6.refs_4_.refs_5_.refs_6_.refs_7_ = bf16[128,3328]{1,0:T(8,128)(2,1)} collective-permute-done((bf16[128,3328]{1,0:T(8,128)(2,1)S(1)}, bf16[128,3328]{1,0:T(8,128)(2,1)}, u32[]{:S(2)}, u32[]{:S(2)}) %collective-permute-start.6) | collective-permute-done | bytes 852000 | tf_op jit(solution)/shard_map/ppermute | solution.py:270
  73.2 8.8 %copy.71 = bf16[512,2,4608]{2,0,1:T(8,128)(2,1)} copy(bf16[512,2,4608]{2,1,0:T(2,128)(2,1)} %param.15) | data formatting | bytes 18874368 | tf_op jit(solution)/shard_map/optimization_barrier | solution.py:305
  82.3 13.8 %collective-permute-done.12.refs_12_ = bf16[2304,256]{1,0:T(8,128)(2,1)} collective-permute-done((bf16[2304,256]{1,0:T(8,128)(2,1)}, bf16[2304,256]{1,0:T(8,128)(2,1)}, u32[]{:S(2)}, u32[]{:S(2)}) %collective-permute-start.12) | collective-permute-done | bytes 1179680 | tf_op jit(solution)/shard_map/ppermute | solution.py:270
  97.3 10.1 %collective-permute-done.7.refs_2_ = bf16[256,1024]{1,0:T(8,128)(2,1)} collective-permute-done((bf16[256,1024]{1,0:T(8,128)(2,1)}, bf16[256,1024]{1,0:T(8,128)(2,1)}, u32[]{:S(2)}, u32[]{:S(2)}) %collective-permute-start.7) | collective-permute-done | bytes 524320 | tf_op jit(solution)/shard_map/ppermute | solution.py:270
  107.4 22.0 %shard_map.196 = (bf16[16,64,256]{2,1,0:T(8,128)(2,1)}, bf16[4096,64]{1,0:T(8,128)(2,1)S(1)}, bf16[64,4096]{1,0:T(8,128)(2,1)S(1)}, bf16[4096,64]{1,0:T(8,128)(2...) custom-call(s32[32]{0:T(128)S(1)} %broadcast_add_fusion.q_slot, ...), custom_call_target="tpu_custom_call" | custom-call | flops 22000001024 | bytes 1 | tf_op jit(solution)/shard_map/pallas_call | solution.py:226
  153.3 16.7 %collective-permute-done.13.refs_3_.refs_7_ = bf16[128,4608]{1,0:T(8,128)(2,1)} collective-permute-done((bf16[128,4608]{1,0:T(8,128)(2,1)}, bf16[128,4608]{1,0:T(8,128)(2,1)}, u32[]{:S(2)}, u32[]{:S(2)}) %collective-permute-start.13) | collective-permute-done | bytes 1179680 | tf_op jit(solution)/shard_map/ppermute | solution.py:270
  180.0 15.8 %shard_map.198 = (bf16[256,1152]{1,0:T(8,128)(2,1)}, bf16[256,1152]{1,0:T(8,128)(2,1)}, bf16[256,1152]{1,0:T(8,128)(2,1)}, bf16[256,1152]{1,0:T(8,128)(2,1)}, bf...) custom-call(s32[4]{0:T(128)} %pad_add_fusion.here, ...), custom_call_target="tpu_custom_call" | custom-call | flops 15000000512 | bytes 1 | tf_op jit(solution)/shard_map/pallas_call | solution.py:320
  206.4 16.2 %shard_map.199 = (bf16[256,1152]{1,0:T(8,128)(2,1)}, bf16[256,1152]{1,0:T(8,128)(2,1)}, bf16[256,1152]{1,0:T(8,128)(2,1)}, bf16[256,1152]{1,0:T(8,128)(2,1)}, bf...) custom-call(s32[4]{0:T(128)} %pad_add_fusion.here, ...), custom_call_target="tpu_custom_call" | custom-call | flops 18000001024 | bytes 1 | tf_op jit(solution)/shard_map/pallas_call | solution.py:320
  239.2 10.2 %all-to-all-done.2.d_ref = bf16[16,64,256]{2,1,0:T(8,128)(2,1)S(1)} async-done(((bf16[16,64,256]{2,1,0:T(8,128)(2,1)}), bf16[16,64,256]{2,1,0:T(8,128)(2,1)S(1)}, u32[]{:S(2)}, u32[]{:S(2)}) %all-to-all-start.2) | async-done | bytes 524320 | tf_op jit(solution)/shard_map/all_to_all | solution.py:1181
  278.9 24.9 %shard_map.201 = bf16[16,192,256]{2,1,0:T(8,128)(2,1)} custom-call(s32[32]{0:T(128)S(1)} %broadcast_add_fusion.q_slot, s32[32]{0:T(128)S(1)} %get-tuple-element.213.kv_slot, s32[16]{0:T(128)S(1)} %get-tuple-element.234.first, s32[16]{0:T(128)S(1)} %get-tuple-element.235.last, bf16[16,64,256]{2,1,0:T(8,128)(2,1)S(1)} %all-to-all-done.2.d_ref, ...), custom_call_target="tpu_custom_call" | custom-call | flops 24999999488 | bytes 1 | tf_op jit(solution)/shard_map/pallas_call | solution.py:226
  317.3 8.7 %shard_map.202 = (bf16[2,288,1024]{2,1,0:T(8,128)(2,1)}, f32[2,288,1024]{2,1,0:T(8,128)}) custom-call(s32[4]{0:T(128)} %pad_add_fusion.here, bf16[256,1024]{1,0:T(8,128)(2,1)} %bitcast.16.refs_1_.refs_0_, bf16[256,1024]{1,0:T(8,128)(2,1)} %collective-permute-done.31.refs_1_, bf16[256,1024]{1,0:T(8,128)(2,1)} %collective-permute-done.7.refs_2_, ...), custom_call_target="tpu_custom_call" | custom-call | flops 8000000000 | bytes 1 | tf_op jit(solution)/shard_map/pallas_call | solution.py:320
  335.5 19.2 %collective-permute-done.41.refs_2_ = bf16[2,1024,256]{2,1,0:T(8,128)(2,1)} collective-permute-done((bf16[2,1024,256]{2,1,0:T(8,128)(2,1)}, bf16[2,1024,256]{2,1,0:T(8,128)(2,1)}, u32[]{:S(2)}, u32[]{:S(2)}) %collective-permute-start.41) | collective-permute-done | bytes 1048608 | tf_op jit(solution)/shard_map/ppermute | solution.py:261
  376.3 8.8 %collective-permute-done.47.refs_6_ = bf16[768,256]{1,0:T(8,128)(2,1)S(1)} collective-permute-done((bf16[768,256]{1,0:T(8,128)(2,1)S(1)}, bf16[768,256]{1,0:T(8,128)(2,1)S(1)}, u32[]{:S(2)}, u32[]{:S(2)}) %collective-permute-start.47) | collective-permute-done | bytes 393248 | tf_op jit(solution)/shard_map/ppermute | solution.py:261
  418.3 11.5 %collective-permute-done.50 = bf16[2,272,768]{2,1,0:T(8,128)(2,1)S(1)} collective-permute-done((bf16[2,272,768]{2,1,0:T(8,128)(2,1)}, bf16[2,272,768]{2,1,0:T(8,128)(2,1)S(1)}, u32[]{:S(2)}, u32[]{:S(2)}) %collective-permute-start.50) | collective-permute-done | bytes 835616 | tf_op jit(solution)/shard_map/ppermute | solution.py:270
  431.6 21.1 %collective-permute-done.63 = bf16[288,1024]{1,0:T(8,128)(2,1)S(1)} collective-permute-done((bf16[288,1024]{1,0:T(8,128)(2,1)S(1)}, bf16[288,1024]{1,0:T(8,128)(2,1)S(1)}, u32[]{:S(2)}, u32[]{:S(2)}) %collective-permute-start.63) | collective-permute-done | bytes 589856 | tf_op jit(solution)/shard_map/ppermute | solution.py:264
  457.5 10.8 %collective-permute-done.71 = bf16[256,1152]{1,0:T(8,128)(2,1)S(1)} collective-permute-done((bf16[256,1152]{1,0:T(8,128)(2,1)S(1)}, bf16[256,1152]{1,0:T(8,128)(2,1)S(1)}, u32[]{:S(2)}, u32[]{:S(2)}) %collective-permute-start.71) | collective-permute-done | bytes 589856 | tf_op jit(solution)/shard_map/ppermute | solution.py:267
  468.5 14.9 %collective-permute-done.64 = bf16[288,1024]{1,0:T(8,128)(2,1)S(1)} collective-permute-done((bf16[288,1024]{1,0:T(8,128)(2,1)S(1)}, bf16[288,1024]{1,0:T(8,128)(2,1)S(1)}, u32[]{:S(2)}, u32[]{:S(2)}) %collective-permute-start.64) | collective-permute-done | bytes 589856 | tf_op jit(solution)/shard_map/ppermute | solution.py:267
  485.5 10.8 %collective-permute-done.72 = bf16[256,1152]{1,0:T(8,128)(2,1)S(1)} collective-permute-done((bf16[256,1152]{1,0:T(8,128)(2,1)S(1)}, bf16[256,1152]{1,0:T(8,128)(2,1)S(1)}, u32[]{:S(2)}, u32[]{:S(2)}) %collective-permute-start.72) | collective-permute-done | bytes 589856 | tf_op jit(solution)/shard_map/ppermute | solution.py:264
  496.5 12.5 %collective-permute-done.65 = bf16[288,1024]{1,0:T(8,128)(2,1)S(1)} collective-permute-done((bf16[288,1024]{1,0:T(8,128)(2,1)S(1)}, bf16[288,1024]{1,0:T(8,128)(2,1)S(1)}, u32[]{:S(2)}, u32[]{:S(2)}) %collective-permute-start.65) | collective-permute-done | bytes 589856 | tf_op jit(solution)/shard_map/ppermute | solution.py:264
  511.4 9.5 %shard_map.206.refs_4_ = f32[512,2,4608]{2,1,0:T(2,128)} custom-call(s32[4]{0:T(128)} %pad_add_fusion.here, bf16[2,256,1152]{2,1,0:T(8,128)(2,1)} %copy-done.13, bf16[2,256,1152]{2,1,0:T(8,128)(2,1)} %copy-done.33, bf16[2,256,1152]{2,1,0:T(8,128)(2,1)} %copy-done.30, bf16[2,256,1152]{2,1,0:T(8,128)(2,1)} %collective-permute-done.61.refs_3_), custom_call_target="tpu_custom_call" | custom-call | flops 10000000000 | bytes 1 | tf_op jit(solution)/shard_map/pallas_call | solution.py:320
  525.7 9.5 %collective-permute-done.67.refs_2_ = bf16[2,288,1024]{2,1,0:T(8,128)(2,1)} collective-permute-done((bf16[2,288,1024]{2,1,0:T(8,128)(2,1)}, bf16[2,288,1024]{2,1,0:T(8,128)(2,1)}, u32[]{:S(2)}, u32[]{:S(2)}) %collective-permute-start.67) | collective-permute-done | bytes 1179680 | tf_op jit(solution)/shard_map/ppermute | solution.py:261
  543.4 17.0 %collective-permute-done.74.refs_2_ = bf16[2,256,1152]{2,1,0:T(8,128)(2,1)S(1)} collective-permute-done((bf16[2,256,1152]{2,1,0:T(8,128)(2,1)S(1)}, bf16[2,256,1152]{2,1,0:T(8,128)(2,1)S(1)}, u32[]{:S(2)}, u32[]{:S(2)}) %collective-permute-start.74) | collective-permute-done | bytes 1179680 | tf_op jit(solution)/shard_map/ppermute | solution.py:261
  573.5 11.9 %collective-permute-done.55.refs_2_ = bf16[2,272,768]{2,1,0:T(8,128)(2,1)} collective-permute-done((bf16[2,272,768]{2,1,0:T(8,128)(2,1)}, bf16[2,272,768]{2,1,0:T(8,128)(2,1)}, u32[]{:S(2)}, u32[]{:S(2)}) %collective-permute-start.55) | collective-permute-done | bytes 835616 | tf_op jit(solution)/shard_map/ppermute | solution.py:261
  587.3 9.5 %shard_map.209 = f32[512,2,4608]{2,1,0:T(2,128)} custom-call(s32[4]{0:T(128)} %pad_add_fusion.here, bf16[2,256,1152]{2,1,0:T(8,128)(2,1)} %copy-done.6, bf16[2,256,1152]{2,1,0:T(8,128)(2,1)} %copy-done.12, bf16[2,256,1152]{2,1,0:T(8,128)(2,1)} %copy-done.11, bf16[2,256,1152]{2,1,0:T(8,128)(2,1)} %collective-permute-done.75.refs_3_, ...), custom_call_target="tpu_custom_call", output_to_operand_aliasing={{}: (5, {})} | custom-call | flops 10000000000 | bytes 1 | tf_op jit(solution)/shard_map/pallas_call | solution.py:320
  (328 shorter events, 277.0 us)
Async XLA Ops:
  41.8 65.6 %all-to-all-start = ((bf16[16,192,256]{2,1,0:T(8,128)(2,1)}), bf16[16,192,256]{2,1,0:T(8,128)(2,1)}, u32[]{:S(2)}, u32[]{:S(2)}) async-start(bf16[16,192,256]{2,1,0:T(8,128)(2,1)} %get-tuple-element.115), calls=%async_computation | async-start | bytes 3145728 | tf_op jit(solution)/shard_map/all_to_all | solution.py:1108
  70.8 36.6 %collective-permute-start.7 = (bf16[256,1024]{1,0:T(8,128)(2,1)}, bf16[256,1024]{1,0:T(8,128)(2,1)}, u32[]{:S(2)}, u32[]{:S(2)}) collective-permute-start(bf16[256,1024]{1,0:T(8,128)(2,1)} %bitcast.16.refs_1_.refs_0_), channel_id=1, source_target_pairs={{0,1},{1,0},{2,3},{3,2},{4,5},{5,4},{6,7},{7,6},{8,9},{9,8},{10,11... | collective-permute-start | bytes 1572872 | tf_op jit(solution)/shard_map/ppermute | solution.py:270
  72.0 60.1 %collective-permute-start.9 = (bf16[128,2304]{1,0:T(8,128)(2,1)}, bf16[128,2304]{1,0:T(8,128)(2,1)}, u32[]{:S(2)}, u32[]{:S(2)}) collective-permute-start(bf16[128,2304]{1,0:T(8,128)(2,1)} %collective-permute-done.1.refs_3_), channel_id=1, source_target_pairs={{0,4},{2,6},{4,0},{6,2},{8,12},{10,14},{12,8},{14,10},{16,20},{18,... | collective-permute-start | bytes 1769480 | tf_op jit(solution)/shard_map/ppermute | solution.py:261
  82.1 50.1 %collective-permute-start.8 = (bf16[128,3328]{1,0:T(8,128)(2,1)}, bf16[128,3328]{1,0:T(8,128)(2,1)}, u32[]{:S(2)}, u32[]{:S(2)}) collective-permute-start(bf16[128,3328]{1,0:T(8,128)(2,1)} %collective-permute-done.6.refs_4_.refs_5_.refs_6_.refs_7_), channel_id=1, source_target_pairs={{0,4},{2,6},{4,0},{6,2},{8,12},{10,14},{12,8},{14,10},{16,20},{18,... | collective-permute-start | bytes 2555912 | tf_op jit(solution)/shard_map/ppermute | solution.py:261
  96.1 48.2 %collective-permute-start.19 = (bf16[2304,256]{1,0:T(8,128)(2,1)}, bf16[2304,256]{1,0:T(8,128)(2,1)}, u32[]{:S(2)}, u32[]{:S(2)}) collective-permute-start(bf16[2304,256]{1,0:T(8,128)(2,1)} %collective-permute-done.12.refs_12_), channel_id=1, source_target_pairs={{0,4},{2,6},{4,0},{6,2},{8,12},{10,14},{12,8},{14,10},{16,20},{18,... | collective-permute-start | bytes 3538952 | tf_op jit(solution)/shard_map/ppermute | solution.py:261
  201.5 28.9 %collective-permute-start.25 = (bf16[2,256,1152]{2,1,0:T(8,128)(2,1)}, bf16[2,256,1152]{2,1,0:T(8,128)(2,1)}, u32[]{:S(2)}, u32[]{:S(2)}) collective-permute-start(bf16[2,256,1152]{2,1,0:T(8,128)(2,1)} %get-tuple-element.156.refs_4_), channel_id=1, source_target_pairs={{1,0},{3,2},{5,4},{7,6},{9,8},{11,10},{13,12},{15,14},{17,16},{19,... | collective-permute-start | bytes 3538952 | tf_op jit(solution)/shard_map/ppermute | solution.py:273
  269.4 34.5 %collective-permute-start.37 = (bf16[256,1152]{1,0:T(8,128)(2,1)S(1)}, bf16[256,1152]{1,0:T(8,128)(2,1)S(1)}, u32[]{:S(2)}, u32[]{:S(2)}) collective-permute-start(bf16[256,1152]{1,0:T(8,128)(2,1)S(1)} %copy-done.41), channel_id=1, source_target_pairs={{0,4},{2,6},{4,0},{6,2},{8,12},{10,14},{12,8},{14,10},{16,20},{18,... | collective-permute-start | bytes 1769480 | tf_op jit(solution)/shard_map/ppermute | solution.py:261
  269.7 34.9 %collective-permute-start.39 = (bf16[256,1152]{1,0:T(8,128)(2,1)}, bf16[256,1152]{1,0:T(8,128)(2,1)S(1)}, u32[]{:S(2)}, u32[]{:S(2)}) collective-permute-start(bf16[256,1152]{1,0:T(8,128)(2,1)} %collective-permute-done.38), channel_id=1, source_target_pairs={{0,4},{2,6},{4,0},{6,2},{8,12},{10,14},{12,8},{14,10},{16,20},{18,... | collective-permute-start | bytes 1769480 | tf_op jit(solution)/shard_map/ppermute | solution.py:261
  276.6 28.8 %collective-permute-start.36 = (bf16[2,256,1152]{2,1,0:T(8,128)(2,1)}, bf16[2,256,1152]{2,1,0:T(8,128)(2,1)}, u32[]{:S(2)}, u32[]{:S(2)}) collective-permute-start(bf16[2,256,1152]{2,1,0:T(8,128)(2,1)} %get-tuple-element.151), channel_id=1, source_target_pairs={{0,1},{1,0},{2,3},{3,2},{4,5},{5,4},{6,7},{7,6},{8,9},{9,8},{10,11... | collective-permute-start | bytes 3538952 | tf_op jit(solution)/shard_map/ppermute | solution.py:270
  305.5 49.2 %all-to-all-start.3 = ((bf16[16,192,256]{2,1,0:T(8,128)(2,1)}), bf16[16,192,256]{2,1,0:T(8,128)(2,1)}, u32[]{:S(2)}, u32[]{:S(2)}) async-start(bf16[16,192,256]{2,1,0:T(8,128)(2,1)} %shard_map.201), calls=%async_computation.3 | async-start | bytes 3145728 | tf_op jit(solution)/shard_map/all_to_all | solution.py:1208
  313.6 41.1 %collective-permute-start.41 = (bf16[2,1024,256]{2,1,0:T(8,128)(2,1)}, bf16[2,1024,256]{2,1,0:T(8,128)(2,1)}, u32[]{:S(2)}, u32[]{:S(2)}) collective-permute-start(bf16[2,1024,256]{2,1,0:T(8,128)(2,1)} %pad_maximum_fusion.4.refs_0_), channel_id=1, source_target_pairs={{0,4},{2,6},{4,0},{6,2},{8,12},{10,14},{12,8},{14,10},{16,20},{18,... | collective-permute-start | bytes 3145736 | tf_op jit(solution)/shard_map/ppermute | solution.py:261
  334.4 40.3 %collective-permute-start.46 = (bf16[2,256,1152]{2,1,0:T(8,128)(2,1)}, bf16[2,256,1152]{2,1,0:T(8,128)(2,1)S(1)}, u32[]{:S(2)}, u32[]{:S(2)}) collective-permute-start(bf16[2,256,1152]{2,1,0:T(8,128)(2,1)} %get-tuple-element.192), channel_id=1, source_target_pairs={{0,1},{1,0},{2,3},{3,2},{4,5},{5,4},{6,7},{7,6},{8,9},{9,8},{10,11... | collective-permute-start | bytes 3538952 | tf_op jit(solution)/shard_map/ppermute | solution.py:270
  393.5 36.4 %collective-permute-start.62 = (bf16[2,288,1024]{2,1,0:T(8,128)(2,1)}, bf16[2,288,1024]{2,1,0:T(8,128)(2,1)S(1)}, u32[]{:S(2)}, u32[]{:S(2)}) collective-permute-start(bf16[2,288,1024]{2,1,0:T(8,128)(2,1)} %get-tuple-element.203), channel_id=1, source_target_pairs={{0,4},{2,6},{4,0},{6,2},{8,12},{10,14},{12,8},{14,10},{16,20},{18,... | collective-permute-start | bytes 3538952 | tf_op jit(solution)/shard_map/ppermute | solution.py:261
  418.0 39.4 %collective-permute-start.60 = (bf16[2,256,1152]{2,1,0:T(8,128)(2,1)S(1)}, bf16[2,256,1152]{2,1,0:T(8,128)(2,1)S(1)}, u32[]{:S(2)}, u32[]{:S(2)}) collective-permute-start(bf16[2,256,1152]{2,1,0:T(8,128)(2,1)S(1)} %pad_maximum_fusion.1.refs_0_), channel_id=1, source_target_pairs={{0,4},{2,6},{4,0},{6,2},{8,12},{10,14},{12,8},{14,10},{16,20},{18,... | collective-permute-start | bytes 3538952 | tf_op jit(solution)/shard_map/ppermute | solution.py:261
  431.5 36.8 %collective-permute-start.71 = (bf16[256,1152]{1,0:T(8,128)(2,1)S(1)}, bf16[256,1152]{1,0:T(8,128)(2,1)S(1)}, u32[]{:S(2)}, u32[]{:S(2)}) collective-permute-start(bf16[256,1152]{1,0:T(8,128)(2,1)S(1)} %fusion), channel_id=1, source_target_pairs={{0,16},{2,18},{4,20},{6,22},{8,24},{10,26},{12,28},{14,30},{16,0},... | collective-permute-start | bytes 1769480 | tf_op jit(solution)/shard_map/ppermute | solution.py:267
  453.0 30.4 %collective-permute-start.64 = (bf16[288,1024]{1,0:T(8,128)(2,1)S(1)}, bf16[288,1024]{1,0:T(8,128)(2,1)S(1)}, u32[]{:S(2)}, u32[]{:S(2)}) collective-permute-start(bf16[288,1024]{1,0:T(8,128)(2,1)S(1)} %fusion.1), channel_id=1, source_target_pairs={{0,16},{2,18},{4,20},{6,22},{8,24},{10,26},{12,28},{14,30},{16,0},... | collective-permute-start | bytes 1769480 | tf_op jit(solution)/shard_map/ppermute | solution.py:267
  454.5 55.9 %collective-permute-start.59 = (bf16[2,256,1152]{2,1,0:T(8,128)(2,1)S(1)}, bf16[2,256,1152]{2,1,0:T(8,128)(2,1)S(1)}, u32[]{:S(2)}, u32[]{:S(2)}) collective-permute-start(bf16[2,256,1152]{2,1,0:T(8,128)(2,1)S(1)} %pad_maximum_fusion.1.refs_0_), channel_id=1, source_target_pairs={{0,2},{2,0},{4,6},{6,4},{8,10},{10,8},{12,14},{14,12},{16,18},{18,... | collective-permute-start | bytes 3538952 | tf_op jit(solution)/shard_map/ppermute | solution.py:258
  457.4 54.0 %collective-permute-start.61 = (bf16[2,256,1152]{2,1,0:T(8,128)(2,1)S(1)}, bf16[2,256,1152]{2,1,0:T(8,128)(2,1)}, u32[]{:S(2)}, u32[]{:S(2)}) collective-permute-start(bf16[2,256,1152]{2,1,0:T(8,128)(2,1)S(1)} %collective-permute-done.60.refs_2_), channel_id=1, source_target_pairs={{0,2},{2,0},{4,6},{6,4},{8,10},{10,8},{12,14},{14,12},{16,18},{18,... | collective-permute-start | bytes 3538952 | tf_op jit(solution)/shard_map/ppermute | solution.py:258
  484.1 38.0 %collective-permute-start.51 = (bf16[272,768]{1,0:T(8,128)(2,1)S(1)}, bf16[272,768]{1,0:T(8,128)(2,1)S(1)}, u32[]{:S(2)}, u32[]{:S(2)}) collective-permute-start(bf16[272,768]{1,0:T(8,128)(2,1)S(1)} %fusion.11), channel_id=1, source_target_pairs={{0,8},{2,10},{4,12},{6,14},{8,0},{10,2},{12,4},{14,6},{16,24},{18,... | collective-permute-start | bytes 1253384 | tf_op jit(solution)/shard_map/ppermute | solution.py:264
  520.9 39.5 %collective-permute-start.74 = (bf16[2,256,1152]{2,1,0:T(8,128)(2,1)S(1)}, bf16[2,256,1152]{2,1,0:T(8,128)(2,1)S(1)}, u32[]{:S(2)}, u32[]{:S(2)}) collective-permute-start(bf16[2,256,1152]{2,1,0:T(8,128)(2,1)S(1)} %pad_maximum_fusion.3.refs_0_), channel_id=1, source_target_pairs={{0,4},{2,6},{4,0},{6,2},{8,12},{10,14},{12,8},{14,10},{16,20},{18,... | collective-permute-start | bytes 3538952 | tf_op jit(solution)/shard_map/ppermute | solution.py:261
  522.3 43.0 %collective-permute-start.66 = (bf16[2,288,1024]{2,1,0:T(8,128)(2,1)}, bf16[2,288,1024]{2,1,0:T(8,128)(2,1)}, u32[]{:S(2)}, u32[]{:S(2)}) collective-permute-start(bf16[2,288,1024]{2,1,0:T(8,128)(2,1)} %pad_maximum_fusion.2.refs_0_), channel_id=1, source_target_pairs={{0,2},{2,0},{4,6},{6,4},{8,10},{10,8},{12,14},{14,12},{16,18},{18,... | collective-permute-start | bytes 3538952 | tf_op jit(solution)/shard_map/ppermute | solution.py:258
  535.2 30.4 %collective-permute-start.68 = (bf16[2,288,1024]{2,1,0:T(8,128)(2,1)}, bf16[2,288,1024]{2,1,0:T(8,128)(2,1)}, u32[]{:S(2)}, u32[]{:S(2)}) collective-permute-start(bf16[2,288,1024]{2,1,0:T(8,128)(2,1)} %collective-permute-done.67.refs_2_), channel_id=1, source_target_pairs={{0,2},{2,0},{4,6},{6,4},{8,10},{10,8},{12,14},{14,12},{16,18},{18,... | collective-permute-start | bytes 3538952 | tf_op jit(solution)/shard_map/ppermute | solution.py:258
  542.9 43.4 %collective-permute-start.73 = (bf16[2,256,1152]{2,1,0:T(8,128)(2,1)S(1)}, bf16[2,256,1152]{2,1,0:T(8,128)(2,1)S(1)}, u32[]{:S(2)}, u32[]{:S(2)}) collective-permute-start(bf16[2,256,1152]{2,1,0:T(8,128)(2,1)S(1)} %pad_maximum_fusion.3.refs_0_), channel_id=1, source_target_pairs={{0,2},{2,0},{4,6},{6,4},{8,10},{10,8},{12,14},{14,12},{16,18},{18,... | collective-permute-start | bytes 3538952 | tf_op jit(solution)/shard_map/ppermute | solution.py:258
  565.2 31.6 %collective-permute-start.54 = (bf16[2,272,768]{2,1,0:T(8,128)(2,1)}, bf16[2,272,768]{2,1,0:T(8,128)(2,1)S(1)}, u32[]{:S(2)}, u32[]{:S(2)}) collective-permute-start(bf16[2,272,768]{2,1,0:T(8,128)(2,1)} %pad_maximum_fusion.6.refs_0_), channel_id=1, source_target_pairs={{0,2},{2,0},{4,6},{6,4},{8,10},{10,8},{12,14},{14,12},{16,18},{18,... | collective-permute-start | bytes 2506760 | tf_op jit(solution)/shard_map/ppermute | solution.py:258
  (111 other events, 1541.8 us)

commit v10 on v6

--- a/solution.py
+++ b/solution.py
@@ -241,7 +241,7 @@
         self.core = index % 2
         self.y = (index // 2) % 2
         self.side = lax.axis_index("fsdp")
-        self.half = ((index // 4 + 1) // 2) % 2
+        self.half = index // 4 % 2
         self.quarter = index % 2 * 2 + self.y
         self.here = jnp.stack([self.half, self.core, self.y, self.side]).astype(jnp.int32)
 
@@ -263,8 +263,8 @@
     def over_z(self, value):
         return lax.ppermute(value, "ctx", self.route(lambda z, y, c: (z ^ 1, y, c)))
 
-    def mirror_z(self, value):
-        return lax.ppermute(value, "ctx", self.route(lambda z, y, c: (self.depth - 1 - z, y, c)))
+    def over_two_z(self, value):
+        return lax.ppermute(value, "ctx", self.route(lambda z, y, c: (z ^ 2, y, c)))
 
     def over_x(self, value):
         return lax.ppermute(value, "fsdp", [(0, 1), (1, 0)])
@@ -278,17 +278,15 @@
         got, got_far = self.over_core(give), self.over_core(give_far)
         return (near, got, self.over_y(far), self.over_y(got_far))
 
-    def sum_depth(self, kept, got):
+    def sum_depth(self, kept, got, time=None):
         def half(index):
             return add(pick(kept, index, 0), pick(got, index, 0))
 
         given = self.over_z(half(1 - self.half))
         part = add(half(self.half), given)
-        full = add(part, self.mirror_z(part))
-        return jnp.stack([full, self.over_z(full)])
-
-    def reduce(self, got, kept):
-        return self.spread_plane(self.sum_depth(kept, got))
+        full = add(part, self.over_two_z(part))
+        other = self.over_z(full)
+        return jnp.stack([full, other if time is None else after(other, time)])
 
 
 def pick(value, index, axis):
@@ -339,8 +337,7 @@
 def project_kernel(here, *refs):
     x_ref, gain_ref, own_ref = refs[:3]
     pieces, q_gain, k_gain, cos_ref, sin_ref = refs[3:7], refs[7], refs[8], refs[9], refs[10]
-    d_ref = refs[11]
-    sent, weight, q_ref, k_ref, q_scale, k_scale, early_ref, scale_ref = refs[12:]
+    sent, weight, q_ref, k_ref, q_scale, k_scale, normed_ref, scale_ref = refs[11:]
     core, y, side = here[1], here[2], here[3]
     rows = own_ref.shape[0]
     part = rows // 4
@@ -353,8 +350,7 @@
     scale = rms_scale(x)
     scale_ref[...] = scale
     normed = (x * scale * gain_ref[...]).astype(bf16)
-    early_ref[0] = d_ref[...]
-    early_ref[1] = normed
+    normed_ref[...] = normed.T
     cosine, sine = cos_ref[...], sin_ref[...]
     half = HD // 2
 
@@ -387,11 +383,11 @@
                 sent[head * per_group + copy, row : row + HD, :] = value
 
 
-def project(here, x, gain, own, pieces, q_gain, k_gain, cosine, sine, d_ffn):
+def project(here, x, gain, own, pieces, q_gain, k_gain, cosine, sine):
     tokens, width = x.shape
     f32, bf16 = jnp.float32, jnp.bfloat16
     shape = jax.ShapeDtypeStruct
-    arrays = [x, gain, own, *pieces, q_gain, k_gain, cosine, sine, d_ffn]
+    arrays = [x, gain, own, *pieces, q_gain, k_gain, cosine, sine]
     outs = [
         shape((HEADS, 3 * HD, tokens), bf16),
         shape((width, own.shape[1]), bf16),
@@ -399,7 +395,7 @@
         shape((KV_HEADS * HD, tokens), f32),
         shape((HEADS, tokens), f32),
         shape((KV_HEADS, tokens), f32),
-        shape((2, tokens, width), bf16),
+        shape((width, tokens), bf16),
         shape((tokens, 1), f32),
     ]
     return call_with_here(
@@ -715,17 +711,17 @@
             pltpu.VMEM((rows, 4 * tokens), jnp.bfloat16),
             pltpu.VMEM((4 * tokens, columns), jnp.bfloat16),
         ],
-        micros=8,
+        micros=3,
     )
 
 
 def down_product_kernel(here, *refs):
     planes, terms = refs[:4], (refs[4:8], refs[8:12])
     sent, kept, left, right = refs[12:]
-    tokens = planes[0].shape[1]
+    tokens = planes[0].shape[0]
     rows = left.shape[0]
     for i in range(4):
-        right[i * tokens : (i + 1) * tokens, :] = planes[i][0]
+        right[i * tokens : (i + 1) * tokens, :] = planes[i][...]
     for chunk in range(2):
         for i in range(4):
             share = terms[chunk][i]
@@ -747,8 +743,8 @@
                 sent[half] = product.astype(sent.dtype)
 
 
-def down_products(here, early_plane, first, second, rows):
-    _, tokens, columns = early_plane[0].shape
+def down_products(here, d_plane, first, second, rows):
+    tokens, columns = d_plane[0].shape
     outs = [
         jax.ShapeDtypeStruct((2, rows // 2, columns), jnp.bfloat16),
         jax.ShapeDtypeStruct((2, rows // 2, columns), jnp.float32),
@@ -757,15 +753,15 @@
         down_product_kernel,
         here,
         (1,),
-        [*early_plane, *first, *second],
-        [layer(a, 0) for a in early_plane] + [whole(a) for a in (*first, *second)],
+        [*d_plane, *first, *second],
+        [whole(a) for a in (*d_plane, *first, *second)],
         outs,
         [whole(o) for o in outs],
         [
             pltpu.VMEM((rows, 4 * tokens), jnp.bfloat16),
             pltpu.VMEM((4 * tokens, columns), jnp.bfloat16),
         ],
-        micros=8,
+        micros=3,
     )
 
 
@@ -851,14 +847,14 @@
 
 
 def attention_product_kernel(here, *refs):
-    normed, attn, terms, gains_ref, ffn_gain_ref = refs[:4], refs[4:8], refs[8:12], refs[12], refs[13]
-    sent, kept, left, right, left_out, right_out = refs[14:]
-    tokens = normed[0].shape[1]
+    planes, terms, gains_ref, ffn_gain_ref = refs[:4], refs[4:8], refs[8], refs[9]
+    sent, kept, left, right, left_out, right_out = refs[10:]
+    tokens = planes[0].shape[2]
     cut = right.shape[1]
     for i in range(4):
         at = slice(i * tokens, (i + 1) * tokens)
-        left[:, at] = normed[i][0].T
-        left_out[:, at] = attn[i][...]
+        left[:, at] = planes[i][0]
+        left_out[:, at] = planes[i][1]
         share = terms[i]
         right[at, :] = share[:cut].T
         right_out[at, :] = share[cut:]
@@ -887,8 +883,8 @@
         out_ref[1, step:, :] = jnp.zeros((GAIN_ROWS, out_ref.shape[2]), out_ref.dtype)
 
 
-def attention_products(here, early_plane, attn_plane, shares, gains, ffn_gain):
-    _, tokens, width = early_plane[0].shape
+def attention_products(here, pair_plane, shares, gains, ffn_gain):
+    _, width, tokens = pair_plane[0].shape
     cut = shares[0].shape[0] - tokens
     shape = (2, width // 4 + GAIN_ROWS, cut + tokens)
     outs = [jax.ShapeDtypeStruct(shape, jnp.bfloat16), jax.ShapeDtypeStruct(shape, jnp.float32)]
@@ -896,9 +892,8 @@
         attention_product_kernel,
         here,
         (1,),
-        [*early_plane, *attn_plane, *shares, gains, ffn_gain],
-        [layer(a, 1) for a in early_plane]
-        + [whole(a) for a in (*attn_plane, *shares, gains, ffn_gain)],
+        [*pair_plane, *shares, gains, ffn_gain],
+        [whole(a) for a in (*pair_plane, *shares, gains, ffn_gain)],
         outs,
         [whole(o) for o in outs],
         [
@@ -907,7 +902,7 @@
             pltpu.VMEM((width, 4 * tokens), jnp.bfloat16),
             pltpu.VMEM((4 * tokens, tokens), jnp.bfloat16),
         ],
-        micros=8,
+        micros=3,
     )
 
 
@@ -1125,18 +1120,16 @@
         qkv_beside,
         links.over_core(after(qkv_beside, gate_up)),
     )
-    sent, w_qkv, q_raw, k_raw, q_scale, k_scale, early, scale_one = project(
+    sent, w_qkv, q_raw, k_raw, q_scale, k_scale, normed, scale_one = project(
         here, tokens_here, gain_attn[None], qkv_weight, qkv_pieces,
-        gain_query[:, None], gain_key[:, None], cosine[0], sine[0], d_ffn,
+        gain_query[:, None], gain_key[:, None], cosine[0], sine[0],
     )
     got = lax.all_to_all(sent, "ctx", 0, 0, tiled=True)
-    early_beside = links.over_y(early)
+    d_beside = links.over_y(after(d_ffn, sent))
     first_there = after(first_there, sent)
     down_there = links.over_x(after(down_piece, first_there))
     first_beside = links.over_y(first_there)
-    second_there = links.over_x(after(second_piece, down_there))
-    down_beside = links.over_y(down_there)
-    got = after(got, down_there)
+    got = after(got, d_beside)
     q_place, q_start = q_place[None], q_start[None]
     shape = jax.ShapeDtypeStruct
     attn_sent, *held = kernel_call(
@@ -1159,7 +1152,9 @@
     attn_in = lax.dynamic_slice_in_dim(
         lax.all_to_all(attn_sent, "ctx", 0, 0, tiled=True), part * HEADS, HEADS
     ).reshape(q_width, rows_here)
-    second_there = after(second_there, attn_sent)
+    down_there = after(down_there, attn_sent)
+    second_there = links.over_x(after(second_piece, down_there))
+    down_beside = links.over_y(down_there)
 
     def spread(there, beside, time):
         there, beside = after(there, time), after(beside, time)
@@ -1167,16 +1162,18 @@
 
     first_pieces = spread(first_there, first_beside, attn_sent)
     down_pieces = spread(down_there, down_beside, attn_in)
-    second_pieces = links.spread_plane(second_there)
+    second_beside = links.over_y(second_there)
     w_out, h_one, scale_two, two, two_t = attend_out(
-        here, after(attn_in, early_beside), tokens_here, gain_ffn[None], out_weight, first_pieces
-    )
-    attn_beside = links.over_y(attn_in)
+        here, attn_in, tokens_here, gain_ffn[None], out_weight, first_pieces
+    )
     two_beside = links.over_y(two_t)
     dealt_here, (out_sum, two_sum) = ffn(
         here, 0, two, d_ffn, gate_up, first_pieces, down_weight, down_pieces, [h_one]
     )
-    two_plane = (two_t, links.over_core(two_t), two_beside, links.over_core(two_beside))
+    second_beside = after(second_beside, out_sum)
+    second_pieces = (
+        second_there, links.over_core(second_there), second_beside, links.over_core(second_beside)
+    )
     near, far, give, give_far = dealt_here
     got_far = links.over_core(give_far)
     first_shares = (near, links.over_core(give), links.over_y(far), links.over_y(got_far))
@@ -1194,6 +1191,8 @@
     columns = ff_chunk // 2
     d_heads = d_heads.reshape(HEADS, HD, rows_here)
     d_got = lax.all_to_all(d_heads, "ctx", 0, 0, tiled=True)
+    pair = jnp.stack([after(normed, d_heads), attn_in])
+    two_plane = plane(two_t, two_beside, pair)
     first_products = wide_products(
         here, two_plane, [after(v, d_heads) for v in first_shares], columns
     )
@@ -1214,16 +1213,14 @@
     first_got = links.over_x(first_products[0])
     d_sent = after(d_sent, first_got)
     d_back = lax.all_to_all(d_sent, "ctx", 0, 0, tiled=True)
+    d_plane = plane(d_ffn, d_beside, d_sent)
     second_products = wide_products(
-        here, two_plane, [after(v, d_sent) for v in second_shares], columns
-    )
-    early_plane = plane(early, early_beside, d_sent)
-    attn_plane = plane(attn_in, attn_beside, d_sent)
+        here, two_plane, [after(v, d_plane[1]) for v in second_shares], columns
+    )
     down_terms = down_products(
-        here, early_plane, first_shares, second_shares, columns // 2
+        here, d_plane, first_shares, second_shares, columns // 2
     )
     second_got = links.over_x(after(second_products[0], first_got))
-    down_got = links.over_x(after(down_terms[0], second_got))
     *d_shares, d_inputs, gain_sums = attention_back(
         here,
         [
@@ -1231,18 +1228,29 @@
             cosine[0], sine[0], w_qkv, tokens_here, scale_one, gain_attn[None], d_h_one, d_attn,
         ],
     )
-    grad_gate_up = None
-    for chunk, (got, kept) in enumerate(
-        ((first_got, first_products[1]), (second_got, second_products[1]))
-    ):
-        grad_gate_up = place_gate_up(here, chunk, links.reduce(got, kept), grad_gate_up)
-    grad_down = place_down(here, links.reduce(down_got, down_terms[1]))
+    near, far, give, give_far = d_shares
+    got, got_far = links.over_core(give), links.over_core(give_far)
+    attention_shares = (near, got, links.over_y(far), links.over_y(got_far))
+    down_got = links.over_x(after(down_terms[0], second_got))
+    pair_plane = plane(pair, links.over_y(after(pair, d_sent)), d_shares[0])
     attention_terms = attention_products(
-        here, early_plane, attn_plane, links.deal_plane(*d_shares), gain_sums, ffn_gain_term
-    )
+        here, pair_plane, attention_shares, gain_sums, ffn_gain_term
+    )
+    first_pair = links.sum_depth(first_products[1], first_got, got_far)
+    second_pair = links.sum_depth(second_products[1], second_got)
+    down_pair = links.sum_depth(down_terms[1], after(down_got, got_far))
+    attention_pair = links.sum_depth(attention_terms[1], links.over_x(attention_terms[0]))
+    first_placed = place_gate_up(here, 0, links.spread_plane(first_pair), None)
+    grad_gate_up = place_gate_up(here, 1, links.spread_plane(second_pair), first_placed)
+
+    def spread_after(value, time):
+        beside = after(links.over_y(value), time)
+        return (value, links.over_core(value), beside, links.over_core(beside))
+
+    grad_down = place_down(here, spread_after(down_pair, first_placed))
     cut = qkv_weight.shape[1] // 4
     grad_qkv, grad_out, gain_sums = place_attention(
-        here, links.reduce(links.over_x(attention_terms[0]), attention_terms[1]), cut
+        here, spread_after(attention_pair, grad_gate_up), cut
     )
     at = links.side * (HD // 2)
     gain_grads = [

time: 554 us -> 566 us (1.022)
  waiting for transfers between devices: 216 us -> 255 us
  starting transfers between devices: 98.4 us -> 69.1 us
    ppermute x4, waiting for transfers between devices: 8.02 us -> 46.2 us  [over_two_z(): return lax.ppermute(value, 'ctx', self.route(lambda z, y, c: (z ^ 2, y, c)))]
    ppermute x8, starting transfers between devices: 26.7 us -> 5.23 us  [over_z(): return lax.ppermute(value, 'ctx', self.route(lambda z, y, c: (z ^ 1, y, c)))]
    ppermute x17, waiting for transfers between devices: 95.7 us -> 74.9 us  [over_y(): return lax.ppermute(value, 'ctx', self.route(lambda z, y, c: (z, 1 - y, c)))]
    ppermute x8, waiting for transfers between devices: 31.7 us -> 47.1 us  [over_z(): return lax.ppermute(value, 'ctx', self.route(lambda z, y, c: (z ^ 1, y, c)))]
    all_to_all x1, waiting for transfers between devices: 11.9 us -> 26.5 us  [on_block(): lax.all_to_all(attn_sent, 'ctx', 0, 0, tiled=True)]
    ppermute x9, waiting for transfers between devices: 68.2 us -> 57 us  [over_x(): return lax.ppermute(value, 'fsdp', [(0, 1), (1, 0)])]
    unnamed x84 -> x104, local copies, waits for them, and re-layouts: 14.9 us -> 18.5 us
  transfers between devices with their start and end apart: 70 -> 70, of which waited for: 23 -> 24; matrix products, arithmetic and copies ran while one was open for 8% -> 7% of each run, Pallas kernels for 30% -> 28%
where the time goes in v10:
time: 566 us; the launch traced here: 557 us
  waiting for transfers between devices  255 us (45%)
  Pallas kernels  167 us (30%)
  starting transfers between devices  69.1 us (12%)
  local copies, waits for them, and re-layouts  46 us (8%)
  other arithmetic  17.6 us (3%)
    pallas_call x13, Pallas kernels, call_with_here(): pl.pallas_call(kernel, grid_spec=pltpu.PrefetchScalarGridSpec(num_scalar_...  121 us
    ppermute x17, waiting for transfers between devices, over_y(): return lax.ppermute(value, 'ctx', self.route(lambda z, y, c: (z, 1 - y, c)))  74.9 us
    ppermute x9, waiting for transfers between devices, over_x(): return lax.ppermute(value, 'fsdp', [(0, 1), (1, 0)])  57 us
    ppermute x8, waiting for transfers between devices, over_z(): return lax.ppermute(value, 'ctx', self.route(lambda z, y, c: (z ^ 1, y, c)))  47.1 us
    pallas_call x2, Pallas kernels, kernel_call(): pl.pallas_call(kernel, out_shape=outs, in_specs=[smem] * len(tables) + [v...  46.9 us
    ppermute x4, waiting for transfers between devices, over_two_z(): return lax.ppermute(value, 'ctx', self.route(lambda z, y, c: (z ^ 2, y, c)))  46.2 us
    all_to_all x1, waiting for transfers between devices, on_block(): lax.all_to_all(attn_sent, 'ctx', 0, 0, tiled=True)  26.5 us
    ppermute x17, starting transfers between devices, over_y(): return lax.ppermute(value, 'ctx', self.route(lambda z, y, c: (z, 1 - y, c)))  21 us
  transfers between devices with their start and end apart: 70, of which 24 were waited for; matrix products, arithmetic and copies ran while one was open for 7% of the time, Pallas kernels for 28%

profile of v10, /device:TPU:0, one launch (start us, length us, event | category | flops | bytes accessed | tf_op | source)
XLA Modules:
  0.0 557.3 jit_solution(11898742261325359964)
XLA Ops:
  20.1 8.9 %copy.71 = bf16[512,2,4608]{2,0,1:T(8,128)(2,1)} copy(bf16[512,2,4608]{2,1,0:T(2,128)(2,1)} %param.15) | data formatting | bytes 18874368 | tf_op jit(solution)/shard_map/optimization_barrier | solution.py:301
  51.3 29.2 %collective-permute-done.6.refs_4_.refs_5_.refs_3_ = bf16[128,5632]{1,0:T(8,128)(2,1)} collective-permute-done((bf16[128,5632]{1,0:T(8,128)(2,1)}, bf16[128,5632]{1,0:T(8,128)(2,1)}, u32[]{:S(2)}, u32[]{:S(2)}) %collective-permute-start.6) | collective-permute-done | bytes 1441824 | tf_op jit(solution)/shard_map/ppermute | solution.py:270
  85.0 12.2 %collective-permute-done.5.refs_2_ = bf16[256,1024]{1,0:T(8,128)(2,1)} collective-permute-done((bf16[256,1024]{1,0:T(8,128)(2,1)}, bf16[256,1024]{1,0:T(8,128)(2,1)}, u32[]{:S(2)}, u32[]{:S(2)}) %collective-permute-start.5) | collective-permute-done | bytes 524320 | tf_op jit(solution)/shard_map/ppermute | solution.py:261
  98.4 22.0 %shard_map.196 = (bf16[16,64,256]{2,1,0:T(8,128)(2,1)}, bf16[4096,64]{1,0:T(8,128)(2,1)S(1)}, bf16[64,4096]{1,0:T(8,128)(2,1)S(1)}, bf16[4096,64]{1,0:T(8,128)(2...) custom-call(s32[32]{0:T(128)S(1)} %broadcast_add_fusion.q_slot, ...), custom_call_target="tpu_custom_call" | custom-call | flops 1 | bytes 1 | tf_op jit(solution)/shard_map/pallas_call | solution.py:226
  130.3 26.5 %all-to-all-done.1 = bf16[16,64,256]{2,1,0:T(8,128)(2,1)S(1)} async-done(((bf16[16,64,256]{2,1,0:T(8,128)(2,1)}), bf16[16,64,256]{2,1,0:T(8,128)(2,1)S(1)}, u32[]{:S(2)}, u32[]{:S(2)}) %all-to-all-start.1) | async-done | bytes 524320 | tf_op jit(solution)/shard_map/all_to_all | solution.py:1153
  166.6 16.8 %shard_map.198 = (bf16[256,1792]{1,0:T(8,128)(2,1)}, bf16[256,1792]{1,0:T(8,128)(2,1)}, bf16[256,1792]{1,0:T(8,128)(2,1)}, bf16[256,1792]{1,0:T(8,128)(2,1)}, f32[256,1024]{1,0:T(8,128)}, /*index=5*/f32[256,1024]{1,0:T(8,128)}) custom-call(s32[4]{0:T(128)} %pad_add_fusion.here, bf16[256,1024]{1,0:T(8,128)(2,1)} %get-tuple-element.116.refs_0_, ...), custom_call_target="tpu_custom_call" | custom-call | flops 1 | bytes 1 | tf_op jit(solution)/shard_map/pallas_call | solution.py:316
  192.5 16.9 %shard_map.199 = (bf16[256,1792]{1,0:T(8,128)(2,1)}, bf16[256,1792]{1,0:T(8,128)(2,1)}, bf16[256,1792]{1,0:T(8,128)(2,1)}, bf16[256,1792]{1,0:T(8,128)(2,1)}, bf...) custom-call(s32[4]{0:T(128)} %pad_add_fusion.here, ...), custom_call_target="tpu_custom_call" | custom-call | flops 1 | bytes 1 | tf_op jit(solution)/shard_map/pallas_call | solution.py:316
  222.9 21.8 %collective-permute-done.24.refs_7_ = bf16[256,1792]{1,0:T(8,128)(2,1)} collective-permute-done((bf16[256,1792]{1,0:T(8,128)(2,1)}, bf16[256,1792]{1,0:T(8,128)(2,1)}, u32[]{:S(2)}, u32[]{:S(2)}) %collective-permute-start.24) | collective-permute-done | bytes 917536 | tf_op jit(solution)/shard_map/ppermute | solution.py:261
  259.8 24.9 %shard_map.201 = bf16[16,192,256]{2,1,0:T(8,128)(2,1)} custom-call(s32[32]{0:T(128)S(1)} %broadcast_add_fusion.q_slot, s32[32]{0:T(128)S(1)} %get-tuple-element.199.kv_slot, s32[16]{0:T(128)S(1)} %get-tuple-element.220.first, s32[16]{0:T(128)S(1)} %get-tuple-element.221.last, bf16[16,64,256]{2,1,0:T(8,128)(2,1)S(1)} %all-to-all-done.2.d_ref, ...), custom_call_target="tpu_custom_call" | custom-call | flops 24999999488 | bytes 1 | tf_op jit(solution)/shard_map/pallas_call | solution.py:226
  305.9 21.6 %collective-permute-done.44 = bf16[2,256,1152]{2,1,0:T(8,128)(2,1)S(1)} collective-permute-done((bf16[2,256,1152]{2,1,0:T(8,128)(2,1)}, bf16[2,256,1152]{2,1,0:T(8,128)(2,1)S(1)}, u32[]{:S(2)}, u32[]{:S(2)}) %collective-permute-start.44) | collective-permute-done | bytes 1179680 | tf_op jit(solution)/shard_map/ppermute | solution.py:270
  331.1 9.9 %shard_map.208 = (bf16[2,288,1024]{2,1,0:T(8,128)(2,1)}, f32[2,288,1024]{2,1,0:T(8,128)}) custom-call(s32[4]{0:T(128)} %pad_add_fusion.here, bf16[256,1024]{1,0:T(8,128)(2,1)} %bitcast.17.refs_1_.refs_0_, bf16[256,1024]{1,0:T(8,128)(2,1)} %copy-done.45, bf16[256,1024]{1,0:T(8,128)(2,1)} %collective-permute-done.5.refs_2_, ...), custom_call_target="tpu_custom_call" | custom-call | flops 3000000000 | bytes 1 | tf_op jit(solution)/shard_map/pallas_call | solution.py:316
  348.0 8.6 %shard_map.202 = (bf16[768,256]{1,0:T(8,128)(2,1)}, bf16[768,256]{1,0:T(8,128)(2,1)}, bf16[768,256]{1,0:T(8,128)(2,1)}, bf16[768,256]{1,0:T(8,128)(2,1)}, f32[256,1024]{1,0:T(8,128)}, /*index=5*/f32[8,1024]{1,0:T(8,128)}) custom-call(s32[4]{0:T(128)} %pad_add_fusion.here, bf16[16,192,256]{2,1,0:T(8,128)(2,1)} %all-to-all-done.3.refs_0_, ...), custom_call_target="tpu_custom_call" | custom-call | flops 12000000000 | bytes 1 | tf_op jit(solution)/shard_map/pallas_call | solution.py:316
  357.2 27.2 %collective-permute-done.52 = bf16[256,1152]{1,0:T(8,128)(2,1)} collective-permute-done((bf16[256,1152]{1,0:T(8,128)(2,1)S(1)}, bf16[256,1152]{1,0:T(8,128)(2,1)}, u32[]{:S(2)}, u32[]{:S(2)}) %collective-permute-start.52) | collective-permute-done | bytes 589856 | tf_op jit(solution)/shard_map/ppermute | solution.py:267
  385.9 10.1 %collective-permute-done.46 = bf16[256,1152]{1,0:T(8,128)(2,1)S(1)} collective-permute-done((bf16[256,1152]{1,0:T(8,128)(2,1)S(1)}, bf16[256,1152]{1,0:T(8,128)(2,1)S(1)}, u32[]{:S(2)}, u32[]{:S(2)}) %collective-permute-start.46) | collective-permute-done | bytes 589856 | tf_op jit(solution)/shard_map/ppermute | solution.py:267
  399.2 9.3 %collective-permute-done.53 = bf16[256,1152]{1,0:T(8,128)(2,1)S(1)} collective-permute-done((bf16[256,1152]{1,0:T(8,128)(2,1)S(1)}, bf16[256,1152]{1,0:T(8,128)(2,1)S(1)}, u32[]{:S(2)}, u32[]{:S(2)}) %collective-permute-start.53) | collective-permute-done | bytes 589856 | tf_op jit(solution)/shard_map/ppermute | solution.py:264
  432.2 10.4 %collective-permute-done.47 = bf16[256,1152]{1,0:T(8,128)(2,1)S(1)} collective-permute-done((bf16[256,1152]{1,0:T(8,128)(2,1)S(1)}, bf16[256,1152]{1,0:T(8,128)(2,1)S(1)}, u32[]{:S(2)}, u32[]{:S(2)}) %collective-permute-start.47) | collective-permute-done | bytes 589856 | tf_op jit(solution)/shard_map/ppermute | solution.py:264
  450.3 9.0 %collective-permute-done.61 = bf16[288,1024]{1,0:T(8,128)(2,1)S(1)} collective-permute-done((bf16[288,1024]{1,0:T(8,128)(2,1)S(1)}, bf16[288,1024]{1,0:T(8,128)(2,1)S(1)}, u32[]{:S(2)}, u32[]{:S(2)}) %collective-permute-start.61) | collective-permute-done | bytes 589856 | tf_op jit(solution)/shard_map/ppermute | solution.py:267
  459.6 8.7 %collective-permute-done.34 = bf16[272,768]{1,0:T(8,128)(2,1)S(1)} collective-permute-done((bf16[272,768]{1,0:T(8,128)(2,1)S(1)}, bf16[272,768]{1,0:T(8,128)(2,1)S(1)}, u32[]{:S(2)}, u32[]{:S(2)}) %collective-permute-start.34) | collective-permute-done | bytes 417824 | tf_op jit(solution)/shard_map/ppermute | solution.py:264
  471.9 17.0 %collective-permute-done.62 = bf16[288,1024]{1,0:T(8,128)(2,1)S(1)} collective-permute-done((bf16[288,1024]{1,0:T(8,128)(2,1)S(1)}, bf16[288,1024]{1,0:T(8,128)(2,1)S(1)}, u32[]{:S(2)}, u32[]{:S(2)}) %collective-permute-start.62) | collective-permute-done | bytes 589856 | tf_op jit(solution)/shard_map/ppermute | solution.py:264
  491.9 10.0 %shard_map.205.refs_4_ = f32[512,2,4608]{2,1,0:T(2,128)} custom-call(s32[4]{0:T(128)} %pad_add_fusion.here, bf16[2,256,1152]{2,1,0:T(8,128)(2,1)} %copy-done.23, bf16[2,256,1152]{2,1,0:T(8,128)(2,1)} %copy-done.38, bf16[2,256,1152]{2,1,0:T(8,128)(2,1)} %collective-permute-done.55.refs_2_, bf16[2,256,1152]{2,1,0:T(8,128)(2,1)} %copy-done.39), custom_call_target="tpu_custom_call" | custom-call | flops 10000000000 | bytes 1 | tf_op jit(solution)/shard_map/pallas_call | solution.py:316
  503.8 13.7 %collective-permute-done.64.refs_2_ = bf16[2,288,1024]{2,1,0:T(8,128)(2,1)} collective-permute-done((bf16[2,288,1024]{2,1,0:T(8,128)(2,1)S(1)}, bf16[2,288,1024]{2,1,0:T(8,128)(2,1)}, u32[]{:S(2)}, u32[]{:S(2)}) %collective-permute-start.64) | collective-permute-done | bytes 1179680 | tf_op jit(solution)/shard_map/ppermute | solution.py:261
  520.2 9.7 %shard_map.206 = f32[512,2,4608]{2,1,0:T(2,128)} custom-call(s32[4]{0:T(128)} %pad_add_fusion.here, bf16[2,256,1152]{2,1,0:T(8,128)(2,1)} %copy-done.10, bf16[2,256,1152]{2,1,0:T(8,128)(2,1)} %copy-done.20, bf16[2,256,1152]{2,1,0:T(8,128)(2,1)} %copy-done.17, bf16[2,256,1152]{2,1,0:T(8,128)(2,1)} %copy-done.21, ...), custom_call_target="tpu_custom_call", output_to_operand_aliasing={{}: (5, {})} | custom-call | flops 10000000000 | bytes 1 | tf_op jit(solution)/shard_map/pallas_call | solution.py:316
  529.9 8.0 %collective-permute-done.38.refs_2_ = bf16[2,272,768]{2,1,0:T(8,128)(2,1)} collective-permute-done((bf16[2,272,768]{2,1,0:T(8,128)(2,1)S(1)}, bf16[2,272,768]{2,1,0:T(8,128)(2,1)}, u32[]{:S(2)}, u32[]{:S(2)}) %collective-permute-start.38) | collective-permute-done | bytes 835616 | tf_op jit(solution)/shard_map/ppermute | solution.py:261
  537.9 7.9 %shard_map.209 = f32[2304,1024]{1,0:T(8,128)} custom-call(s32[4]{0:T(128)} %pad_add_fusion.here, bf16[2,288,1024]{2,1,0:T(8,128)(2,1)} %copy-done.24, bf16[2,288,1024]{2,1,0:T(8,128)(2,1)} %collective-permute-done.63.refs_1_, bf16[2,288,1024]{2,1,0:T(8,128)(2,1)} %collective-permute-done.64.refs_2_, bf16[2,288,1024]{2,1,0:T(8,128)(2,1)} %collective-permute-done.65.refs_3_), custom_call_target="tpu_custom_call" | custom-call | flops 5000000000 | bytes 1 | tf_op jit(solution)/shard_map/pallas_call | solution.py:316
  (302 shorter events, 195.4 us)
Async XLA Ops:
  40.0 57.3 %all-to-all-start = ((bf16[16,192,256]{2,1,0:T(8,128)(2,1)}), bf16[16,192,256]{2,1,0:T(8,128)(2,1)S(1)}, u32[]{:S(2)}, u32[]{:S(2)}) async-start(bf16[16,192,256]{2,1,0:T(8,128)(2,1)} %get-tuple-element.108), calls=%async_computation | async-start | bytes 3145728 | tf_op jit(solution)/shard_map/all_to_all | solution.py:1127
  80.5 40.7 %collective-permute-start.10 = (bf16[2304,256]{1,0:T(8,128)(2,1)}, bf16[2304,256]{1,0:T(8,128)(2,1)}, u32[]{:S(2)}, u32[]{:S(2)}) collective-permute-start(bf16[2304,256]{1,0:T(8,128)(2,1)} %constant_dynamic-slice_fusion.3), channel_id=1, source_target_pairs={{0,1},{1,0},{2,3},{3,2},{4,5},{5,4},{6,7},{7,6},{8,9},{9,8},{10,11... | collective-permute-start | bytes 3538952 | tf_op jit(solution)/shard_map/ppermute | solution.py:270
  84.7 45.5 %collective-permute-start.8 = (bf16[128,5632]{1,0:T(8,128)(2,1)}, bf16[128,5632]{1,0:T(8,128)(2,1)}, u32[]{:S(2)}, u32[]{:S(2)}) collective-permute-start(bf16[128,5632]{1,0:T(8,128)(2,1)} %collective-permute-done.6.refs_4_.refs_5_.refs_3_), channel_id=1, source_target_pairs={{0,4},{2,6},{4,0},{6,2},{8,12},{10,14},{12,8},{14,10},{16,20},{18,... | collective-permute-start | bytes 4325384 | tf_op jit(solution)/shard_map/ppermute | solution.py:261
  121.1 35.8 %collective-permute-start.15 = (bf16[2304,256]{1,0:T(8,128)(2,1)}, bf16[2304,256]{1,0:T(8,128)(2,1)}, u32[]{:S(2)}, u32[]{:S(2)}) collective-permute-start(bf16[2304,256]{1,0:T(8,128)(2,1)} %collective-permute-done.10.refs_8_), channel_id=1, source_target_pairs={{0,4},{2,6},{4,0},{6,2},{8,12},{10,14},{12,8},{14,10},{16,20},{18,... | collective-permute-start | bytes 3538952 | tf_op jit(solution)/shard_map/ppermute | solution.py:261
  187.8 35.1 %collective-permute-start.23 = (bf16[256,1792]{1,0:T(8,128)(2,1)}, bf16[256,1792]{1,0:T(8,128)(2,1)}, u32[]{:S(2)}, u32[]{:S(2)}) collective-permute-start(bf16[256,1792]{1,0:T(8,128)(2,1)} %get-tuple-element.141), channel_id=1, source_target_pairs={{0,4},{2,6},{4,0},{6,2},{8,12},{10,14},{12,8},{14,10},{16,20},{18,... | collective-permute-start | bytes 2752520 | tf_op jit(solution)/shard_map/ppermute | solution.py:261
  189.7 54.9 %collective-permute-start.24 = (bf16[256,1792]{1,0:T(8,128)(2,1)}, bf16[256,1792]{1,0:T(8,128)(2,1)}, u32[]{:S(2)}, u32[]{:S(2)}) collective-permute-start(bf16[256,1792]{1,0:T(8,128)(2,1)} %collective-permute-done.18), channel_id=1, source_target_pairs={{0,4},{2,6},{4,0},{6,2},{8,12},{10,14},{12,8},{14,10},{16,20},{18,... | collective-permute-start | bytes 2752520 | tf_op jit(solution)/shard_map/ppermute | solution.py:261
  209.4 46.9 %all-to-all-start.2 = ((bf16[16,64,256]{2,1,0:T(8,128)(2,1)}), bf16[16,64,256]{2,1,0:T(8,128)(2,1)S(1)}, u32[]{:S(2)}, u32[]{:S(2)}) async-start(bf16[16,64,256]{2,1,0:T(8,128)(2,1)} %bitcast.97), calls=%async_computation.2 | async-start | bytes 1048576 | tf_op jit(solution)/shard_map/all_to_all | solution.py:1193
  214.3 41.7 %collective-permute-start.42 = (bf16[256,1792]{1,0:T(8,128)(2,1)}, bf16[256,1792]{1,0:T(8,128)(2,1)}, u32[]{:S(2)}, u32[]{:S(2)}) collective-permute-start(bf16[256,1792]{1,0:T(8,128)(2,1)} %get-tuple-element.181), channel_id=1, source_target_pairs={{0,2},{2,0},{4,6},{6,4},{8,10},{10,8},{12,14},{14,12},{16,18},{18,... | collective-permute-start | bytes 2752520 | tf_op jit(solution)/shard_map/ppermute | solution.py:258
  222.9 68.6 %collective-permute-start.40 = (bf16[256,1792]{1,0:T(8,128)(2,1)}, bf16[256,1792]{1,0:T(8,128)(2,1)}, u32[]{:S(2)}, u32[]{:S(2)}) collective-permute-start(bf16[256,1792]{1,0:T(8,128)(2,1)} %get-tuple-element.177), channel_id=1, source_target_pairs={{0,2},{2,0},{4,6},{6,4},{8,10},{10,8},{12,14},{14,12},{16,18},{18,... | collective-permute-start | bytes 2752520 | tf_op jit(solution)/shard_map/ppermute | solution.py:258
  244.7 46.8 %collective-permute-start.41 = (bf16[256,1792]{1,0:T(8,128)(2,1)}, bf16[256,1792]{1,0:T(8,128)(2,1)}, u32[]{:S(2)}, u32[]{:S(2)}) collective-permute-start(bf16[256,1792]{1,0:T(8,128)(2,1)} %get-tuple-element.179), channel_id=1, source_target_pairs={{0,4},{2,6},{4,0},{6,2},{8,12},{10,14},{12,8},{14,10},{16,20},{18,... | collective-permute-start | bytes 2752520 | tf_op jit(solution)/shard_map/ppermute | solution.py:261
  256.0 35.5 %collective-permute-start.43 = (bf16[256,1792]{1,0:T(8,128)(2,1)}, bf16[256,1792]{1,0:T(8,128)(2,1)}, u32[]{:S(2)}, u32[]{:S(2)}) collective-permute-start(bf16[256,1792]{1,0:T(8,128)(2,1)} %collective-permute-done.42), channel_id=1, source_target_pairs={{0,4},{2,6},{4,0},{6,2},{8,12},{10,14},{12,8},{14,10},{16,20},{18,... | collective-permute-start | bytes 2752520 | tf_op jit(solution)/shard_map/ppermute | solution.py:261
  284.7 63.3 %all-to-all-start.3 = ((bf16[16,192,256]{2,1,0:T(8,128)(2,1)}), bf16[16,192,256]{2,1,0:T(8,128)(2,1)}, u32[]{:S(2)}, u32[]{:S(2)}) async-start(bf16[16,192,256]{2,1,0:T(8,128)(2,1)} %shard_map.201), calls=%async_computation.3 | async-start | bytes 3145728 | tf_op jit(solution)/shard_map/all_to_all | solution.py:1215
  302.7 38.3 %collective-permute-start.51 = (bf16[256,1152]{1,0:T(8,128)(2,1)}, bf16[256,1152]{1,0:T(8,128)(2,1)}, u32[]{:S(2)}, u32[]{:S(2)}) collective-permute-start(bf16[256,1152]{1,0:T(8,128)(2,1)} %fusion.7), channel_id=1, source_target_pairs={{0,8},{2,10},{4,12},{6,14},{8,0},{10,2},{12,4},{14,6},{16,24},{18,... | collective-permute-start | bytes 1769480 | tf_op jit(solution)/shard_map/ppermute | solution.py:264
  304.5 52.2 %collective-permute-start.27 = (bf16[2,1024,256]{2,1,0:T(8,128)(2,1)}, bf16[2,1024,256]{2,1,0:T(8,128)(2,1)}, u32[]{:S(2)}, u32[]{:S(2)}) collective-permute-start(bf16[2,1024,256]{2,1,0:T(8,128)(2,1)} %pad_maximum_fusion.5.refs_0_), channel_id=1, source_target_pairs={{0,4},{2,6},{4,0},{6,2},{8,12},{10,14},{12,8},{14,10},{16,20},{18,... | collective-permute-start | bytes 3145736 | tf_op jit(solution)/shard_map/ppermute | solution.py:261
  342.6 41.8 %collective-permute-start.52 = (bf16[256,1152]{1,0:T(8,128)(2,1)S(1)}, bf16[256,1152]{1,0:T(8,128)(2,1)}, u32[]{:S(2)}, u32[]{:S(2)}) collective-permute-start(bf16[256,1152]{1,0:T(8,128)(2,1)S(1)} %fusion.1), channel_id=1, source_target_pairs={{0,16},{2,18},{4,20},{6,22},{8,24},{10,26},{12,28},{14,30},{16,0},... | collective-permute-start | bytes 1769480 | tf_op jit(solution)/shard_map/ppermute | solution.py:267
  345.0 40.8 %collective-permute-start.59 = (bf16[2,288,1024]{2,1,0:T(8,128)(2,1)}, bf16[2,288,1024]{2,1,0:T(8,128)(2,1)S(1)}, u32[]{:S(2)}, u32[]{:S(2)}) collective-permute-start(bf16[2,288,1024]{2,1,0:T(8,128)(2,1)} %get-tuple-element.194), channel_id=1, source_target_pairs={{0,1},{1,0},{2,3},{3,2},{4,5},{5,4},{6,7},{7,6},{8,9},{9,8},{10,11... | collective-permute-start | bytes 3538952 | tf_op jit(solution)/shard_map/ppermute | solution.py:270
  346.7 49.2 %collective-permute-start.46 = (bf16[256,1152]{1,0:T(8,128)(2,1)S(1)}, bf16[256,1152]{1,0:T(8,128)(2,1)S(1)}, u32[]{:S(2)}, u32[]{:S(2)}) collective-permute-start(bf16[256,1152]{1,0:T(8,128)(2,1)S(1)} %fusion.2), channel_id=1, source_target_pairs={{0,16},{2,18},{4,20},{6,22},{8,24},{10,26},{12,28},{14,30},{16,0},... | collective-permute-start | bytes 1769480 | tf_op jit(solution)/shard_map/ppermute | solution.py:267
  356.6 64.4 %collective-permute-start.26 = (bf16[2,1024,256]{2,1,0:T(8,128)(2,1)S(1)}, bf16[2,1024,256]{2,1,0:T(8,128)(2,1)S(1)}, u32[]{:S(2)}, u32[]{:S(2)}) collective-permute-start(bf16[2,1024,256]{2,1,0:T(8,128)(2,1)S(1)} %copy-done.27), channel_id=1, source_target_pairs={{0,2},{2,0},{4,6},{6,4},{8,10},{10,8},{12,14},{14,12},{16,18},{18,... | collective-permute-start | bytes 3145736 | tf_op jit(solution)/shard_map/ppermute | solution.py:258
  356.7 65.3 %collective-permute-start.28 = (bf16[2,1024,256]{2,1,0:T(8,128)(2,1)}, bf16[2,1024,256]{2,1,0:T(8,128)(2,1)S(1)}, u32[]{:S(2)}, u32[]{:S(2)}) collective-permute-start(bf16[2,1024,256]{2,1,0:T(8,128)(2,1)} %collective-permute-done.27.refs_2_), channel_id=1, source_target_pairs={{0,2},{2,0},{4,6},{6,4},{8,10},{10,8},{12,14},{14,12},{16,18},{18,... | collective-permute-start | bytes 3145736 | tf_op jit(solution)/shard_map/ppermute | solution.py:258
  449.7 40.0 %collective-permute-start.54 = (bf16[2,256,1152]{2,1,0:T(8,128)(2,1)S(1)}, bf16[2,256,1152]{2,1,0:T(8,128)(2,1)S(1)}, u32[]{:S(2)}, u32[]{:S(2)}) collective-permute-start(bf16[2,256,1152]{2,1,0:T(8,128)(2,1)S(1)} %pad_maximum_fusion.3.refs_0_), channel_id=1, source_target_pairs={{0,2},{2,0},{4,6},{6,4},{8,10},{10,8},{12,14},{14,12},{16,18},{18,... | collective-permute-start | bytes 3538952 | tf_op jit(solution)/shard_map/ppermute | solution.py:258
  449.8 41.0 %collective-permute-start.56 = (bf16[2,256,1152]{2,1,0:T(8,128)(2,1)}, bf16[2,256,1152]{2,1,0:T(8,128)(2,1)S(1)}, u32[]{:S(2)}, u32[]{:S(2)}) collective-permute-start(bf16[2,256,1152]{2,1,0:T(8,128)(2,1)} %collective-permute-done.55.refs_2_), channel_id=1, source_target_pairs={{0,2},{2,0},{4,6},{6,4},{8,10},{10,8},{12,14},{14,12},{16,18},{18,... | collective-permute-start | bytes 3538952 | tf_op jit(solution)/shard_map/ppermute | solution.py:258
  471.9 46.2 %collective-permute-start.48 = (bf16[2,256,1152]{2,1,0:T(8,128)(2,1)S(1)}, bf16[2,256,1152]{2,1,0:T(8,128)(2,1)S(1)}, u32[]{:S(2)}, u32[]{:S(2)}) collective-permute-start(bf16[2,256,1152]{2,1,0:T(8,128)(2,1)S(1)} %pad_maximum_fusion.2.refs_0_), channel_id=1, source_target_pairs={{0,2},{2,0},{4,6},{6,4},{8,10},{10,8},{12,14},{14,12},{16,18},{18,... | collective-permute-start | bytes 3538952 | tf_op jit(solution)/shard_map/ppermute | solution.py:258
  489.7 48.1 %collective-permute-start.63 = (bf16[2,288,1024]{2,1,0:T(8,128)(2,1)S(1)}, bf16[2,288,1024]{2,1,0:T(8,128)(2,1)}, u32[]{:S(2)}, u32[]{:S(2)}) collective-permute-start(bf16[2,288,1024]{2,1,0:T(8,128)(2,1)S(1)} %pad_maximum_fusion.4.refs_0_), channel_id=1, source_target_pairs={{0,2},{2,0},{4,6},{6,4},{8,10},{10,8},{12,14},{14,12},{16,18},{18,... | collective-permute-start | bytes 3538952 | tf_op jit(solution)/shard_map/ppermute | solution.py:258
  503.7 42.1 %collective-permute-start.37 = (bf16[2,272,768]{2,1,0:T(8,128)(2,1)S(1)}, bf16[2,272,768]{2,1,0:T(8,128)(2,1)S(1)}, u32[]{:S(2)}, u32[]{:S(2)}) collective-permute-start(bf16[2,272,768]{2,1,0:T(8,128)(2,1)S(1)} %pad_maximum_fusion.6.refs_0_), channel_id=1, source_target_pairs={{0,2},{2,0},{4,6},{6,4},{8,10},{10,8},{12,14},{14,12},{16,18},{18,... | collective-permute-start | bytes 2506760 | tf_op jit(solution)/shard_map/ppermute | solution.py:258
  (98 other events, 1445.9 us)

commit v11 on v10

--- a/solution.py
+++ b/solution.py
@@ -284,9 +284,9 @@
 
         given = self.over_z(half(1 - self.half))
         part = add(half(self.half), given)
-        full = add(part, self.over_two_z(part))
-        other = self.over_z(full)
-        return jnp.stack([full, other if time is None else after(other, time)])
+        other = self.over_two_z(part)
+        full = add(part, other if time is None else after(other, time))
+        return jnp.stack([full, self.over_z(full)])
 
 
 def pick(value, index, axis):
@@ -1102,7 +1102,9 @@
         )
         return [piece[:, 0], piece[:, 1]]
 
-    qkv_there = links.over_x(qkv_piece)
+    d_ffn = cotangent[0]
+    d_beside = links.over_y(d_ffn)
+    qkv_there = after(links.over_x(qkv_piece), d_beside)
     first_piece = jnp.concatenate([*gate_up_piece(0), quarter_rows(out_weight)], axis=1)
     second_piece = jnp.concatenate(gate_up_piece(1), axis=1)
     down_piece = lax.dynamic_slice_in_dim(
@@ -1125,11 +1127,9 @@
         gain_query[:, None], gain_key[:, None], cosine[0], sine[0],
     )
     got = lax.all_to_all(sent, "ctx", 0, 0, tiled=True)
-    d_beside = links.over_y(after(d_ffn, sent))
     first_there = after(first_there, sent)
     down_there = links.over_x(after(down_piece, first_there))
     first_beside = links.over_y(first_there)
-    got = after(got, d_beside)
     q_place, q_start = q_place[None], q_start[None]
     shape = jax.ShapeDtypeStruct
     attn_sent, *held = kernel_call(
@@ -1211,7 +1211,7 @@
         ATTEND_BACK,
     )
     first_got = links.over_x(first_products[0])
-    d_sent = after(d_sent, first_got)
+    d_sent = after(d_sent, first_got, *second_shares[2:])
     d_back = lax.all_to_all(d_sent, "ctx", 0, 0, tiled=True)
     d_plane = plane(d_ffn, d_beside, d_sent)
     second_products = wide_products(
@@ -1228,6 +1228,7 @@
             cosine[0], sine[0], w_qkv, tokens_here, scale_one, gain_attn[None], d_h_one, d_attn,
         ],
     )
+    second_got = after(second_got, d_shares[0])
     near, far, give, give_far = d_shares
     got, got_far = links.over_core(give), links.over_core(give_far)
     attention_shares = (near, got, links.over_y(far), links.over_y(got_far))
@@ -1236,8 +1237,8 @@
     attention_terms = attention_products(
         here, pair_plane, attention_shares, gain_sums, ffn_gain_term
     )
-    first_pair = links.sum_depth(first_products[1], first_got, got_far)
-    second_pair = links.sum_depth(second_products[1], second_got)
+    first_pair = links.sum_depth(first_products[1], first_got, attention_shares[2])
+    second_pair = links.sum_depth(second_products[1], second_got, attention_shares[3])
     down_pair = links.sum_depth(down_terms[1], after(down_got, got_far))
     attention_pair = links.sum_depth(attention_terms[1], links.over_x(attention_terms[0]))
     first_placed = place_gate_up(here, 0, links.spread_plane(first_pair), None)

time: 566 us -> 563 us (level)
    ppermute x8, waiting for transfers between devices: 47.1 us -> 81.5 us  [over_z(): return lax.ppermute(value, 'ctx', self.route(lambda z, y, c: (z ^ 1, y, c)))]
    ppermute x17, waiting for transfers between devices: 74.9 us -> 50.1 us  [over_y(): return lax.ppermute(value, 'ctx', self.route(lambda z, y, c: (z, 1 - y, c)))]
    ppermute x9, waiting for transfers between devices: 57 us -> 33.1 us  [over_x(): return lax.ppermute(value, 'fsdp', [(0, 1), (1, 0)])]
    ppermute x4, waiting for transfers between devices: 46.2 us -> 56.1 us  [over_two_z(): return lax.ppermute(value, 'ctx', self.route(lambda z, y, c: (z ^ 2, y, c)))]
    unnamed x104 -> x98, local copies, waits for them, and re-layouts: 18.5 us -> 14.7 us
  transfers between devices with their start and end apart: 70 -> 70, of which waited for: 24 -> 25; matrix products, arithmetic and copies ran while one was open for 7% -> 8% of each run, Pallas kernels for 28% -> 28%
where the time goes in v11:
time: 563 us; the launch traced here: 554 us
  waiting for transfers between devices  254 us (45%)
  Pallas kernels  167 us (30%)
  starting transfers between devices  72.7 us (13%)
  local copies, waits for them, and re-layouts  42.2 us (7%)
  other arithmetic  16.1 us (3%)
    pallas_call x13, Pallas kernels, call_with_here(): pl.pallas_call(kernel, grid_spec=pltpu.PrefetchScalarGridSpec(num_scalar_...  120 us
    ppermute x8, waiting for transfers between devices, over_z(): return lax.ppermute(value, 'ctx', self.route(lambda z, y, c: (z ^ 1, y, c)))  81.5 us
    ppermute x4, waiting for transfers between devices, over_two_z(): return lax.ppermute(value, 'ctx', self.route(lambda z, y, c: (z ^ 2, y, c)))  56.1 us
    ppermute x17, waiting for transfers between devices, over_y(): return lax.ppermute(value, 'ctx', self.route(lambda z, y, c: (z, 1 - y, c)))  50.1 us
    pallas_call x2, Pallas kernels, kernel_call(): pl.pallas_call(kernel, out_shape=outs, in_specs=[smem] * len(tables) + [v...  46.9 us
    ppermute x9, waiting for transfers between devices, over_x(): return lax.ppermute(value, 'fsdp', [(0, 1), (1, 0)])  33.1 us
    all_to_all x1, waiting for transfers between devices, on_block(): lax.all_to_all(attn_sent, 'ctx', 0, 0, tiled=True)  28.4 us
    ppermute x17, starting transfers between devices, over_y(): return lax.ppermute(value, 'ctx', self.route(lambda z, y, c: (z, 1 - y, c)))  26.2 us
  transfers between devices with their start and end apart: 70, of which 25 were waited for; matrix products, arithmetic and copies ran while one was open for 8% of the time, Pallas kernels for 28%

profile of v11, /device:TPU:0, one launch (start us, length us, event | category | flops | bytes accessed | tf_op | source)
XLA Modules:
  0.0 554.3 jit_solution(14322523433165354940)
XLA Ops:
  23.8 8.9 %copy.71 = bf16[512,2,4608]{2,0,1:T(8,128)(2,1)} copy(bf16[512,2,4608]{2,1,0:T(2,128)(2,1)} %param.15) | data formatting | bytes 18874368 | tf_op jit(solution)/shard_map/optimization_barrier | solution.py:301
  54.0 29.2 %collective-permute-done.6.refs_4_.refs_5_.refs_3_ = bf16[128,5632]{1,0:T(8,128)(2,1)} collective-permute-done((bf16[128,5632]{1,0:T(8,128)(2,1)}, bf16[128,5632]{1,0:T(8,128)(2,1)}, u32[]{:S(2)}, u32[]{:S(2)}) %collective-permute-start.6) | collective-permute-done | bytes 1441824 | tf_op jit(solution)/shard_map/ppermute | solution.py:270
  88.5 22.0 %shard_map.196 = (bf16[16,64,256]{2,1,0:T(8,128)(2,1)}, bf16[4096,64]{1,0:T(8,128)(2,1)S(1)}, bf16[64,4096]{1,0:T(8,128)(2,1)S(1)}, bf16[4096,64]{1,0:T(8,128)(2...) custom-call(s32[32]{0:T(128)S(1)} %broadcast_add_fusion.q_slot, ...), custom_call_target="tpu_custom_call" | custom-call | flops 1 | bytes 1 | tf_op jit(solution)/shard_map/pallas_call | solution.py:226
  120.7 28.4 %all-to-all-done.1 = bf16[16,64,256]{2,1,0:T(8,128)(2,1)S(1)} async-done(((bf16[16,64,256]{2,1,0:T(8,128)(2,1)}), bf16[16,64,256]{2,1,0:T(8,128)(2,1)S(1)}, u32[]{:S(2)}, u32[]{:S(2)}) %all-to-all-start.1) | async-done | bytes 524320 | tf_op jit(solution)/shard_map/all_to_all | solution.py:1153
  158.9 16.8 %shard_map.198 = (bf16[256,1792]{1,0:T(8,128)(2,1)}, bf16[256,1792]{1,0:T(8,128)(2,1)}, bf16[256,1792]{1,0:T(8,128)(2,1)}, bf16[256,1792]{1,0:T(8,128)(2,1)}, f32[256,1024]{1,0:T(8,128)}, /*index=5*/f32[256,1024]{1,0:T(8,128)}) custom-call(s32[4]{0:T(128)} %pad_add_fusion.here, bf16[256,1024]{1,0:T(8,128)(2,1)} %get-tuple-element.116.refs_0_, ...), custom_call_target="tpu_custom_call" | custom-call | flops 1 | bytes 1 | tf_op jit(solution)/shard_map/pallas_call | solution.py:316
  184.8 16.9 %shard_map.199 = (bf16[256,1792]{1,0:T(8,128)(2,1)}, bf16[256,1792]{1,0:T(8,128)(2,1)}, bf16[256,1792]{1,0:T(8,128)(2,1)}, bf16[256,1792]{1,0:T(8,128)(2,1)}, bf...) custom-call(s32[4]{0:T(128)} %pad_add_fusion.here, ...), custom_call_target="tpu_custom_call" | custom-call | flops 1 | bytes 1 | tf_op jit(solution)/shard_map/pallas_call | solution.py:316
  217.7 19.3 %collective-permute-done.24.refs_7_ = bf16[256,1792]{1,0:T(8,128)(2,1)} collective-permute-done((bf16[256,1792]{1,0:T(8,128)(2,1)}, bf16[256,1792]{1,0:T(8,128)(2,1)}, u32[]{:S(2)}, u32[]{:S(2)}) %collective-permute-start.24) | collective-permute-done | bytes 917536 | tf_op jit(solution)/shard_map/ppermute | solution.py:261
  238.6 7.5 %shard_map.200 = (bf16[2,256,1152]{2,1,0:T(8,128)(2,1)}, f32[2,256,1152]{2,1,0:T(8,128)}) custom-call(s32[4]{0:T(128)} %pad_add_fusion.here, bf16[1024,256]{1,0:T(8,128)(2,1)} %get-tuple-element.135.refs_0_, bf16[1024,256]{1,0:T(8,128)(2,1)} %copy-done.42, bf16[1024,256]{1,0:T(8,128)(2,1)} %collective-permute-done.20.refs_2_, bf16[1024,256]{1,0:T(8,128)(2,1)} %copy-done.43, ...), custom_call_target="tpu_custom_call" | custom-call | flops 3000000000 | bytes 1 | tf_op jit(solution)/shard_map/pallas_call | solution.py:316
  251.8 24.9 %shard_map.201 = bf16[16,192,256]{2,1,0:T(8,128)(2,1)} custom-call(s32[32]{0:T(128)S(1)} %broadcast_add_fusion.q_slot, s32[32]{0:T(128)S(1)} %get-tuple-element.201.kv_slot, s32[16]{0:T(128)S(1)} %get-tuple-element.222.first, s32[16]{0:T(128)S(1)} %get-tuple-element.223.last, bf16[16,64,256]{2,1,0:T(8,128)(2,1)S(1)} %all-to-all-done.2.d_ref, ...), custom_call_target="tpu_custom_call" | custom-call | flops 24999999488 | bytes 1 | tf_op jit(solution)/shard_map/pallas_call | solution.py:226
  288.3 7.5 %shard_map.204 = (bf16[2,256,1152]{2,1,0:T(8,128)(2,1)}, f32[2,256,1152]{2,1,0:T(8,128)}) custom-call(s32[4]{0:T(128)} %pad_add_fusion.here, bf16[1024,256]{1,0:T(8,128)(2,1)} %get-tuple-element.135.refs_0_, bf16[1024,256]{1,0:T(8,128)(2,1)} %copy-done.42, bf16[1024,256]{1,0:T(8,128)(2,1)} %collective-permute-done.20.refs_2_, bf16[1024,256]{1,0:T(8,128)(2,1)} %copy-done.43, ...), custom_call_target="tpu_custom_call" | custom-call | flops 3000000000 | bytes 1 | tf_op jit(solution)/shard_map/pallas_call | solution.py:316
  296.3 28.0 %collective-permute-done.51 = bf16[256,1152]{1,0:T(8,128)(2,1)} collective-permute-done((bf16[256,1152]{1,0:T(8,128)(2,1)S(1)}, bf16[256,1152]{1,0:T(8,128)(2,1)}, u32[]{:S(2)}, u32[]{:S(2)}) %collective-permute-start.51) | collective-permute-done | bytes 589856 | tf_op jit(solution)/shard_map/ppermute | solution.py:264
  328.4 8.5 %shard_map.202 = (bf16[768,256]{1,0:T(8,128)(2,1)}, bf16[768,256]{1,0:T(8,128)(2,1)}, bf16[768,256]{1,0:T(8,128)(2,1)}, bf16[768,256]{1,0:T(8,128)(2,1)}, f32[256,1024]{1,0:T(8,128)}, /*index=5*/f32[8,1024]{1,0:T(8,128)}) custom-call(s32[4]{0:T(128)} %pad_add_fusion.here, bf16[16,192,256]{2,1,0:T(8,128)(2,1)} %all-to-all-done.3.refs_0_, ...), custom_call_target="tpu_custom_call" | custom-call | flops 12000000000 | bytes 1 | tf_op jit(solution)/shard_map/pallas_call | solution.py:316
  340.7 13.6 %collective-permute-done.52 = bf16[256,1152]{1,0:T(8,128)(2,1)S(1)} collective-permute-done((bf16[256,1152]{1,0:T(8,128)(2,1)S(1)}, bf16[256,1152]{1,0:T(8,128)(2,1)S(1)}, u32[]{:S(2)}, u32[]{:S(2)}) %collective-permute-start.52) | collective-permute-done | bytes 589856 | tf_op jit(solution)/shard_map/ppermute | solution.py:267
  354.4 9.8 %shard_map.208 = (bf16[2,288,1024]{2,1,0:T(8,128)(2,1)}, f32[2,288,1024]{2,1,0:T(8,128)}) custom-call(s32[4]{0:T(128)} %pad_add_fusion.here, bf16[256,1024]{1,0:T(8,128)(2,1)} %bitcast.93, bf16[256,1024]{1,0:T(8,128)(2,1)} %collective-permute-done.42.refs_1_, bf16[256,1024]{1,0:T(8,128)(2,1)} %copy-done.41, ...), custom_call_target="tpu_custom_call" | custom-call | flops 3000000000 | bytes 1 | tf_op jit(solution)/shard_map/pallas_call | solution.py:316
  368.5 7.8 %collective-permute-done.35.refs_7_ = bf16[768,256]{1,0:T(8,128)(2,1)S(1)} collective-permute-done((bf16[768,256]{1,0:T(8,128)(2,1)}, bf16[768,256]{1,0:T(8,128)(2,1)S(1)}, u32[]{:S(2)}, u32[]{:S(2)}) %collective-permute-start.35) | collective-permute-done | bytes 393248 | tf_op jit(solution)/shard_map/ppermute | solution.py:261
  377.0 7.1 %shard_map.203 = (bf16[2,272,768]{2,1,0:T(8,128)(2,1)}, f32[2,272,768]{2,1,0:T(8,128)}) custom-call(s32[4]{0:T(128)} %pad_add_fusion.here, bf16[2,1024,256]{2,1,0:T(8,128)(2,1)} %pad_maximum_fusion.5.refs_0_, bf16[2,1024,256]{2,1,0:T(8,128)(2,1)} %collective-permute-done.29.refs_1_, bf16[2,1024,256]{2,1,0:T(8,128)(2,1)} %collective-permute-done.30.refs_2_, ...), custom_call_target="tpu_custom_call" | custom-call | flops 3000000000 | bytes 1 | tf_op jit(solution)/shard_map/pallas_call | solution.py:316
  385.6 10.6 %collective-permute-done.46 = bf16[256,1152]{1,0:T(8,128)(2,1)S(1)} collective-permute-done((bf16[256,1152]{1,0:T(8,128)(2,1)S(1)}, bf16[256,1152]{1,0:T(8,128)(2,1)S(1)}, u32[]{:S(2)}, u32[]{:S(2)}) %collective-permute-start.46) | collective-permute-done | bytes 589856 | tf_op jit(solution)/shard_map/ppermute | solution.py:267
  411.0 21.8 %collective-permute-done.60 = bf16[288,1024]{1,0:T(8,128)(2,1)S(1)} collective-permute-done((bf16[288,1024]{1,0:T(8,128)(2,1)S(1)}, bf16[288,1024]{1,0:T(8,128)(2,1)S(1)}, u32[]{:S(2)}, u32[]{:S(2)}) %collective-permute-start.60) | collective-permute-done | bytes 589856 | tf_op jit(solution)/shard_map/ppermute | solution.py:264
  441.2 26.2 %collective-permute-done.61 = bf16[288,1024]{1,0:T(8,128)(2,1)S(1)} collective-permute-done((bf16[288,1024]{1,0:T(8,128)(2,1)S(1)}, bf16[288,1024]{1,0:T(8,128)(2,1)S(1)}, u32[]{:S(2)}, u32[]{:S(2)}) %collective-permute-start.61) | collective-permute-done | bytes 589856 | tf_op jit(solution)/shard_map/ppermute | solution.py:267
  473.6 12.4 %collective-permute-done.62 = bf16[288,1024]{1,0:T(8,128)(2,1)S(1)} collective-permute-done((bf16[288,1024]{1,0:T(8,128)(2,1)S(1)}, bf16[288,1024]{1,0:T(8,128)(2,1)S(1)}, u32[]{:S(2)}, u32[]{:S(2)}) %collective-permute-start.62) | collective-permute-done | bytes 589856 | tf_op jit(solution)/shard_map/ppermute | solution.py:264
  487.5 7.4 %collective-permute-done.39 = bf16[272,768]{1,0:T(8,128)(2,1)S(1)} collective-permute-done((bf16[272,768]{1,0:T(8,128)(2,1)S(1)}, bf16[272,768]{1,0:T(8,128)(2,1)S(1)}, u32[]{:S(2)}, u32[]{:S(2)}) %collective-permute-start.39) | collective-permute-done | bytes 417824 | tf_op jit(solution)/shard_map/ppermute | solution.py:264
  498.5 9.7 %shard_map.205.refs_4_ = f32[512,2,4608]{2,1,0:T(2,128)} custom-call(s32[4]{0:T(128)} %pad_add_fusion.here, bf16[2,256,1152]{2,1,0:T(8,128)(2,1)} %copy-done.24, bf16[2,256,1152]{2,1,0:T(8,128)(2,1)} %copy-done.38, bf16[2,256,1152]{2,1,0:T(8,128)(2,1)} %copy-done.37, bf16[2,256,1152]{2,1,0:T(8,128)(2,1)} %copy-done.39), custom_call_target="tpu_custom_call" | custom-call | flops 10000000000 | bytes 1 | tf_op jit(solution)/shard_map/pallas_call | solution.py:316
  517.3 9.7 %shard_map.206 = f32[512,2,4608]{2,1,0:T(2,128)} custom-call(s32[4]{0:T(128)} %pad_add_fusion.here, bf16[2,256,1152]{2,1,0:T(8,128)(2,1)} %copy-done.10, bf16[2,256,1152]{2,1,0:T(8,128)(2,1)} %copy-done.22, bf16[2,256,1152]{2,1,0:T(8,128)(2,1)} %copy-done.18, bf16[2,256,1152]{2,1,0:T(8,128)(2,1)} %copy-done.23, ...), custom_call_target="tpu_custom_call", output_to_operand_aliasing={{}: (5, {})} | custom-call | flops 10000000000 | bytes 1 | tf_op jit(solution)/shard_map/pallas_call | solution.py:316
  545.9 7.9 %shard_map.209 = f32[2304,1024]{1,0:T(8,128)} custom-call(s32[4]{0:T(128)} %pad_add_fusion.here, bf16[2,288,1024]{2,1,0:T(8,128)(2,1)} %copy-done.25, bf16[2,288,1024]{2,1,0:T(8,128)(2,1)} %collective-permute-done.63.refs_1_, bf16[2,288,1024]{2,1,0:T(8,128)(2,1)} %collective-permute-done.64.refs_2_, bf16[2,288,1024]{2,1,0:T(8,128)(2,1)} %collective-permute-done.65.refs_3_), custom_call_target="tpu_custom_call" | custom-call | flops 5000000000 | bytes 1 | tf_op jit(solution)/shard_map/pallas_call | solution.py:316
  (296 shorter events, 190.5 us)
Async XLA Ops:
  43.0 44.3 %all-to-all-start = ((bf16[16,192,256]{2,1,0:T(8,128)(2,1)}), bf16[16,192,256]{2,1,0:T(8,128)(2,1)S(1)}, u32[]{:S(2)}, u32[]{:S(2)}) async-start(bf16[16,192,256]{2,1,0:T(8,128)(2,1)} %get-tuple-element.110), calls=%async_computation | async-start | bytes 3145728 | tf_op jit(solution)/shard_map/all_to_all | solution.py:1129
  85.7 35.0 %collective-permute-start.8 = (bf16[128,5632]{1,0:T(8,128)(2,1)}, bf16[128,5632]{1,0:T(8,128)(2,1)}, u32[]{:S(2)}, u32[]{:S(2)}) collective-permute-start(bf16[128,5632]{1,0:T(8,128)(2,1)} %collective-permute-done.6.refs_4_.refs_5_.refs_3_), channel_id=1, source_target_pairs={{0,4},{2,6},{4,0},{6,2},{8,12},{10,14},{12,8},{14,10},{16,20},{18,... | collective-permute-start | bytes 4325384 | tf_op jit(solution)/shard_map/ppermute | solution.py:261
  111.3 38.1 %collective-permute-start.15 = (bf16[2304,256]{1,0:T(8,128)(2,1)}, bf16[2304,256]{1,0:T(8,128)(2,1)}, u32[]{:S(2)}, u32[]{:S(2)}) collective-permute-start(bf16[2304,256]{1,0:T(8,128)(2,1)} %collective-permute-done.10.refs_8_), channel_id=1, source_target_pairs={{0,4},{2,6},{4,0},{6,2},{8,12},{10,14},{12,8},{14,10},{16,20},{18,... | collective-permute-start | bytes 3538952 | tf_op jit(solution)/shard_map/ppermute | solution.py:261
  113.5 36.2 %collective-permute-start.11 = (bf16[128,4608]{1,0:T(8,128)(2,1)}, bf16[128,4608]{1,0:T(8,128)(2,1)}, u32[]{:S(2)}, u32[]{:S(2)}) collective-permute-start(bf16[128,4608]{1,0:T(8,128)(2,1)} %pad_maximum_fusion.1), channel_id=1, source_target_pairs={{0,1},{1,0},{2,3},{3,2},{4,5},{5,4},{6,7},{7,6},{8,9},{9,8},{10,11... | collective-permute-start | bytes 3538952 | tf_op jit(solution)/shard_map/ppermute | solution.py:270
  180.2 35.1 %collective-permute-start.23 = (bf16[256,1792]{1,0:T(8,128)(2,1)}, bf16[256,1792]{1,0:T(8,128)(2,1)}, u32[]{:S(2)}, u32[]{:S(2)}) collective-permute-start(bf16[256,1792]{1,0:T(8,128)(2,1)} %get-tuple-element.141), channel_id=1, source_target_pairs={{0,4},{2,6},{4,0},{6,2},{8,12},{10,14},{12,8},{14,10},{16,20},{18,... | collective-permute-start | bytes 2752520 | tf_op jit(solution)/shard_map/ppermute | solution.py:261
  182.1 54.9 %collective-permute-start.24 = (bf16[256,1792]{1,0:T(8,128)(2,1)}, bf16[256,1792]{1,0:T(8,128)(2,1)}, u32[]{:S(2)}, u32[]{:S(2)}) collective-permute-start(bf16[256,1792]{1,0:T(8,128)(2,1)} %collective-permute-done.18), channel_id=1, source_target_pairs={{0,4},{2,6},{4,0},{6,2},{8,12},{10,14},{12,8},{14,10},{16,20},{18,... | collective-permute-start | bytes 2752520 | tf_op jit(solution)/shard_map/ppermute | solution.py:261
  201.7 46.6 %all-to-all-start.2 = ((bf16[16,64,256]{2,1,0:T(8,128)(2,1)}), bf16[16,64,256]{2,1,0:T(8,128)(2,1)S(1)}, u32[]{:S(2)}, u32[]{:S(2)}) async-start(bf16[16,64,256]{2,1,0:T(8,128)(2,1)} %bitcast.102), calls=%async_computation.2 | async-start | bytes 1048576 | tf_op jit(solution)/shard_map/all_to_all | solution.py:1193
  206.6 40.0 %collective-permute-start.27 = (bf16[256,1792]{1,0:T(8,128)(2,1)}, bf16[256,1792]{1,0:T(8,128)(2,1)}, u32[]{:S(2)}, u32[]{:S(2)}) collective-permute-start(bf16[256,1792]{1,0:T(8,128)(2,1)} %get-tuple-element.154), channel_id=1, source_target_pairs={{0,2},{2,0},{4,6},{6,4},{8,10},{10,8},{12,14},{14,12},{16,18},{18,... | collective-permute-start | bytes 2752520 | tf_op jit(solution)/shard_map/ppermute | solution.py:258
  215.3 61.5 %collective-permute-start.26 = (bf16[256,1792]{1,0:T(8,128)(2,1)}, bf16[256,1792]{1,0:T(8,128)(2,1)}, u32[]{:S(2)}, u32[]{:S(2)}) collective-permute-start(bf16[256,1792]{1,0:T(8,128)(2,1)} %get-tuple-element.153), channel_id=1, source_target_pairs={{0,4},{2,6},{4,0},{6,2},{8,12},{10,14},{12,8},{14,10},{16,20},{18,... | collective-permute-start | bytes 2752520 | tf_op jit(solution)/shard_map/ppermute | solution.py:261
  277.4 51.0 %all-to-all-start.3 = ((bf16[16,192,256]{2,1,0:T(8,128)(2,1)}), bf16[16,192,256]{2,1,0:T(8,128)(2,1)}, u32[]{:S(2)}, u32[]{:S(2)}) async-start(bf16[16,192,256]{2,1,0:T(8,128)(2,1)} %shard_map.201), calls=%async_computation.3 | async-start | bytes 3145728 | tf_op jit(solution)/shard_map/all_to_all | solution.py:1215
  285.0 39.4 %collective-permute-start.51 = (bf16[256,1152]{1,0:T(8,128)(2,1)S(1)}, bf16[256,1152]{1,0:T(8,128)(2,1)}, u32[]{:S(2)}, u32[]{:S(2)}) collective-permute-start(bf16[256,1152]{1,0:T(8,128)(2,1)S(1)} %fusion.7), channel_id=1, source_target_pairs={{0,8},{2,10},{4,12},{6,14},{8,0},{10,2},{12,4},{14,6},{16,24},{18,... | collective-permute-start | bytes 1769480 | tf_op jit(solution)/shard_map/ppermute | solution.py:264
  286.8 53.4 %collective-permute-start.30 = (bf16[2,1024,256]{2,1,0:T(8,128)(2,1)}, bf16[2,1024,256]{2,1,0:T(8,128)(2,1)}, u32[]{:S(2)}, u32[]{:S(2)}) collective-permute-start(bf16[2,1024,256]{2,1,0:T(8,128)(2,1)} %pad_maximum_fusion.5.refs_0_), channel_id=1, source_target_pairs={{0,4},{2,6},{4,0},{6,2},{8,12},{10,14},{12,8},{14,10},{16,20},{18,... | collective-permute-start | bytes 3145736 | tf_op jit(solution)/shard_map/ppermute | solution.py:261
  288.3 51.9 %collective-permute-start.58 = (bf16[256,1024]{1,0:T(8,128)(2,1)}, bf16[256,1024]{1,0:T(8,128)(2,1)}, u32[]{:S(2)}, u32[]{:S(2)}) collective-permute-start(bf16[256,1024]{1,0:T(8,128)(2,1)} %copy-done.41), channel_id=1, source_target_pairs={{0,2},{2,0},{4,6},{6,4},{8,10},{10,8},{12,14},{14,12},{16,18},{18,... | collective-permute-start | bytes 1572872 | tf_op jit(solution)/shard_map/ppermute | solution.py:258
  295.8 41.2 %collective-permute-start.44 = (bf16[2,256,1152]{2,1,0:T(8,128)(2,1)}, bf16[2,256,1152]{2,1,0:T(8,128)(2,1)}, u32[]{:S(2)}, u32[]{:S(2)}) collective-permute-start(bf16[2,256,1152]{2,1,0:T(8,128)(2,1)} %get-tuple-element.185), channel_id=1, source_target_pairs={{0,1},{1,0},{2,3},{3,2},{4,5},{5,4},{6,7},{7,6},{8,9},{9,8},{10,11... | collective-permute-start | bytes 3538952 | tf_op jit(solution)/shard_map/ppermute | solution.py:270
  340.2 36.0 %collective-permute-start.29 = (bf16[2,1024,256]{2,1,0:T(8,128)(2,1)S(1)}, bf16[2,1024,256]{2,1,0:T(8,128)(2,1)}, u32[]{:S(2)}, u32[]{:S(2)}) collective-permute-start(bf16[2,1024,256]{2,1,0:T(8,128)(2,1)S(1)} %copy-done.26), channel_id=1, source_target_pairs={{0,2},{2,0},{4,6},{6,4},{8,10},{10,8},{12,14},{14,12},{16,18},{18,... | collective-permute-start | bytes 3145736 | tf_op jit(solution)/shard_map/ppermute | solution.py:258
  396.3 36.8 %collective-permute-start.47 = (bf16[256,1152]{1,0:T(8,128)(2,1)S(1)}, bf16[256,1152]{1,0:T(8,128)(2,1)S(1)}, u32[]{:S(2)}, u32[]{:S(2)}) collective-permute-start(bf16[256,1152]{1,0:T(8,128)(2,1)S(1)} %add_convert_fusion.6), channel_id=1, source_target_pairs={{0,8},{2,10},{4,12},{6,14},{8,0},{10,2},{12,4},{14,6},{16,24},{18,... | collective-permute-start | bytes 1769480 | tf_op jit(solution)/shard_map/ppermute | solution.py:264
  396.6 36.1 %collective-permute-start.60 = (bf16[288,1024]{1,0:T(8,128)(2,1)S(1)}, bf16[288,1024]{1,0:T(8,128)(2,1)S(1)}, u32[]{:S(2)}, u32[]{:S(2)}) collective-permute-start(bf16[288,1024]{1,0:T(8,128)(2,1)S(1)} %fusion.9), channel_id=1, source_target_pairs={{0,8},{2,10},{4,12},{6,14},{8,0},{10,2},{12,4},{14,6},{16,24},{18,... | collective-permute-start | bytes 1769480 | tf_op jit(solution)/shard_map/ppermute | solution.py:264
  405.2 35.5 %collective-permute-start.55 = (bf16[2,256,1152]{2,1,0:T(8,128)(2,1)S(1)}, bf16[2,256,1152]{2,1,0:T(8,128)(2,1)S(1)}, u32[]{:S(2)}, u32[]{:S(2)}) collective-permute-start(bf16[2,256,1152]{2,1,0:T(8,128)(2,1)S(1)} %pad_maximum_fusion.3.refs_0_), channel_id=1, source_target_pairs={{0,4},{2,6},{4,0},{6,2},{8,12},{10,14},{12,8},{14,10},{16,20},{18,... | collective-permute-start | bytes 3538952 | tf_op jit(solution)/shard_map/ppermute | solution.py:261
  433.0 34.5 %collective-permute-start.61 = (bf16[288,1024]{1,0:T(8,128)(2,1)S(1)}, bf16[288,1024]{1,0:T(8,128)(2,1)S(1)}, u32[]{:S(2)}, u32[]{:S(2)}) collective-permute-start(bf16[288,1024]{1,0:T(8,128)(2,1)S(1)} %fusion), channel_id=1, source_target_pairs={{0,16},{2,18},{4,20},{6,22},{8,24},{10,26},{12,28},{14,30},{16,0},... | collective-permute-start | bytes 1769480 | tf_op jit(solution)/shard_map/ppermute | solution.py:267
  433.2 54.2 %collective-permute-start.49 = (bf16[2,256,1152]{2,1,0:T(8,128)(2,1)S(1)}, bf16[2,256,1152]{2,1,0:T(8,128)(2,1)S(1)}, u32[]{:S(2)}, u32[]{:S(2)}) collective-permute-start(bf16[2,256,1152]{2,1,0:T(8,128)(2,1)S(1)} %pad_maximum_fusion.2.refs_0_), channel_id=1, source_target_pairs={{0,4},{2,6},{4,0},{6,2},{8,12},{10,14},{12,8},{14,10},{16,20},{18,... | collective-permute-start | bytes 3538952 | tf_op jit(solution)/shard_map/ppermute | solution.py:261
  440.7 54.4 %collective-permute-start.54 = (bf16[2,256,1152]{2,1,0:T(8,128)(2,1)S(1)}, bf16[2,256,1152]{2,1,0:T(8,128)(2,1)S(1)}, u32[]{:S(2)}, u32[]{:S(2)}) collective-permute-start(bf16[2,256,1152]{2,1,0:T(8,128)(2,1)S(1)} %pad_maximum_fusion.3.refs_0_), channel_id=1, source_target_pairs={{0,2},{2,0},{4,6},{6,4},{8,10},{10,8},{12,14},{14,12},{16,18},{18,... | collective-permute-start | bytes 3538952 | tf_op jit(solution)/shard_map/ppermute | solution.py:258
  440.7 54.9 %collective-permute-start.56 = (bf16[2,256,1152]{2,1,0:T(8,128)(2,1)S(1)}, bf16[2,256,1152]{2,1,0:T(8,128)(2,1)S(1)}, u32[]{:S(2)}, u32[]{:S(2)}) collective-permute-start(bf16[2,256,1152]{2,1,0:T(8,128)(2,1)S(1)} %collective-permute-done.55.refs_2_), channel_id=1, source_target_pairs={{0,2},{2,0},{4,6},{6,4},{8,10},{10,8},{12,14},{14,12},{16,18},{18,... | collective-permute-start | bytes 3538952 | tf_op jit(solution)/shard_map/ppermute | solution.py:258
  495.2 37.4 %collective-permute-start.40 = (bf16[2,272,768]{2,1,0:T(8,128)(2,1)S(1)}, bf16[2,272,768]{2,1,0:T(8,128)(2,1)S(1)}, u32[]{:S(2)}, u32[]{:S(2)}) collective-permute-start(bf16[2,272,768]{2,1,0:T(8,128)(2,1)S(1)} %pad_maximum_fusion.6.refs_0_), channel_id=1, source_target_pairs={{0,2},{2,0},{4,6},{6,4},{8,10},{10,8},{12,14},{14,12},{16,18},{18,... | collective-permute-start | bytes 2506760 | tf_op jit(solution)/shard_map/ppermute | solution.py:258
  497.3 34.7 %collective-permute-start.41 = (bf16[2,272,768]{2,1,0:T(8,128)(2,1)S(1)}, bf16[2,272,768]{2,1,0:T(8,128)(2,1)}, u32[]{:S(2)}, u32[]{:S(2)}) collective-permute-start(bf16[2,272,768]{2,1,0:T(8,128)(2,1)S(1)} %pad_maximum_fusion.6.refs_0_), channel_id=1, source_target_pairs={{0,4},{2,6},{4,0},{6,2},{8,12},{10,14},{12,8},{14,10},{16,20},{18,... | collective-permute-start | bytes 2506760 | tf_op jit(solution)/shard_map/ppermute | solution.py:261
  (95 other events, 1439.3 us)

commit v12 on v11

--- a/solution.py
+++ b/solution.py
@@ -278,15 +278,16 @@
         got, got_far = self.over_core(give), self.over_core(give_far)
         return (near, got, self.over_y(far), self.over_y(got_far))
 
-    def sum_depth(self, kept, got, time=None):
+    def sum_depth(self, kept, got, time=None, last=None):
         def half(index):
             return add(pick(kept, index, 0), pick(got, index, 0))
 
         given = self.over_z(half(1 - self.half))
         part = add(half(self.half), given)
         other = self.over_two_z(part)
-        full = add(part, other if time is None else after(other, time))
-        return jnp.stack([full, self.over_z(full)])
+        full = add(part, other if time is None else after(other, *jax.tree.leaves(time)))
+        other = self.over_z(full)
+        return jnp.stack([full, other if last is None else after(other, last)])
 
 
 def pick(value, index, axis):
@@ -1221,6 +1222,8 @@
         here, d_plane, first_shares, second_shares, columns // 2
     )
     second_got = links.over_x(after(second_products[0], first_got))
+    pair_beside = links.over_y(after(pair, d_sent))
+    d_back = after(d_back, down_terms[0], pair_beside, second_got)
     *d_shares, d_inputs, gain_sums = attention_back(
         here,
         [
@@ -1228,20 +1231,20 @@
             cosine[0], sine[0], w_qkv, tokens_here, scale_one, gain_attn[None], d_h_one, d_attn,
         ],
     )
+    down_got = links.over_x(after(down_terms[0], second_got))
+    near, far, give, give_far = d_shares
     second_got = after(second_got, d_shares[0])
-    near, far, give, give_far = d_shares
     got, got_far = links.over_core(give), links.over_core(give_far)
     attention_shares = (near, got, links.over_y(far), links.over_y(got_far))
-    down_got = links.over_x(after(down_terms[0], second_got))
-    pair_plane = plane(pair, links.over_y(after(pair, d_sent)), d_shares[0])
+    pair_plane = plane(pair, pair_beside, d_sent)
     attention_terms = attention_products(
         here, pair_plane, attention_shares, gain_sums, ffn_gain_term
     )
-    first_pair = links.sum_depth(first_products[1], first_got, attention_shares[2])
+    first_pair = links.sum_depth(first_products[1], first_got, (*attention_shares[1:], down_got, pair_plane[3]), attention_terms[0])
     second_pair = links.sum_depth(second_products[1], second_got, attention_shares[3])
-    down_pair = links.sum_depth(down_terms[1], after(down_got, got_far))
     attention_pair = links.sum_depth(attention_terms[1], links.over_x(attention_terms[0]))
     first_placed = place_gate_up(here, 0, links.spread_plane(first_pair), None)
+    down_pair = links.sum_depth(down_terms[1], after(down_got, got_far), first_placed)
     grad_gate_up = place_gate_up(here, 1, links.spread_plane(second_pair), first_placed)
 
     def spread_after(value, time):

time: 563 us -> 567 us (level)
    ppermute x4, waiting for transfers between devices: 56.1 us -> 37.8 us  [over_two_z(): return lax.ppermute(value, 'ctx', self.route(lambda z, y, c: (z ^ 2, y, c)))]
    ppermute x17, waiting for transfers between devices: 50.1 us -> 64 us  [over_y(): return lax.ppermute(value, 'ctx', self.route(lambda z, y, c: (z, 1 - y, c)))]
  transfers between devices with their start and end apart: 70 -> 70, of which waited for: 25 -> 26; matrix products, arithmetic and copies ran while one was open for 8% -> 8% of each run, Pallas kernels for 28% -> 27%
where the time goes in v12:
time: 567 us; the launch traced here: 558 us
  waiting for transfers between devices  252 us (44%)
  Pallas kernels  167 us (29%)
  starting transfers between devices  76.4 us (13%)
  local copies, waits for them, and re-layouts  44.6 us (8%)
  other arithmetic  15.8 us (3%)
    pallas_call x13, Pallas kernels, call_with_here(): pl.pallas_call(kernel, grid_spec=pltpu.PrefetchScalarGridSpec(num_scalar_...  120 us
    ppermute x8, waiting for transfers between devices, over_z(): return lax.ppermute(value, 'ctx', self.route(lambda z, y, c: (z ^ 1, y, c)))  83.1 us
    ppermute x17, waiting for transfers between devices, over_y(): return lax.ppermute(value, 'ctx', self.route(lambda z, y, c: (z, 1 - y, c)))  64 us
    pallas_call x2, Pallas kernels, kernel_call(): pl.pallas_call(kernel, out_shape=outs, in_specs=[smem] * len(tables) + [v...  46.9 us
    ppermute x4, waiting for transfers between devices, over_two_z(): return lax.ppermute(value, 'ctx', self.route(lambda z, y, c: (z ^ 2, y, c)))  37.8 us
    ppermute x9, waiting for transfers between devices, over_x(): return lax.ppermute(value, 'fsdp', [(0, 1), (1, 0)])  31 us
    all_to_all x1, waiting for transfers between devices, on_block(): lax.all_to_all(attn_sent, 'ctx', 0, 0, tiled=True)  28.4 us
    ppermute x17, starting transfers between devices, over_y(): return lax.ppermute(value, 'ctx', self.route(lambda z, y, c: (z, 1 - y, c)))  24.5 us
  transfers between devices with their start and end apart: 70, of which 26 were waited for; matrix products, arithmetic and copies ran while one was open for 8% of the time, Pallas kernels for 27%

profile of v12, /device:TPU:0, one launch (start us, length us, event | category | flops | bytes accessed | tf_op | source)
XLA Modules:
  0.0 558.4 jit_solution(4249476382129390923)
XLA Ops:
  23.9 8.9 %copy.71 = bf16[512,2,4608]{2,0,1:T(8,128)(2,1)} copy(bf16[512,2,4608]{2,1,0:T(2,128)(2,1)} %param.15) | data formatting | bytes 18874368 | tf_op jit(solution)/shard_map/optimization_barrier | solution.py:302
  54.1 29.2 %collective-permute-done.6.refs_4_.refs_5_.refs_3_ = bf16[128,5632]{1,0:T(8,128)(2,1)} collective-permute-done((bf16[128,5632]{1,0:T(8,128)(2,1)}, bf16[128,5632]{1,0:T(8,128)(2,1)}, u32[]{:S(2)}, u32[]{:S(2)}) %collective-permute-start.6) | collective-permute-done | bytes 1441824 | tf_op jit(solution)/shard_map/ppermute | solution.py:270
  88.6 22.0 %shard_map.196 = (bf16[16,64,256]{2,1,0:T(8,128)(2,1)}, bf16[4096,64]{1,0:T(8,128)(2,1)S(1)}, bf16[64,4096]{1,0:T(8,128)(2,1)S(1)}, bf16[4096,64]{1,0:T(8,128)(2...) custom-call(s32[32]{0:T(128)S(1)} %broadcast_add_fusion.q_slot, ...), custom_call_target="tpu_custom_call" | custom-call | flops 1 | bytes 1 | tf_op jit(solution)/shard_map/pallas_call | solution.py:226
  120.9 28.4 %all-to-all-done.1 = bf16[16,64,256]{2,1,0:T(8,128)(2,1)S(1)} async-done(((bf16[16,64,256]{2,1,0:T(8,128)(2,1)}), bf16[16,64,256]{2,1,0:T(8,128)(2,1)S(1)}, u32[]{:S(2)}, u32[]{:S(2)}) %all-to-all-start.1) | async-done | bytes 524320 | tf_op jit(solution)/shard_map/all_to_all | solution.py:1154
  159.1 16.8 %shard_map.198 = (bf16[256,1792]{1,0:T(8,128)(2,1)}, bf16[256,1792]{1,0:T(8,128)(2,1)}, bf16[256,1792]{1,0:T(8,128)(2,1)}, bf16[256,1792]{1,0:T(8,128)(2,1)}, f32[256,1024]{1,0:T(8,128)}, /*index=5*/f32[256,1024]{1,0:T(8,128)}) custom-call(s32[4]{0:T(128)} %pad_add_fusion.here, bf16[256,1024]{1,0:T(8,128)(2,1)} %get-tuple-element.118.refs_0_, ...), custom_call_target="tpu_custom_call" | custom-call | flops 1 | bytes 1 | tf_op jit(solution)/shard_map/pallas_call | solution.py:317
  184.9 17.0 %shard_map.199 = (bf16[256,1792]{1,0:T(8,128)(2,1)}, bf16[256,1792]{1,0:T(8,128)(2,1)}, bf16[256,1792]{1,0:T(8,128)(2,1)}, bf16[256,1792]{1,0:T(8,128)(2,1)}, bf...) custom-call(s32[4]{0:T(128)} %pad_add_fusion.here, ...), custom_call_target="tpu_custom_call" | custom-call | flops 1 | bytes 1 | tf_op jit(solution)/shard_map/pallas_call | solution.py:317
  217.8 19.4 %collective-permute-done.24.refs_7_ = bf16[256,1792]{1,0:T(8,128)(2,1)} collective-permute-done((bf16[256,1792]{1,0:T(8,128)(2,1)}, bf16[256,1792]{1,0:T(8,128)(2,1)}, u32[]{:S(2)}, u32[]{:S(2)}) %collective-permute-start.24) | collective-permute-done | bytes 917536 | tf_op jit(solution)/shard_map/ppermute | solution.py:261
  238.8 7.5 %shard_map.200 = (bf16[2,256,1152]{2,1,0:T(8,128)(2,1)}, f32[2,256,1152]{2,1,0:T(8,128)}) custom-call(s32[4]{0:T(128)} %pad_add_fusion.here, bf16[1024,256]{1,0:T(8,128)(2,1)} %get-tuple-element.137.refs_0_, bf16[1024,256]{1,0:T(8,128)(2,1)} %copy-done.43, bf16[1024,256]{1,0:T(8,128)(2,1)} %collective-permute-done.20.refs_2_, bf16[1024,256]{1,0:T(8,128)(2,1)} %copy-done.44, ...), custom_call_target="tpu_custom_call" | custom-call | flops 3000000000 | bytes 1 | tf_op jit(solution)/shard_map/pallas_call | solution.py:317
  251.9 24.9 %shard_map.201 = bf16[16,192,256]{2,1,0:T(8,128)(2,1)} custom-call(s32[32]{0:T(128)S(1)} %broadcast_add_fusion.q_slot, s32[32]{0:T(128)S(1)} %get-tuple-element.205.kv_slot, s32[16]{0:T(128)S(1)} %get-tuple-element.226.first, s32[16]{0:T(128)S(1)} %get-tuple-element.227.last, bf16[16,64,256]{2,1,0:T(8,128)(2,1)S(1)} %all-to-all-done.2.d_ref, ...), custom_call_target="tpu_custom_call" | custom-call | flops 24999999488 | bytes 1 | tf_op jit(solution)/shard_map/pallas_call | solution.py:226
  288.2 7.6 %shard_map.203 = (bf16[2,256,1152]{2,1,0:T(8,128)(2,1)}, f32[2,256,1152]{2,1,0:T(8,128)}) custom-call(s32[4]{0:T(128)} %pad_add_fusion.here, bf16[1024,256]{1,0:T(8,128)(2,1)} %get-tuple-element.137.refs_0_, bf16[1024,256]{1,0:T(8,128)(2,1)} %copy-done.43, bf16[1024,256]{1,0:T(8,128)(2,1)} %collective-permute-done.20.refs_2_, bf16[1024,256]{1,0:T(8,128)(2,1)} %copy-done.44, ...), custom_call_target="tpu_custom_call" | custom-call | flops 3000000000 | bytes 1 | tf_op jit(solution)/shard_map/pallas_call | solution.py:317
  300.8 9.8 %shard_map.202 = (bf16[2,288,1024]{2,1,0:T(8,128)(2,1)}, f32[2,288,1024]{2,1,0:T(8,128)}) custom-call(s32[4]{0:T(128)} %pad_add_fusion.here, bf16[256,1024]{1,0:T(8,128)(2,1)} %bitcast.93, bf16[256,1024]{1,0:T(8,128)(2,1)} %copy-done.45, bf16[256,1024]{1,0:T(8,128)(2,1)} %collective-permute-done.2.refs_2_, ...), custom_call_target="tpu_custom_call" | custom-call | flops 3000000000 | bytes 1 | tf_op jit(solution)/shard_map/pallas_call | solution.py:317
  310.6 13.8 %collective-permute-done.52 = bf16[256,1152]{1,0:T(8,128)(2,1)S(1)} collective-permute-done((bf16[256,1152]{1,0:T(8,128)(2,1)S(1)}, bf16[256,1152]{1,0:T(8,128)(2,1)S(1)}, u32[]{:S(2)}, u32[]{:S(2)}) %collective-permute-start.52) | collective-permute-done | bytes 589856 | tf_op jit(solution)/shard_map/ppermute | solution.py:264
  330.9 8.5 %shard_map.204 = (bf16[768,256]{1,0:T(8,128)(2,1)}, bf16[768,256]{1,0:T(8,128)(2,1)}, bf16[768,256]{1,0:T(8,128)(2,1)}, bf16[768,256]{1,0:T(8,128)(2,1)}, f32[256,1024]{1,0:T(8,128)}, /*index=5*/f32[8,1024]{1,0:T(8,128)}) custom-call(s32[4]{0:T(128)} %pad_add_fusion.here, bf16[16,192,256]{2,1,0:T(8,128)(2,1)} %all-to-all-done.3.refs_0_, ...), custom_call_target="tpu_custom_call" | custom-call | flops 12000000000 | bytes 1 | tf_op jit(solution)/shard_map/pallas_call | solution.py:317
  340.0 14.2 %collective-permute-done.53 = bf16[256,1152]{1,0:T(8,128)(2,1)S(1)} collective-permute-done((bf16[256,1152]{1,0:T(8,128)(2,1)S(1)}, bf16[256,1152]{1,0:T(8,128)(2,1)S(1)}, u32[]{:S(2)}, u32[]{:S(2)}) %collective-permute-start.53) | collective-permute-done | bytes 589856 | tf_op jit(solution)/shard_map/ppermute | solution.py:267
  358.1 8.4 %collective-permute-done.37.refs_6_ = bf16[768,256]{1,0:T(8,128)(2,1)S(1)} collective-permute-done((bf16[768,256]{1,0:T(8,128)(2,1)}, bf16[768,256]{1,0:T(8,128)(2,1)S(1)}, u32[]{:S(2)}, u32[]{:S(2)}) %collective-permute-start.37) | collective-permute-done | bytes 393248 | tf_op jit(solution)/shard_map/ppermute | solution.py:261
  392.0 8.4 %collective-permute-done.46 = bf16[256,1152]{1,0:T(8,128)(2,1)S(1)} collective-permute-done((bf16[256,1152]{1,0:T(8,128)(2,1)S(1)}, bf16[256,1152]{1,0:T(8,128)(2,1)S(1)}, u32[]{:S(2)}, u32[]{:S(2)}) %collective-permute-start.46) | collective-permute-done | bytes 589856 | tf_op jit(solution)/shard_map/ppermute | solution.py:264
  404.9 23.6 %collective-permute-done.47 = bf16[256,1152]{1,0:T(8,128)(2,1)S(1)} collective-permute-done((bf16[256,1152]{1,0:T(8,128)(2,1)S(1)}, bf16[256,1152]{1,0:T(8,128)(2,1)S(1)}, u32[]{:S(2)}, u32[]{:S(2)}) %collective-permute-start.47) | collective-permute-done | bytes 589856 | tf_op jit(solution)/shard_map/ppermute | solution.py:267
  432.3 24.4 %collective-permute-done.48 = bf16[256,1152]{1,0:T(8,128)(2,1)S(1)} collective-permute-done((bf16[256,1152]{1,0:T(8,128)(2,1)S(1)}, bf16[256,1152]{1,0:T(8,128)(2,1)S(1)}, u32[]{:S(2)}, u32[]{:S(2)}) %collective-permute-start.48) | collective-permute-done | bytes 589856 | tf_op jit(solution)/shard_map/ppermute | solution.py:264
  458.8 10.0 %shard_map.206.refs_4_ = f32[512,2,4608]{2,1,0:T(2,128)} custom-call(s32[4]{0:T(128)} %pad_add_fusion.here, bf16[2,256,1152]{2,1,0:T(8,128)(2,1)} %copy-done.25, bf16[2,256,1152]{2,1,0:T(8,128)(2,1)} %copy-done.39, bf16[2,256,1152]{2,1,0:T(8,128)(2,1)} %copy-done.38, bf16[2,256,1152]{2,1,0:T(8,128)(2,1)} %collective-permute-done.58.refs_3_), custom_call_target="tpu_custom_call" | custom-call | flops 10000000000 | bytes 1 | tf_op jit(solution)/shard_map/pallas_call | solution.py:317
  472.3 18.9 %collective-permute-done.62 = bf16[288,1024]{1,0:T(8,128)(2,1)S(1)} collective-permute-done((bf16[288,1024]{1,0:T(8,128)(2,1)S(1)}, bf16[288,1024]{1,0:T(8,128)(2,1)S(1)}, u32[]{:S(2)}, u32[]{:S(2)}) %collective-permute-start.62) | collective-permute-done | bytes 589856 | tf_op jit(solution)/shard_map/ppermute | solution.py:264
  493.2 11.6 %collective-permute-done.43 = bf16[272,768]{1,0:T(8,128)(2,1)S(1)} collective-permute-done((bf16[272,768]{1,0:T(8,128)(2,1)S(1)}, bf16[272,768]{1,0:T(8,128)(2,1)S(1)}, u32[]{:S(2)}, u32[]{:S(2)}) %collective-permute-start.43) | collective-permute-done | bytes 417824 | tf_op jit(solution)/shard_map/ppermute | solution.py:264
  506.0 14.4 %collective-permute-done.64.refs_2_ = bf16[2,288,1024]{2,1,0:T(8,128)(2,1)} collective-permute-done((bf16[2,288,1024]{2,1,0:T(8,128)(2,1)S(1)}, bf16[2,288,1024]{2,1,0:T(8,128)(2,1)}, u32[]{:S(2)}, u32[]{:S(2)}) %collective-permute-start.64) | collective-permute-done | bytes 1179680 | tf_op jit(solution)/shard_map/ppermute | solution.py:261
  522.5 9.7 %shard_map.207 = f32[512,2,4608]{2,1,0:T(2,128)} custom-call(s32[4]{0:T(128)} %pad_add_fusion.here, bf16[2,256,1152]{2,1,0:T(8,128)(2,1)} %copy-done.10, bf16[2,256,1152]{2,1,0:T(8,128)(2,1)} %copy-done.22, bf16[2,256,1152]{2,1,0:T(8,128)(2,1)} %copy-done.19, bf16[2,256,1152]{2,1,0:T(8,128)(2,1)} %copy-done.23, ...), custom_call_target="tpu_custom_call", output_to_operand_aliasing={{}: (5, {})} | custom-call | flops 10000000000 | bytes 1 | tf_op jit(solution)/shard_map/pallas_call | solution.py:317
  549.9 7.9 %shard_map.209 = f32[2304,1024]{1,0:T(8,128)} custom-call(s32[4]{0:T(128)} %pad_add_fusion.here, bf16[2,288,1024]{2,1,0:T(8,128)(2,1)} %copy-done.24, bf16[2,288,1024]{2,1,0:T(8,128)(2,1)} %collective-permute-done.63.refs_1_, bf16[2,288,1024]{2,1,0:T(8,128)(2,1)} %collective-permute-done.64.refs_2_, bf16[2,288,1024]{2,1,0:T(8,128)(2,1)} %collective-permute-done.65.refs_3_), custom_call_target="tpu_custom_call" | custom-call | flops 5000000000 | bytes 1 | tf_op jit(solution)/shard_map/pallas_call | solution.py:317
  (296 shorter events, 191.5 us)
Async XLA Ops:
  43.1 44.3 %all-to-all-start = ((bf16[16,192,256]{2,1,0:T(8,128)(2,1)}), bf16[16,192,256]{2,1,0:T(8,128)(2,1)S(1)}, u32[]{:S(2)}, u32[]{:S(2)}) async-start(bf16[16,192,256]{2,1,0:T(8,128)(2,1)} %get-tuple-element.112), calls=%async_computation | async-start | bytes 3145728 | tf_op jit(solution)/shard_map/all_to_all | solution.py:1130
  49.1 34.2 %collective-permute-start.6 = (bf16[128,5632]{1,0:T(8,128)(2,1)}, bf16[128,5632]{1,0:T(8,128)(2,1)}, u32[]{:S(2)}, u32[]{:S(2)}) collective-permute-start(bf16[128,5632]{1,0:T(8,128)(2,1)} %pad_maximum_fusion), channel_id=1, source_target_pairs={{0,1},{1,0},{2,3},{3,2},{4,5},{5,4},{6,7},{7,6},{8,9},{9,8},{10,11... | collective-permute-start | bytes 4325384 | tf_op jit(solution)/shard_map/ppermute | solution.py:270
  85.8 35.0 %collective-permute-start.8 = (bf16[128,5632]{1,0:T(8,128)(2,1)}, bf16[128,5632]{1,0:T(8,128)(2,1)}, u32[]{:S(2)}, u32[]{:S(2)}) collective-permute-start(bf16[128,5632]{1,0:T(8,128)(2,1)} %collective-permute-done.6.refs_4_.refs_5_.refs_3_), channel_id=1, source_target_pairs={{0,4},{2,6},{4,0},{6,2},{8,12},{10,14},{12,8},{14,10},{16,20},{18,... | collective-permute-start | bytes 4325384 | tf_op jit(solution)/shard_map/ppermute | solution.py:261
  111.3 38.1 %collective-permute-start.15 = (bf16[2304,256]{1,0:T(8,128)(2,1)}, bf16[2304,256]{1,0:T(8,128)(2,1)}, u32[]{:S(2)}, u32[]{:S(2)}) collective-permute-start(bf16[2304,256]{1,0:T(8,128)(2,1)} %collective-permute-done.10.refs_8_), channel_id=1, source_target_pairs={{0,4},{2,6},{4,0},{6,2},{8,12},{10,14},{12,8},{14,10},{16,20},{18,... | collective-permute-start | bytes 3538952 | tf_op jit(solution)/shard_map/ppermute | solution.py:261
  113.6 36.2 %collective-permute-start.11 = (bf16[128,4608]{1,0:T(8,128)(2,1)}, bf16[128,4608]{1,0:T(8,128)(2,1)}, u32[]{:S(2)}, u32[]{:S(2)}) collective-permute-start(bf16[128,4608]{1,0:T(8,128)(2,1)} %pad_maximum_fusion.1), channel_id=1, source_target_pairs={{0,1},{1,0},{2,3},{3,2},{4,5},{5,4},{6,7},{7,6},{8,9},{9,8},{10,11... | collective-permute-start | bytes 3538952 | tf_op jit(solution)/shard_map/ppermute | solution.py:270
  115.1 34.2 %all-to-all-start.1 = ((bf16[16,64,256]{2,1,0:T(8,128)(2,1)}), bf16[16,64,256]{2,1,0:T(8,128)(2,1)S(1)}, u32[]{:S(2)}, u32[]{:S(2)}) async-start(bf16[16,64,256]{2,1,0:T(8,128)(2,1)} %get-tuple-element.113), calls=%async_computation.1 | async-start | bytes 1048576 | tf_op jit(solution)/shard_map/all_to_all | solution.py:1154
  120.2 31.4 %collective-permute-start.7 = (bf16[128,5632]{1,0:T(8,128)(2,1)}, bf16[128,5632]{1,0:T(8,128)(2,1)}, u32[]{:S(2)}, u32[]{:S(2)}) collective-permute-start(bf16[128,5632]{1,0:T(8,128)(2,1)} %collective-permute-done.6.refs_4_.refs_5_.refs_3_), channel_id=1, source_target_pairs={{0,2},{2,0},{4,6},{6,4},{8,10},{10,8},{12,14},{14,12},{16,18},{18,... | collective-permute-start | bytes 4325384 | tf_op jit(solution)/shard_map/ppermute | solution.py:258
  120.8 31.4 %collective-permute-start.9 = (bf16[128,5632]{1,0:T(8,128)(2,1)}, bf16[128,5632]{1,0:T(8,128)(2,1)}, u32[]{:S(2)}, u32[]{:S(2)}) collective-permute-start(bf16[128,5632]{1,0:T(8,128)(2,1)} %collective-permute-done.8.refs_8_.refs_9_.refs_5_), channel_id=1, source_target_pairs={{0,2},{2,0},{4,6},{6,4},{8,10},{10,8},{12,14},{14,12},{16,18},{18,... | collective-permute-start | bytes 4325384 | tf_op jit(solution)/shard_map/ppermute | solution.py:258
  178.6 31.1 %collective-permute-start.22 = (bf16[256,1792]{1,0:T(8,128)(2,1)}, bf16[256,1792]{1,0:T(8,128)(2,1)}, u32[]{:S(2)}, u32[]{:S(2)}) collective-permute-start(bf16[256,1792]{1,0:T(8,128)(2,1)} %get-tuple-element.141), channel_id=1, source_target_pairs={{0,2},{2,0},{4,6},{6,4},{8,10},{10,8},{12,14},{14,12},{16,18},{18,... | collective-permute-start | bytes 2752520 | tf_op jit(solution)/shard_map/ppermute | solution.py:258
  178.6 31.1 %collective-permute-start.20 = (bf16[1024,256]{1,0:T(8,128)(2,1)}, bf16[1024,256]{1,0:T(8,128)(2,1)}, u32[]{:S(2)}, u32[]{:S(2)}) collective-permute-start(bf16[1024,256]{1,0:T(8,128)(2,1)} %get-tuple-element.137.refs_0_), channel_id=1, source_target_pairs={{0,4},{2,6},{4,0},{6,2},{8,12},{10,14},{12,8},{14,10},{16,20},{18,... | collective-permute-start | bytes 1572872 | tf_op jit(solution)/shard_map/ppermute | solution.py:261
  180.3 35.1 %collective-permute-start.23 = (bf16[256,1792]{1,0:T(8,128)(2,1)}, bf16[256,1792]{1,0:T(8,128)(2,1)}, u32[]{:S(2)}, u32[]{:S(2)}) collective-permute-start(bf16[256,1792]{1,0:T(8,128)(2,1)} %get-tuple-element.143), channel_id=1, source_target_pairs={{0,4},{2,6},{4,0},{6,2},{8,12},{10,14},{12,8},{14,10},{16,20},{18,... | collective-permute-start | bytes 2752520 | tf_op jit(solution)/shard_map/ppermute | solution.py:261
  182.2 54.9 %collective-permute-start.24 = (bf16[256,1792]{1,0:T(8,128)(2,1)}, bf16[256,1792]{1,0:T(8,128)(2,1)}, u32[]{:S(2)}, u32[]{:S(2)}) collective-permute-start(bf16[256,1792]{1,0:T(8,128)(2,1)} %collective-permute-done.18), channel_id=1, source_target_pairs={{0,4},{2,6},{4,0},{6,2},{8,12},{10,14},{12,8},{14,10},{16,20},{18,... | collective-permute-start | bytes 2752520 | tf_op jit(solution)/shard_map/ppermute | solution.py:261
  201.9 46.5 %all-to-all-start.2 = ((bf16[16,64,256]{2,1,0:T(8,128)(2,1)}), bf16[16,64,256]{2,1,0:T(8,128)(2,1)S(1)}, u32[]{:S(2)}, u32[]{:S(2)}) async-start(bf16[16,64,256]{2,1,0:T(8,128)(2,1)} %bitcast.102), calls=%async_computation.2 | async-start | bytes 1048576 | tf_op jit(solution)/shard_map/all_to_all | solution.py:1194
  206.8 40.0 %collective-permute-start.27 = (bf16[256,1792]{1,0:T(8,128)(2,1)}, bf16[256,1792]{1,0:T(8,128)(2,1)}, u32[]{:S(2)}, u32[]{:S(2)}) collective-permute-start(bf16[256,1792]{1,0:T(8,128)(2,1)} %get-tuple-element.156), channel_id=1, source_target_pairs={{0,2},{2,0},{4,6},{6,4},{8,10},{10,8},{12,14},{14,12},{16,18},{18,... | collective-permute-start | bytes 2752520 | tf_op jit(solution)/shard_map/ppermute | solution.py:258
  215.4 61.5 %collective-permute-start.26 = (bf16[256,1792]{1,0:T(8,128)(2,1)}, bf16[256,1792]{1,0:T(8,128)(2,1)}, u32[]{:S(2)}, u32[]{:S(2)}) collective-permute-start(bf16[256,1792]{1,0:T(8,128)(2,1)} %get-tuple-element.155), channel_id=1, source_target_pairs={{0,4},{2,6},{4,0},{6,2},{8,12},{10,14},{12,8},{14,10},{16,20},{18,... | collective-permute-start | bytes 2752520 | tf_op jit(solution)/shard_map/ppermute | solution.py:261
  246.2 30.7 %collective-permute-start.25 = (bf16[2,256,1152]{2,1,0:T(8,128)(2,1)}, bf16[2,256,1152]{2,1,0:T(8,128)(2,1)}, u32[]{:S(2)}, u32[]{:S(2)}) collective-permute-start(bf16[2,256,1152]{2,1,0:T(8,128)(2,1)} %get-tuple-element.146), channel_id=1, source_target_pairs={{0,1},{1,0},{2,3},{3,2},{4,5},{5,4},{6,7},{7,6},{8,9},{9,8},{10,11... | collective-permute-start | bytes 3538952 | tf_op jit(solution)/shard_map/ppermute | solution.py:270
  246.8 30.7 %collective-permute-start.28 = (bf16[256,1792]{1,0:T(8,128)(2,1)}, bf16[256,1792]{1,0:T(8,128)(2,1)}, u32[]{:S(2)}, u32[]{:S(2)}) collective-permute-start(bf16[256,1792]{1,0:T(8,128)(2,1)} %collective-permute-done.27), channel_id=1, source_target_pairs={{0,4},{2,6},{4,0},{6,2},{8,12},{10,14},{12,8},{14,10},{16,20},{18,... | collective-permute-start | bytes 2752520 | tf_op jit(solution)/shard_map/ppermute | solution.py:261
  277.5 53.4 %all-to-all-start.3 = ((bf16[16,192,256]{2,1,0:T(8,128)(2,1)}), bf16[16,192,256]{2,1,0:T(8,128)(2,1)}, u32[]{:S(2)}, u32[]{:S(2)}) async-start(bf16[16,192,256]{2,1,0:T(8,128)(2,1)} %shard_map.201), calls=%async_computation.3 | async-start | bytes 3145728 | tf_op jit(solution)/shard_map/all_to_all | solution.py:1216
  295.8 33.7 %collective-permute-start.33 = (bf16[2,256,1152]{2,1,0:T(8,128)(2,1)}, bf16[2,256,1152]{2,1,0:T(8,128)(2,1)}, u32[]{:S(2)}, u32[]{:S(2)}) collective-permute-start(bf16[2,256,1152]{2,1,0:T(8,128)(2,1)} %get-tuple-element.169), channel_id=1, source_target_pairs={{0,1},{1,0},{2,3},{3,2},{4,5},{5,4},{6,7},{7,6},{8,9},{9,8},{10,11... | collective-permute-start | bytes 3538952 | tf_op jit(solution)/shard_map/ppermute | solution.py:270
  390.2 38.3 %collective-permute-start.57 = (bf16[2,256,1152]{2,1,0:T(8,128)(2,1)S(1)}, bf16[2,256,1152]{2,1,0:T(8,128)(2,1)S(1)}, u32[]{:S(2)}, u32[]{:S(2)}) collective-permute-start(bf16[2,256,1152]{2,1,0:T(8,128)(2,1)S(1)} %pad_maximum_fusion.3.refs_0_), channel_id=1, source_target_pairs={{0,4},{2,6},{4,0},{6,2},{8,12},{10,14},{12,8},{14,10},{16,20},{18,... | collective-permute-start | bytes 3538952 | tf_op jit(solution)/shard_map/ppermute | solution.py:261
  429.6 39.3 %collective-permute-start.61 = (bf16[288,1024]{1,0:T(8,128)(2,1)S(1)}, bf16[288,1024]{1,0:T(8,128)(2,1)S(1)}, u32[]{:S(2)}, u32[]{:S(2)}) collective-permute-start(bf16[288,1024]{1,0:T(8,128)(2,1)S(1)} %fusion), channel_id=1, source_target_pairs={{0,16},{2,18},{4,20},{6,22},{8,24},{10,26},{12,28},{14,30},{16,0},... | collective-permute-start | bytes 1769480 | tf_op jit(solution)/shard_map/ppermute | solution.py:267
  432.3 36.9 %collective-permute-start.41 = (bf16[272,768]{1,0:T(8,128)(2,1)S(1)}, bf16[272,768]{1,0:T(8,128)(2,1)S(1)}, u32[]{:S(2)}, u32[]{:S(2)}) collective-permute-start(bf16[272,768]{1,0:T(8,128)(2,1)S(1)} %fusion.11), channel_id=1, source_target_pairs={{0,8},{2,10},{4,12},{6,14},{8,0},{10,2},{12,4},{14,6},{16,24},{18,... | collective-permute-start | bytes 1253384 | tf_op jit(solution)/shard_map/ppermute | solution.py:264
  456.9 35.7 %collective-permute-start.50 = (bf16[2,256,1152]{2,1,0:T(8,128)(2,1)S(1)}, bf16[2,256,1152]{2,1,0:T(8,128)(2,1)S(1)}, u32[]{:S(2)}, u32[]{:S(2)}) collective-permute-start(bf16[2,256,1152]{2,1,0:T(8,128)(2,1)S(1)} %pad_maximum_fusion.2.refs_0_), channel_id=1, source_target_pairs={{0,4},{2,6},{4,0},{6,2},{8,12},{10,14},{12,8},{14,10},{16,20},{18,... | collective-permute-start | bytes 3538952 | tf_op jit(solution)/shard_map/ppermute | solution.py:261
  504.9 30.9 %collective-permute-start.44 = (bf16[2,272,768]{2,1,0:T(8,128)(2,1)S(1)}, bf16[2,272,768]{2,1,0:T(8,128)(2,1)}, u32[]{:S(2)}, u32[]{:S(2)}) collective-permute-start(bf16[2,272,768]{2,1,0:T(8,128)(2,1)S(1)} %pad_maximum_fusion.6.refs_0_), channel_id=1, source_target_pairs={{0,2},{2,0},{4,6},{6,4},{8,10},{10,8},{12,14},{14,12},{16,18},{18,... | collective-permute-start | bytes 2506760 | tf_op jit(solution)/shard_map/ppermute | solution.py:258
  (95 other events, 1385.5 us)

commit v13 on v12

--- a/solution.py
+++ b/solution.py
@@ -278,16 +278,9 @@
         got, got_far = self.over_core(give), self.over_core(give_far)
         return (near, got, self.over_y(far), self.over_y(got_far))
 
-    def sum_depth(self, kept, got, time=None, last=None):
-        def half(index):
-            return add(pick(kept, index, 0), pick(got, index, 0))
-
-        given = self.over_z(half(1 - self.half))
-        part = add(half(self.half), given)
-        other = self.over_two_z(part)
-        full = add(part, other if time is None else after(other, *jax.tree.leaves(time)))
-        other = self.over_z(full)
-        return jnp.stack([full, other if last is None else after(other, last)])
+    def half_of(self, kept, got, own):
+        index = self.half if own else 1 - self.half
+        return add(pick(kept, index, 0), pick(got, index, 0))
 
 
 def pick(value, index, axis):
@@ -299,7 +292,7 @@
 
 
 def after(value, *others):
-    return lax.optimization_barrier((value, *others))[0]
+    return lax.optimization_barrier((value, *jax.tree.leaves(others)))[0]
 
 
 def contract(left, right, axes):
@@ -312,7 +305,7 @@
 
 
 def call_with_here(
-    kernel, here, grid, arrays, specs, outs, out_specs, scratch=(), aliases=None, micros=5
+    kernel, here, grid, arrays, specs, outs, out_specs, scratch=(), aliases=None, micros=0
 ):
     return pl.pallas_call(
         kernel,
@@ -843,7 +836,7 @@
         attention_back_kernel, here, (1,), arrays, [whole(a) for a in arrays], outs,
         [whole(o) for o in outs],
         [pltpu.VMEM((weight.shape[1], tokens), bf16), pltpu.VMEM((tokens, weight.shape[1]), bf16)],
-        micros=12,
+        micros=0,
     )
 
 
@@ -948,7 +941,7 @@
         [jax.ShapeDtypeStruct((2 * rows, 2, 2 * wide * CHUNKS), jnp.float32)],
         [pl.BlockSpec((step, 2, 2 * wide), lambda i, here: (i, 0, chunk))],
         aliases=aliases,
-        micros=10,
+        micros=0,
     )
     return out
 
@@ -1197,7 +1190,8 @@
     first_products = wide_products(
         here, two_plane, [after(v, d_heads) for v in first_shares], columns
     )
-    d_got = after(d_got, first_products[0])
+    pair_across = links.over_core(pair)
+    d_got = after(d_got, first_products[0], pair_across)
     (d_sent,) = kernel_call(
         attend_back_kernel,
         tables,
@@ -1233,29 +1227,65 @@
     )
     down_got = links.over_x(after(down_terms[0], second_got))
     near, far, give, give_far = d_shares
-    second_got = after(second_got, d_shares[0])
     got, got_far = links.over_core(give), links.over_core(give_far)
     attention_shares = (near, got, links.over_y(far), links.over_y(got_far))
-    pair_plane = plane(pair, pair_beside, d_sent)
+    pair_plane = (pair, pair_across, pair_beside, links.over_core(after(pair_beside, d_sent)))
+
+    kept = [first_products[1], second_products[1], down_terms[1], None]
+    got = [first_got, second_got, down_got, None]
+    given, part, across, full, back, beside = ([None] * 4 for _ in range(6))
+
+    def give_half(n):
+        given[n] = links.over_z(links.half_of(kept[n], got[n], False))
+
+    def sum_part(n, time):
+        part[n] = add(links.half_of(kept[n], got[n], True), after(given[n], time))
+        across[n] = links.over_two_z(part[n])
+
+    def sum_full(n, time):
+        full[n] = add(part[n], after(across[n], time))
+        back[n] = links.over_z(full[n])
+
+    def spread_y(n, time):
+        full[n] = jnp.stack([full[n], after(back[n], time)])
+        beside[n] = links.over_y(full[n])
+
+    def spread_core(n, time):
+        beside[n] = after(beside[n], time)
+        return (full[n], links.over_core(full[n]), beside[n], links.over_core(beside[n]))
+
+    give_half(0)
+    given[0] = after(given[0], down_terms[0])
+    sum_part(0, second_got)
+    give_half(1)
+    sum_part(1, got_far)
+    got[2] = after(got[2], part[1], attention_shares[1], pair_plane[3])
+    give_half(2)
+    sum_full(0, got[2])
+    attention_shares = (*attention_shares[:2], *(after(v, full[0]) for v in attention_shares[2:]))
     attention_terms = attention_products(
         here, pair_plane, attention_shares, gain_sums, ffn_gain_term
     )
-    first_pair = links.sum_depth(first_products[1], first_got, (*attention_shares[1:], down_got, pair_plane[3]), attention_terms[0])
-    second_pair = links.sum_depth(second_products[1], second_got, attention_shares[3])
-    attention_pair = links.sum_depth(attention_terms[1], links.over_x(attention_terms[0]))
-    first_placed = place_gate_up(here, 0, links.spread_plane(first_pair), None)
-    down_pair = links.sum_depth(down_terms[1], after(down_got, got_far), first_placed)
-    grad_gate_up = place_gate_up(here, 1, links.spread_plane(second_pair), first_placed)
-
-    def spread_after(value, time):
-        beside = after(links.over_y(value), time)
-        return (value, links.over_core(value), beside, links.over_core(beside))
-
-    grad_down = place_down(here, spread_after(down_pair, first_placed))
+    kept[3] = attention_terms[1]
+    attention_got = links.over_x(attention_terms[0])
+    spread_y(0, attention_terms[0])
+    sum_part(2, full[0])
+    sum_full(1, part[2])
+    got[3] = after(attention_got, full[1])
+    give_half(3)
+    first_pieces = spread_core(0, got[3])
+    spread_y(1, beside[0])
+    sum_part(3, full[1])
+    sum_full(2, part[3])
+    first_placed = place_gate_up(here, 0, first_pieces, None)
+    second_pieces = spread_core(1, full[2])
+    spread_y(2, (first_placed, beside[1]))
+    sum_full(3, full[2])
+    grad_gate_up = place_gate_up(here, 1, second_pieces, first_placed)
+    spread_y(3, full[2])
+    grad_down = place_down(here, spread_core(2, grad_gate_up))
     cut = qkv_weight.shape[1] // 4
-    grad_qkv, grad_out, gain_sums = place_attention(
-        here, spread_after(attention_pair, grad_gate_up), cut
-    )
+    grad_qkv, grad_out, gain_sums = place_attention(here, spread_core(3, grad_gate_up), cut)
     at = links.side * (HD // 2)
     gain_grads = [
         gain_sums[0, :rows],

time: 567 us -> 553 us (0.975)
  waiting for transfers between devices: 252 us -> 241 us
  starting transfers between devices: 76.4 us -> 70 us
    ppermute x4, waiting for transfers between devices: 37.8 us -> 17.1 us  [over_two_z(): return lax.ppermute(value, 'ctx', self.route(lambda z, y, c: (z ^ 2, y, c)))]
    ppermute x17, waiting for transfers between devices: 64 us -> 84.1 us  [over_y(): return lax.ppermute(value, 'ctx', self.route(lambda z, y, c: (z, 1 - y, c)))]
    ppermute x8, waiting for transfers between devices: 83.1 us -> 67.8 us  [over_z(): return lax.ppermute(value, 'ctx', self.route(lambda z, y, c: (z ^ 1, y, c)))]
    ppermute x4, starting transfers between devices: 8.57 us -> 2.89 us  [over_two_z(): return lax.ppermute(value, 'ctx', self.route(lambda z, y, c: (z ^ 2, y, c)))]
    unnamed x98 -> x114, local copies, waits for them, and re-layouts: 17 us -> 20.4 us
  transfers between devices with their start and end apart: 70 -> 70, of which waited for: 26 -> 27; matrix products, arithmetic and copies ran while one was open for 8% -> 8% of each run, Pallas kernels for 27% -> 28%
where the time goes in v13:
time: 553 us; the launch traced here: 545 us
  waiting for transfers between devices  241 us (44%)
  Pallas kernels  168 us (30%)
  starting transfers between devices  70 us (13%)
  local copies, waits for them, and re-layouts  48.8 us (9%)
  other arithmetic  15.5 us (3%)
    pallas_call x13, Pallas kernels, call_with_here(): pl.pallas_call(kernel, grid_spec=pltpu.PrefetchScalarGridSpec(num_scalar_...  121 us
    ppermute x17, waiting for transfers between devices, over_y(): return lax.ppermute(value, 'ctx', self.route(lambda z, y, c: (z, 1 - y, c)))  84.1 us
    ppermute x8, waiting for transfers between devices, over_z(): return lax.ppermute(value, 'ctx', self.route(lambda z, y, c: (z ^ 1, y, c)))  67.8 us
    pallas_call x2, Pallas kernels, kernel_call(): pl.pallas_call(kernel, out_shape=outs, in_specs=[smem] * len(tables) + [v...  46.9 us
    ppermute x9, waiting for transfers between devices, over_x(): return lax.ppermute(value, 'fsdp', [(0, 1), (1, 0)])  35.6 us
    all_to_all x1, waiting for transfers between devices, on_block(): lax.all_to_all(attn_sent, 'ctx', 0, 0, tiled=True)  28.2 us
    ppermute x17, starting transfers between devices, over_y(): return lax.ppermute(value, 'ctx', self.route(lambda z, y, c: (z, 1 - y, c)))  20.6 us
    unnamed x114, local copies, waits for them, and re-layouts  20.4 us
  transfers between devices with their start and end apart: 70, of which 27 were waited for; matrix products, arithmetic and copies ran while one was open for 8% of the time, Pallas kernels for 28%

profile of v13, /device:TPU:0, one launch (start us, length us, event | category | flops | bytes accessed | tf_op | source)
XLA Modules:
  0.0 544.6 jit_solution(2502298187026596446)
XLA Ops:
  22.1 8.9 %copy.71 = bf16[512,2,4608]{2,0,1:T(8,128)(2,1)} copy(bf16[512,2,4608]{2,1,0:T(2,128)(2,1)} %param.15) | data formatting | bytes 18874368 | tf_op jit(solution)/shard_map/optimization_barrier | solution.py:295
  52.3 29.2 %collective-permute-done.6.refs_4_.refs_5_.refs_3_ = bf16[128,5632]{1,0:T(8,128)(2,1)} collective-permute-done((bf16[128,5632]{1,0:T(8,128)(2,1)}, bf16[128,5632]{1,0:T(8,128)(2,1)}, u32[]{:S(2)}, u32[]{:S(2)}) %collective-permute-start.6) | collective-permute-done | bytes 1441824 | tf_op jit(solution)/shard_map/ppermute | solution.py:270
  86.8 22.0 %shard_map.196 = (bf16[16,64,256]{2,1,0:T(8,128)(2,1)}, bf16[4096,64]{1,0:T(8,128)(2,1)S(1)}, bf16[64,4096]{1,0:T(8,128)(2,1)S(1)}, bf16[4096,64]{1,0:T(8,128)(2...) custom-call(s32[32]{0:T(128)S(1)} %broadcast_add_fusion.q_slot, ...), custom_call_target="tpu_custom_call" | custom-call | flops 1 | bytes 1 | tf_op jit(solution)/shard_map/pallas_call | solution.py:226
  119.3 28.2 %all-to-all-done.1 = bf16[16,64,256]{2,1,0:T(8,128)(2,1)S(1)} async-done(((bf16[16,64,256]{2,1,0:T(8,128)(2,1)}), bf16[16,64,256]{2,1,0:T(8,128)(2,1)S(1)}, u32[]{:S(2)}, u32[]{:S(2)}) %all-to-all-start.1) | async-done | bytes 524320 | tf_op jit(solution)/shard_map/all_to_all | solution.py:1147
  157.3 16.8 %shard_map.198 = (bf16[256,1792]{1,0:T(8,128)(2,1)}, bf16[256,1792]{1,0:T(8,128)(2,1)}, bf16[256,1792]{1,0:T(8,128)(2,1)}, bf16[256,1792]{1,0:T(8,128)(2,1)}, f32[256,1024]{1,0:T(8,128)}, /*index=5*/f32[256,1024]{1,0:T(8,128)}) custom-call(s32[4]{0:T(128)} %pad_add_fusion.here, bf16[256,1024]{1,0:T(8,128)(2,1)} %get-tuple-element.131.refs_0_, ...), custom_call_target="tpu_custom_call" | custom-call | flops 1 | bytes 1 | tf_op jit(solution)/shard_map/pallas_call | solution.py:310
  183.1 17.0 %shard_map.199 = (bf16[256,1792]{1,0:T(8,128)(2,1)}, bf16[256,1792]{1,0:T(8,128)(2,1)}, bf16[256,1792]{1,0:T(8,128)(2,1)}, bf16[256,1792]{1,0:T(8,128)(2,1)}, bf...) custom-call(s32[4]{0:T(128)} %pad_add_fusion.here, ...), custom_call_target="tpu_custom_call" | custom-call | flops 1 | bytes 1 | tf_op jit(solution)/shard_map/pallas_call | solution.py:310
  213.5 21.6 %collective-permute-done.24.refs_7_ = bf16[256,1792]{1,0:T(8,128)(2,1)} collective-permute-done((bf16[256,1792]{1,0:T(8,128)(2,1)}, bf16[256,1792]{1,0:T(8,128)(2,1)}, u32[]{:S(2)}, u32[]{:S(2)}) %collective-permute-start.24) | collective-permute-done | bytes 917536 | tf_op jit(solution)/shard_map/ppermute | solution.py:261
  238.4 7.5 %shard_map.200 = (bf16[2,256,1152]{2,1,0:T(8,128)(2,1)}, f32[2,256,1152]{2,1,0:T(8,128)}) custom-call(s32[4]{0:T(128)} %pad_add_fusion.here, bf16[1024,256]{1,0:T(8,128)(2,1)} %get-tuple-element.150.refs_0_, bf16[1024,256]{1,0:T(8,128)(2,1)} %copy-done.50, bf16[1024,256]{1,0:T(8,128)(2,1)} %collective-permute-done.20.refs_2_, bf16[1024,256]{1,0:T(8,128)(2,1)} %copy-done.49, ...), custom_call_target="tpu_custom_call" | custom-call | flops 3000000000 | bytes 1 | tf_op jit(solution)/shard_map/pallas_call | solution.py:310
  250.3 24.9 %shard_map.201 = bf16[16,192,256]{2,1,0:T(8,128)(2,1)} custom-call(s32[32]{0:T(128)S(1)} %broadcast_add_fusion.q_slot, s32[32]{0:T(128)S(1)} %get-tuple-element.231.kv_slot, s32[16]{0:T(128)S(1)} %get-tuple-element.252.first, s32[16]{0:T(128)S(1)} %get-tuple-element.253.last, bf16[16,64,256]{2,1,0:T(8,128)(2,1)S(1)} %all-to-all-done.2.d_ref, ...), custom_call_target="tpu_custom_call" | custom-call | flops 24999999488 | bytes 1 | tf_op jit(solution)/shard_map/pallas_call | solution.py:226
  285.9 7.5 %shard_map.203 = (bf16[2,256,1152]{2,1,0:T(8,128)(2,1)}, f32[2,256,1152]{2,1,0:T(8,128)}) custom-call(s32[4]{0:T(128)} %pad_add_fusion.here, bf16[1024,256]{1,0:T(8,128)(2,1)} %get-tuple-element.150.refs_0_, bf16[1024,256]{1,0:T(8,128)(2,1)} %copy-done.50, bf16[1024,256]{1,0:T(8,128)(2,1)} %collective-permute-done.20.refs_2_, bf16[1024,256]{1,0:T(8,128)(2,1)} %copy-done.49, ...), custom_call_target="tpu_custom_call" | custom-call | flops 3000000000 | bytes 1 | tf_op jit(solution)/shard_map/pallas_call | solution.py:310
  300.2 9.9 %shard_map.202 = (bf16[2,288,1024]{2,1,0:T(8,128)(2,1)}, f32[2,288,1024]{2,1,0:T(8,128)}) custom-call(s32[4]{0:T(128)} %pad_add_fusion.here, bf16[256,1024]{1,0:T(8,128)(2,1)} %bitcast.96, bf16[256,1024]{1,0:T(8,128)(2,1)} %copy-done.51, bf16[256,1024]{1,0:T(8,128)(2,1)} %collective-permute-done.2.refs_2_, bf16[256,1024]{1,0:T(8,128)(2,1)} %copy-done.52, ...), custom_call_target="tpu_custom_call" | custom-call | flops 3000000000 | bytes 1 | tf_op jit(solution)/shard_map/pallas_call | solution.py:310
  310.1 12.6 %collective-permute-done.38 = bf16[256,1152]{1,0:T(8,128)(2,1)S(1)} collective-permute-done((bf16[256,1152]{1,0:T(8,128)(2,1)S(1)}, bf16[256,1152]{1,0:T(8,128)(2,1)S(1)}, u32[]{:S(2)}, u32[]{:S(2)}) %collective-permute-start.38) | collective-permute-done | bytes 589856 | tf_op jit(solution)/shard_map/ppermute | solution.py:264
  333.4 8.6 %shard_map.204 = (bf16[768,256]{1,0:T(8,128)(2,1)}, bf16[768,256]{1,0:T(8,128)(2,1)}, bf16[768,256]{1,0:T(8,128)(2,1)}, bf16[768,256]{1,0:T(8,128)(2,1)}, f32[256,1024]{1,0:T(8,128)}, /*index=5*/f32[8,1024]{1,0:T(8,128)}) custom-call(s32[4]{0:T(128)} %pad_add_fusion.here, bf16[16,192,256]{2,1,0:T(8,128)(2,1)} %copy-done.7, ...), custom_call_target="tpu_custom_call" | custom-call | flops 1 | bytes 1 | tf_op jit(solution)/shard_map/pallas_call | solution.py:310
  355.6 17.1 %collective-permute-done.39 = bf16[256,1152]{1,0:T(8,128)(2,1)S(1)} collective-permute-done((bf16[256,1152]{1,0:T(8,128)(2,1)S(1)}, bf16[256,1152]{1,0:T(8,128)(2,1)S(1)}, u32[]{:S(2)}, u32[]{:S(2)}) %collective-permute-start.39) | collective-permute-done | bytes 589856 | tf_op jit(solution)/shard_map/ppermute | solution.py:267
  376.4 7.2 %collective-permute-done.43.refs_7_ = bf16[768,256]{1,0:T(8,128)(2,1)S(1)} collective-permute-done((bf16[768,256]{1,0:T(8,128)(2,1)S(1)}, bf16[768,256]{1,0:T(8,128)(2,1)S(1)}, u32[]{:S(2)}, u32[]{:S(2)}) %collective-permute-start.43) | collective-permute-done | bytes 393248 | tf_op jit(solution)/shard_map/ppermute | solution.py:261
  384.4 6.9 %shard_map.205 = (bf16[2,272,768]{2,1,0:T(8,128)(2,1)}, f32[2,272,768]{2,1,0:T(8,128)}) custom-call(s32[4]{0:T(128)} %pad_add_fusion.here, bf16[2,1024,256]{2,1,0:T(8,128)(2,1)} %pad_maximum_fusion.5.refs_0_, bf16[2,1024,256]{2,1,0:T(8,128)(2,1)} %collective-permute-done.25.refs_1_, bf16[2,1024,256]{2,1,0:T(8,128)(2,1)} %collective-permute-done.33.refs_2_, ...), custom_call_target="tpu_custom_call" | custom-call | flops 3000000000 | bytes 1 | tf_op jit(solution)/shard_map/pallas_call | solution.py:310
  392.3 10.6 %collective-permute-done.47 = bf16[256,1152]{1,0:T(8,128)(2,1)S(1)} collective-permute-done((bf16[256,1152]{1,0:T(8,128)(2,1)S(1)}, bf16[256,1152]{1,0:T(8,128)(2,1)S(1)}, u32[]{:S(2)}, u32[]{:S(2)}) %collective-permute-start.47) | collective-permute-done | bytes 589856 | tf_op jit(solution)/shard_map/ppermute | solution.py:264
  404.1 10.3 %collective-permute-done.46 = bf16[288,1024]{1,0:T(8,128)(2,1)S(1)} collective-permute-done((bf16[288,1024]{1,0:T(8,128)(2,1)S(1)}, bf16[288,1024]{1,0:T(8,128)(2,1)S(1)}, u32[]{:S(2)}, u32[]{:S(2)}) %collective-permute-start.46) | collective-permute-done | bytes 589856 | tf_op jit(solution)/shard_map/ppermute | solution.py:264
  418.0 10.7 %collective-permute-done.50.refs_2_ = bf16[2,256,1152]{2,1,0:T(8,128)(2,1)S(1)} collective-permute-done((bf16[2,256,1152]{2,1,0:T(8,128)(2,1)S(1)}, bf16[2,256,1152]{2,1,0:T(8,128)(2,1)S(1)}, u32[]{:S(2)}, u32[]{:S(2)}) %collective-permute-start.50) | collective-permute-done | bytes 1179680 | tf_op jit(solution)/shard_map/ppermute | solution.py:261
  428.8 15.1 %collective-permute-done.49 = bf16[256,1152]{1,0:T(8,128)(2,1)S(1)} collective-permute-done((bf16[256,1152]{1,0:T(8,128)(2,1)S(1)}, bf16[256,1152]{1,0:T(8,128)(2,1)S(1)}, u32[]{:S(2)}, u32[]{:S(2)}) %collective-permute-start.49) | collective-permute-done | bytes 589856 | tf_op jit(solution)/shard_map/ppermute | solution.py:264
  455.1 10.0 %shard_map.206.refs_4_ = f32[512,2,4608]{2,1,0:T(2,128)} custom-call(s32[4]{0:T(128)} %pad_add_fusion.here, bf16[2,256,1152]{2,1,0:T(8,128)(2,1)} %copy-done.12, bf16[2,256,1152]{2,1,0:T(8,128)(2,1)} %copy-done.29, bf16[2,256,1152]{2,1,0:T(8,128)(2,1)} %copy-done.27, bf16[2,256,1152]{2,1,0:T(8,128)(2,1)} %copy-done.30), custom_call_target="tpu_custom_call" | custom-call | flops 1 | bytes 1 | tf_op jit(solution)/shard_map/pallas_call | solution.py:310
  485.7 9.7 %shard_map.207 = f32[512,2,4608]{2,1,0:T(2,128)} custom-call(s32[4]{0:T(128)} %pad_add_fusion.here, bf16[2,256,1152]{2,1,0:T(8,128)(2,1)} %copy-done.11, bf16[2,256,1152]{2,1,0:T(8,128)(2,1)} %copy-done.31, bf16[2,256,1152]{2,1,0:T(8,128)(2,1)} %copy-done.26, bf16[2,256,1152]{2,1,0:T(8,128)(2,1)} %copy-done.32, ...), custom_call_target="tpu_custom_call", output_to_operand_aliasing={{}: (5, {})} | custom-call | flops 1 | bytes 1 | tf_op jit(solution)/shard_map/pallas_call | solution.py:310
  495.4 25.8 %collective-permute-done.59.refs_2_ = bf16[2,272,768]{2,1,0:T(8,128)(2,1)} collective-permute-done((bf16[2,272,768]{2,1,0:T(8,128)(2,1)S(1)}, bf16[2,272,768]{2,1,0:T(8,128)(2,1)}, u32[]{:S(2)}, u32[]{:S(2)}) %collective-permute-start.59) | collective-permute-done | bytes 835616 | tf_op jit(solution)/shard_map/ppermute | solution.py:261
  536.2 7.9 %shard_map.209 = f32[2304,1024]{1,0:T(8,128)} custom-call(s32[4]{0:T(128)} %pad_add_fusion.here, bf16[2,288,1024]{2,1,0:T(8,128)(2,1)} %copy-done.15, bf16[2,288,1024]{2,1,0:T(8,128)(2,1)} %copy-done.33, bf16[2,288,1024]{2,1,0:T(8,128)(2,1)} %collective-permute-done.64.refs_2_, bf16[2,288,1024]{2,1,0:T(8,128)(2,1)} %collective-permute-done.65.refs_3_), custom_call_target="tpu_custom_call" | custom-call | flops 1 | bytes 1 | tf_op jit(solution)/shard_map/pallas_call | solution.py:310
  (312 shorter events, 196.6 us)
Async XLA Ops:
  42.3 43.4 %all-to-all-start = ((bf16[16,192,256]{2,1,0:T(8,128)(2,1)}), bf16[16,192,256]{2,1,0:T(8,128)(2,1)S(1)}, u32[]{:S(2)}, u32[]{:S(2)}) async-start(bf16[16,192,256]{2,1,0:T(8,128)(2,1)} %get-tuple-element.125), calls=%async_computation | async-start | bytes 3145728 | tf_op jit(solution)/shard_map/all_to_all | solution.py:1123
  47.3 34.2 %collective-permute-start.6 = (bf16[128,5632]{1,0:T(8,128)(2,1)}, bf16[128,5632]{1,0:T(8,128)(2,1)}, u32[]{:S(2)}, u32[]{:S(2)}) collective-permute-start(bf16[128,5632]{1,0:T(8,128)(2,1)} %pad_maximum_fusion), channel_id=1, source_target_pairs={{0,1},{1,0},{2,3},{3,2},{4,5},{5,4},{6,7},{7,6},{8,9},{9,8},{10,11... | collective-permute-start | bytes 4325384 | tf_op jit(solution)/shard_map/ppermute | solution.py:270
  83.9 34.8 %collective-permute-start.8 = (bf16[128,5632]{1,0:T(8,128)(2,1)}, bf16[128,5632]{1,0:T(8,128)(2,1)}, u32[]{:S(2)}, u32[]{:S(2)}) collective-permute-start(bf16[128,5632]{1,0:T(8,128)(2,1)} %collective-permute-done.6.refs_4_.refs_5_.refs_3_), channel_id=1, source_target_pairs={{0,4},{2,6},{4,0},{6,2},{8,12},{10,14},{12,8},{14,10},{16,20},{18,... | collective-permute-start | bytes 4325384 | tf_op jit(solution)/shard_map/ppermute | solution.py:261
  109.6 38.1 %collective-permute-start.15 = (bf16[2304,256]{1,0:T(8,128)(2,1)}, bf16[2304,256]{1,0:T(8,128)(2,1)}, u32[]{:S(2)}, u32[]{:S(2)}) collective-permute-start(bf16[2304,256]{1,0:T(8,128)(2,1)} %collective-permute-done.10.refs_8_), channel_id=1, source_target_pairs={{0,4},{2,6},{4,0},{6,2},{8,12},{10,14},{12,8},{14,10},{16,20},{18,... | collective-permute-start | bytes 3538952 | tf_op jit(solution)/shard_map/ppermute | solution.py:261
  111.8 36.2 %collective-permute-start.11 = (bf16[128,4608]{1,0:T(8,128)(2,1)}, bf16[128,4608]{1,0:T(8,128)(2,1)}, u32[]{:S(2)}, u32[]{:S(2)}) collective-permute-start(bf16[128,4608]{1,0:T(8,128)(2,1)} %pad_maximum_fusion.1), channel_id=1, source_target_pairs={{0,1},{1,0},{2,3},{3,2},{4,5},{5,4},{6,7},{7,6},{8,9},{9,8},{10,11... | collective-permute-start | bytes 3538952 | tf_op jit(solution)/shard_map/ppermute | solution.py:270
  113.2 34.2 %all-to-all-start.1 = ((bf16[16,64,256]{2,1,0:T(8,128)(2,1)}), bf16[16,64,256]{2,1,0:T(8,128)(2,1)S(1)}, u32[]{:S(2)}, u32[]{:S(2)}) async-start(bf16[16,64,256]{2,1,0:T(8,128)(2,1)} %get-tuple-element.126), calls=%async_computation.1 | async-start | bytes 1048576 | tf_op jit(solution)/shard_map/all_to_all | solution.py:1147
  176.7 36.2 %collective-permute-start.23 = (bf16[256,1792]{1,0:T(8,128)(2,1)}, bf16[256,1792]{1,0:T(8,128)(2,1)}, u32[]{:S(2)}, u32[]{:S(2)}) collective-permute-start(bf16[256,1792]{1,0:T(8,128)(2,1)} %get-tuple-element.156), channel_id=1, source_target_pairs={{0,4},{2,6},{4,0},{6,2},{8,12},{10,14},{12,8},{14,10},{16,20},{18,... | collective-permute-start | bytes 2752520 | tf_op jit(solution)/shard_map/ppermute | solution.py:261
  178.4 35.0 %collective-permute-start.22 = (bf16[256,1792]{1,0:T(8,128)(2,1)}, bf16[256,1792]{1,0:T(8,128)(2,1)}, u32[]{:S(2)}, u32[]{:S(2)}) collective-permute-start(bf16[256,1792]{1,0:T(8,128)(2,1)} %get-tuple-element.154), channel_id=1, source_target_pairs={{0,2},{2,0},{4,6},{6,4},{8,10},{10,8},{12,14},{14,12},{16,18},{18,... | collective-permute-start | bytes 2752520 | tf_op jit(solution)/shard_map/ppermute | solution.py:258
  178.4 34.5 %collective-permute-start.20 = (bf16[1024,256]{1,0:T(8,128)(2,1)}, bf16[1024,256]{1,0:T(8,128)(2,1)}, u32[]{:S(2)}, u32[]{:S(2)}) collective-permute-start(bf16[1024,256]{1,0:T(8,128)(2,1)} %get-tuple-element.150.refs_0_), channel_id=1, source_target_pairs={{0,4},{2,6},{4,0},{6,2},{8,12},{10,14},{12,8},{14,10},{16,20},{18,... | collective-permute-start | bytes 1572872 | tf_op jit(solution)/shard_map/ppermute | solution.py:261
  180.4 54.7 %collective-permute-start.24 = (bf16[256,1792]{1,0:T(8,128)(2,1)}, bf16[256,1792]{1,0:T(8,128)(2,1)}, u32[]{:S(2)}, u32[]{:S(2)}) collective-permute-start(bf16[256,1792]{1,0:T(8,128)(2,1)} %collective-permute-done.18), channel_id=1, source_target_pairs={{0,4},{2,6},{4,0},{6,2},{8,12},{10,14},{12,8},{14,10},{16,20},{18,... | collective-permute-start | bytes 2752520 | tf_op jit(solution)/shard_map/ppermute | solution.py:261
  201.3 45.5 %collective-permute-start.25 = (bf16[2,1024,256]{2,1,0:T(8,128)(2,1)}, bf16[2,1024,256]{2,1,0:T(8,128)(2,1)}, u32[]{:S(2)}, u32[]{:S(2)}) collective-permute-start(bf16[2,1024,256]{2,1,0:T(8,128)(2,1)} %pad_maximum_fusion.5.refs_0_), channel_id=1, source_target_pairs={{0,2},{2,0},{4,6},{6,4},{8,10},{10,8},{12,14},{14,12},{16,18},{18,... | collective-permute-start | bytes 3145736 | tf_op jit(solution)/shard_map/ppermute | solution.py:258
  201.3 45.4 %all-to-all-start.2 = ((bf16[16,64,256]{2,1,0:T(8,128)(2,1)}), bf16[16,64,256]{2,1,0:T(8,128)(2,1)S(1)}, u32[]{:S(2)}, u32[]{:S(2)}) async-start(bf16[16,64,256]{2,1,0:T(8,128)(2,1)} %bitcast.102), calls=%async_computation.2 | async-start | bytes 1048576 | tf_op jit(solution)/shard_map/all_to_all | solution.py:1187
  212.9 33.5 %collective-permute-start.28 = (bf16[256,1792]{1,0:T(8,128)(2,1)}, bf16[256,1792]{1,0:T(8,128)(2,1)}, u32[]{:S(2)}, u32[]{:S(2)}) collective-permute-start(bf16[256,1792]{1,0:T(8,128)(2,1)} %get-tuple-element.169), channel_id=1, source_target_pairs={{0,2},{2,0},{4,6},{6,4},{8,10},{10,8},{12,14},{14,12},{16,18},{18,... | collective-permute-start | bytes 2752520 | tf_op jit(solution)/shard_map/ppermute | solution.py:258
  235.1 40.1 %collective-permute-start.27 = (bf16[256,1792]{1,0:T(8,128)(2,1)}, bf16[256,1792]{1,0:T(8,128)(2,1)}, u32[]{:S(2)}, u32[]{:S(2)}) collective-permute-start(bf16[256,1792]{1,0:T(8,128)(2,1)} %get-tuple-element.168), channel_id=1, source_target_pairs={{0,4},{2,6},{4,0},{6,2},{8,12},{10,14},{12,8},{14,10},{16,20},{18,... | collective-permute-start | bytes 2752520 | tf_op jit(solution)/shard_map/ppermute | solution.py:261
  275.8 56.5 %all-to-all-start.3 = ((bf16[16,192,256]{2,1,0:T(8,128)(2,1)}), bf16[16,192,256]{2,1,0:T(8,128)(2,1)S(1)}, u32[]{:S(2)}, u32[]{:S(2)}) async-start(bf16[16,192,256]{2,1,0:T(8,128)(2,1)} %shard_map.201), calls=%async_computation.3 | async-start | bytes 3145728 | tf_op jit(solution)/shard_map/all_to_all | solution.py:1210
  293.4 33.7 %collective-permute-start.34 = (bf16[2,256,1152]{2,1,0:T(8,128)(2,1)}, bf16[2,256,1152]{2,1,0:T(8,128)(2,1)}, u32[]{:S(2)}, u32[]{:S(2)}) collective-permute-start(bf16[2,256,1152]{2,1,0:T(8,128)(2,1)} %get-tuple-element.182), channel_id=1, source_target_pairs={{0,1},{1,0},{2,3},{3,2},{4,5},{5,4},{6,7},{7,6},{8,9},{9,8},{10,11... | collective-permute-start | bytes 3538952 | tf_op jit(solution)/shard_map/ppermute | solution.py:270
  374.3 40.1 %collective-permute-start.46 = (bf16[288,1024]{1,0:T(8,128)(2,1)S(1)}, bf16[288,1024]{1,0:T(8,128)(2,1)S(1)}, u32[]{:S(2)}, u32[]{:S(2)}) collective-permute-start(bf16[288,1024]{1,0:T(8,128)(2,1)S(1)} %fusion.9), channel_id=1, source_target_pairs={{0,8},{2,10},{4,12},{6,14},{8,0},{10,2},{12,4},{14,6},{16,24},{18,... | collective-permute-start | bytes 1769480 | tf_op jit(solution)/shard_map/ppermute | solution.py:264
  376.4 38.3 %collective-permute-start.45 = (bf16[256,1152]{1,0:T(8,128)(2,1)S(1)}, bf16[256,1152]{1,0:T(8,128)(2,1)S(1)}, u32[]{:S(2)}, u32[]{:S(2)}) collective-permute-start(bf16[256,1152]{1,0:T(8,128)(2,1)S(1)} %fusion.1), channel_id=1, source_target_pairs={{0,16},{2,18},{4,20},{6,22},{8,24},{10,26},{12,28},{14,30},{16,0},... | collective-permute-start | bytes 1769480 | tf_op jit(solution)/shard_map/ppermute | solution.py:267
  416.2 34.4 %collective-permute-start.48 = (bf16[272,768]{1,0:T(8,128)(2,1)S(1)}, bf16[272,768]{1,0:T(8,128)(2,1)S(1)}, u32[]{:S(2)}, u32[]{:S(2)}) collective-permute-start(bf16[272,768]{1,0:T(8,128)(2,1)S(1)} %fusion.11), channel_id=1, source_target_pairs={{0,8},{2,10},{4,12},{6,14},{8,0},{10,2},{12,4},{14,6},{16,24},{18,... | collective-permute-start | bytes 1253384 | tf_op jit(solution)/shard_map/ppermute | solution.py:264
  417.1 33.7 %collective-permute-start.52 = (bf16[288,1024]{1,0:T(8,128)(2,1)S(1)}, bf16[288,1024]{1,0:T(8,128)(2,1)S(1)}, u32[]{:S(2)}, u32[]{:S(2)}) collective-permute-start(bf16[288,1024]{1,0:T(8,128)(2,1)S(1)} %fusion), channel_id=1, source_target_pairs={{0,16},{2,18},{4,20},{6,22},{8,24},{10,26},{12,28},{14,30},{16,0},... | collective-permute-start | bytes 1769480 | tf_op jit(solution)/shard_map/ppermute | solution.py:267
  418.0 35.0 %collective-permute-start.54 = (bf16[2,256,1152]{2,1,0:T(8,128)(2,1)S(1)}, bf16[2,256,1152]{2,1,0:T(8,128)(2,1)S(1)}, u32[]{:S(2)}, u32[]{:S(2)}) collective-permute-start(bf16[2,256,1152]{2,1,0:T(8,128)(2,1)S(1)} %pad_maximum_fusion.2.refs_0_), channel_id=1, source_target_pairs={{0,2},{2,0},{4,6},{6,4},{8,10},{10,8},{12,14},{14,12},{16,18},{18,... | collective-permute-start | bytes 3538952 | tf_op jit(solution)/shard_map/ppermute | solution.py:258
  475.3 46.5 %collective-permute-start.64 = (bf16[2,288,1024]{2,1,0:T(8,128)(2,1)S(1)}, bf16[2,288,1024]{2,1,0:T(8,128)(2,1)}, u32[]{:S(2)}, u32[]{:S(2)}) collective-permute-start(bf16[2,288,1024]{2,1,0:T(8,128)(2,1)S(1)} %pad_maximum_fusion.4.refs_0_), channel_id=1, source_target_pairs={{0,4},{2,6},{4,0},{6,2},{8,12},{10,14},{12,8},{14,10},{16,20},{18,... | collective-permute-start | bytes 3538952 | tf_op jit(solution)/shard_map/ppermute | solution.py:261
  483.2 38.0 %collective-permute-start.59 = (bf16[2,272,768]{2,1,0:T(8,128)(2,1)S(1)}, bf16[2,272,768]{2,1,0:T(8,128)(2,1)}, u32[]{:S(2)}, u32[]{:S(2)}) collective-permute-start(bf16[2,272,768]{2,1,0:T(8,128)(2,1)S(1)} %pad_maximum_fusion.6.refs_0_), channel_id=1, source_target_pairs={{0,4},{2,6},{4,0},{6,2},{8,12},{10,14},{12,8},{14,10},{16,20},{18,... | collective-permute-start | bytes 2506760 | tf_op jit(solution)/shard_map/ppermute | solution.py:261
  483.6 38.2 %collective-permute-start.58 = (bf16[2,272,768]{2,1,0:T(8,128)(2,1)S(1)}, bf16[2,272,768]{2,1,0:T(8,128)(2,1)}, u32[]{:S(2)}, u32[]{:S(2)}) collective-permute-start(bf16[2,272,768]{2,1,0:T(8,128)(2,1)S(1)} %pad_maximum_fusion.6.refs_0_), channel_id=1, source_target_pairs={{0,2},{2,0},{4,6},{6,4},{8,10},{10,8},{12,14},{14,12},{16,18},{18,... | collective-permute-start | bytes 2506760 | tf_op jit(solution)/shard_map/ppermute | solution.py:258
  (103 other events, 1301.4 us)

commit v14 on v13

--- a/solution.py
+++ b/solution.py
@@ -11,7 +11,7 @@
 KV_HEADS = 8
 HD = 64
 BLK = 128
-TILE = 256
+TILE = 512
 CHUNKS = 2
 PROJECT = 0
 ATTEND = 0
@@ -1285,7 +1285,9 @@
     spread_y(3, full[2])
     grad_down = place_down(here, spread_core(2, grad_gate_up))
     cut = qkv_weight.shape[1] // 4
-    grad_qkv, grad_out, gain_sums = place_attention(here, spread_core(3, grad_gate_up), cut)
+    grad_qkv, grad_out, gain_sums = place_attention(
+        here, spread_core(3, (grad_gate_up, grad_down)), cut
+    )
     at = links.side * (HD // 2)
     gain_grads = [
         gain_sums[0, :rows],

time: 553 us -> 557 us (level)
  waiting for transfers between devices: 241 us -> 264 us
  Pallas kernels: 168 us -> 150 us
    ppermute x4, waiting for transfers between devices: 17.1 us -> 37.7 us  [over_two_z(): return lax.ppermute(value, 'ctx', self.route(lambda z, y, c: (z ^ 2, y, c)))]
    pallas_call x2, Pallas kernels: 46.9 us -> 29 us  [kernel_call(): pl.pallas_call(kernel, out_shape=outs, in_specs=[smem] * len(tables) + [v...]
    ppermute x9, waiting for transfers between devices: 35.6 us -> 49.9 us  [over_x(): return lax.ppermute(value, 'fsdp', [(0, 1), (1, 0)])]
    ppermute x8, waiting for transfers between devices: 67.8 us -> 56.4 us  [over_z(): return lax.ppermute(value, 'ctx', self.route(lambda z, y, c: (z ^ 1, y, c)))]
    unnamed x114 -> x120, local copies, waits for them, and re-layouts: 20.4 us -> 20.4 us
  transfers between devices with their start and end apart: 70 -> 70, of which waited for: 27 -> 29; matrix products, arithmetic and copies ran while one was open for 8% -> 7% of each run, Pallas kernels for 28% -> 25%
where the time goes in v14:
time: 557 us; the launch traced here: 549 us
  waiting for transfers between devices  264 us (47%)
  Pallas kernels  150 us (27%)
  starting transfers between devices  68.3 us (12%)
  local copies, waits for them, and re-layouts  48.8 us (9%)
  other arithmetic  16.6 us (3%)
    pallas_call x13, Pallas kernels, call_with_here(): pl.pallas_call(kernel, grid_spec=pltpu.PrefetchScalarGridSpec(num_scalar_...  121 us
    ppermute x17, waiting for transfers between devices, over_y(): return lax.ppermute(value, 'ctx', self.route(lambda z, y, c: (z, 1 - y, c)))  82.9 us
    ppermute x8, waiting for transfers between devices, over_z(): return lax.ppermute(value, 'ctx', self.route(lambda z, y, c: (z ^ 1, y, c)))  56.4 us
    ppermute x9, waiting for transfers between devices, over_x(): return lax.ppermute(value, 'fsdp', [(0, 1), (1, 0)])  49.9 us
    ppermute x4, waiting for transfers between devices, over_two_z(): return lax.ppermute(value, 'ctx', self.route(lambda z, y, c: (z ^ 2, y, c)))  37.7 us
    pallas_call x2, Pallas kernels, kernel_call(): pl.pallas_call(kernel, out_shape=outs, in_specs=[smem] * len(tables) + [v...  29 us
    all_to_all x1, waiting for transfers between devices, on_block(): lax.all_to_all(attn_sent, 'ctx', 0, 0, tiled=True)  28.2 us
    unnamed x120, local copies, waits for them, and re-layouts  20.4 us
  transfers between devices with their start and end apart: 70, of which 29 were waited for; matrix products, arithmetic and copies ran while one was open for 7% of the time, Pallas kernels for 25%

profile of v14, /device:TPU:0, one launch (start us, length us, event | category | flops | bytes accessed | tf_op | source)
XLA Modules:
  0.0 549.0 jit_solution(13971976159678814047)
XLA Ops:
  22.1 8.9 %copy.71 = bf16[512,2,4608]{2,0,1:T(8,128)(2,1)} copy(bf16[512,2,4608]{2,1,0:T(2,128)(2,1)} %param.15) | data formatting | bytes 18874368 | tf_op jit(solution)/shard_map/optimization_barrier | solution.py:295
  52.3 29.2 %collective-permute-done.6.refs_4_.refs_5_.refs_3_ = bf16[128,5632]{1,0:T(8,128)(2,1)} collective-permute-done((bf16[128,5632]{1,0:T(8,128)(2,1)}, bf16[128,5632]{1,0:T(8,128)(2,1)}, u32[]{:S(2)}, u32[]{:S(2)}) %collective-permute-start.6) | collective-permute-done | bytes 1441824 | tf_op jit(solution)/shard_map/ppermute | solution.py:270
  86.8 12.4 %shard_map.196 = (bf16[16,64,256]{2,1,0:T(8,128)(2,1)}, bf16[4096,64]{1,0:T(8,128)(2,1)S(1)}, bf16[64,4096]{1,0:T(8,128)(2,1)S(1)}, bf16[4096,64]{1,0:T(8,128)(2...) custom-call(s32[32]{0:T(128)S(1)} %broadcast_add_fusion.q_slot, ...), custom_call_target="tpu_custom_call" | custom-call | flops 1 | bytes 1 | tf_op jit(solution)/shard_map/pallas_call | solution.py:226
  100.0 9.2 %collective-permute-done.10.refs_8_ = bf16[2304,256]{1,0:T(8,128)(2,1)} collective-permute-done((bf16[2304,256]{1,0:T(8,128)(2,1)}, bf16[2304,256]{1,0:T(8,128)(2,1)}, u32[]{:S(2)}, u32[]{:S(2)}) %collective-permute-start.10) | collective-permute-done | bytes 1179680 | tf_op jit(solution)/shard_map/ppermute | solution.py:270
  119.3 28.2 %all-to-all-done.1 = bf16[16,64,256]{2,1,0:T(8,128)(2,1)S(1)} async-done(((bf16[16,64,256]{2,1,0:T(8,128)(2,1)}), bf16[16,64,256]{2,1,0:T(8,128)(2,1)S(1)}, u32[]{:S(2)}, u32[]{:S(2)}) %all-to-all-start.1) | async-done | bytes 524320 | tf_op jit(solution)/shard_map/all_to_all | solution.py:1147
  157.3 16.8 %shard_map.198 = (bf16[256,1792]{1,0:T(8,128)(2,1)}, bf16[256,1792]{1,0:T(8,128)(2,1)}, bf16[256,1792]{1,0:T(8,128)(2,1)}, bf16[256,1792]{1,0:T(8,128)(2,1)}, f32[256,1024]{1,0:T(8,128)}, /*index=5*/f32[256,1024]{1,0:T(8,128)}) custom-call(s32[4]{0:T(128)} %pad_add_fusion.here, bf16[256,1024]{1,0:T(8,128)(2,1)} %get-tuple-element.131.refs_0_, ...), custom_call_target="tpu_custom_call" | custom-call | flops 1 | bytes 1 | tf_op jit(solution)/shard_map/pallas_call | solution.py:310
  183.1 17.0 %shard_map.199 = (bf16[256,1792]{1,0:T(8,128)(2,1)}, bf16[256,1792]{1,0:T(8,128)(2,1)}, bf16[256,1792]{1,0:T(8,128)(2,1)}, bf16[256,1792]{1,0:T(8,128)(2,1)}, bf...) custom-call(s32[4]{0:T(128)} %pad_add_fusion.here, ...), custom_call_target="tpu_custom_call" | custom-call | flops 1 | bytes 1 | tf_op jit(solution)/shard_map/pallas_call | solution.py:310
  213.5 21.6 %collective-permute-done.24.refs_7_ = bf16[256,1792]{1,0:T(8,128)(2,1)} collective-permute-done((bf16[256,1792]{1,0:T(8,128)(2,1)}, bf16[256,1792]{1,0:T(8,128)(2,1)}, u32[]{:S(2)}, u32[]{:S(2)}) %collective-permute-start.24) | collective-permute-done | bytes 917536 | tf_op jit(solution)/shard_map/ppermute | solution.py:261
  238.4 7.5 %shard_map.200 = (bf16[2,256,1152]{2,1,0:T(8,128)(2,1)}, f32[2,256,1152]{2,1,0:T(8,128)}) custom-call(s32[4]{0:T(128)} %pad_add_fusion.here, bf16[1024,256]{1,0:T(8,128)(2,1)} %get-tuple-element.150.refs_0_, bf16[1024,256]{1,0:T(8,128)(2,1)} %copy-done.53, bf16[1024,256]{1,0:T(8,128)(2,1)} %collective-permute-done.20.refs_2_, bf16[1024,256]{1,0:T(8,128)(2,1)} %copy-done.52, ...), custom_call_target="tpu_custom_call" | custom-call | flops 3000000000 | bytes 1 | tf_op jit(solution)/shard_map/pallas_call | solution.py:310
  250.3 16.6 %shard_map.201 = bf16[16,192,256]{2,1,0:T(8,128)(2,1)} custom-call(s32[32]{0:T(128)S(1)} %broadcast_add_fusion.q_slot, s32[32]{0:T(128)S(1)} %get-tuple-element.231.kv_slot, s32[8]{0:T(128)S(1)} %get-tuple-element.252.first, s32[8]{0:T(128)S(1)} %get-tuple-element.253.last, bf16[16,64,256]{2,1,0:T(8,128)(2,1)S(1)} %all-to-all-done.2.d_ref, ...), custom_call_target="tpu_custom_call" | custom-call | flops 24999999488 | bytes 1 | tf_op jit(solution)/shard_map/pallas_call | solution.py:226
  299.6 9.9 %shard_map.202 = (bf16[2,288,1024]{2,1,0:T(8,128)(2,1)}, f32[2,288,1024]{2,1,0:T(8,128)}) custom-call(s32[4]{0:T(128)} %pad_add_fusion.here, bf16[256,1024]{1,0:T(8,128)(2,1)} %bitcast.96, bf16[256,1024]{1,0:T(8,128)(2,1)} %copy-done.54, bf16[256,1024]{1,0:T(8,128)(2,1)} %collective-permute-done.2.refs_2_, bf16[256,1024]{1,0:T(8,128)(2,1)} %copy-done.55, ...), custom_call_target="tpu_custom_call" | custom-call | flops 3000000000 | bytes 1 | tf_op jit(solution)/shard_map/pallas_call | solution.py:310
  309.5 13.1 %collective-permute-done.38 = bf16[256,1152]{1,0:T(8,128)(2,1)S(1)} collective-permute-done((bf16[256,1152]{1,0:T(8,128)(2,1)S(1)}, bf16[256,1152]{1,0:T(8,128)(2,1)S(1)}, u32[]{:S(2)}, u32[]{:S(2)}) %collective-permute-start.38) | collective-permute-done | bytes 589856 | tf_op jit(solution)/shard_map/ppermute | solution.py:264
  332.9 8.6 %shard_map.204 = (bf16[768,256]{1,0:T(8,128)(2,1)}, bf16[768,256]{1,0:T(8,128)(2,1)}, bf16[768,256]{1,0:T(8,128)(2,1)}, bf16[768,256]{1,0:T(8,128)(2,1)}, f32[256,1024]{1,0:T(8,128)}, /*index=5*/f32[8,1024]{1,0:T(8,128)}) custom-call(s32[4]{0:T(128)} %pad_add_fusion.here, bf16[16,192,256]{2,1,0:T(8,128)(2,1)} %copy-done.7, ...), custom_call_target="tpu_custom_call" | custom-call | flops 1 | bytes 1 | tf_op jit(solution)/shard_map/pallas_call | solution.py:310
  355.4 17.0 %collective-permute-done.39 = bf16[256,1152]{1,0:T(8,128)(2,1)S(1)} collective-permute-done((bf16[256,1152]{1,0:T(8,128)(2,1)S(1)}, bf16[256,1152]{1,0:T(8,128)(2,1)S(1)}, u32[]{:S(2)}, u32[]{:S(2)}) %collective-permute-start.39) | collective-permute-done | bytes 589856 | tf_op jit(solution)/shard_map/ppermute | solution.py:267
  392.2 10.8 %collective-permute-done.47 = bf16[256,1152]{1,0:T(8,128)(2,1)S(1)} collective-permute-done((bf16[256,1152]{1,0:T(8,128)(2,1)S(1)}, bf16[256,1152]{1,0:T(8,128)(2,1)S(1)}, u32[]{:S(2)}, u32[]{:S(2)}) %collective-permute-start.47) | collective-permute-done | bytes 589856 | tf_op jit(solution)/shard_map/ppermute | solution.py:264
  403.7 10.7 %collective-permute-done.46 = bf16[288,1024]{1,0:T(8,128)(2,1)S(1)} collective-permute-done((bf16[288,1024]{1,0:T(8,128)(2,1)S(1)}, bf16[288,1024]{1,0:T(8,128)(2,1)S(1)}, u32[]{:S(2)}, u32[]{:S(2)}) %collective-permute-start.46) | collective-permute-done | bytes 589856 | tf_op jit(solution)/shard_map/ppermute | solution.py:264
  418.0 10.7 %collective-permute-done.50.refs_2_ = bf16[2,256,1152]{2,1,0:T(8,128)(2,1)S(1)} collective-permute-done((bf16[2,256,1152]{2,1,0:T(8,128)(2,1)S(1)}, bf16[2,256,1152]{2,1,0:T(8,128)(2,1)S(1)}, u32[]{:S(2)}, u32[]{:S(2)}) %collective-permute-start.50) | collective-permute-done | bytes 1179680 | tf_op jit(solution)/shard_map/ppermute | solution.py:261
  428.8 15.1 %collective-permute-done.49 = bf16[256,1152]{1,0:T(8,128)(2,1)S(1)} collective-permute-done((bf16[256,1152]{1,0:T(8,128)(2,1)S(1)}, bf16[256,1152]{1,0:T(8,128)(2,1)S(1)}, u32[]{:S(2)}, u32[]{:S(2)}) %collective-permute-start.49) | collective-permute-done | bytes 589856 | tf_op jit(solution)/shard_map/ppermute | solution.py:264
  452.2 15.6 %collective-permute-done.56.refs_2_ = bf16[2,256,1152]{2,1,0:T(8,128)(2,1)S(1)} collective-permute-done((bf16[2,256,1152]{2,1,0:T(8,128)(2,1)S(1)}, bf16[2,256,1152]{2,1,0:T(8,128)(2,1)S(1)}, u32[]{:S(2)}, u32[]{:S(2)}) %collective-permute-start.56) | collective-permute-done | bytes 1179680 | tf_op jit(solution)/shard_map/ppermute | solution.py:261
  468.9 10.0 %shard_map.206.refs_4_ = f32[512,2,4608]{2,1,0:T(2,128)} custom-call(s32[4]{0:T(128)} %pad_add_fusion.here, bf16[2,256,1152]{2,1,0:T(8,128)(2,1)} %copy-done.11, bf16[2,256,1152]{2,1,0:T(8,128)(2,1)} %copy-done.31, bf16[2,256,1152]{2,1,0:T(8,128)(2,1)} %copy-done.25, bf16[2,256,1152]{2,1,0:T(8,128)(2,1)} %collective-permute-done.55.refs_3_), custom_call_target="tpu_custom_call" | custom-call | flops 1 | bytes 1 | tf_op jit(solution)/shard_map/pallas_call | solution.py:310
  481.1 20.7 %collective-permute-done.51 = bf16[272,768]{1,0:T(8,128)(2,1)S(1)} collective-permute-done((bf16[272,768]{1,0:T(8,128)(2,1)S(1)}, bf16[272,768]{1,0:T(8,128)(2,1)S(1)}, u32[]{:S(2)}, u32[]{:S(2)}) %collective-permute-start.51) | collective-permute-done | bytes 417824 | tf_op jit(solution)/shard_map/ppermute | solution.py:267
  504.2 9.7 %shard_map.207 = f32[512,2,4608]{2,1,0:T(2,128)} custom-call(s32[4]{0:T(128)} %pad_add_fusion.here, bf16[2,256,1152]{2,1,0:T(8,128)(2,1)} %copy-done.12, bf16[2,256,1152]{2,1,0:T(8,128)(2,1)} %copy-done.29, bf16[2,256,1152]{2,1,0:T(8,128)(2,1)} %copy-done.27, bf16[2,256,1152]{2,1,0:T(8,128)(2,1)} %copy-done.30, ...), custom_call_target="tpu_custom_call", output_to_operand_aliasing={{}: (5, {})} | custom-call | flops 1 | bytes 1 | tf_op jit(solution)/shard_map/pallas_call | solution.py:310
  517.8 7.9 %shard_map.208 = f32[2304,1024]{1,0:T(8,128)} custom-call(s32[4]{0:T(128)} %pad_add_fusion.here, bf16[2,288,1024]{2,1,0:T(8,128)(2,1)} %copy-done.15, bf16[2,288,1024]{2,1,0:T(8,128)(2,1)} %collective-permute-done.62.refs_1_, bf16[2,288,1024]{2,1,0:T(8,128)(2,1)} %copy-done.32, bf16[2,288,1024]{2,1,0:T(8,128)(2,1)} %copy-done.33), custom_call_target="tpu_custom_call" | custom-call | flops 1 | bytes 1 | tf_op jit(solution)/shard_map/pallas_call | solution.py:310
  525.8 9.4 %collective-permute-done.59.refs_2_ = bf16[2,272,768]{2,1,0:T(8,128)(2,1)S(1)} collective-permute-done((bf16[2,272,768]{2,1,0:T(8,128)(2,1)S(1)}, bf16[2,272,768]{2,1,0:T(8,128)(2,1)S(1)}, u32[]{:S(2)}, u32[]{:S(2)}) %collective-permute-start.59) | collective-permute-done | bytes 835616 | tf_op jit(solution)/shard_map/ppermute | solution.py:261
  (318 shorter events, 210.4 us)
Async XLA Ops:
  42.3 43.4 %all-to-all-start = ((bf16[16,192,256]{2,1,0:T(8,128)(2,1)}), bf16[16,192,256]{2,1,0:T(8,128)(2,1)S(1)}, u32[]{:S(2)}, u32[]{:S(2)}) async-start(bf16[16,192,256]{2,1,0:T(8,128)(2,1)} %get-tuple-element.125), calls=%async_computation | async-start | bytes 3145728 | tf_op jit(solution)/shard_map/all_to_all | solution.py:1123
  47.3 34.2 %collective-permute-start.6 = (bf16[128,5632]{1,0:T(8,128)(2,1)}, bf16[128,5632]{1,0:T(8,128)(2,1)}, u32[]{:S(2)}, u32[]{:S(2)}) collective-permute-start(bf16[128,5632]{1,0:T(8,128)(2,1)} %pad_maximum_fusion), channel_id=1, source_target_pairs={{0,1},{1,0},{2,3},{3,2},{4,5},{5,4},{6,7},{7,6},{8,9},{9,8},{10,11... | collective-permute-start | bytes 4325384 | tf_op jit(solution)/shard_map/ppermute | solution.py:270
  83.9 34.8 %collective-permute-start.8 = (bf16[128,5632]{1,0:T(8,128)(2,1)}, bf16[128,5632]{1,0:T(8,128)(2,1)}, u32[]{:S(2)}, u32[]{:S(2)}) collective-permute-start(bf16[128,5632]{1,0:T(8,128)(2,1)} %collective-permute-done.6.refs_4_.refs_5_.refs_3_), channel_id=1, source_target_pairs={{0,4},{2,6},{4,0},{6,2},{8,12},{10,14},{12,8},{14,10},{16,20},{18,... | collective-permute-start | bytes 4325384 | tf_op jit(solution)/shard_map/ppermute | solution.py:261
  109.2 38.4 %collective-permute-start.15 = (bf16[2304,256]{1,0:T(8,128)(2,1)}, bf16[2304,256]{1,0:T(8,128)(2,1)}, u32[]{:S(2)}, u32[]{:S(2)}) collective-permute-start(bf16[2304,256]{1,0:T(8,128)(2,1)} %collective-permute-done.10.refs_8_), channel_id=1, source_target_pairs={{0,4},{2,6},{4,0},{6,2},{8,12},{10,14},{12,8},{14,10},{16,20},{18,... | collective-permute-start | bytes 3538952 | tf_op jit(solution)/shard_map/ppermute | solution.py:261
  111.8 36.2 %collective-permute-start.11 = (bf16[128,4608]{1,0:T(8,128)(2,1)}, bf16[128,4608]{1,0:T(8,128)(2,1)}, u32[]{:S(2)}, u32[]{:S(2)}) collective-permute-start(bf16[128,4608]{1,0:T(8,128)(2,1)} %pad_maximum_fusion.1), channel_id=1, source_target_pairs={{0,1},{1,0},{2,3},{3,2},{4,5},{5,4},{6,7},{7,6},{8,9},{9,8},{10,11... | collective-permute-start | bytes 3538952 | tf_op jit(solution)/shard_map/ppermute | solution.py:270
  113.2 34.2 %all-to-all-start.1 = ((bf16[16,64,256]{2,1,0:T(8,128)(2,1)}), bf16[16,64,256]{2,1,0:T(8,128)(2,1)S(1)}, u32[]{:S(2)}, u32[]{:S(2)}) async-start(bf16[16,64,256]{2,1,0:T(8,128)(2,1)} %get-tuple-element.126), calls=%async_computation.1 | async-start | bytes 1048576 | tf_op jit(solution)/shard_map/all_to_all | solution.py:1147
  176.7 36.2 %collective-permute-start.23 = (bf16[256,1792]{1,0:T(8,128)(2,1)}, bf16[256,1792]{1,0:T(8,128)(2,1)}, u32[]{:S(2)}, u32[]{:S(2)}) collective-permute-start(bf16[256,1792]{1,0:T(8,128)(2,1)} %get-tuple-element.156), channel_id=1, source_target_pairs={{0,4},{2,6},{4,0},{6,2},{8,12},{10,14},{12,8},{14,10},{16,20},{18,... | collective-permute-start | bytes 2752520 | tf_op jit(solution)/shard_map/ppermute | solution.py:261
  178.4 35.0 %collective-permute-start.22 = (bf16[256,1792]{1,0:T(8,128)(2,1)}, bf16[256,1792]{1,0:T(8,128)(2,1)}, u32[]{:S(2)}, u32[]{:S(2)}) collective-permute-start(bf16[256,1792]{1,0:T(8,128)(2,1)} %get-tuple-element.154), channel_id=1, source_target_pairs={{0,2},{2,0},{4,6},{6,4},{8,10},{10,8},{12,14},{14,12},{16,18},{18,... | collective-permute-start | bytes 2752520 | tf_op jit(solution)/shard_map/ppermute | solution.py:258
  178.4 34.5 %collective-permute-start.20 = (bf16[1024,256]{1,0:T(8,128)(2,1)}, bf16[1024,256]{1,0:T(8,128)(2,1)}, u32[]{:S(2)}, u32[]{:S(2)}) collective-permute-start(bf16[1024,256]{1,0:T(8,128)(2,1)} %get-tuple-element.150.refs_0_), channel_id=1, source_target_pairs={{0,4},{2,6},{4,0},{6,2},{8,12},{10,14},{12,8},{14,10},{16,20},{18,... | collective-permute-start | bytes 1572872 | tf_op jit(solution)/shard_map/ppermute | solution.py:261
  180.4 54.7 %collective-permute-start.24 = (bf16[256,1792]{1,0:T(8,128)(2,1)}, bf16[256,1792]{1,0:T(8,128)(2,1)}, u32[]{:S(2)}, u32[]{:S(2)}) collective-permute-start(bf16[256,1792]{1,0:T(8,128)(2,1)} %collective-permute-done.18), channel_id=1, source_target_pairs={{0,4},{2,6},{4,0},{6,2},{8,12},{10,14},{12,8},{14,10},{16,20},{18,... | collective-permute-start | bytes 2752520 | tf_op jit(solution)/shard_map/ppermute | solution.py:261
  201.3 45.5 %collective-permute-start.25 = (bf16[2,1024,256]{2,1,0:T(8,128)(2,1)}, bf16[2,1024,256]{2,1,0:T(8,128)(2,1)}, u32[]{:S(2)}, u32[]{:S(2)}) collective-permute-start(bf16[2,1024,256]{2,1,0:T(8,128)(2,1)} %pad_maximum_fusion.5.refs_0_), channel_id=1, source_target_pairs={{0,2},{2,0},{4,6},{6,4},{8,10},{10,8},{12,14},{14,12},{16,18},{18,... | collective-permute-start | bytes 3145736 | tf_op jit(solution)/shard_map/ppermute | solution.py:258
  201.4 45.4 %all-to-all-start.2 = ((bf16[16,64,256]{2,1,0:T(8,128)(2,1)}), bf16[16,64,256]{2,1,0:T(8,128)(2,1)S(1)}, u32[]{:S(2)}, u32[]{:S(2)}) async-start(bf16[16,64,256]{2,1,0:T(8,128)(2,1)} %bitcast.101), calls=%async_computation.2 | async-start | bytes 1048576 | tf_op jit(solution)/shard_map/all_to_all | solution.py:1187
  212.9 33.6 %collective-permute-start.28 = (bf16[256,1792]{1,0:T(8,128)(2,1)}, bf16[256,1792]{1,0:T(8,128)(2,1)}, u32[]{:S(2)}, u32[]{:S(2)}) collective-permute-start(bf16[256,1792]{1,0:T(8,128)(2,1)} %get-tuple-element.169), channel_id=1, source_target_pairs={{0,2},{2,0},{4,6},{6,4},{8,10},{10,8},{12,14},{14,12},{16,18},{18,... | collective-permute-start | bytes 2752520 | tf_op jit(solution)/shard_map/ppermute | solution.py:258
  235.1 31.8 %collective-permute-start.27 = (bf16[256,1792]{1,0:T(8,128)(2,1)}, bf16[256,1792]{1,0:T(8,128)(2,1)}, u32[]{:S(2)}, u32[]{:S(2)}) collective-permute-start(bf16[256,1792]{1,0:T(8,128)(2,1)} %get-tuple-element.168), channel_id=1, source_target_pairs={{0,4},{2,6},{4,0},{6,2},{8,12},{10,14},{12,8},{14,10},{16,20},{18,... | collective-permute-start | bytes 2752520 | tf_op jit(solution)/shard_map/ppermute | solution.py:261
  275.8 56.0 %all-to-all-start.3 = ((bf16[16,192,256]{2,1,0:T(8,128)(2,1)}), bf16[16,192,256]{2,1,0:T(8,128)(2,1)S(1)}, u32[]{:S(2)}, u32[]{:S(2)}) async-start(bf16[16,192,256]{2,1,0:T(8,128)(2,1)} %shard_map.201), calls=%async_computation.3 | async-start | bytes 3145728 | tf_op jit(solution)/shard_map/all_to_all | solution.py:1210
  293.4 33.4 %collective-permute-start.34 = (bf16[2,256,1152]{2,1,0:T(8,128)(2,1)}, bf16[2,256,1152]{2,1,0:T(8,128)(2,1)}, u32[]{:S(2)}, u32[]{:S(2)}) collective-permute-start(bf16[2,256,1152]{2,1,0:T(8,128)(2,1)} %get-tuple-element.182), channel_id=1, source_target_pairs={{0,1},{1,0},{2,3},{3,2},{4,5},{5,4},{6,7},{7,6},{8,9},{9,8},{10,11... | collective-permute-start | bytes 3538952 | tf_op jit(solution)/shard_map/ppermute | solution.py:270
  293.9 32.8 %collective-permute-start.33 = (bf16[2,1024,256]{2,1,0:T(8,128)(2,1)}, bf16[2,1024,256]{2,1,0:T(8,128)(2,1)}, u32[]{:S(2)}, u32[]{:S(2)}) collective-permute-start(bf16[2,1024,256]{2,1,0:T(8,128)(2,1)} %pad_maximum_fusion.5.refs_0_), channel_id=1, source_target_pairs={{0,4},{2,6},{4,0},{6,2},{8,12},{10,14},{12,8},{14,10},{16,20},{18,... | collective-permute-start | bytes 3145736 | tf_op jit(solution)/shard_map/ppermute | solution.py:261
  374.3 40.1 %collective-permute-start.46 = (bf16[288,1024]{1,0:T(8,128)(2,1)S(1)}, bf16[288,1024]{1,0:T(8,128)(2,1)S(1)}, u32[]{:S(2)}, u32[]{:S(2)}) collective-permute-start(bf16[288,1024]{1,0:T(8,128)(2,1)S(1)} %fusion.9), channel_id=1, source_target_pairs={{0,8},{2,10},{4,12},{6,14},{8,0},{10,2},{12,4},{14,6},{16,24},{18,... | collective-permute-start | bytes 1769480 | tf_op jit(solution)/shard_map/ppermute | solution.py:264
  376.4 38.3 %collective-permute-start.45 = (bf16[256,1152]{1,0:T(8,128)(2,1)S(1)}, bf16[256,1152]{1,0:T(8,128)(2,1)S(1)}, u32[]{:S(2)}, u32[]{:S(2)}) collective-permute-start(bf16[256,1152]{1,0:T(8,128)(2,1)S(1)} %fusion.1), channel_id=1, source_target_pairs={{0,16},{2,18},{4,20},{6,22},{8,24},{10,26},{12,28},{14,30},{16,0},... | collective-permute-start | bytes 1769480 | tf_op jit(solution)/shard_map/ppermute | solution.py:267
  416.2 34.4 %collective-permute-start.48 = (bf16[272,768]{1,0:T(8,128)(2,1)S(1)}, bf16[272,768]{1,0:T(8,128)(2,1)S(1)}, u32[]{:S(2)}, u32[]{:S(2)}) collective-permute-start(bf16[272,768]{1,0:T(8,128)(2,1)S(1)} %fusion.11), channel_id=1, source_target_pairs={{0,8},{2,10},{4,12},{6,14},{8,0},{10,2},{12,4},{14,6},{16,24},{18,... | collective-permute-start | bytes 1253384 | tf_op jit(solution)/shard_map/ppermute | solution.py:264
  417.1 33.7 %collective-permute-start.52 = (bf16[288,1024]{1,0:T(8,128)(2,1)S(1)}, bf16[288,1024]{1,0:T(8,128)(2,1)S(1)}, u32[]{:S(2)}, u32[]{:S(2)}) collective-permute-start(bf16[288,1024]{1,0:T(8,128)(2,1)S(1)} %fusion), channel_id=1, source_target_pairs={{0,16},{2,18},{4,20},{6,22},{8,24},{10,26},{12,28},{14,30},{16,0},... | collective-permute-start | bytes 1769480 | tf_op jit(solution)/shard_map/ppermute | solution.py:267
  452.2 49.9 %collective-permute-start.60 = (bf16[2,256,1152]{2,1,0:T(8,128)(2,1)S(1)}, bf16[2,256,1152]{2,1,0:T(8,128)(2,1)S(1)}, u32[]{:S(2)}, u32[]{:S(2)}) collective-permute-start(bf16[2,256,1152]{2,1,0:T(8,128)(2,1)S(1)} %pad_maximum_fusion.3.refs_0_), channel_id=1, source_target_pairs={{0,2},{2,0},{4,6},{6,4},{8,10},{10,8},{12,14},{14,12},{16,18},{18,... | collective-permute-start | bytes 3538952 | tf_op jit(solution)/shard_map/ppermute | solution.py:258
  467.8 34.3 %collective-permute-start.61 = (bf16[2,256,1152]{2,1,0:T(8,128)(2,1)S(1)}, bf16[2,256,1152]{2,1,0:T(8,128)(2,1)S(1)}, u32[]{:S(2)}, u32[]{:S(2)}) collective-permute-start(bf16[2,256,1152]{2,1,0:T(8,128)(2,1)S(1)} %collective-permute-done.56.refs_2_), channel_id=1, source_target_pairs={{0,2},{2,0},{4,6},{6,4},{8,10},{10,8},{12,14},{14,12},{16,18},{18,... | collective-permute-start | bytes 3538952 | tf_op jit(solution)/shard_map/ppermute | solution.py:258
  480.1 33.8 %collective-permute-start.63 = (bf16[2,288,1024]{2,1,0:T(8,128)(2,1)S(1)}, bf16[2,288,1024]{2,1,0:T(8,128)(2,1)S(1)}, u32[]{:S(2)}, u32[]{:S(2)}) collective-permute-start(bf16[2,288,1024]{2,1,0:T(8,128)(2,1)S(1)} %pad_maximum_fusion.4.refs_0_), channel_id=1, source_target_pairs={{0,4},{2,6},{4,0},{6,2},{8,12},{10,14},{12,8},{14,10},{16,20},{18,... | collective-permute-start | bytes 3538952 | tf_op jit(solution)/shard_map/ppermute | solution.py:261
  (106 other events, 1346.0 us)

commit v15 on v13

--- a/solution.py
+++ b/solution.py
@@ -11,7 +11,7 @@
 KV_HEADS = 8
 HD = 64
 BLK = 128
-TILE = 256
+TILE = 512
 CHUNKS = 2
 PROJECT = 0
 ATTEND = 0
@@ -404,16 +404,16 @@
 
 def attend_out_kernel(here, *refs):
     attn_ref, x_ref, gain_ref, own_ref = refs[:4]
-    pieces = refs[4:12]
-    weight, h_ref, scale_ref, two_ref, two_t_ref = refs[12:]
+    pieces = refs[4:20]
+    weight, h_ref, scale_ref, two_ref, two_t_ref = refs[20:]
     core, y, side = here[1], here[2], here[3]
     rows = own_ref.shape[0]
     part = rows // 4
     weight[pl.ds(pl.multiple_of(side * rows, rows), rows), :] = own_ref[...]
     for p in range(4):
         at = (1 - side) * rows + (((p % 2) ^ core) * 2 + ((p // 2) ^ y)) * part
-        for n in range(2):
-            piece = pieces[2 * p + n]
+        for n in range(4):
+            piece = pieces[4 * p + n]
             wide = piece.shape[1]
             weight[pl.ds(pl.multiple_of(at, part), part), n * wide : (n + 1) * wide] = piece[...]
     attn = attn_ref[...].T
@@ -433,14 +433,15 @@
     f32, bf16 = jnp.float32, jnp.bfloat16
     shape = jax.ShapeDtypeStruct
     part = own.shape[0] // 4
-    half = width // 2
-    first = pieces[0].shape[1] // half - 2
+    cuts = 4
+    part_width = width // cuts
+    first = pieces[0].shape[1] // part_width - cuts
     arrays = [attn, x, gain, own]
     specs = [whole(a) for a in arrays]
     for piece in pieces:
-        for n in range(2):
+        for n in range(cuts):
             arrays.append(piece)
-            specs.append(pl.BlockSpec((part, half), lambda i, here, n=n: (0, first + n)))
+            specs.append(pl.BlockSpec((part, part_width), lambda i, here, n=n: (0, first + n)))
     outs = [
         shape((width, width), bf16),
         shape((tokens, width), f32),
@@ -455,7 +456,8 @@
 
 def ffn_kernel(chunk, here, *refs):
     two_ref, d_ref, own_ref = refs[:3]
-    pieces, down_ref, down_pieces = refs[3:7], refs[7], refs[8:12]
+    pieces, down_ref, down_pieces = (refs[3:7], refs[7:11]), refs[11], refs[12:16]
+    refs = refs[4:]
     if chunk == 0:
         before_refs, refs = refs[12:13], refs[13:]
         near, far, give, give_far, out_ref, d_two_ref = refs[:6]
@@ -490,10 +492,10 @@
         for p in range(4):
             rows = pl.ds(pl.multiple_of((1 - side) * own_rows + quarter(p) * part, part), part)
             for kind in range(2):
-                begin = kind * columns + n * tile
+                begin = n * tile + (columns if kind == 1 and chunk == 1 else 0)
                 found.append(
                     pltpu.make_async_copy(
-                        pieces[p].at[:, begin : begin + tile],
+                        pieces[kind][p].at[:, begin : begin + tile],
                         weight.at[kind, rows, at],
                         weight_sem.at[n, 1 + 2 * p + kind],
                     )
@@ -636,7 +638,7 @@
             shape((1, width), f32),
         ]
     far_away = pl.BlockSpec(memory_space=pl.ANY)
-    arrays = [two, d_ffn, own, *pieces, down, *down_pieces, *before]
+    arrays = [two, d_ffn, own, *pieces[0], *pieces[1], down, *down_pieces, *before]
     specs = [whole(two), whole(d_ffn)] + [far_away] * (len(arrays) - 2)
     if gain is not None:
         arrays.append(gain)
@@ -1099,7 +1101,8 @@
     d_ffn = cotangent[0]
     d_beside = links.over_y(d_ffn)
     qkv_there = after(links.over_x(qkv_piece), d_beside)
-    first_piece = jnp.concatenate([*gate_up_piece(0), quarter_rows(out_weight)], axis=1)
+    first_piece, first_up = gate_up_piece(0)
+    up_piece = jnp.concatenate([first_up, quarter_rows(out_weight)], axis=1)
     second_piece = jnp.concatenate(gate_up_piece(1), axis=1)
     down_piece = lax.dynamic_slice_in_dim(
         down_weight, links.quarter * (width // 4), width // 4, 1
@@ -1108,6 +1111,7 @@
     tokens_here = tokens[0]
     qkv_there = after(qkv_there, first_piece)
     first_there = links.over_x(after(first_piece, qkv_there))
+    up_there = links.over_x(after(up_piece, first_there))
     gate_up = jnp.transpose(after(gate_up_weight, qkv_there), (1, 0, 2))
     qkv_beside = links.over_y(qkv_there)
     qkv_pieces = (
@@ -1117,13 +1121,14 @@
         links.over_core(after(qkv_beside, gate_up)),
     )
     sent, w_qkv, q_raw, k_raw, q_scale, k_scale, normed, scale_one = project(
-        here, tokens_here, gain_attn[None], qkv_weight, qkv_pieces,
+        here, after(tokens_here, first_there), gain_attn[None], qkv_weight, qkv_pieces,
         gain_query[:, None], gain_key[:, None], cosine[0], sine[0],
     )
     got = lax.all_to_all(sent, "ctx", 0, 0, tiled=True)
-    first_there = after(first_there, sent)
-    down_there = links.over_x(after(down_piece, first_there))
+    up_there = after(up_there, sent)
+    down_there = links.over_x(after(down_piece, up_there))
     first_beside = links.over_y(first_there)
+    up_beside = links.over_y(up_there)
     q_place, q_start = q_place[None], q_start[None]
     shape = jax.ShapeDtypeStruct
     attn_sent, *held = kernel_call(
@@ -1143,6 +1148,7 @@
         [pltpu.VMEM((HD, kv_rows), bf16)],
         ATTEND,
     )
+    attn_sent = after(attn_sent, first_beside)
     attn_in = lax.dynamic_slice_in_dim(
         lax.all_to_all(attn_sent, "ctx", 0, 0, tiled=True), part * HEADS, HEADS
     ).reshape(q_width, rows_here)
@@ -1154,15 +1160,16 @@
         there, beside = after(there, time), after(beside, time)
         return (there, links.over_core(there), beside, links.over_core(beside))
 
-    first_pieces = spread(first_there, first_beside, attn_sent)
+    first_pieces = spread(first_there, first_beside, attn_in)
+    up_pieces = spread(up_there, up_beside, attn_sent)
     down_pieces = spread(down_there, down_beside, attn_in)
     second_beside = links.over_y(second_there)
     w_out, h_one, scale_two, two, two_t = attend_out(
-        here, attn_in, tokens_here, gain_ffn[None], out_weight, first_pieces
+        here, attn_in, tokens_here, gain_ffn[None], out_weight, up_pieces
     )
     two_beside = links.over_y(two_t)
     dealt_here, (out_sum, two_sum) = ffn(
-        here, 0, two, d_ffn, gate_up, first_pieces, down_weight, down_pieces, [h_one]
+        here, 0, two, d_ffn, gate_up, (first_pieces, up_pieces), down_weight, down_pieces, [h_one]
     )
     second_beside = after(second_beside, out_sum)
     second_pieces = (
@@ -1173,7 +1180,7 @@
     first_shares = (near, links.over_core(give), links.over_y(far), links.over_y(got_far))
     out_sum = after(out_sum, got_far)
     dealt_here, (output, d_h_one, d_attn, d_heads, ffn_gain_term) = ffn(
-        here, 1, two, d_ffn, gate_up, second_pieces, down_weight, down_pieces,
+        here, 1, two, d_ffn, gate_up, (second_pieces, second_pieces), down_weight, down_pieces,
         [out_sum, two_sum, h_one, scale_two, w_out], gain_ffn[None],
     )
     second_shares = links.deal_plane(*dealt_here)

time: 553 us -> 546 us (0.987)
  Pallas kernels: 168 us -> 149 us
  waiting for transfers between devices: 241 us -> 250 us
    pallas_call x2, Pallas kernels: 46.9 us -> 29 us  [kernel_call(): pl.pallas_call(kernel, out_shape=outs, in_specs=[smem] * len(tables) + [v...]
    ppermute x28 -> x30, waiting for transfers between devices: 8.18 us -> 11.7 us  [over_core(): return lax.ppermute(value, 'ctx', self.route(lambda z, y, c: (z, y, 1 - c)))]
    ppermute x17 -> x18, waiting for transfers between devices: 84.1 us -> 85.2 us  [over_y(): return lax.ppermute(value, 'ctx', self.route(lambda z, y, c: (z, 1 - y, c)))]
    unnamed x114 -> x120, local copies, waits for them, and re-layouts: 20.4 us -> 21.3 us
    ppermute x9 -> x10, starting transfers between devices: 11.7 us -> 12.1 us  [over_x(): return lax.ppermute(value, 'fsdp', [(0, 1), (1, 0)])]
    ppermute x9 -> x10, waiting for transfers between devices: 35.6 us -> 35.9 us  [over_x(): return lax.ppermute(value, 'fsdp', [(0, 1), (1, 0)])]
    ppermute x17 -> x18, starting transfers between devices: 20.6 us -> 20.4 us  [over_y(): return lax.ppermute(value, 'ctx', self.route(lambda z, y, c: (z, 1 - y, c)))]
  transfers between devices with their start and end apart: 70 -> 74, of which waited for: 27 -> 31; matrix products, arithmetic and copies ran while one was open for 8% -> 8% of each run, Pallas kernels for 28% -> 25%
where the time goes in v15:
time: 546 us; the launch traced here: 537 us
  waiting for transfers between devices  250 us (46%)
  Pallas kernels  149 us (27%)
  starting transfers between devices  70.7 us (13%)
  local copies, waits for them, and re-layouts  49.2 us (9%)
  other arithmetic  16.3 us (3%)
    pallas_call x13, Pallas kernels, call_with_here(): pl.pallas_call(kernel, grid_spec=pltpu.PrefetchScalarGridSpec(num_scalar_...  120 us
    ppermute x18, waiting for transfers between devices, over_y(): return lax.ppermute(value, 'ctx', self.route(lambda z, y, c: (z, 1 - y, c)))  85.2 us
    ppermute x8, waiting for transfers between devices, over_z(): return lax.ppermute(value, 'ctx', self.route(lambda z, y, c: (z ^ 1, y, c)))  67.3 us
    ppermute x10, waiting for transfers between devices, over_x(): return lax.ppermute(value, 'fsdp', [(0, 1), (1, 0)])  35.9 us
    pallas_call x2, Pallas kernels, kernel_call(): pl.pallas_call(kernel, out_shape=outs, in_specs=[smem] * len(tables) + [v...  29 us
    all_to_all x1, waiting for transfers between devices, on_block(): lax.all_to_all(attn_sent, 'ctx', 0, 0, tiled=True)  28.8 us
    unnamed x120, local copies, waits for them, and re-layouts  21.3 us
    ppermute x18, starting transfers between devices, over_y(): return lax.ppermute(value, 'ctx', self.route(lambda z, y, c: (z, 1 - y, c)))  20.4 us
  transfers between devices with their start and end apart: 74, of which 31 were waited for; matrix products, arithmetic and copies ran while one was open for 8% of the time, Pallas kernels for 25%

profile of v15, /device:TPU:0, one launch (start us, length us, event | category | flops | bytes accessed | tf_op | source)
XLA Modules:
  0.0 537.2 jit_solution(13855774922847952826)
XLA Ops:
  22.0 8.9 %copy.71 = bf16[512,2,4608]{2,0,1:T(8,128)(2,1)} copy(bf16[512,2,4608]{2,1,0:T(2,128)(2,1)} %param.15) | data formatting | bytes 18874368 | tf_op jit(solution)/shard_map/optimization_barrier | solution.py:295
  53.8 16.9 %collective-permute-done.8.refs_4_.refs_5_.refs_6_.refs_7_ = bf16[128,3328]{1,0:T(8,128)(2,1)S(1)} collective-permute-done((bf16[128,3328]{1,0:T(8,128)(2,1)}, bf16[128,3328]{1,0:T(8,128)(2,1)S(1)}, u32[]{:S(2)}, u32[]{:S(2)}) %collective-permute-start.8) | collective-permute-done | bytes 852000 | tf_op jit(solution)/shard_map/ppermute | solution.py:270
  80.3 12.4 %shard_map.196 = (bf16[16,64,256]{2,1,0:T(8,128)(2,1)}, bf16[4096,64]{1,0:T(8,128)(2,1)S(1)}, bf16[64,4096]{1,0:T(8,128)(2,1)S(1)}, bf16[4096,64]{1,0:T(8,128)(2...) custom-call(s32[32]{0:T(128)S(1)} %broadcast_add_fusion.q_slot, ...), custom_call_target="tpu_custom_call" | custom-call | flops 1 | bytes 1 | tf_op jit(solution)/shard_map/pallas_call | solution.py:226
  111.2 28.8 %all-to-all-done.1 = bf16[16,64,256]{2,1,0:T(8,128)(2,1)} async-done(((bf16[16,64,256]{2,1,0:T(8,128)(2,1)}), bf16[16,64,256]{2,1,0:T(8,128)(2,1)}, u32[]{:S(2)}, u32[]{:S(2)}) %all-to-all-start.1) | async-done | bytes 524320 | tf_op jit(solution)/shard_map/all_to_all | solution.py:1153
  152.0 16.9 %shard_map.198 = (bf16[256,1792]{1,0:T(8,128)(2,1)}, bf16[256,1792]{1,0:T(8,128)(2,1)}, bf16[256,1792]{1,0:T(8,128)(2,1)}, bf16[256,1792]{1,0:T(8,128)(2,1)}, f32[256,1024]{1,0:T(8,128)}, /*index=5*/f32[256,1024]{1,0:T(8,128)}) custom-call(s32[4]{0:T(128)} %pad_add_fusion.here, bf16[256,1024]{1,0:T(8,128)(2,1)} %get-tuple-element.139.refs_0_, ...), custom_call_target="tpu_custom_call" | custom-call | flops 1 | bytes 1 | tf_op jit(solution)/shard_map/pallas_call | solution.py:310
  176.2 17.1 %shard_map.199 = (bf16[256,1792]{1,0:T(8,128)(2,1)}, bf16[256,1792]{1,0:T(8,128)(2,1)}, bf16[256,1792]{1,0:T(8,128)(2,1)}, bf16[256,1792]{1,0:T(8,128)(2,1)}, bf...) custom-call(s32[4]{0:T(128)} %pad_add_fusion.here, ...), custom_call_target="tpu_custom_call" | custom-call | flops 1 | bytes 1 | tf_op jit(solution)/shard_map/pallas_call | solution.py:310
  204.8 23.3 %collective-permute-done.28.refs_7_ = bf16[256,1792]{1,0:T(8,128)(2,1)} collective-permute-done((bf16[256,1792]{1,0:T(8,128)(2,1)}, bf16[256,1792]{1,0:T(8,128)(2,1)}, u32[]{:S(2)}, u32[]{:S(2)}) %collective-permute-start.28) | collective-permute-done | bytes 917536 | tf_op jit(solution)/shard_map/ppermute | solution.py:261
  231.3 7.5 %shard_map.200 = (bf16[2,256,1152]{2,1,0:T(8,128)(2,1)}, f32[2,256,1152]{2,1,0:T(8,128)}) custom-call(s32[4]{0:T(128)} %pad_add_fusion.here, bf16[1024,256]{1,0:T(8,128)(2,1)} %get-tuple-element.160.refs_0_, bf16[1024,256]{1,0:T(8,128)(2,1)} %copy-done.52, bf16[1024,256]{1,0:T(8,128)(2,1)} %collective-permute-done.24.refs_2_, bf16[1024,256]{1,0:T(8,128)(2,1)} %copy-done.51, ...), custom_call_target="tpu_custom_call" | custom-call | flops 3000000000 | bytes 1 | tf_op jit(solution)/shard_map/pallas_call | solution.py:310
  243.4 16.6 %shard_map.201 = bf16[16,192,256]{2,1,0:T(8,128)(2,1)} custom-call(s32[32]{0:T(128)S(1)} %broadcast_add_fusion.q_slot, s32[32]{0:T(128)S(1)} %get-tuple-element.241.kv_slot, s32[8]{0:T(128)S(1)} %get-tuple-element.262.first, s32[8]{0:T(128)S(1)} %get-tuple-element.263.last, bf16[16,64,256]{2,1,0:T(8,128)(2,1)S(1)} %all-to-all-done.2.d_ref, ...), custom_call_target="tpu_custom_call" | custom-call | flops 24999999488 | bytes 1 | tf_op jit(solution)/shard_map/pallas_call | solution.py:226
  278.3 7.5 %shard_map.203 = (bf16[2,256,1152]{2,1,0:T(8,128)(2,1)}, f32[2,256,1152]{2,1,0:T(8,128)}) custom-call(s32[4]{0:T(128)} %pad_add_fusion.here, bf16[1024,256]{1,0:T(8,128)(2,1)} %get-tuple-element.160.refs_0_, bf16[1024,256]{1,0:T(8,128)(2,1)} %copy-done.52, bf16[1024,256]{1,0:T(8,128)(2,1)} %collective-permute-done.24.refs_2_, bf16[1024,256]{1,0:T(8,128)(2,1)} %copy-done.51, ...), custom_call_target="tpu_custom_call" | custom-call | flops 3000000000 | bytes 1 | tf_op jit(solution)/shard_map/pallas_call | solution.py:310
  292.8 9.9 %shard_map.202 = (bf16[2,288,1024]{2,1,0:T(8,128)(2,1)}, f32[2,288,1024]{2,1,0:T(8,128)}) custom-call(s32[4]{0:T(128)} %pad_add_fusion.here, bf16[256,1024]{1,0:T(8,128)(2,1)} %bitcast.97, bf16[256,1024]{1,0:T(8,128)(2,1)} %copy-done.53, bf16[256,1024]{1,0:T(8,128)(2,1)} %collective-permute-done.1.refs_2_, bf16[256,1024]{1,0:T(8,128)(2,1)} %copy-done.54, ...), custom_call_target="tpu_custom_call" | custom-call | flops 3000000000 | bytes 1 | tf_op jit(solution)/shard_map/pallas_call | solution.py:310
  302.6 12.4 %collective-permute-done.42 = bf16[256,1152]{1,0:T(8,128)(2,1)S(1)} collective-permute-done((bf16[256,1152]{1,0:T(8,128)(2,1)S(1)}, bf16[256,1152]{1,0:T(8,128)(2,1)S(1)}, u32[]{:S(2)}, u32[]{:S(2)}) %collective-permute-start.42) | collective-permute-done | bytes 589856 | tf_op jit(solution)/shard_map/ppermute | solution.py:264
  326.0 8.6 %shard_map.204 = (bf16[768,256]{1,0:T(8,128)(2,1)}, bf16[768,256]{1,0:T(8,128)(2,1)}, bf16[768,256]{1,0:T(8,128)(2,1)}, bf16[768,256]{1,0:T(8,128)(2,1)}, f32[256,1024]{1,0:T(8,128)}, /*index=5*/f32[8,1024]{1,0:T(8,128)}) custom-call(s32[4]{0:T(128)} %pad_add_fusion.here, bf16[16,192,256]{2,1,0:T(8,128)(2,1)} %copy-done.8, ...), custom_call_target="tpu_custom_call" | custom-call | flops 1 | bytes 1 | tf_op jit(solution)/shard_map/pallas_call | solution.py:310
  348.1 17.1 %collective-permute-done.43 = bf16[256,1152]{1,0:T(8,128)(2,1)S(1)} collective-permute-done((bf16[256,1152]{1,0:T(8,128)(2,1)S(1)}, bf16[256,1152]{1,0:T(8,128)(2,1)S(1)}, u32[]{:S(2)}, u32[]{:S(2)}) %collective-permute-start.43) | collective-permute-done | bytes 589856 | tf_op jit(solution)/shard_map/ppermute | solution.py:267
  368.8 7.3 %collective-permute-done.47.refs_7_ = bf16[768,256]{1,0:T(8,128)(2,1)S(1)} collective-permute-done((bf16[768,256]{1,0:T(8,128)(2,1)S(1)}, bf16[768,256]{1,0:T(8,128)(2,1)S(1)}, u32[]{:S(2)}, u32[]{:S(2)}) %collective-permute-start.47) | collective-permute-done | bytes 393248 | tf_op jit(solution)/shard_map/ppermute | solution.py:261
  376.9 6.9 %shard_map.205 = (bf16[2,272,768]{2,1,0:T(8,128)(2,1)}, f32[2,272,768]{2,1,0:T(8,128)}) custom-call(s32[4]{0:T(128)} %pad_add_fusion.here, bf16[2,1024,256]{2,1,0:T(8,128)(2,1)} %pad_maximum_fusion.4.refs_0_, bf16[2,1024,256]{2,1,0:T(8,128)(2,1)} %collective-permute-done.29.refs_1_, bf16[2,1024,256]{2,1,0:T(8,128)(2,1)} %collective-permute-done.37.refs_2_, ...), custom_call_target="tpu_custom_call" | custom-call | flops 3000000000 | bytes 1 | tf_op jit(solution)/shard_map/pallas_call | solution.py:310
  384.8 10.6 %collective-permute-done.51 = bf16[256,1152]{1,0:T(8,128)(2,1)S(1)} collective-permute-done((bf16[256,1152]{1,0:T(8,128)(2,1)S(1)}, bf16[256,1152]{1,0:T(8,128)(2,1)S(1)}, u32[]{:S(2)}, u32[]{:S(2)}) %collective-permute-start.51) | collective-permute-done | bytes 589856 | tf_op jit(solution)/shard_map/ppermute | solution.py:264
  396.6 10.2 %collective-permute-done.50 = bf16[288,1024]{1,0:T(8,128)(2,1)S(1)} collective-permute-done((bf16[288,1024]{1,0:T(8,128)(2,1)S(1)}, bf16[288,1024]{1,0:T(8,128)(2,1)S(1)}, u32[]{:S(2)}, u32[]{:S(2)}) %collective-permute-start.50) | collective-permute-done | bytes 589856 | tf_op jit(solution)/shard_map/ppermute | solution.py:264
  410.6 10.5 %collective-permute-done.54.refs_2_ = bf16[2,256,1152]{2,1,0:T(8,128)(2,1)S(1)} collective-permute-done((bf16[2,256,1152]{2,1,0:T(8,128)(2,1)S(1)}, bf16[2,256,1152]{2,1,0:T(8,128)(2,1)S(1)}, u32[]{:S(2)}, u32[]{:S(2)}) %collective-permute-start.54) | collective-permute-done | bytes 1179680 | tf_op jit(solution)/shard_map/ppermute | solution.py:261
  421.2 15.1 %collective-permute-done.53 = bf16[256,1152]{1,0:T(8,128)(2,1)S(1)} collective-permute-done((bf16[256,1152]{1,0:T(8,128)(2,1)S(1)}, bf16[256,1152]{1,0:T(8,128)(2,1)S(1)}, u32[]{:S(2)}, u32[]{:S(2)}) %collective-permute-start.53) | collective-permute-done | bytes 589856 | tf_op jit(solution)/shard_map/ppermute | solution.py:264
  447.7 10.0 %shard_map.206.refs_4_ = f32[512,2,4608]{2,1,0:T(2,128)} custom-call(s32[4]{0:T(128)} %pad_add_fusion.here, bf16[2,256,1152]{2,1,0:T(8,128)(2,1)} %copy-done.17, bf16[2,256,1152]{2,1,0:T(8,128)(2,1)} %copy-done.30, bf16[2,256,1152]{2,1,0:T(8,128)(2,1)} %copy-done.29, bf16[2,256,1152]{2,1,0:T(8,128)(2,1)} %copy-done.31), custom_call_target="tpu_custom_call" | custom-call | flops 1 | bytes 1 | tf_op jit(solution)/shard_map/pallas_call | solution.py:310
  478.3 9.7 %shard_map.207 = f32[512,2,4608]{2,1,0:T(2,128)} custom-call(s32[4]{0:T(128)} %pad_add_fusion.here, bf16[2,256,1152]{2,1,0:T(8,128)(2,1)} %copy-done.16, bf16[2,256,1152]{2,1,0:T(8,128)(2,1)} %copy-done.32, bf16[2,256,1152]{2,1,0:T(8,128)(2,1)} %copy-done.28, bf16[2,256,1152]{2,1,0:T(8,128)(2,1)} %copy-done.33, ...), custom_call_target="tpu_custom_call", output_to_operand_aliasing={{}: (5, {})} | custom-call | flops 1 | bytes 1 | tf_op jit(solution)/shard_map/pallas_call | solution.py:310
  488.0 25.8 %collective-permute-done.63.refs_2_ = bf16[2,272,768]{2,1,0:T(8,128)(2,1)} collective-permute-done((bf16[2,272,768]{2,1,0:T(8,128)(2,1)S(1)}, bf16[2,272,768]{2,1,0:T(8,128)(2,1)}, u32[]{:S(2)}, u32[]{:S(2)}) %collective-permute-start.63) | collective-permute-done | bytes 835616 | tf_op jit(solution)/shard_map/ppermute | solution.py:261
  528.7 7.9 %shard_map.209 = f32[2304,1024]{1,0:T(8,128)} custom-call(s32[4]{0:T(128)} %pad_add_fusion.here, bf16[2,288,1024]{2,1,0:T(8,128)(2,1)} %copy-done.18, bf16[2,288,1024]{2,1,0:T(8,128)(2,1)} %copy-done.34, bf16[2,288,1024]{2,1,0:T(8,128)(2,1)} %collective-permute-done.68.refs_2_, bf16[2,288,1024]{2,1,0:T(8,128)(2,1)} %collective-permute-done.69.refs_3_), custom_call_target="tpu_custom_call" | custom-call | flops 1 | bytes 1 | tf_op jit(solution)/shard_map/pallas_call | solution.py:310
  (325 shorter events, 217.3 us)
Async XLA Ops:
  42.1 37.1 %all-to-all-start = ((bf16[16,192,256]{2,1,0:T(8,128)(2,1)}), bf16[16,192,256]{2,1,0:T(8,128)(2,1)S(1)}, u32[]{:S(2)}, u32[]{:S(2)}) async-start(bf16[16,192,256]{2,1,0:T(8,128)(2,1)} %get-tuple-element.132), calls=%async_computation | async-start | bytes 3145728 | tf_op jit(solution)/shard_map/all_to_all | solution.py:1127
  74.9 35.8 %collective-permute-start.10 = (bf16[128,3328]{1,0:T(8,128)(2,1)S(1)}, bf16[128,3328]{1,0:T(8,128)(2,1)}, u32[]{:S(2)}, u32[]{:S(2)}) collective-permute-start(bf16[128,3328]{1,0:T(8,128)(2,1)S(1)} %collective-permute-done.8.refs_4_.refs_5_.refs_6_.refs_7_), channel_id=1, source_target_pairs={{0,4},{2,6},{4,0},{6,2},{8,12},{10,14},{12,8},{14,10},{16,20},{18,... | collective-permute-start | bytes 2555912 | tf_op jit(solution)/shard_map/ppermute | solution.py:261
  98.5 41.7 %collective-permute-start.19 = (bf16[2304,256]{1,0:T(8,128)(2,1)}, bf16[2304,256]{1,0:T(8,128)(2,1)}, u32[]{:S(2)}, u32[]{:S(2)}) collective-permute-start(bf16[2304,256]{1,0:T(8,128)(2,1)} %collective-permute-done.12.refs_12_), channel_id=1, source_target_pairs={{0,4},{2,6},{4,0},{6,2},{8,12},{10,14},{12,8},{14,10},{16,20},{18,... | collective-permute-start | bytes 3538952 | tf_op jit(solution)/shard_map/ppermute | solution.py:261
  100.9 39.6 %collective-permute-start.13 = (bf16[128,4608]{1,0:T(8,128)(2,1)}, bf16[128,4608]{1,0:T(8,128)(2,1)}, u32[]{:S(2)}, u32[]{:S(2)}) collective-permute-start(bf16[128,4608]{1,0:T(8,128)(2,1)} %pad_maximum_fusion), channel_id=1, source_target_pairs={{0,1},{1,0},{2,3},{3,2},{4,5},{5,4},{6,7},{7,6},{8,9},{9,8},{10,11... | collective-permute-start | bytes 3538952 | tf_op jit(solution)/shard_map/ppermute | solution.py:270
  102.3 37.7 %all-to-all-start.1 = ((bf16[16,64,256]{2,1,0:T(8,128)(2,1)}), bf16[16,64,256]{2,1,0:T(8,128)(2,1)}, u32[]{:S(2)}, u32[]{:S(2)}) async-start(bf16[16,64,256]{2,1,0:T(8,128)(2,1)} %get-tuple-element.134), calls=%async_computation.1 | async-start | bytes 1048576 | tf_op jit(solution)/shard_map/all_to_all | solution.py:1153
  169.5 34.7 %collective-permute-start.27 = (bf16[256,1792]{1,0:T(8,128)(2,1)}, bf16[256,1792]{1,0:T(8,128)(2,1)}, u32[]{:S(2)}, u32[]{:S(2)}) collective-permute-start(bf16[256,1792]{1,0:T(8,128)(2,1)} %get-tuple-element.166), channel_id=1, source_target_pairs={{0,4},{2,6},{4,0},{6,2},{8,12},{10,14},{12,8},{14,10},{16,20},{18,... | collective-permute-start | bytes 2752520 | tf_op jit(solution)/shard_map/ppermute | solution.py:261
  171.1 33.6 %collective-permute-start.26 = (bf16[256,1792]{1,0:T(8,128)(2,1)}, bf16[256,1792]{1,0:T(8,128)(2,1)}, u32[]{:S(2)}, u32[]{:S(2)}) collective-permute-start(bf16[256,1792]{1,0:T(8,128)(2,1)} %get-tuple-element.164), channel_id=1, source_target_pairs={{0,2},{2,0},{4,6},{6,4},{8,10},{10,8},{12,14},{14,12},{16,18},{18,... | collective-permute-start | bytes 2752520 | tf_op jit(solution)/shard_map/ppermute | solution.py:258
  171.2 33.0 %collective-permute-start.24 = (bf16[1024,256]{1,0:T(8,128)(2,1)}, bf16[1024,256]{1,0:T(8,128)(2,1)}, u32[]{:S(2)}, u32[]{:S(2)}) collective-permute-start(bf16[1024,256]{1,0:T(8,128)(2,1)} %get-tuple-element.160.refs_0_), channel_id=1, source_target_pairs={{0,4},{2,6},{4,0},{6,2},{8,12},{10,14},{12,8},{14,10},{16,20},{18,... | collective-permute-start | bytes 1572872 | tf_op jit(solution)/shard_map/ppermute | solution.py:261
  173.5 54.6 %collective-permute-start.28 = (bf16[256,1792]{1,0:T(8,128)(2,1)}, bf16[256,1792]{1,0:T(8,128)(2,1)}, u32[]{:S(2)}, u32[]{:S(2)}) collective-permute-start(bf16[256,1792]{1,0:T(8,128)(2,1)} %collective-permute-done.22), channel_id=1, source_target_pairs={{0,4},{2,6},{4,0},{6,2},{8,12},{10,14},{12,8},{14,10},{16,20},{18,... | collective-permute-start | bytes 2752520 | tf_op jit(solution)/shard_map/ppermute | solution.py:261
  195.4 44.5 %collective-permute-start.29 = (bf16[2,1024,256]{2,1,0:T(8,128)(2,1)}, bf16[2,1024,256]{2,1,0:T(8,128)(2,1)}, u32[]{:S(2)}, u32[]{:S(2)}) collective-permute-start(bf16[2,1024,256]{2,1,0:T(8,128)(2,1)} %pad_maximum_fusion.4.refs_0_), channel_id=1, source_target_pairs={{0,2},{2,0},{4,6},{6,4},{8,10},{10,8},{12,14},{14,12},{16,18},{18,... | collective-permute-start | bytes 3145736 | tf_op jit(solution)/shard_map/ppermute | solution.py:258
  195.5 44.4 %all-to-all-start.2 = ((bf16[16,64,256]{2,1,0:T(8,128)(2,1)}), bf16[16,64,256]{2,1,0:T(8,128)(2,1)S(1)}, u32[]{:S(2)}, u32[]{:S(2)}) async-start(bf16[16,64,256]{2,1,0:T(8,128)(2,1)} %bitcast.104), calls=%async_computation.2 | async-start | bytes 1048576 | tf_op jit(solution)/shard_map/all_to_all | solution.py:1194
  204.3 35.2 %collective-permute-start.32 = (bf16[256,1792]{1,0:T(8,128)(2,1)}, bf16[256,1792]{1,0:T(8,128)(2,1)}, u32[]{:S(2)}, u32[]{:S(2)}) collective-permute-start(bf16[256,1792]{1,0:T(8,128)(2,1)} %get-tuple-element.179), channel_id=1, source_target_pairs={{0,2},{2,0},{4,6},{6,4},{8,10},{10,8},{12,14},{14,12},{16,18},{18,... | collective-permute-start | bytes 2752520 | tf_op jit(solution)/shard_map/ppermute | solution.py:258
  228.1 31.9 %collective-permute-start.31 = (bf16[256,1792]{1,0:T(8,128)(2,1)}, bf16[256,1792]{1,0:T(8,128)(2,1)}, u32[]{:S(2)}, u32[]{:S(2)}) collective-permute-start(bf16[256,1792]{1,0:T(8,128)(2,1)} %get-tuple-element.178), channel_id=1, source_target_pairs={{0,4},{2,6},{4,0},{6,2},{8,12},{10,14},{12,8},{14,10},{16,20},{18,... | collective-permute-start | bytes 2752520 | tf_op jit(solution)/shard_map/ppermute | solution.py:261
  269.4 55.5 %all-to-all-start.3 = ((bf16[16,192,256]{2,1,0:T(8,128)(2,1)}), bf16[16,192,256]{2,1,0:T(8,128)(2,1)S(1)}, u32[]{:S(2)}, u32[]{:S(2)}) async-start(bf16[16,192,256]{2,1,0:T(8,128)(2,1)} %shard_map.201), calls=%async_computation.3 | async-start | bytes 3145728 | tf_op jit(solution)/shard_map/all_to_all | solution.py:1217
  285.7 33.8 %collective-permute-start.38 = (bf16[2,256,1152]{2,1,0:T(8,128)(2,1)}, bf16[2,256,1152]{2,1,0:T(8,128)(2,1)}, u32[]{:S(2)}, u32[]{:S(2)}) collective-permute-start(bf16[2,256,1152]{2,1,0:T(8,128)(2,1)} %get-tuple-element.192), channel_id=1, source_target_pairs={{0,1},{1,0},{2,3},{3,2},{4,5},{5,4},{6,7},{7,6},{8,9},{9,8},{10,11... | collective-permute-start | bytes 3538952 | tf_op jit(solution)/shard_map/ppermute | solution.py:270
  287.0 32.5 %collective-permute-start.37 = (bf16[2,1024,256]{2,1,0:T(8,128)(2,1)}, bf16[2,1024,256]{2,1,0:T(8,128)(2,1)}, u32[]{:S(2)}, u32[]{:S(2)}) collective-permute-start(bf16[2,1024,256]{2,1,0:T(8,128)(2,1)} %pad_maximum_fusion.4.refs_0_), channel_id=1, source_target_pairs={{0,4},{2,6},{4,0},{6,2},{8,12},{10,14},{12,8},{14,10},{16,20},{18,... | collective-permute-start | bytes 3145736 | tf_op jit(solution)/shard_map/ppermute | solution.py:261
  366.7 40.1 %collective-permute-start.50 = (bf16[288,1024]{1,0:T(8,128)(2,1)S(1)}, bf16[288,1024]{1,0:T(8,128)(2,1)S(1)}, u32[]{:S(2)}, u32[]{:S(2)}) collective-permute-start(bf16[288,1024]{1,0:T(8,128)(2,1)S(1)} %fusion.9), channel_id=1, source_target_pairs={{0,8},{2,10},{4,12},{6,14},{8,0},{10,2},{12,4},{14,6},{16,24},{18,... | collective-permute-start | bytes 1769480 | tf_op jit(solution)/shard_map/ppermute | solution.py:264
  368.8 38.3 %collective-permute-start.49 = (bf16[256,1152]{1,0:T(8,128)(2,1)S(1)}, bf16[256,1152]{1,0:T(8,128)(2,1)S(1)}, u32[]{:S(2)}, u32[]{:S(2)}) collective-permute-start(bf16[256,1152]{1,0:T(8,128)(2,1)S(1)} %fusion.1), channel_id=1, source_target_pairs={{0,16},{2,18},{4,20},{6,22},{8,24},{10,26},{12,28},{14,30},{16,0},... | collective-permute-start | bytes 1769480 | tf_op jit(solution)/shard_map/ppermute | solution.py:267
  408.6 34.4 %collective-permute-start.52 = (bf16[272,768]{1,0:T(8,128)(2,1)S(1)}, bf16[272,768]{1,0:T(8,128)(2,1)S(1)}, u32[]{:S(2)}, u32[]{:S(2)}) collective-permute-start(bf16[272,768]{1,0:T(8,128)(2,1)S(1)} %fusion.11), channel_id=1, source_target_pairs={{0,8},{2,10},{4,12},{6,14},{8,0},{10,2},{12,4},{14,6},{16,24},{18,... | collective-permute-start | bytes 1253384 | tf_op jit(solution)/shard_map/ppermute | solution.py:264
  409.5 33.7 %collective-permute-start.56 = (bf16[288,1024]{1,0:T(8,128)(2,1)S(1)}, bf16[288,1024]{1,0:T(8,128)(2,1)S(1)}, u32[]{:S(2)}, u32[]{:S(2)}) collective-permute-start(bf16[288,1024]{1,0:T(8,128)(2,1)S(1)} %fusion), channel_id=1, source_target_pairs={{0,16},{2,18},{4,20},{6,22},{8,24},{10,26},{12,28},{14,30},{16,0},... | collective-permute-start | bytes 1769480 | tf_op jit(solution)/shard_map/ppermute | solution.py:267
  410.6 35.0 %collective-permute-start.58 = (bf16[2,256,1152]{2,1,0:T(8,128)(2,1)S(1)}, bf16[2,256,1152]{2,1,0:T(8,128)(2,1)S(1)}, u32[]{:S(2)}, u32[]{:S(2)}) collective-permute-start(bf16[2,256,1152]{2,1,0:T(8,128)(2,1)S(1)} %pad_maximum_fusion.1.refs_0_), channel_id=1, source_target_pairs={{0,2},{2,0},{4,6},{6,4},{8,10},{10,8},{12,14},{14,12},{16,18},{18,... | collective-permute-start | bytes 3538952 | tf_op jit(solution)/shard_map/ppermute | solution.py:258
  467.9 46.5 %collective-permute-start.68 = (bf16[2,288,1024]{2,1,0:T(8,128)(2,1)S(1)}, bf16[2,288,1024]{2,1,0:T(8,128)(2,1)}, u32[]{:S(2)}, u32[]{:S(2)}) collective-permute-start(bf16[2,288,1024]{2,1,0:T(8,128)(2,1)S(1)} %pad_maximum_fusion.3.refs_0_), channel_id=1, source_target_pairs={{0,4},{2,6},{4,0},{6,2},{8,12},{10,14},{12,8},{14,10},{16,20},{18,... | collective-permute-start | bytes 3538952 | tf_op jit(solution)/shard_map/ppermute | solution.py:261
  475.6 38.2 %collective-permute-start.63 = (bf16[2,272,768]{2,1,0:T(8,128)(2,1)S(1)}, bf16[2,272,768]{2,1,0:T(8,128)(2,1)}, u32[]{:S(2)}, u32[]{:S(2)}) collective-permute-start(bf16[2,272,768]{2,1,0:T(8,128)(2,1)S(1)} %pad_maximum_fusion.6.refs_0_), channel_id=1, source_target_pairs={{0,4},{2,6},{4,0},{6,2},{8,12},{10,14},{12,8},{14,10},{16,20},{18,... | collective-permute-start | bytes 2506760 | tf_op jit(solution)/shard_map/ppermute | solution.py:261
  476.2 38.2 %collective-permute-start.62 = (bf16[2,272,768]{2,1,0:T(8,128)(2,1)S(1)}, bf16[2,272,768]{2,1,0:T(8,128)(2,1)}, u32[]{:S(2)}, u32[]{:S(2)}) collective-permute-start(bf16[2,272,768]{2,1,0:T(8,128)(2,1)S(1)} %pad_maximum_fusion.6.refs_0_), channel_id=1, source_target_pairs={{0,2},{2,0},{4,6},{6,4},{8,10},{10,8},{12,14},{14,12},{16,18},{18,... | collective-permute-start | bytes 2506760 | tf_op jit(solution)/shard_map/ppermute | solution.py:258
  (109 other events, 1416.3 us)

commit v16 on v15

--- a/solution.py
+++ b/solution.py
@@ -948,6 +948,12 @@
     return out
 
 
+def half_by_step(array, number):
+    return pl.BlockSpec(
+        (1, *array.shape[1:]), lambda s, here: (jnp.where(s > number, 1, 0), 0, 0)
+    )
+
+
 def place_down(here, pieces):
     _, rows, columns = pieces[0].shape
 
@@ -956,7 +962,7 @@
 
             @pl.when(pl.program_id(0) == s)
             def _(s=s):
-                refs[4][...] = refs[s % 4][s // 4].astype(jnp.float32)
+                refs[4][...] = refs[s % 4][0].astype(jnp.float32)
 
     def target(s, here):
         half = (s // 4) ^ here[0]
@@ -969,7 +975,7 @@
         here,
         (8,),
         list(pieces),
-        [whole(v) for v in pieces],
+        [half_by_step(v, a) for a, v in enumerate(pieces)],
         [jax.ShapeDtypeStruct((rows * 8, columns), jnp.float32)],
         [pl.BlockSpec((rows, columns), target)],
     )
@@ -986,7 +992,7 @@
 
             @pl.when(pl.program_id(0) == s)
             def _(s=s):
-                value = refs[s % 4][s // 4]
+                value = refs[s % 4][0]
                 qkv_ref[...] = value[:rows, :cut].astype(jnp.float32)
                 out_ref[...] = value[:rows, cut:].astype(jnp.float32)
                 gains = value[rows:].astype(jnp.float32)
@@ -1004,7 +1010,7 @@
         here,
         (8,),
         list(pieces),
-        [whole(v) for v in pieces],
+        [half_by_step(v, a) for a, v in enumerate(pieces)],
         [
             shape((2 * rows, 4 * cut), f32),
             shape((2 * rows, 4 * (columns - cut)), f32),
@@ -1292,7 +1298,9 @@
     spread_y(3, full[2])
     grad_down = place_down(here, spread_core(2, grad_gate_up))
     cut = qkv_weight.shape[1] // 4
-    grad_qkv, grad_out, gain_sums = place_attention(here, spread_core(3, grad_gate_up), cut)
+    last_pieces = spread_core(3, grad_gate_up)
+    last_pieces = (*last_pieces[:3], after(last_pieces[3], grad_down))
+    grad_qkv, grad_out, gain_sums = place_attention(here, last_pieces, cut)
     at = links.side * (HD // 2)
     gain_grads = [
         gain_sums[0, :rows],

time: 546 us -> 548 us (level)
    ppermute x18, waiting for transfers between devices: 85.2 us -> 93.1 us  [over_y(): return lax.ppermute(value, 'ctx', self.route(lambda z, y, c: (z, 1 - y, c)))]
    unnamed x120 -> x116, local copies, waits for them, and re-layouts: 21.3 us -> 18.8 us
  transfers between devices with their start and end apart: 74 -> 74, of which waited for: 31 -> 30; matrix products, arithmetic and copies ran while one was open for 8% -> 8% of each run, Pallas kernels for 25% -> 25%
where the time goes in v16:
time: 548 us; the launch traced here: 539 us
  waiting for transfers between devices  254 us (46%)
  Pallas kernels  150 us (27%)
  starting transfers between devices  69.3 us (13%)
  local copies, waits for them, and re-layouts  46.7 us (9%)
  other arithmetic  17.3 us (3%)
    pallas_call x13, Pallas kernels, call_with_here(): pl.pallas_call(kernel, grid_spec=pltpu.PrefetchScalarGridSpec(num_scalar_...  121 us
    ppermute x18, waiting for transfers between devices, over_y(): return lax.ppermute(value, 'ctx', self.route(lambda z, y, c: (z, 1 - y, c)))  93.1 us
    ppermute x8, waiting for transfers between devices, over_z(): return lax.ppermute(value, 'ctx', self.route(lambda z, y, c: (z ^ 1, y, c)))  67 us
    ppermute x10, waiting for transfers between devices, over_x(): return lax.ppermute(value, 'fsdp', [(0, 1), (1, 0)])  35.9 us
    pallas_call x2, Pallas kernels, kernel_call(): pl.pallas_call(kernel, out_shape=outs, in_specs=[smem] * len(tables) + [v...  29 us
    all_to_all x1, waiting for transfers between devices, on_block(): lax.all_to_all(attn_sent, 'ctx', 0, 0, tiled=True)  28.8 us
    ppermute x18, starting transfers between devices, over_y(): return lax.ppermute(value, 'ctx', self.route(lambda z, y, c: (z, 1 - y, c)))  20 us
    unnamed x116, local copies, waits for them, and re-layouts  18.8 us
  transfers between devices with their start and end apart: 74, of which 30 were waited for; matrix products, arithmetic and copies ran while one was open for 8% of the time, Pallas kernels for 25%

profile of v16, /device:TPU:0, one launch (start us, length us, event | category | flops | bytes accessed | tf_op | source)
XLA Modules:
  0.0 539.4 jit_solution(8213596091432372896)
XLA Ops:
  22.0 8.9 %copy.71 = bf16[512,2,4608]{2,0,1:T(8,128)(2,1)} copy(bf16[512,2,4608]{2,1,0:T(2,128)(2,1)} %param.15) | data formatting | bytes 18874368 | tf_op jit(solution)/shard_map/optimization_barrier | solution.py:295
  53.7 16.9 %collective-permute-done.8.refs_4_.refs_5_.refs_6_.refs_7_ = bf16[128,3328]{1,0:T(8,128)(2,1)S(1)} collective-permute-done((bf16[128,3328]{1,0:T(8,128)(2,1)}, bf16[128,3328]{1,0:T(8,128)(2,1)S(1)}, u32[]{:S(2)}, u32[]{:S(2)}) %collective-permute-start.8) | collective-permute-done | bytes 852000 | tf_op jit(solution)/shard_map/ppermute | solution.py:270
  80.3 12.4 %shard_map.196 = (bf16[16,64,256]{2,1,0:T(8,128)(2,1)}, bf16[4096,64]{1,0:T(8,128)(2,1)S(1)}, bf16[64,4096]{1,0:T(8,128)(2,1)S(1)}, bf16[4096,64]{1,0:T(8,128)(2...) custom-call(s32[32]{0:T(128)S(1)} %broadcast_add_fusion.q_slot, ...), custom_call_target="tpu_custom_call" | custom-call | flops 1 | bytes 1 | tf_op jit(solution)/shard_map/pallas_call | solution.py:226
  111.1 28.8 %all-to-all-done.1 = bf16[16,64,256]{2,1,0:T(8,128)(2,1)} async-done(((bf16[16,64,256]{2,1,0:T(8,128)(2,1)}), bf16[16,64,256]{2,1,0:T(8,128)(2,1)}, u32[]{:S(2)}, u32[]{:S(2)}) %all-to-all-start.1) | async-done | bytes 524320 | tf_op jit(solution)/shard_map/all_to_all | solution.py:1159
  152.0 16.9 %shard_map.198 = (bf16[256,1792]{1,0:T(8,128)(2,1)}, bf16[256,1792]{1,0:T(8,128)(2,1)}, bf16[256,1792]{1,0:T(8,128)(2,1)}, bf16[256,1792]{1,0:T(8,128)(2,1)}, f32[256,1024]{1,0:T(8,128)}, /*index=5*/f32[256,1024]{1,0:T(8,128)}) custom-call(s32[4]{0:T(128)} %pad_add_fusion.here, bf16[256,1024]{1,0:T(8,128)(2,1)} %get-tuple-element.140.refs_0_, ...), custom_call_target="tpu_custom_call" | custom-call | flops 1 | bytes 1 | tf_op jit(solution)/shard_map/pallas_call | solution.py:310
  176.1 17.1 %shard_map.199 = (bf16[256,1792]{1,0:T(8,128)(2,1)}, bf16[256,1792]{1,0:T(8,128)(2,1)}, bf16[256,1792]{1,0:T(8,128)(2,1)}, bf16[256,1792]{1,0:T(8,128)(2,1)}, bf...) custom-call(s32[4]{0:T(128)} %pad_add_fusion.here, ...), custom_call_target="tpu_custom_call" | custom-call | flops 1 | bytes 1 | tf_op jit(solution)/shard_map/pallas_call | solution.py:310
  204.8 23.3 %collective-permute-done.28.refs_7_ = bf16[256,1792]{1,0:T(8,128)(2,1)} collective-permute-done((bf16[256,1792]{1,0:T(8,128)(2,1)}, bf16[256,1792]{1,0:T(8,128)(2,1)}, u32[]{:S(2)}, u32[]{:S(2)}) %collective-permute-start.28) | collective-permute-done | bytes 917536 | tf_op jit(solution)/shard_map/ppermute | solution.py:261
  231.2 7.5 %shard_map.200 = (bf16[2,256,1152]{2,1,0:T(8,128)(2,1)}, f32[2,256,1152]{2,1,0:T(8,128)}) custom-call(s32[4]{0:T(128)} %pad_add_fusion.here, bf16[1024,256]{1,0:T(8,128)(2,1)} %get-tuple-element.161.refs_0_, bf16[1024,256]{1,0:T(8,128)(2,1)} %copy-done.50, bf16[1024,256]{1,0:T(8,128)(2,1)} %collective-permute-done.24.refs_2_, bf16[1024,256]{1,0:T(8,128)(2,1)} %copy-done.49, ...), custom_call_target="tpu_custom_call" | custom-call | flops 3000000000 | bytes 1 | tf_op jit(solution)/shard_map/pallas_call | solution.py:310
  243.4 16.6 %shard_map.201 = bf16[16,192,256]{2,1,0:T(8,128)(2,1)} custom-call(s32[32]{0:T(128)S(1)} %broadcast_add_fusion.q_slot, s32[32]{0:T(128)S(1)} %get-tuple-element.243.kv_slot, s32[8]{0:T(128)S(1)} %get-tuple-element.264.first, s32[8]{0:T(128)S(1)} %get-tuple-element.265.last, bf16[16,64,256]{2,1,0:T(8,128)(2,1)S(1)} %all-to-all-done.2.d_ref, ...), custom_call_target="tpu_custom_call" | custom-call | flops 24999999488 | bytes 1 | tf_op jit(solution)/shard_map/pallas_call | solution.py:226
  278.2 7.5 %shard_map.203 = (bf16[2,256,1152]{2,1,0:T(8,128)(2,1)}, f32[2,256,1152]{2,1,0:T(8,128)}) custom-call(s32[4]{0:T(128)} %pad_add_fusion.here, bf16[1024,256]{1,0:T(8,128)(2,1)} %get-tuple-element.161.refs_0_, bf16[1024,256]{1,0:T(8,128)(2,1)} %copy-done.50, bf16[1024,256]{1,0:T(8,128)(2,1)} %collective-permute-done.24.refs_2_, bf16[1024,256]{1,0:T(8,128)(2,1)} %copy-done.49, ...), custom_call_target="tpu_custom_call" | custom-call | flops 3000000000 | bytes 1 | tf_op jit(solution)/shard_map/pallas_call | solution.py:310
  292.7 9.9 %shard_map.202 = (bf16[2,288,1024]{2,1,0:T(8,128)(2,1)}, f32[2,288,1024]{2,1,0:T(8,128)}) custom-call(s32[4]{0:T(128)} %pad_add_fusion.here, bf16[256,1024]{1,0:T(8,128)(2,1)} %bitcast.97, bf16[256,1024]{1,0:T(8,128)(2,1)} %copy-done.51, bf16[256,1024]{1,0:T(8,128)(2,1)} %collective-permute-done.1.refs_2_, bf16[256,1024]{1,0:T(8,128)(2,1)} %copy-done.52, ...), custom_call_target="tpu_custom_call" | custom-call | flops 3000000000 | bytes 1 | tf_op jit(solution)/shard_map/pallas_call | solution.py:310
  302.5 12.5 %collective-permute-done.42 = bf16[256,1152]{1,0:T(8,128)(2,1)S(1)} collective-permute-done((bf16[256,1152]{1,0:T(8,128)(2,1)S(1)}, bf16[256,1152]{1,0:T(8,128)(2,1)S(1)}, u32[]{:S(2)}, u32[]{:S(2)}) %collective-permute-start.42) | collective-permute-done | bytes 589856 | tf_op jit(solution)/shard_map/ppermute | solution.py:264
  325.9 8.6 %shard_map.204 = (bf16[768,256]{1,0:T(8,128)(2,1)}, bf16[768,256]{1,0:T(8,128)(2,1)}, bf16[768,256]{1,0:T(8,128)(2,1)}, bf16[768,256]{1,0:T(8,128)(2,1)}, f32[256,1024]{1,0:T(8,128)}, /*index=5*/f32[8,1024]{1,0:T(8,128)}) custom-call(s32[4]{0:T(128)} %pad_add_fusion.here, bf16[16,192,256]{2,1,0:T(8,128)(2,1)} %copy-done.8, ...), custom_call_target="tpu_custom_call" | custom-call | flops 1 | bytes 1 | tf_op jit(solution)/shard_map/pallas_call | solution.py:310
  348.1 17.1 %collective-permute-done.43 = bf16[256,1152]{1,0:T(8,128)(2,1)S(1)} collective-permute-done((bf16[256,1152]{1,0:T(8,128)(2,1)S(1)}, bf16[256,1152]{1,0:T(8,128)(2,1)S(1)}, u32[]{:S(2)}, u32[]{:S(2)}) %collective-permute-start.43) | collective-permute-done | bytes 589856 | tf_op jit(solution)/shard_map/ppermute | solution.py:267
  384.7 10.6 %collective-permute-done.51 = bf16[256,1152]{1,0:T(8,128)(2,1)S(1)} collective-permute-done((bf16[256,1152]{1,0:T(8,128)(2,1)S(1)}, bf16[256,1152]{1,0:T(8,128)(2,1)S(1)}, u32[]{:S(2)}, u32[]{:S(2)}) %collective-permute-start.51) | collective-permute-done | bytes 589856 | tf_op jit(solution)/shard_map/ppermute | solution.py:264
  396.5 10.2 %collective-permute-done.50 = bf16[288,1024]{1,0:T(8,128)(2,1)S(1)} collective-permute-done((bf16[288,1024]{1,0:T(8,128)(2,1)S(1)}, bf16[288,1024]{1,0:T(8,128)(2,1)S(1)}, u32[]{:S(2)}, u32[]{:S(2)}) %collective-permute-start.50) | collective-permute-done | bytes 589856 | tf_op jit(solution)/shard_map/ppermute | solution.py:264
  410.5 10.6 %collective-permute-done.54.refs_2_ = bf16[2,256,1152]{2,1,0:T(8,128)(2,1)S(1)} collective-permute-done((bf16[2,256,1152]{2,1,0:T(8,128)(2,1)S(1)}, bf16[2,256,1152]{2,1,0:T(8,128)(2,1)S(1)}, u32[]{:S(2)}, u32[]{:S(2)}) %collective-permute-start.54) | collective-permute-done | bytes 1179680 | tf_op jit(solution)/shard_map/ppermute | solution.py:261
  421.1 15.1 %collective-permute-done.53 = bf16[256,1152]{1,0:T(8,128)(2,1)S(1)} collective-permute-done((bf16[256,1152]{1,0:T(8,128)(2,1)S(1)}, bf16[256,1152]{1,0:T(8,128)(2,1)S(1)}, u32[]{:S(2)}, u32[]{:S(2)}) %collective-permute-start.53) | collective-permute-done | bytes 589856 | tf_op jit(solution)/shard_map/ppermute | solution.py:264
  445.5 14.6 %collective-permute-done.60.refs_2_ = bf16[2,256,1152]{2,1,0:T(8,128)(2,1)S(1)} collective-permute-done((bf16[2,256,1152]{2,1,0:T(8,128)(2,1)S(1)}, bf16[2,256,1152]{2,1,0:T(8,128)(2,1)S(1)}, u32[]{:S(2)}, u32[]{:S(2)}) %collective-permute-start.60) | collective-permute-done | bytes 1179680 | tf_op jit(solution)/shard_map/ppermute | solution.py:261
  462.2 10.0 %shard_map.206.refs_4_ = f32[512,2,4608]{2,1,0:T(2,128)} custom-call(s32[4]{0:T(128)} %pad_add_fusion.here, bf16[2,256,1152]{2,1,0:T(8,128)(2,1)} %copy-done.16, bf16[2,256,1152]{2,1,0:T(8,128)(2,1)} %copy-done.30, bf16[2,256,1152]{2,1,0:T(8,128)(2,1)} %copy-done.28, bf16[2,256,1152]{2,1,0:T(8,128)(2,1)} %copy-done.31), custom_call_target="tpu_custom_call" | custom-call | flops 1 | bytes 1 | tf_op jit(solution)/shard_map/pallas_call | solution.py:310
  474.0 11.8 %collective-permute-done.61 = bf16[272,768]{1,0:T(8,128)(2,1)S(1)} collective-permute-done((bf16[272,768]{1,0:T(8,128)(2,1)S(1)}, bf16[272,768]{1,0:T(8,128)(2,1)S(1)}, u32[]{:S(2)}, u32[]{:S(2)}) %collective-permute-start.61) | collective-permute-done | bytes 417824 | tf_op jit(solution)/shard_map/ppermute | solution.py:264
  487.4 9.7 %shard_map.207 = f32[512,2,4608]{2,1,0:T(2,128)} custom-call(s32[4]{0:T(128)} %pad_add_fusion.here, bf16[2,256,1152]{2,1,0:T(8,128)(2,1)} %copy-done.17, bf16[2,256,1152]{2,1,0:T(8,128)(2,1)} %collective-permute-done.64.refs_1_, bf16[2,256,1152]{2,1,0:T(8,128)(2,1)} %copy-done.29, ...), custom_call_target="tpu_custom_call", output_to_operand_aliasing={{}: (5, {})} | custom-call | flops 1 | bytes 1 | tf_op jit(solution)/shard_map/pallas_call | solution.py:310
  501.3 17.2 %collective-permute-done.63.refs_2_ = bf16[2,272,768]{2,1,0:T(8,128)(2,1)} collective-permute-done((bf16[2,272,768]{2,1,0:T(8,128)(2,1)S(1)}, bf16[2,272,768]{2,1,0:T(8,128)(2,1)}, u32[]{:S(2)}, u32[]{:S(2)}) %collective-permute-start.63) | collective-permute-done | bytes 835616 | tf_op jit(solution)/shard_map/ppermute | solution.py:261
  520.1 8.3 %shard_map.208 = f32[2304,1024]{1,0:T(8,128)} custom-call(s32[4]{0:T(128)} %pad_add_fusion.here, bf16[2,288,1024]{2,1,0:T(8,128)(2,1)} %copy-done.18, bf16[2,288,1024]{2,1,0:T(8,128)(2,1)} %collective-permute-done.67.refs_1_, bf16[2,288,1024]{2,1,0:T(8,128)(2,1)} %collective-permute-done.68.refs_2_, bf16[2,288,1024]{2,1,0:T(8,128)(2,1)} %copy-done.32), custom_call_target="tpu_custom_call" | custom-call | flops 1 | bytes 1 | tf_op jit(solution)/shard_map/pallas_call | solution.py:310
  (321 shorter events, 215.5 us)
Async XLA Ops:
  42.1 37.1 %all-to-all-start = ((bf16[16,192,256]{2,1,0:T(8,128)(2,1)}), bf16[16,192,256]{2,1,0:T(8,128)(2,1)S(1)}, u32[]{:S(2)}, u32[]{:S(2)}) async-start(bf16[16,192,256]{2,1,0:T(8,128)(2,1)} %get-tuple-element.133), calls=%async_computation | async-start | bytes 3145728 | tf_op jit(solution)/shard_map/all_to_all | solution.py:1133
  74.8 35.8 %collective-permute-start.10 = (bf16[128,3328]{1,0:T(8,128)(2,1)S(1)}, bf16[128,3328]{1,0:T(8,128)(2,1)}, u32[]{:S(2)}, u32[]{:S(2)}) collective-permute-start(bf16[128,3328]{1,0:T(8,128)(2,1)S(1)} %collective-permute-done.8.refs_4_.refs_5_.refs_6_.refs_7_), channel_id=1, source_target_pairs={{0,4},{2,6},{4,0},{6,2},{8,12},{10,14},{12,8},{14,10},{16,20},{18,... | collective-permute-start | bytes 2555912 | tf_op jit(solution)/shard_map/ppermute | solution.py:261
  98.4 41.7 %collective-permute-start.19 = (bf16[2304,256]{1,0:T(8,128)(2,1)}, bf16[2304,256]{1,0:T(8,128)(2,1)}, u32[]{:S(2)}, u32[]{:S(2)}) collective-permute-start(bf16[2304,256]{1,0:T(8,128)(2,1)} %collective-permute-done.12.refs_12_), channel_id=1, source_target_pairs={{0,4},{2,6},{4,0},{6,2},{8,12},{10,14},{12,8},{14,10},{16,20},{18,... | collective-permute-start | bytes 3538952 | tf_op jit(solution)/shard_map/ppermute | solution.py:261
  100.9 39.6 %collective-permute-start.13 = (bf16[128,4608]{1,0:T(8,128)(2,1)}, bf16[128,4608]{1,0:T(8,128)(2,1)}, u32[]{:S(2)}, u32[]{:S(2)}) collective-permute-start(bf16[128,4608]{1,0:T(8,128)(2,1)} %pad_maximum_fusion), channel_id=1, source_target_pairs={{0,1},{1,0},{2,3},{3,2},{4,5},{5,4},{6,7},{7,6},{8,9},{9,8},{10,11... | collective-permute-start | bytes 3538952 | tf_op jit(solution)/shard_map/ppermute | solution.py:270
  102.2 37.7 %all-to-all-start.1 = ((bf16[16,64,256]{2,1,0:T(8,128)(2,1)}), bf16[16,64,256]{2,1,0:T(8,128)(2,1)}, u32[]{:S(2)}, u32[]{:S(2)}) async-start(bf16[16,64,256]{2,1,0:T(8,128)(2,1)} %get-tuple-element.135), calls=%async_computation.1 | async-start | bytes 1048576 | tf_op jit(solution)/shard_map/all_to_all | solution.py:1159
  110.6 30.1 %collective-permute-start.9 = (bf16[128,3328]{1,0:T(8,128)(2,1)S(1)}, bf16[128,3328]{1,0:T(8,128)(2,1)}, u32[]{:S(2)}, u32[]{:S(2)}) collective-permute-start(bf16[128,3328]{1,0:T(8,128)(2,1)S(1)} %collective-permute-done.8.refs_4_.refs_5_.refs_6_.refs_7_), channel_id=1, source_target_pairs={{0,2},{2,0},{4,6},{6,4},{8,10},{10,8},{12,14},{14,12},{16,18},{18,... | collective-permute-start | bytes 2555912 | tf_op jit(solution)/shard_map/ppermute | solution.py:258
  169.5 34.7 %collective-permute-start.27 = (bf16[256,1792]{1,0:T(8,128)(2,1)}, bf16[256,1792]{1,0:T(8,128)(2,1)}, u32[]{:S(2)}, u32[]{:S(2)}) collective-permute-start(bf16[256,1792]{1,0:T(8,128)(2,1)} %get-tuple-element.167), channel_id=1, source_target_pairs={{0,4},{2,6},{4,0},{6,2},{8,12},{10,14},{12,8},{14,10},{16,20},{18,... | collective-permute-start | bytes 2752520 | tf_op jit(solution)/shard_map/ppermute | solution.py:261
  171.1 33.6 %collective-permute-start.26 = (bf16[256,1792]{1,0:T(8,128)(2,1)}, bf16[256,1792]{1,0:T(8,128)(2,1)}, u32[]{:S(2)}, u32[]{:S(2)}) collective-permute-start(bf16[256,1792]{1,0:T(8,128)(2,1)} %get-tuple-element.165), channel_id=1, source_target_pairs={{0,2},{2,0},{4,6},{6,4},{8,10},{10,8},{12,14},{14,12},{16,18},{18,... | collective-permute-start | bytes 2752520 | tf_op jit(solution)/shard_map/ppermute | solution.py:258
  171.1 33.0 %collective-permute-start.24 = (bf16[1024,256]{1,0:T(8,128)(2,1)}, bf16[1024,256]{1,0:T(8,128)(2,1)}, u32[]{:S(2)}, u32[]{:S(2)}) collective-permute-start(bf16[1024,256]{1,0:T(8,128)(2,1)} %get-tuple-element.161.refs_0_), channel_id=1, source_target_pairs={{0,4},{2,6},{4,0},{6,2},{8,12},{10,14},{12,8},{14,10},{16,20},{18,... | collective-permute-start | bytes 1572872 | tf_op jit(solution)/shard_map/ppermute | solution.py:261
  173.5 54.6 %collective-permute-start.28 = (bf16[256,1792]{1,0:T(8,128)(2,1)}, bf16[256,1792]{1,0:T(8,128)(2,1)}, u32[]{:S(2)}, u32[]{:S(2)}) collective-permute-start(bf16[256,1792]{1,0:T(8,128)(2,1)} %collective-permute-done.22), channel_id=1, source_target_pairs={{0,4},{2,6},{4,0},{6,2},{8,12},{10,14},{12,8},{14,10},{16,20},{18,... | collective-permute-start | bytes 2752520 | tf_op jit(solution)/shard_map/ppermute | solution.py:261
  195.3 44.6 %collective-permute-start.29 = (bf16[2,1024,256]{2,1,0:T(8,128)(2,1)}, bf16[2,1024,256]{2,1,0:T(8,128)(2,1)}, u32[]{:S(2)}, u32[]{:S(2)}) collective-permute-start(bf16[2,1024,256]{2,1,0:T(8,128)(2,1)} %pad_maximum_fusion.4.refs_0_), channel_id=1, source_target_pairs={{0,2},{2,0},{4,6},{6,4},{8,10},{10,8},{12,14},{14,12},{16,18},{18,... | collective-permute-start | bytes 3145736 | tf_op jit(solution)/shard_map/ppermute | solution.py:258
  195.3 44.5 %all-to-all-start.2 = ((bf16[16,64,256]{2,1,0:T(8,128)(2,1)}), bf16[16,64,256]{2,1,0:T(8,128)(2,1)S(1)}, u32[]{:S(2)}, u32[]{:S(2)}) async-start(bf16[16,64,256]{2,1,0:T(8,128)(2,1)} %bitcast.104), calls=%async_computation.2 | async-start | bytes 1048576 | tf_op jit(solution)/shard_map/all_to_all | solution.py:1200
  204.2 35.2 %collective-permute-start.32 = (bf16[256,1792]{1,0:T(8,128)(2,1)}, bf16[256,1792]{1,0:T(8,128)(2,1)}, u32[]{:S(2)}, u32[]{:S(2)}) collective-permute-start(bf16[256,1792]{1,0:T(8,128)(2,1)} %get-tuple-element.180), channel_id=1, source_target_pairs={{0,2},{2,0},{4,6},{6,4},{8,10},{10,8},{12,14},{14,12},{16,18},{18,... | collective-permute-start | bytes 2752520 | tf_op jit(solution)/shard_map/ppermute | solution.py:258
  228.1 32.0 %collective-permute-start.31 = (bf16[256,1792]{1,0:T(8,128)(2,1)}, bf16[256,1792]{1,0:T(8,128)(2,1)}, u32[]{:S(2)}, u32[]{:S(2)}) collective-permute-start(bf16[256,1792]{1,0:T(8,128)(2,1)} %get-tuple-element.179), channel_id=1, source_target_pairs={{0,4},{2,6},{4,0},{6,2},{8,12},{10,14},{12,8},{14,10},{16,20},{18,... | collective-permute-start | bytes 2752520 | tf_op jit(solution)/shard_map/ppermute | solution.py:261
  269.3 55.5 %all-to-all-start.3 = ((bf16[16,192,256]{2,1,0:T(8,128)(2,1)}), bf16[16,192,256]{2,1,0:T(8,128)(2,1)S(1)}, u32[]{:S(2)}, u32[]{:S(2)}) async-start(bf16[16,192,256]{2,1,0:T(8,128)(2,1)} %shard_map.201), calls=%async_computation.3 | async-start | bytes 3145728 | tf_op jit(solution)/shard_map/all_to_all | solution.py:1223
  285.7 33.8 %collective-permute-start.38 = (bf16[2,256,1152]{2,1,0:T(8,128)(2,1)}, bf16[2,256,1152]{2,1,0:T(8,128)(2,1)}, u32[]{:S(2)}, u32[]{:S(2)}) collective-permute-start(bf16[2,256,1152]{2,1,0:T(8,128)(2,1)} %get-tuple-element.193), channel_id=1, source_target_pairs={{0,1},{1,0},{2,3},{3,2},{4,5},{5,4},{6,7},{7,6},{8,9},{9,8},{10,11... | collective-permute-start | bytes 3538952 | tf_op jit(solution)/shard_map/ppermute | solution.py:270
  286.9 32.5 %collective-permute-start.37 = (bf16[2,1024,256]{2,1,0:T(8,128)(2,1)}, bf16[2,1024,256]{2,1,0:T(8,128)(2,1)}, u32[]{:S(2)}, u32[]{:S(2)}) collective-permute-start(bf16[2,1024,256]{2,1,0:T(8,128)(2,1)} %pad_maximum_fusion.4.refs_0_), channel_id=1, source_target_pairs={{0,4},{2,6},{4,0},{6,2},{8,12},{10,14},{12,8},{14,10},{16,20},{18,... | collective-permute-start | bytes 3145736 | tf_op jit(solution)/shard_map/ppermute | solution.py:261
  338.5 30.2 %collective-permute-start.41 = (bf16[768,256]{1,0:T(8,128)(2,1)S(1)}, bf16[768,256]{1,0:T(8,128)(2,1)S(1)}, u32[]{:S(2)}, u32[]{:S(2)}) collective-permute-start(bf16[768,256]{1,0:T(8,128)(2,1)S(1)} %copy-done.53), channel_id=1, source_target_pairs={{0,4},{2,6},{4,0},{6,2},{8,12},{10,14},{12,8},{14,10},{16,20},{18,... | collective-permute-start | bytes 1179656 | tf_op jit(solution)/shard_map/ppermute | solution.py:261
  366.7 40.1 %collective-permute-start.50 = (bf16[288,1024]{1,0:T(8,128)(2,1)S(1)}, bf16[288,1024]{1,0:T(8,128)(2,1)S(1)}, u32[]{:S(2)}, u32[]{:S(2)}) collective-permute-start(bf16[288,1024]{1,0:T(8,128)(2,1)S(1)} %fusion.9), channel_id=1, source_target_pairs={{0,8},{2,10},{4,12},{6,14},{8,0},{10,2},{12,4},{14,6},{16,24},{18,... | collective-permute-start | bytes 1769480 | tf_op jit(solution)/shard_map/ppermute | solution.py:264
  368.7 38.3 %collective-permute-start.49 = (bf16[256,1152]{1,0:T(8,128)(2,1)S(1)}, bf16[256,1152]{1,0:T(8,128)(2,1)S(1)}, u32[]{:S(2)}, u32[]{:S(2)}) collective-permute-start(bf16[256,1152]{1,0:T(8,128)(2,1)S(1)} %fusion.1), channel_id=1, source_target_pairs={{0,16},{2,18},{4,20},{6,22},{8,24},{10,26},{12,28},{14,30},{16,0},... | collective-permute-start | bytes 1769480 | tf_op jit(solution)/shard_map/ppermute | solution.py:267
  408.6 34.4 %collective-permute-start.52 = (bf16[272,768]{1,0:T(8,128)(2,1)S(1)}, bf16[272,768]{1,0:T(8,128)(2,1)S(1)}, u32[]{:S(2)}, u32[]{:S(2)}) collective-permute-start(bf16[272,768]{1,0:T(8,128)(2,1)S(1)} %fusion.11), channel_id=1, source_target_pairs={{0,8},{2,10},{4,12},{6,14},{8,0},{10,2},{12,4},{14,6},{16,24},{18,... | collective-permute-start | bytes 1253384 | tf_op jit(solution)/shard_map/ppermute | solution.py:264
  409.4 33.7 %collective-permute-start.56 = (bf16[288,1024]{1,0:T(8,128)(2,1)S(1)}, bf16[288,1024]{1,0:T(8,128)(2,1)S(1)}, u32[]{:S(2)}, u32[]{:S(2)}) collective-permute-start(bf16[288,1024]{1,0:T(8,128)(2,1)S(1)} %fusion), channel_id=1, source_target_pairs={{0,16},{2,18},{4,20},{6,22},{8,24},{10,26},{12,28},{14,30},{16,0},... | collective-permute-start | bytes 1769480 | tf_op jit(solution)/shard_map/ppermute | solution.py:267
  485.9 32.7 %collective-permute-start.63 = (bf16[2,272,768]{2,1,0:T(8,128)(2,1)S(1)}, bf16[2,272,768]{2,1,0:T(8,128)(2,1)}, u32[]{:S(2)}, u32[]{:S(2)}) collective-permute-start(bf16[2,272,768]{2,1,0:T(8,128)(2,1)S(1)} %pad_maximum_fusion.6.refs_0_), channel_id=1, source_target_pairs={{0,4},{2,6},{4,0},{6,2},{8,12},{10,14},{12,8},{14,10},{16,20},{18,... | collective-permute-start | bytes 2506760 | tf_op jit(solution)/shard_map/ppermute | solution.py:261
  487.3 31.8 %collective-permute-start.67 = (bf16[2,288,1024]{2,1,0:T(8,128)(2,1)S(1)}, bf16[2,288,1024]{2,1,0:T(8,128)(2,1)}, u32[]{:S(2)}, u32[]{:S(2)}) collective-permute-start(bf16[2,288,1024]{2,1,0:T(8,128)(2,1)S(1)} %pad_maximum_fusion.3.refs_0_), channel_id=1, source_target_pairs={{0,2},{2,0},{4,6},{6,4},{8,10},{10,8},{12,14},{14,12},{16,18},{18,... | collective-permute-start | bytes 3538952 | tf_op jit(solution)/shard_map/ppermute | solution.py:258
  (107 other events, 1476.1 us)

commit v17 on v15

--- a/solution.py
+++ b/solution.py
@@ -921,7 +921,7 @@
 
 def place_gate_up(here, chunk, pieces, before):
     _, rows, wide = pieces[0].shape
-    step = 64
+    step = 128
     blocks = rows // step
 
     def source(i, here):

time: 546 us -> 546 us (level)
  transfers between devices with their start and end apart: 74 -> 74, of which waited for: 31 -> 31; matrix products, arithmetic and copies ran while one was open for 8% -> 8% of each run, Pallas kernels for 25% -> 24%
where the time goes in v17:
time: 546 us; the launch traced here: 537 us
  waiting for transfers between devices  254 us (47%)
  Pallas kernels  145 us (27%)
  starting transfers between devices  70.3 us (13%)
  local copies, waits for them, and re-layouts  49.2 us (9%)
  other arithmetic  16.3 us (3%)
    pallas_call x13, Pallas kernels, call_with_here(): pl.pallas_call(kernel, grid_spec=pltpu.PrefetchScalarGridSpec(num_scalar_...  116 us
    ppermute x18, waiting for transfers between devices, over_y(): return lax.ppermute(value, 'ctx', self.route(lambda z, y, c: (z, 1 - y, c)))  89.4 us
    ppermute x8, waiting for transfers between devices, over_z(): return lax.ppermute(value, 'ctx', self.route(lambda z, y, c: (z ^ 1, y, c)))  67.4 us
    ppermute x10, waiting for transfers between devices, over_x(): return lax.ppermute(value, 'fsdp', [(0, 1), (1, 0)])  35.9 us
    pallas_call x2, Pallas kernels, kernel_call(): pl.pallas_call(kernel, out_shape=outs, in_specs=[smem] * len(tables) + [v...  29 us
    all_to_all x1, waiting for transfers between devices, on_block(): lax.all_to_all(attn_sent, 'ctx', 0, 0, tiled=True)  28.8 us
    unnamed x120, local copies, waits for them, and re-layouts  21.3 us
    ppermute x18, starting transfers between devices, over_y(): return lax.ppermute(value, 'ctx', self.route(lambda z, y, c: (z, 1 - y, c)))  20.4 us
  transfers between devices with their start and end apart: 74, of which 31 were waited for; matrix products, arithmetic and copies ran while one was open for 8% of the time, Pallas kernels for 24%

profile of v17, /device:TPU:0, one launch (start us, length us, event | category | flops | bytes accessed | tf_op | source)
XLA Modules:
  0.0 537.3 jit_solution(13042928332820061293)
XLA Ops:
  22.0 8.9 %copy.71 = bf16[512,2,4608]{2,0,1:T(8,128)(2,1)} copy(bf16[512,2,4608]{2,1,0:T(2,128)(2,1)} %param.15) | data formatting | bytes 18874368 | tf_op jit(solution)/shard_map/optimization_barrier | solution.py:295
  53.8 16.9 %collective-permute-done.8.refs_4_.refs_5_.refs_6_.refs_7_ = bf16[128,3328]{1,0:T(8,128)(2,1)S(1)} collective-permute-done((bf16[128,3328]{1,0:T(8,128)(2,1)}, bf16[128,3328]{1,0:T(8,128)(2,1)S(1)}, u32[]{:S(2)}, u32[]{:S(2)}) %collective-permute-start.8) | collective-permute-done | bytes 852000 | tf_op jit(solution)/shard_map/ppermute | solution.py:270
  80.3 12.4 %shard_map.196 = (bf16[16,64,256]{2,1,0:T(8,128)(2,1)}, bf16[4096,64]{1,0:T(8,128)(2,1)S(1)}, bf16[64,4096]{1,0:T(8,128)(2,1)S(1)}, bf16[4096,64]{1,0:T(8,128)(2...) custom-call(s32[32]{0:T(128)S(1)} %broadcast_add_fusion.q_slot, ...), custom_call_target="tpu_custom_call" | custom-call | flops 1 | bytes 1 | tf_op jit(solution)/shard_map/pallas_call | solution.py:226
  111.2 28.8 %all-to-all-done.1 = bf16[16,64,256]{2,1,0:T(8,128)(2,1)} async-done(((bf16[16,64,256]{2,1,0:T(8,128)(2,1)}), bf16[16,64,256]{2,1,0:T(8,128)(2,1)}, u32[]{:S(2)}, u32[]{:S(2)}) %all-to-all-start.1) | async-done | bytes 524320 | tf_op jit(solution)/shard_map/all_to_all | solution.py:1153
  152.0 17.2 %shard_map.198 = (bf16[256,1792]{1,0:T(8,128)(2,1)}, bf16[256,1792]{1,0:T(8,128)(2,1)}, bf16[256,1792]{1,0:T(8,128)(2,1)}, bf16[256,1792]{1,0:T(8,128)(2,1)}, f32[256,1024]{1,0:T(8,128)}, /*index=5*/f32[256,1024]{1,0:T(8,128)}) custom-call(s32[4]{0:T(128)} %pad_add_fusion.here, bf16[256,1024]{1,0:T(8,128)(2,1)} %get-tuple-element.139.refs_0_, ...), custom_call_target="tpu_custom_call" | custom-call | flops 1 | bytes 1 | tf_op jit(solution)/shard_map/pallas_call | solution.py:310
  176.4 17.1 %shard_map.199 = (bf16[256,1792]{1,0:T(8,128)(2,1)}, bf16[256,1792]{1,0:T(8,128)(2,1)}, bf16[256,1792]{1,0:T(8,128)(2,1)}, bf16[256,1792]{1,0:T(8,128)(2,1)}, bf...) custom-call(s32[4]{0:T(128)} %pad_add_fusion.here, ...), custom_call_target="tpu_custom_call" | custom-call | flops 1 | bytes 1 | tf_op jit(solution)/shard_map/pallas_call | solution.py:310
  205.1 23.3 %collective-permute-done.28.refs_7_ = bf16[256,1792]{1,0:T(8,128)(2,1)} collective-permute-done((bf16[256,1792]{1,0:T(8,128)(2,1)}, bf16[256,1792]{1,0:T(8,128)(2,1)}, u32[]{:S(2)}, u32[]{:S(2)}) %collective-permute-start.28) | collective-permute-done | bytes 917536 | tf_op jit(solution)/shard_map/ppermute | solution.py:261
  231.6 7.5 %shard_map.200 = (bf16[2,256,1152]{2,1,0:T(8,128)(2,1)}, f32[2,256,1152]{2,1,0:T(8,128)}) custom-call(s32[4]{0:T(128)} %pad_add_fusion.here, bf16[1024,256]{1,0:T(8,128)(2,1)} %get-tuple-element.160.refs_0_, bf16[1024,256]{1,0:T(8,128)(2,1)} %copy-done.52, bf16[1024,256]{1,0:T(8,128)(2,1)} %collective-permute-done.24.refs_2_, bf16[1024,256]{1,0:T(8,128)(2,1)} %copy-done.51, ...), custom_call_target="tpu_custom_call" | custom-call | flops 3000000000 | bytes 1 | tf_op jit(solution)/shard_map/pallas_call | solution.py:310
  243.6 16.6 %shard_map.201 = bf16[16,192,256]{2,1,0:T(8,128)(2,1)} custom-call(s32[32]{0:T(128)S(1)} %broadcast_add_fusion.q_slot, s32[32]{0:T(128)S(1)} %get-tuple-element.241.kv_slot, s32[8]{0:T(128)S(1)} %get-tuple-element.262.first, s32[8]{0:T(128)S(1)} %get-tuple-element.263.last, bf16[16,64,256]{2,1,0:T(8,128)(2,1)S(1)} %all-to-all-done.2.d_ref, ...), custom_call_target="tpu_custom_call" | custom-call | flops 24999999488 | bytes 1 | tf_op jit(solution)/shard_map/pallas_call | solution.py:226
  278.5 7.5 %shard_map.203 = (bf16[2,256,1152]{2,1,0:T(8,128)(2,1)}, f32[2,256,1152]{2,1,0:T(8,128)}) custom-call(s32[4]{0:T(128)} %pad_add_fusion.here, bf16[1024,256]{1,0:T(8,128)(2,1)} %get-tuple-element.160.refs_0_, bf16[1024,256]{1,0:T(8,128)(2,1)} %copy-done.52, bf16[1024,256]{1,0:T(8,128)(2,1)} %collective-permute-done.24.refs_2_, bf16[1024,256]{1,0:T(8,128)(2,1)} %copy-done.51, ...), custom_call_target="tpu_custom_call" | custom-call | flops 3000000000 | bytes 1 | tf_op jit(solution)/shard_map/pallas_call | solution.py:310
  293.0 9.8 %shard_map.202 = (bf16[2,288,1024]{2,1,0:T(8,128)(2,1)}, f32[2,288,1024]{2,1,0:T(8,128)}) custom-call(s32[4]{0:T(128)} %pad_add_fusion.here, bf16[256,1024]{1,0:T(8,128)(2,1)} %bitcast.97, bf16[256,1024]{1,0:T(8,128)(2,1)} %copy-done.53, bf16[256,1024]{1,0:T(8,128)(2,1)} %collective-permute-done.1.refs_2_, bf16[256,1024]{1,0:T(8,128)(2,1)} %copy-done.54, ...), custom_call_target="tpu_custom_call" | custom-call | flops 3000000000 | bytes 1 | tf_op jit(solution)/shard_map/pallas_call | solution.py:310
  302.8 12.5 %collective-permute-done.42 = bf16[256,1152]{1,0:T(8,128)(2,1)S(1)} collective-permute-done((bf16[256,1152]{1,0:T(8,128)(2,1)S(1)}, bf16[256,1152]{1,0:T(8,128)(2,1)S(1)}, u32[]{:S(2)}, u32[]{:S(2)}) %collective-permute-start.42) | collective-permute-done | bytes 589856 | tf_op jit(solution)/shard_map/ppermute | solution.py:264
  326.2 8.6 %shard_map.204 = (bf16[768,256]{1,0:T(8,128)(2,1)}, bf16[768,256]{1,0:T(8,128)(2,1)}, bf16[768,256]{1,0:T(8,128)(2,1)}, bf16[768,256]{1,0:T(8,128)(2,1)}, f32[256,1024]{1,0:T(8,128)}, /*index=5*/f32[8,1024]{1,0:T(8,128)}) custom-call(s32[4]{0:T(128)} %pad_add_fusion.here, bf16[16,192,256]{2,1,0:T(8,128)(2,1)} %copy-done.8, ...), custom_call_target="tpu_custom_call" | custom-call | flops 1 | bytes 1 | tf_op jit(solution)/shard_map/pallas_call | solution.py:310
  348.3 17.1 %collective-permute-done.43 = bf16[256,1152]{1,0:T(8,128)(2,1)S(1)} collective-permute-done((bf16[256,1152]{1,0:T(8,128)(2,1)S(1)}, bf16[256,1152]{1,0:T(8,128)(2,1)S(1)}, u32[]{:S(2)}, u32[]{:S(2)}) %collective-permute-start.43) | collective-permute-done | bytes 589856 | tf_op jit(solution)/shard_map/ppermute | solution.py:267
  369.0 7.3 %collective-permute-done.47.refs_7_ = bf16[768,256]{1,0:T(8,128)(2,1)S(1)} collective-permute-done((bf16[768,256]{1,0:T(8,128)(2,1)S(1)}, bf16[768,256]{1,0:T(8,128)(2,1)S(1)}, u32[]{:S(2)}, u32[]{:S(2)}) %collective-permute-start.47) | collective-permute-done | bytes 393248 | tf_op jit(solution)/shard_map/ppermute | solution.py:261
  377.1 6.9 %shard_map.205 = (bf16[2,272,768]{2,1,0:T(8,128)(2,1)}, f32[2,272,768]{2,1,0:T(8,128)}) custom-call(s32[4]{0:T(128)} %pad_add_fusion.here, bf16[2,1024,256]{2,1,0:T(8,128)(2,1)} %pad_maximum_fusion.4.refs_0_, bf16[2,1024,256]{2,1,0:T(8,128)(2,1)} %collective-permute-done.29.refs_1_, bf16[2,1024,256]{2,1,0:T(8,128)(2,1)} %collective-permute-done.37.refs_2_, ...), custom_call_target="tpu_custom_call" | custom-call | flops 3000000000 | bytes 1 | tf_op jit(solution)/shard_map/pallas_call | solution.py:310
  385.0 10.6 %collective-permute-done.51 = bf16[256,1152]{1,0:T(8,128)(2,1)S(1)} collective-permute-done((bf16[256,1152]{1,0:T(8,128)(2,1)S(1)}, bf16[256,1152]{1,0:T(8,128)(2,1)S(1)}, u32[]{:S(2)}, u32[]{:S(2)}) %collective-permute-start.51) | collective-permute-done | bytes 589856 | tf_op jit(solution)/shard_map/ppermute | solution.py:264
  396.8 10.2 %collective-permute-done.50 = bf16[288,1024]{1,0:T(8,128)(2,1)S(1)} collective-permute-done((bf16[288,1024]{1,0:T(8,128)(2,1)S(1)}, bf16[288,1024]{1,0:T(8,128)(2,1)S(1)}, u32[]{:S(2)}, u32[]{:S(2)}) %collective-permute-start.50) | collective-permute-done | bytes 589856 | tf_op jit(solution)/shard_map/ppermute | solution.py:264
  410.8 10.5 %collective-permute-done.54.refs_2_ = bf16[2,256,1152]{2,1,0:T(8,128)(2,1)S(1)} collective-permute-done((bf16[2,256,1152]{2,1,0:T(8,128)(2,1)S(1)}, bf16[2,256,1152]{2,1,0:T(8,128)(2,1)S(1)}, u32[]{:S(2)}, u32[]{:S(2)}) %collective-permute-start.54) | collective-permute-done | bytes 1179680 | tf_op jit(solution)/shard_map/ppermute | solution.py:261
  421.4 15.1 %collective-permute-done.53 = bf16[256,1152]{1,0:T(8,128)(2,1)S(1)} collective-permute-done((bf16[256,1152]{1,0:T(8,128)(2,1)S(1)}, bf16[256,1152]{1,0:T(8,128)(2,1)S(1)}, u32[]{:S(2)}, u32[]{:S(2)}) %collective-permute-start.53) | collective-permute-done | bytes 589856 | tf_op jit(solution)/shard_map/ppermute | solution.py:264
  447.9 8.0 %shard_map.206.refs_4_ = f32[512,2,4608]{2,1,0:T(2,128)} custom-call(s32[4]{0:T(128)} %pad_add_fusion.here, bf16[2,256,1152]{2,1,0:T(8,128)(2,1)} %copy-done.17, bf16[2,256,1152]{2,1,0:T(8,128)(2,1)} %copy-done.30, bf16[2,256,1152]{2,1,0:T(8,128)(2,1)} %copy-done.29, bf16[2,256,1152]{2,1,0:T(8,128)(2,1)} %copy-done.31), custom_call_target="tpu_custom_call" | custom-call | flops 1 | bytes 1 | tf_op jit(solution)/shard_map/pallas_call | solution.py:310
  478.5 7.8 %shard_map.207 = f32[512,2,4608]{2,1,0:T(2,128)} custom-call(s32[4]{0:T(128)} %pad_add_fusion.here, bf16[2,256,1152]{2,1,0:T(8,128)(2,1)} %copy-done.16, bf16[2,256,1152]{2,1,0:T(8,128)(2,1)} %copy-done.32, bf16[2,256,1152]{2,1,0:T(8,128)(2,1)} %copy-done.28, bf16[2,256,1152]{2,1,0:T(8,128)(2,1)} %copy-done.33, ...), custom_call_target="tpu_custom_call", output_to_operand_aliasing={{}: (5, {})} | custom-call | flops 1 | bytes 1 | tf_op jit(solution)/shard_map/pallas_call | solution.py:310
  486.3 27.7 %collective-permute-done.63.refs_2_ = bf16[2,272,768]{2,1,0:T(8,128)(2,1)} collective-permute-done((bf16[2,272,768]{2,1,0:T(8,128)(2,1)S(1)}, bf16[2,272,768]{2,1,0:T(8,128)(2,1)}, u32[]{:S(2)}, u32[]{:S(2)}) %collective-permute-start.63) | collective-permute-done | bytes 835616 | tf_op jit(solution)/shard_map/ppermute | solution.py:261
  529.0 7.9 %shard_map.209 = f32[2304,1024]{1,0:T(8,128)} custom-call(s32[4]{0:T(128)} %pad_add_fusion.here, bf16[2,288,1024]{2,1,0:T(8,128)(2,1)} %copy-done.18, bf16[2,288,1024]{2,1,0:T(8,128)(2,1)} %copy-done.34, bf16[2,288,1024]{2,1,0:T(8,128)(2,1)} %collective-permute-done.68.refs_2_, bf16[2,288,1024]{2,1,0:T(8,128)(2,1)} %collective-permute-done.69.refs_3_), custom_call_target="tpu_custom_call" | custom-call | flops 1 | bytes 1 | tf_op jit(solution)/shard_map/pallas_call | solution.py:310
  (325 shorter events, 219.2 us)
Async XLA Ops:
  42.1 37.1 %all-to-all-start = ((bf16[16,192,256]{2,1,0:T(8,128)(2,1)}), bf16[16,192,256]{2,1,0:T(8,128)(2,1)S(1)}, u32[]{:S(2)}, u32[]{:S(2)}) async-start(bf16[16,192,256]{2,1,0:T(8,128)(2,1)} %get-tuple-element.132), calls=%async_computation | async-start | bytes 3145728 | tf_op jit(solution)/shard_map/all_to_all | solution.py:1127
  74.9 35.8 %collective-permute-start.10 = (bf16[128,3328]{1,0:T(8,128)(2,1)S(1)}, bf16[128,3328]{1,0:T(8,128)(2,1)}, u32[]{:S(2)}, u32[]{:S(2)}) collective-permute-start(bf16[128,3328]{1,0:T(8,128)(2,1)S(1)} %collective-permute-done.8.refs_4_.refs_5_.refs_6_.refs_7_), channel_id=1, source_target_pairs={{0,4},{2,6},{4,0},{6,2},{8,12},{10,14},{12,8},{14,10},{16,20},{18,... | collective-permute-start | bytes 2555912 | tf_op jit(solution)/shard_map/ppermute | solution.py:261
  98.5 41.7 %collective-permute-start.19 = (bf16[2304,256]{1,0:T(8,128)(2,1)}, bf16[2304,256]{1,0:T(8,128)(2,1)}, u32[]{:S(2)}, u32[]{:S(2)}) collective-permute-start(bf16[2304,256]{1,0:T(8,128)(2,1)} %collective-permute-done.12.refs_12_), channel_id=1, source_target_pairs={{0,4},{2,6},{4,0},{6,2},{8,12},{10,14},{12,8},{14,10},{16,20},{18,... | collective-permute-start | bytes 3538952 | tf_op jit(solution)/shard_map/ppermute | solution.py:261
  100.9 39.6 %collective-permute-start.13 = (bf16[128,4608]{1,0:T(8,128)(2,1)}, bf16[128,4608]{1,0:T(8,128)(2,1)}, u32[]{:S(2)}, u32[]{:S(2)}) collective-permute-start(bf16[128,4608]{1,0:T(8,128)(2,1)} %pad_maximum_fusion), channel_id=1, source_target_pairs={{0,1},{1,0},{2,3},{3,2},{4,5},{5,4},{6,7},{7,6},{8,9},{9,8},{10,11... | collective-permute-start | bytes 3538952 | tf_op jit(solution)/shard_map/ppermute | solution.py:270
  102.3 37.7 %all-to-all-start.1 = ((bf16[16,64,256]{2,1,0:T(8,128)(2,1)}), bf16[16,64,256]{2,1,0:T(8,128)(2,1)}, u32[]{:S(2)}, u32[]{:S(2)}) async-start(bf16[16,64,256]{2,1,0:T(8,128)(2,1)} %get-tuple-element.134), calls=%async_computation.1 | async-start | bytes 1048576 | tf_op jit(solution)/shard_map/all_to_all | solution.py:1153
  169.8 34.7 %collective-permute-start.27 = (bf16[256,1792]{1,0:T(8,128)(2,1)}, bf16[256,1792]{1,0:T(8,128)(2,1)}, u32[]{:S(2)}, u32[]{:S(2)}) collective-permute-start(bf16[256,1792]{1,0:T(8,128)(2,1)} %get-tuple-element.166), channel_id=1, source_target_pairs={{0,4},{2,6},{4,0},{6,2},{8,12},{10,14},{12,8},{14,10},{16,20},{18,... | collective-permute-start | bytes 2752520 | tf_op jit(solution)/shard_map/ppermute | solution.py:261
  171.4 33.6 %collective-permute-start.26 = (bf16[256,1792]{1,0:T(8,128)(2,1)}, bf16[256,1792]{1,0:T(8,128)(2,1)}, u32[]{:S(2)}, u32[]{:S(2)}) collective-permute-start(bf16[256,1792]{1,0:T(8,128)(2,1)} %get-tuple-element.164), channel_id=1, source_target_pairs={{0,2},{2,0},{4,6},{6,4},{8,10},{10,8},{12,14},{14,12},{16,18},{18,... | collective-permute-start | bytes 2752520 | tf_op jit(solution)/shard_map/ppermute | solution.py:258
  171.5 33.0 %collective-permute-start.24 = (bf16[1024,256]{1,0:T(8,128)(2,1)}, bf16[1024,256]{1,0:T(8,128)(2,1)}, u32[]{:S(2)}, u32[]{:S(2)}) collective-permute-start(bf16[1024,256]{1,0:T(8,128)(2,1)} %get-tuple-element.160.refs_0_), channel_id=1, source_target_pairs={{0,4},{2,6},{4,0},{6,2},{8,12},{10,14},{12,8},{14,10},{16,20},{18,... | collective-permute-start | bytes 1572872 | tf_op jit(solution)/shard_map/ppermute | solution.py:261
  173.8 54.6 %collective-permute-start.28 = (bf16[256,1792]{1,0:T(8,128)(2,1)}, bf16[256,1792]{1,0:T(8,128)(2,1)}, u32[]{:S(2)}, u32[]{:S(2)}) collective-permute-start(bf16[256,1792]{1,0:T(8,128)(2,1)} %collective-permute-done.22), channel_id=1, source_target_pairs={{0,4},{2,6},{4,0},{6,2},{8,12},{10,14},{12,8},{14,10},{16,20},{18,... | collective-permute-start | bytes 2752520 | tf_op jit(solution)/shard_map/ppermute | solution.py:261
  195.6 44.5 %collective-permute-start.29 = (bf16[2,1024,256]{2,1,0:T(8,128)(2,1)}, bf16[2,1024,256]{2,1,0:T(8,128)(2,1)}, u32[]{:S(2)}, u32[]{:S(2)}) collective-permute-start(bf16[2,1024,256]{2,1,0:T(8,128)(2,1)} %pad_maximum_fusion.4.refs_0_), channel_id=1, source_target_pairs={{0,2},{2,0},{4,6},{6,4},{8,10},{10,8},{12,14},{14,12},{16,18},{18,... | collective-permute-start | bytes 3145736 | tf_op jit(solution)/shard_map/ppermute | solution.py:258
  195.7 44.4 %all-to-all-start.2 = ((bf16[16,64,256]{2,1,0:T(8,128)(2,1)}), bf16[16,64,256]{2,1,0:T(8,128)(2,1)S(1)}, u32[]{:S(2)}, u32[]{:S(2)}) async-start(bf16[16,64,256]{2,1,0:T(8,128)(2,1)} %bitcast.104), calls=%async_computation.2 | async-start | bytes 1048576 | tf_op jit(solution)/shard_map/all_to_all | solution.py:1194
  204.5 35.2 %collective-permute-start.32 = (bf16[256,1792]{1,0:T(8,128)(2,1)}, bf16[256,1792]{1,0:T(8,128)(2,1)}, u32[]{:S(2)}, u32[]{:S(2)}) collective-permute-start(bf16[256,1792]{1,0:T(8,128)(2,1)} %get-tuple-element.179), channel_id=1, source_target_pairs={{0,2},{2,0},{4,6},{6,4},{8,10},{10,8},{12,14},{14,12},{16,18},{18,... | collective-permute-start | bytes 2752520 | tf_op jit(solution)/shard_map/ppermute | solution.py:258
  228.4 31.9 %collective-permute-start.31 = (bf16[256,1792]{1,0:T(8,128)(2,1)}, bf16[256,1792]{1,0:T(8,128)(2,1)}, u32[]{:S(2)}, u32[]{:S(2)}) collective-permute-start(bf16[256,1792]{1,0:T(8,128)(2,1)} %get-tuple-element.178), channel_id=1, source_target_pairs={{0,4},{2,6},{4,0},{6,2},{8,12},{10,14},{12,8},{14,10},{16,20},{18,... | collective-permute-start | bytes 2752520 | tf_op jit(solution)/shard_map/ppermute | solution.py:261
  269.6 55.5 %all-to-all-start.3 = ((bf16[16,192,256]{2,1,0:T(8,128)(2,1)}), bf16[16,192,256]{2,1,0:T(8,128)(2,1)S(1)}, u32[]{:S(2)}, u32[]{:S(2)}) async-start(bf16[16,192,256]{2,1,0:T(8,128)(2,1)} %shard_map.201), calls=%async_computation.3 | async-start | bytes 3145728 | tf_op jit(solution)/shard_map/all_to_all | solution.py:1217
  286.0 33.8 %collective-permute-start.38 = (bf16[2,256,1152]{2,1,0:T(8,128)(2,1)}, bf16[2,256,1152]{2,1,0:T(8,128)(2,1)}, u32[]{:S(2)}, u32[]{:S(2)}) collective-permute-start(bf16[2,256,1152]{2,1,0:T(8,128)(2,1)} %get-tuple-element.192), channel_id=1, source_target_pairs={{0,1},{1,0},{2,3},{3,2},{4,5},{5,4},{6,7},{7,6},{8,9},{9,8},{10,11... | collective-permute-start | bytes 3538952 | tf_op jit(solution)/shard_map/ppermute | solution.py:270
  287.2 32.5 %collective-permute-start.37 = (bf16[2,1024,256]{2,1,0:T(8,128)(2,1)}, bf16[2,1024,256]{2,1,0:T(8,128)(2,1)}, u32[]{:S(2)}, u32[]{:S(2)}) collective-permute-start(bf16[2,1024,256]{2,1,0:T(8,128)(2,1)} %pad_maximum_fusion.4.refs_0_), channel_id=1, source_target_pairs={{0,4},{2,6},{4,0},{6,2},{8,12},{10,14},{12,8},{14,10},{16,20},{18,... | collective-permute-start | bytes 3145736 | tf_op jit(solution)/shard_map/ppermute | solution.py:261
  366.9 40.1 %collective-permute-start.50 = (bf16[288,1024]{1,0:T(8,128)(2,1)S(1)}, bf16[288,1024]{1,0:T(8,128)(2,1)S(1)}, u32[]{:S(2)}, u32[]{:S(2)}) collective-permute-start(bf16[288,1024]{1,0:T(8,128)(2,1)S(1)} %fusion.9), channel_id=1, source_target_pairs={{0,8},{2,10},{4,12},{6,14},{8,0},{10,2},{12,4},{14,6},{16,24},{18,... | collective-permute-start | bytes 1769480 | tf_op jit(solution)/shard_map/ppermute | solution.py:264
  369.0 38.3 %collective-permute-start.49 = (bf16[256,1152]{1,0:T(8,128)(2,1)S(1)}, bf16[256,1152]{1,0:T(8,128)(2,1)S(1)}, u32[]{:S(2)}, u32[]{:S(2)}) collective-permute-start(bf16[256,1152]{1,0:T(8,128)(2,1)S(1)} %fusion.1), channel_id=1, source_target_pairs={{0,16},{2,18},{4,20},{6,22},{8,24},{10,26},{12,28},{14,30},{16,0},... | collective-permute-start | bytes 1769480 | tf_op jit(solution)/shard_map/ppermute | solution.py:267
  408.9 34.4 %collective-permute-start.52 = (bf16[272,768]{1,0:T(8,128)(2,1)S(1)}, bf16[272,768]{1,0:T(8,128)(2,1)S(1)}, u32[]{:S(2)}, u32[]{:S(2)}) collective-permute-start(bf16[272,768]{1,0:T(8,128)(2,1)S(1)} %fusion.11), channel_id=1, source_target_pairs={{0,8},{2,10},{4,12},{6,14},{8,0},{10,2},{12,4},{14,6},{16,24},{18,... | collective-permute-start | bytes 1253384 | tf_op jit(solution)/shard_map/ppermute | solution.py:264
  409.7 33.7 %collective-permute-start.56 = (bf16[288,1024]{1,0:T(8,128)(2,1)S(1)}, bf16[288,1024]{1,0:T(8,128)(2,1)S(1)}, u32[]{:S(2)}, u32[]{:S(2)}) collective-permute-start(bf16[288,1024]{1,0:T(8,128)(2,1)S(1)} %fusion), channel_id=1, source_target_pairs={{0,16},{2,18},{4,20},{6,22},{8,24},{10,26},{12,28},{14,30},{16,0},... | collective-permute-start | bytes 1769480 | tf_op jit(solution)/shard_map/ppermute | solution.py:267
  410.8 35.0 %collective-permute-start.58 = (bf16[2,256,1152]{2,1,0:T(8,128)(2,1)S(1)}, bf16[2,256,1152]{2,1,0:T(8,128)(2,1)S(1)}, u32[]{:S(2)}, u32[]{:S(2)}) collective-permute-start(bf16[2,256,1152]{2,1,0:T(8,128)(2,1)S(1)} %pad_maximum_fusion.1.refs_0_), channel_id=1, source_target_pairs={{0,2},{2,0},{4,6},{6,4},{8,10},{10,8},{12,14},{14,12},{16,18},{18,... | collective-permute-start | bytes 3538952 | tf_op jit(solution)/shard_map/ppermute | solution.py:258
  468.1 46.5 %collective-permute-start.68 = (bf16[2,288,1024]{2,1,0:T(8,128)(2,1)S(1)}, bf16[2,288,1024]{2,1,0:T(8,128)(2,1)}, u32[]{:S(2)}, u32[]{:S(2)}) collective-permute-start(bf16[2,288,1024]{2,1,0:T(8,128)(2,1)S(1)} %pad_maximum_fusion.3.refs_0_), channel_id=1, source_target_pairs={{0,4},{2,6},{4,0},{6,2},{8,12},{10,14},{12,8},{14,10},{16,20},{18,... | collective-permute-start | bytes 3538952 | tf_op jit(solution)/shard_map/ppermute | solution.py:261
  475.8 38.2 %collective-permute-start.63 = (bf16[2,272,768]{2,1,0:T(8,128)(2,1)S(1)}, bf16[2,272,768]{2,1,0:T(8,128)(2,1)}, u32[]{:S(2)}, u32[]{:S(2)}) collective-permute-start(bf16[2,272,768]{2,1,0:T(8,128)(2,1)S(1)} %pad_maximum_fusion.6.refs_0_), channel_id=1, source_target_pairs={{0,4},{2,6},{4,0},{6,2},{8,12},{10,14},{12,8},{14,10},{16,20},{18,... | collective-permute-start | bytes 2506760 | tf_op jit(solution)/shard_map/ppermute | solution.py:261
  476.4 38.2 %collective-permute-start.62 = (bf16[2,272,768]{2,1,0:T(8,128)(2,1)S(1)}, bf16[2,272,768]{2,1,0:T(8,128)(2,1)}, u32[]{:S(2)}, u32[]{:S(2)}) collective-permute-start(bf16[2,272,768]{2,1,0:T(8,128)(2,1)S(1)} %pad_maximum_fusion.6.refs_0_), channel_id=1, source_target_pairs={{0,2},{2,0},{4,6},{6,4},{8,10},{10,8},{12,14},{14,12},{16,18},{18,... | collective-permute-start | bytes 2506760 | tf_op jit(solution)/shard_map/ppermute | solution.py:258
  (109 other events, 1414.9 us)
